TPU v7x, 32 devices: a whole 2x2x4 slice. The times are simulated.
32 devices in a mesh: groups: 2 (over x), heads: 16 (over z, y, core).
Axes of the slice: x: 2, y: 2, z: 4, core: 2. Of those that a mesh axis runs over, the one named last changes fastest.
Arguments:
- tokens: bfloat16 [64, 4, 2304], P('groups'), parts along dimension 0, may hold values from -6 to 6
- qkv_weight: bfloat16 [4608, 12288], P(('groups', 'heads')), parts along dimension 0, may hold values from -0.125 to 0.125
- gate_weight: bfloat16 [4608, 64], P(('groups', 'heads')), parts along dimension 0, may hold values from -0.125 to 0.125
- conv_weight: bfloat16 [8, 12288], P('groups', 'heads'), parts along dimension 0, may hold values from -3 to 3
- delta_state: float32 [64, 32, 128, 128], P(('groups', 'heads')), parts along dimension 0, may hold values from -0.8 to 0.8
- conv_state: float32 [64, 3, 12288], P(('groups', 'heads')), parts along dimension 0, may hold values from -6 to 6
- old_heads: int32 [32], replicated, may hold values from 0 to 31, each once
- new_units: int32 [64], replicated, may hold values from 0 to 63, each once
- slot_of: int32 [64], P('groups'), parts along dimension 0, may hold values from 0 to 31, each once
- lengths: int32 [64], P('groups'), parts along dimension 0, may hold values from 1 to 4, as said below
Outputs:
- readout: bfloat16 [64, 4, 4096], P('groups', None, 'heads'), parts along dimension 0
There are 2 independent parts, one for each index of `groups`. A program takes and returns all parts, laid end to end along the dimension named above; an argument that names none is the same for every part. Nothing has to cross between parts.
Inputs may be any that keep to these rules, and one draw needn't show every extreme that they name: `old_heads`: a permutation of the heads; old column slot p holds head old_heads[p]. `new_units`: a permutation of the head units; unit u is the half u % 2 of the values of head u // 2. `slot_of`: a permutation of the rows. `lengths`: some row decodes all 4 steps and some row only one.
All inputs are finite; a program needn't handle non-finite values.
Results may differ from a plain program's by a relative error of at most 0.001.
Values may be sent and summed in bfloat16 or wider, within the bound.
No kernel may reach another device: no remote copies, remote signals or barrier semaphores. Data moves between devices by JAX's collectives and lax.ppermute only.
A program may use at most 128 MiB of HBM per device.

v0:
```python
import functools

import jax
import jax.numpy as jnp
from jax import lax
from jax.experimental import pallas as pl
from jax.experimental.pallas import tpu as pltpu
from jax.sharding import PartitionSpec as P

D = 2304
H = 32
DK = 128
TAPS = 4
STEPS = 4
HALF = 64
UNITS = 64
LOCAL = 2
ROWS = LOCAL * STEPS
HEADS_WIDTH = H * DK
LEVELS = 32767.0
SCALE_LANES = 128
EXPONENT_AT = 64
BLOCKS = HEADS_WIDTH // DK
STATE_COPIES = 4
TAP_WIDTH = 384
TAP_BLOCKS = 3 * HEADS_WIDTH // TAP_WIDTH


norm_eps = 1e-06


def unit_tables(old_heads, new_units):
    positions = jnp.arange(H, dtype=jnp.int32)
    inverse = jnp.sum(
        jnp.where(old_heads[None, :] == positions[:, None], positions[None, :], 0), axis=1
    )
    heads_of = new_units // 2
    halves = new_units % 2
    old_slots = jnp.sum(
        jnp.where(heads_of[:, None] == positions[None, :], inverse[None, :], 0), axis=1
    )
    return (old_slots, halves)


def shift_rows(value, lag, row_step):
    if lag == 0:
        return value
    moved = pltpu.roll(value, lag, 0)
    return jnp.where(row_step >= lag, moved, 0.0)


def lane_sum(value):
    return jnp.sum(value, axis=-1, keepdims=True)


def unit_length(value):
    return value * lax.rsqrt(lane_sum(value * value) + norm_eps)


def pack_rows(total, packed_ref):
    rows, width = total.shape
    blocks = width // DK
    lane = lax.broadcasted_iota(jnp.int32, (rows, SCALE_LANES), 1)
    scales = jnp.zeros((rows, SCALE_LANES), jnp.float32)
    for block in range(blocks):
        part = total[:, block * DK : (block + 1) * DK]
        top = jnp.max(jnp.abs(part), axis=-1, keepdims=True) + 1e-30
        exponent = jnp.ceil(jnp.log2(top))
        mantissa = jnp.ceil(jnp.minimum(top * jnp.exp2(-exponent) * LEVELS, LEVELS))
        factor = LEVELS * LEVELS * jnp.exp2(-exponent) / mantissa
        coded = jnp.clip(jnp.floor(part * factor + 0.5), -LEVELS, LEVELS)
        packed_ref[:, block * DK : (block + 1) * DK] = coded.astype(jnp.int32).astype(jnp.int16)
        scales = jnp.where(lane == block, mantissa, scales)
        scales = jnp.where(lane == EXPONENT_AT + block, exponent, scales)
    packed_ref[:, width:] = scales.astype(jnp.int32).astype(jnp.int16)


def to_float(coded):
    return coded.astype(jnp.int32).astype(jnp.float32)


def steps_of(packed_ref):
    scales = to_float(packed_ref[:, packed_ref.shape[1] - SCALE_LANES :])
    exponents = pltpu.roll(scales, EXPONENT_AT, 1)
    return scales * jnp.exp2(exponents) * (1.0 / (LEVELS * LEVELS))


def unpack_block(packed_ref, steps, block):
    return to_float(packed_ref[:, block * DK : (block + 1) * DK]) * steps[:, block : block + 1]


def fold_rows(value):
    half = value.shape[1] // 2
    return jnp.concatenate([value[:, :half], value[:, half:]], axis=0)


def received(kept_ref, got_ref, steps, block):
    half = kept_ref.shape[1] // DK // 2
    rows = unpack_block(got_ref, steps, block % half)
    rows = rows[:ROWS] if block < half else rows[ROWS:]
    return kept_ref[:, block * DK : (block + 1) * DK] + rows


def activate(kept_ref, got_ref, steps, part, head, history_ref, taps_ref, twist, row_step):
    fresh = received(kept_ref, got_ref, steps, head)
    column = part * HEADS_WIDTH + head * DK
    carried = history_ref[:, column : column + DK]
    taps = taps_ref[jnp.bitwise_xor(column // TAP_WIDTH, twist)]
    inner = column % TAP_WIDTH
    total = taps[TAPS - 1 :, inner : inner + DK] * fresh
    for lag in range(1, TAPS):
        source = jnp.where(row_step >= STEPS - lag, carried, fresh)
        tap = taps[TAPS - 1 - lag : TAPS - lag, inner : inner + DK]
        total = total + tap * pltpu.roll(source, lag, 0)
    return total / (1.0 + jnp.exp(-total))


def keys_kernel(
    twist_ref, query_ref, query_got_ref, key_ref, key_got_ref, history_ref, near_ref, far_ref,
    state_hbm, beta_ref, key_seen_ref, query_seen_ref, pulls_ref, weights_ref, taps_ref,
    state_ref, sems,
):
    per_copy = H // STATE_COPIES
    copies = []
    for at in range(STATE_COPIES):
        some = pl.ds(at * per_copy, per_copy)
        copies.append(
            pltpu.make_async_copy(state_hbm.at[:, some], state_ref.at[:, some], sems.at[at])
        )
        copies[-1].start()
    twist = twist_ref[0]
    half = TAP_BLOCKS // 2
    for at in range(TAP_BLOCKS):
        source = near_ref if at < half else far_ref
        if at % 4 == 0:
            some = source[at % half * TAPS : (at % half + 4) * TAPS, :].astype(jnp.float32)
        taps_ref[at] = some[at % 4 * TAPS : (at % 4 + 1) * TAPS]
    row = lax.broadcasted_iota(jnp.int32, (ROWS, DK), 0)
    row_step = row % STEPS
    query_steps, key_steps = steps_of(query_got_ref), steps_of(key_got_ref)
    gates = received(key_ref, key_got_ref, key_steps, BLOCKS)
    for head in range(H):
        key = unit_length(
            activate(
                key_ref, key_got_ref, key_steps, 1, head, history_ref, taps_ref, twist, row_step
            )
        )
        query = unit_length(
            activate(
                query_ref, query_got_ref, query_steps, 0, head, history_ref, taps_ref, twist,
                row_step,
            )
        )
        beta_logit = jnp.broadcast_to(gates[:, head : head + 1], (ROWS, DK))
        decay_logit = jnp.broadcast_to(gates[:, H + head : H + head + 1], (ROWS, DK))
        beta = 1.0 / (1.0 + jnp.exp(-beta_logit))
        decay = 1.0 / (1.0 + jnp.exp(decay_logit))
        fades = [jnp.ones_like(decay), decay]
        for lag in range(2, STEPS + 1):
            earlier = pltpu.roll(decay, lag - 1, 0)
            fades.append(jnp.where(row_step >= lag - 1, fades[-1] * earlier, fades[-1]))
        both = jnp.concatenate([key, query], axis=0)
        if head % per_copy == 0:
            copies[head // per_copy].wait()
        both_high = both.astype(jnp.bfloat16)
        both_low = (both - both_high.astype(jnp.float32)).astype(jnp.bfloat16)
        stacked = jnp.concatenate([both_high, both_low], axis=0)
        seen = []
        for r in range(LOCAL):
            state = state_ref[r, head]
            high = state.astype(jnp.bfloat16)
            low = (state - high.astype(jnp.float32)).astype(jnp.bfloat16)
            main = jnp.dot(stacked, high, preferred_element_type=jnp.float32)
            rest = jnp.dot(both_high, low, preferred_element_type=jnp.float32)
            seen.append(main[: 2 * ROWS] + main[2 * ROWS :] + rest)
        beta_ref[head] = beta
        key_seen_ref[head] = beta * fades[STEPS] * jnp.where(
            row < STEPS, seen[0][:ROWS], seen[1][:ROWS]
        )
        query_seen_ref[head] = fades[STEPS] * jnp.where(
            row < STEPS, seen[0][ROWS:], seen[1][ROWS:]
        )
        for lag in range(STEPS):
            moved_key = shift_rows(key, lag, row_step)
            if lag:
                pulls_ref[lag - 1, head] = beta * fades[lag] * lane_sum(key * moved_key)
            weights_ref[lag, head] = fades[lag] * lane_sum(query * moved_key)


def values_kernel(
    slots_ref, halves_ref, lengths_ref, twist_ref, value_ref, value_got_ref, history_ref,
    beta_ref, key_seen_ref, query_seen_ref, pulls_ref, weights_ref, taps_ref, out_ref, heads_ref,
):
    twist = twist_ref[0]
    row = lax.broadcasted_iota(jnp.int32, (ROWS, DK), 0)
    row_step = row % STEPS
    lane = lax.broadcasted_iota(jnp.int32, (ROWS, DK), 1)
    row_length = jnp.where(row < STEPS, lengths_ref[0], lengths_ref[1])
    live = row_step < row_length
    value_steps = steps_of(value_got_ref)
    for head in range(H):
        value = activate(
            value_ref, value_got_ref, value_steps, 2, head, history_ref, taps_ref, twist, row_step
        )
        base = beta_ref[head] * value - key_seen_ref[head]
        solved = base
        for _ in range(STEPS - 1):
            following = base
            for lag in range(1, STEPS):
                following = following - pulls_ref[lag - 1, head] * shift_rows(
                    solved, lag, row_step
                )
            solved = following
        out = query_seen_ref[head]
        for lag in range(STEPS):
            out = out + weights_ref[lag, head] * shift_rows(solved, lag, row_step)
        heads_ref[head] = jnp.where(live, out, 0.0)
    for quad in range(UNITS // 4):
        joined = []
        for pair in (2 * quad, 2 * quad + 1):
            first = heads_ref[slots_ref[2 * pair]]
            second = heads_ref[slots_ref[2 * pair + 1]]
            first = jnp.where(halves_ref[2 * pair] == 0, first, pltpu.roll(first, HALF, 1))
            second = jnp.where(halves_ref[2 * pair + 1] == 0, pltpu.roll(second, HALF, 1), second)
            joined.append(jnp.where(lane < HALF, first, second))
        out_ref[quad] = jnp.concatenate(joined, axis=0).astype(jnp.bfloat16)


def run_delta(slots, halves, lengths, queries, keys, values, history, twist, taps, state):
    smem = pl.BlockSpec(memory_space=pltpu.SMEM)
    vmem = pl.BlockSpec(memory_space=pltpu.VMEM)
    params = pltpu.CompilerParams(vmem_limit_bytes=32 * 1024 * 1024)
    per_head = jax.ShapeDtypeStruct((H, ROWS, DK), jnp.float32)
    lags = [
        jax.ShapeDtypeStruct((count, H, ROWS, DK), jnp.float32) for count in (STEPS - 1, STEPS)
    ]
    tap_blocks = jax.ShapeDtypeStruct((TAP_BLOCKS, TAPS, TAP_WIDTH), jnp.float32)
    prepared = pl.pallas_call(
        keys_kernel,
        out_shape=[per_head] * 3 + lags + [tap_blocks],
        in_specs=[smem] + [vmem] * 7 + [pl.BlockSpec(memory_space=pl.ANY)],
        out_specs=[vmem] * 6,
        scratch_shapes=[
            pltpu.VMEM(state.shape, jnp.float32),
            pltpu.SemaphoreType.DMA((STATE_COPIES,)),
        ],
        compiler_params=params,
        cost_estimate=pl.CostEstimate(flops=40_000_000, bytes_accessed=9_000_000, transcendentals=0),
        name="keys_part",
    )(twist, *queries, *keys, history, *taps, state)
    return pl.pallas_call(
        values_kernel,
        out_shape=jax.ShapeDtypeStruct((UNITS // 4, 2 * ROWS, DK), jnp.bfloat16),
        in_specs=[smem] * 4 + [vmem] * 9,
        out_specs=vmem,
        scratch_shapes=[pltpu.VMEM((H, ROWS, DK), jnp.float32)],
        compiler_params=params,
        cost_estimate=pl.CostEstimate(flops=4_000_000, bytes_accessed=2_000_000, transcendentals=0),
        name="values_part",
    )(slots, halves, lengths, twist, *values, history, *prepared)


def rows_kernel(
    depth, me_ref, slot_of_ref, tokens_hbm, mine_ref, theirs_ref, window_ref, sem
):
    me = me_ref[0]
    width = window_ref.shape[2]
    offset = me // 2 * (2 * depth)
    start = jnp.minimum(offset // DK * DK, D - width)
    columns = pl.ds(pl.multiple_of(start, DK), width)
    copy = pltpu.make_async_copy(tokens_hbm.at[:, :, columns], window_ref, sem)
    copy.start()
    shape = (mine_ref.shape[0], slot_of_ref.shape[1])
    row = lax.broadcasted_iota(jnp.int32, shape, 0)
    place = row // ROWS
    count = (shape[0] // ROWS).bit_length() - 1
    holder = jnp.zeros(shape, jnp.int32)
    for at in range(count):
        holder = holder + ((place >> (count - 1 - at)) & 1) * (2 << at)
    holder = jnp.bitwise_xor(holder, me)
    match = holder * LOCAL + row % ROWS // STEPS == slot_of_ref[...]
    copy.wait()
    window = window_ref[...].astype(jnp.float32)
    total = jnp.zeros((shape[0], width), jnp.float32)
    for step in range(STEPS):
        picker = jnp.where(match & (row % STEPS == step), 1.0, 0.0).astype(jnp.bfloat16)
        here = window[:, step, :].astype(jnp.bfloat16)
        total = total + jnp.dot(picker, here, preferred_element_type=jnp.float32)
    total = pltpu.roll(total, lax.rem(width - (offset - start), width), 1)
    low, high = total[:, :depth], total[:, depth : 2 * depth]
    first_core = me % 2 == 0
    mine_ref[...] = jnp.where(first_core, low, high).astype(jnp.bfloat16)
    theirs_ref[...] = jnp.where(first_core, high, low).astype(jnp.bfloat16)


def run_rows(me, slot_of, tokens, depth, chips):
    width = -(-(2 * depth + DK - 1) // DK) * DK
    out = jax.ShapeDtypeStruct((chips * ROWS, depth), jnp.bfloat16)
    vmem = pl.BlockSpec(memory_space=pltpu.VMEM)
    return pl.pallas_call(
        functools.partial(rows_kernel, depth),
        out_shape=[out, out],
        in_specs=[
            pl.BlockSpec(memory_space=pltpu.SMEM), vmem, pl.BlockSpec(memory_space=pltpu.HBM)
        ],
        out_specs=[vmem, vmem],
        scratch_shapes=[
            pltpu.VMEM((tokens.shape[0], STEPS, width), jnp.bfloat16),
            pltpu.SemaphoreType.DMA,
        ],
        compiler_params=pltpu.CompilerParams(vmem_limit_bytes=32 * 1024 * 1024),
        cost_estimate=pl.CostEstimate(flops=0, bytes_accessed=0, transcendentals=0),
        name="token_rows",
    )(me.reshape(1), slot_of.reshape(1, -1), tokens)


def product_kernel(mine_ref, theirs_ref, block_ref, other_ref, *refs):
    gate_refs, (kept_ref, packed_ref) = refs[:-2], refs[-2:]
    half = mine_ref.shape[0] // 2

    def product(own, other):
        total = jnp.dot(mine_ref[...], own, preferred_element_type=jnp.float32)
        return total + jnp.dot(theirs_ref[...], other, preferred_element_type=jnp.float32)

    total = product(block_ref[...], other_ref[...])
    if gate_refs:
        gates = product(gate_refs[0][...], gate_refs[1][...])
        zeros = jnp.zeros((gates.shape[0], 2 * DK - gates.shape[1]), jnp.float32)
        total = jnp.concatenate([total, gates, zeros], axis=1)
    kept_ref[...] = total[:half]
    pack_rows(total[half:], packed_ref)


def run_product(mine, theirs, weights, part, gates=()):
    vmem = pl.BlockSpec(memory_space=pltpu.VMEM)
    block = pl.BlockSpec((mine.shape[1], HEADS_WIDTH), lambda i: (0, part))
    half = mine.shape[0] // 2
    width = HEADS_WIDTH + len(gates) * DK
    return pl.pallas_call(
        product_kernel,
        grid=(1,),
        out_shape=[
            jax.ShapeDtypeStruct((half, width), jnp.float32),
            jax.ShapeDtypeStruct((half, width + SCALE_LANES), jnp.int16),
        ],
        in_specs=[vmem, vmem, block, block] + [vmem] * len(gates),
        out_specs=[vmem] * 2,
        compiler_params=pltpu.CompilerParams(vmem_limit_bytes=32 * 1024 * 1024),
        cost_estimate=pl.CostEstimate(flops=0, bytes_accessed=0, transcendentals=0),
        name="partial_product",
    )(mine, theirs, *weights, *gates)


def combine_kernel(kept_ref, got_ref, *refs):
    tap_refs, (still_ref, packed_ref), wide_refs = refs[:-2], refs[-2:], ()
    if tap_refs:
        tap_refs, wide_refs = refs[:2], refs[2:3]
        still_ref, packed_ref = refs[3:]
    half = still_ref.shape[0]
    steps = steps_of(got_ref)
    sent = []
    for block in range(kept_ref.shape[1] // DK):
        columns = pl.ds(block * DK, DK)
        total = kept_ref[:, columns] + unpack_block(got_ref, steps, block)
        still_ref[:, columns] = total[:half]
        sent.append(total[half:])
    sent = jnp.concatenate(sent, axis=1)
    pack_rows(fold_rows(sent) if half == ROWS else sent, packed_ref)
    for wide_ref in wide_refs:
        rows = tap_refs[0].shape[0]
        wide_ref[:rows] = tap_refs[0][...]
        wide_ref[rows:] = tap_refs[1][...]


def run_combine(kept, got, taps=()):
    vmem = pl.BlockSpec(memory_space=pltpu.VMEM)
    half, width = kept.shape[0] // 2, kept.shape[1]
    packed = (2 * ROWS, width // 2 + SCALE_LANES) if half == ROWS else (half, width + SCALE_LANES)
    wide = [jax.ShapeDtypeStruct((2 * taps[0].shape[0], TAP_WIDTH), jnp.bfloat16)] if taps else []
    return pl.pallas_call(
        combine_kernel,
        out_shape=wide
        + [
            jax.ShapeDtypeStruct((half, width), jnp.float32),
            jax.ShapeDtypeStruct(packed, jnp.int16),
        ],
        in_specs=[vmem] * (2 + len(taps)),
        out_specs=[vmem] * (2 + len(wide)),
        compiler_params=pltpu.CompilerParams(vmem_limit_bytes=32 * 1024 * 1024),
        cost_estimate=pl.CostEstimate(flops=0, bytes_accessed=0, transcendentals=0),
        name="combine",
    )(kept, got, *taps)


def swap(value, bit, devices):
    return lax.ppermute(value, "heads", [(i, i ^ bit) for i in range(devices)])


def on_device(
    tokens,
    qkv_weight,
    gate_weight,
    conv_weight,
    delta_state,
    conv_state,
    old_heads,
    new_units,
    slot_of,
    lengths,
):
    devices = lax.axis_size("heads")
    me = lax.axis_index("heads")
    per_device = UNITS // devices
    depth = qkv_weight.shape[0]
    row_count = tokens.shape[0]
    chips = devices // 2

    old_slots, halves = unit_tables(old_heads, new_units)
    bits = [1 << b for b in range(1, devices.bit_length() - 1)]
    steps = jnp.arange(STEPS, dtype=jnp.int32)
    offered = (slot_of[:, None] * STEPS + steps[None, :]).reshape(-1)

    mine, theirs = run_rows(me, slot_of, tokens, depth, chips)

    weights = (qkv_weight, swap(qkv_weight, 1, devices))
    gates = (gate_weight, swap(gate_weight, 1, devices))

    def in_order(value, *earlier):
        return lax.optimization_barrier((value,) + earlier)[0]

    ride = conv_weight.shape[1] == 2 * TAP_WIDTH and len(bits) == 3
    taps = conv_weight
    if ride:
        taps = jnp.concatenate([taps, swap(taps, 1, devices)], axis=1)
    else:
        taps = lax.all_gather(taps, "heads", axis=1, tiled=True)
    blocks = range(0, taps.shape[1], TAP_WIDTH)
    taps = jnp.concatenate([taps[:, at : at + TAP_WIDTH] for at in blocks], axis=0)
    my_rows = me * LOCAL + jnp.arange(LOCAL, dtype=jnp.int32)
    my_lengths = jnp.sum(
        jnp.where(slot_of[None, :] == my_rows[:, None], lengths[None, :], 0), axis=1
    )
    carried = conv_state.reshape(LOCAL, TAPS - 1, -1)
    blank = jnp.zeros((1, carried.shape[2]), jnp.float32)
    history = jnp.concatenate([blank, carried[1], blank, carried[0]], axis=0)
    mine = in_order(mine, taps, history, my_lengths, old_slots, halves)
    query = run_product(mine, theirs, weights, 0)
    mine = in_order(mine, *query)
    key = run_product(mine, theirs, weights, 1, gates)
    mine = in_order(mine, *key)
    value = run_product(mine, theirs, weights, 2)

    chunks = [query, key, value]
    got = [swap(packed, bits[0], devices) for _, packed in chunks]
    got[0] = in_order(got[0], *value)
    far = swap(taps, bits[0], devices) if ride else taps
    for level, bit in enumerate(bits[1:]):
        for at in range(len(chunks)):
            arrived = in_order(got[at], *chunks[at - 1]) if at else got[at]
            if ride and level == 0 and at != 1:
                taps, *chunks[at] = run_combine(chunks[at][0], arrived, (taps, far))
                far = swap(taps, bits[1 + at // 2], devices)
            else:
                chunks[at] = run_combine(chunks[at][0], arrived)
            got[at] = swap(chunks[at][1], bit, devices)
    queries, keys, values = [(kept, came) for (kept, _), came in zip(chunks, got)]
    if ride:
        twist, taps = (2 * me).reshape(1), (taps, far)
    else:
        half = TAP_BLOCKS // 2 * TAPS
        twist, taps = jnp.zeros(1, jnp.int32), (taps[:half], taps[half:])

    local_out = run_delta(
        old_slots, halves, my_lengths, queries, keys, values, history, twist, taps, delta_state
    )

    placer = (offered[:, None] == jnp.arange(row_count * STEPS, dtype=jnp.int32)[None, :]).astype(
        jnp.bfloat16
    )
    if per_device % 2 == 0:
        pairs = per_device // 2
        sending = local_out.reshape(devices, pairs * ROWS, DK)
        got = lax.all_to_all(sending, "heads", split_axis=0, concat_axis=0, tiled=True)
        got = got.reshape(devices, pairs, ROWS, DK)
        got = jnp.concatenate([got[:, pair] for pair in range(pairs)], axis=-1)
        got = got.reshape(devices * ROWS, pairs * DK)
    else:
        units = local_out.reshape(UNITS // 2, ROWS, 2, HALF).transpose(0, 2, 1, 3)
        sending = units.reshape(devices, per_device * ROWS, HALF)
        got = lax.all_to_all(sending, "heads", split_axis=0, concat_axis=0, tiled=True)
        got = got.reshape(devices, per_device, ROWS, HALF).transpose(0, 2, 1, 3)
        got = got.reshape(devices * ROWS, per_device * HALF)
    outputs = jnp.dot(placer, got, preferred_element_type=jnp.float32).astype(jnp.bfloat16)
    return outputs.reshape(row_count, STEPS, per_device * HALF)


def solution(mesh):
    in_specs = (
        P("groups", None, None),
        P(("groups", "heads"), None),
        P(("groups", "heads"), None),
        P("groups", "heads"),
        P(("groups", "heads"), None, None, None),
        P(("groups", "heads"), None, None),
        P(),
        P(),
        P("groups"),
        P("groups"),
    )
    out_specs = P("groups", None, "heads")
    return jax.shard_map(
        on_device, mesh=mesh, in_specs=in_specs, out_specs=out_specs, check_vma=False
    )
```

profile of v0, /device:TPU:0, one launch (start us, length us, event | category | flops | bytes accessed | tf_op | source)
XLA Modules:
  0.0 79.4 jit_solution(2657793431860889175)
XLA Ops:
  0.5 1.5 %copy.22.refs_0_ = bf16[144,64]{1,0:T(8,128)(2,1)} copy(bf16[144,64]{0,1:T(8,128)(2,1)} %param.12) | data formatting | bytes 36864 | tf_op args[2]
  2.4 0.7 fusion.7
  3.1 2.1 %fusion.6 = (f32[1,3,12288]{2,0,1:T(1,128)}, f32[1,3,12288]{2,0,1:T(1,128)}) fusion(f32[2,3,12288]{2,0,1:T(2,128)} %param.15), kind=kLoop, calls=%fused_computation.27 | loop fusion | bytes 589824 | tf_op jit(solution)/shard_map/slice | solution.py:445
  5.3 0.7 and_select_fusion
  5.9 0.8 select_reduce_fusion.1
  6.7 0.9 %fusion.4.lengths_ref = s32[2]{0:T(128)S(1)} fusion(s32[32]{0:T(128)} %param.19, s32[32]{0:T(128)} %param.18, s32[2]{0:T(128)S(1)} %iota_add_fusion.1), kind=kLoop, calls=%fused_computation.23 | loop fusion | flops 190 | bytes 272 | tf_op jit(solution)/shard_map/reduce_sum | solution.py:440
  7.6 1.2 %copy_bitcast_fusion = (f32[3,12288]{1,0:T(4,128)S(1)}, f32[3,12288]{1,0:T(4,128)S(1)}) fusion(f32[1,3,12288]{2,0,1:T(1,128)} %get-tuple-element.78, f32[1,3,12288]{2,0,1:T(1,128)} %get-tuple-element.77), kind=kLoop, calls=%fused_computation.2 | loop fusion | bytes 589824 | tf_op jit(solution)/shard_map/squeeze | solution.py:445
  9.1 1.1 %copy-done.2 = bf16[32,4,2304]{2,1,0:T(4,128)(2,1)S(1)} copy-done((bf16[32,4,2304]{2,1,0:T(4,128)(2,1)S(1)}, bf16[32,4,2304]{2,1,0:T(4,128)(2,1)}, u32[]{:S(2)}) %copy-start.2) | copy-done | bytes 589848
  10.8 0.8 %token_rows.1 = (bf16[64,144]{1,0:T(8,128)(2,1)S(1)}, bf16[64,144]{1,0:T(8,128)(2,1)S(1)}) custom-call(s32[1]{0:T(128)} %bitcast.1.me_ref, s32[1,32]{1,0:T(1,128)S(1)} %bitcast.12, bf16[32,4,2304]{2,1,0:T(4,128)(2,1)S(1)} %copy-done.2), custom_call_target="tpu_custom_call" | custom-call | tf_op jit(solution)/shard_map/token_rows/pallas_call | solution.py:300
  11.7 2.0 %copy-done = bf16[144,12288]{1,0:T(8,128)(2,1)S(1)} copy-done((bf16[144,12288]{1,0:T(8,128)(2,1)S(1)}, bf16[144,12288]{1,0:T(8,128)(2,1)}, u32[]{:S(2)}) %copy-start) | copy-done | bytes 3538968
  13.7 0.8 %partial_product.3 = (f32[32,4096]{1,0:T(8,128)S(1)}, s16[32,4224]{1,0:T(8,128)(2,1)S(1)}) custom-call(bf16[64,144]{1,0:T(8,128)(2,1)S(1)} %get-tuple-element.49.mine_ref, bf16[64,144]{1,0:T(8,128)(2,1)S(1)} %get-tuple-element.43.theirs_ref, bf16[144,12288]{1,0:T(8,128)(2,1)S(1)} %copy-done, bf16[144,12288]{1,0:T(8,128)(2,1)S(1)} %collective-permute-done.1.other_ref), custom_call_target="tpu_custom_call" | custom-call | tf_op jit(solution)/shard_map/partial_product/pallas_call | solution.py:339
  14.5 1.8 %partial_product.4 = (f32[32,4352]{1,0:T(8,128)S(1)}, s16[32,4480]{1,0:T(8,128)(2,1)S(1)}) custom-call(bf16[64,144]{1,0:T(8,128)(2,1)S(1)} %get-tuple-element.49.mine_ref, bf16[64,144]{1,0:T(8,128)(2,1)S(1)} %get-tuple-element.43.theirs_ref, bf16[144,12288]{1,0:T(8,128)(2,1)S(1)} %copy-done, bf16[144,12288]{1,0:T(8,128)(2,1)S(1)} %collective-permute-done.1.other_ref, ...), custom_call_target="tpu_custom_call" | custom-call | tf_op jit(solution)/shard_map/partial_product/pallas_call | solution.py:339
  16.3 2.6 %collective-permute-start.4 = (s16[32,4480]{1,0:T(8,128)(2,1)S(1)}, s16[32,4480]{1,0:T(8,128)(2,1)S(1)}, u32[]{:S(2)}, u32[]{:S(2)}) collective-permute-start(s16[32,4480]{1,0:T(8,128)(2,1)S(1)} %get-tuple-element.48), channel_id=1, source_target_pairs={{0,2},{1,3},{2,0},{3,1},{4,6},{5,7},{6,4},{7,5},{8,10},{9,11},{10,... | collective-permute-start | bytes 860168 | tf_op jit(solution)/shard_map/ppermute | solution.py:396
  18.9 0.8 %partial_product.5 = (f32[32,4096]{1,0:T(8,128)S(1)}, s16[32,4224]{1,0:T(8,128)(2,1)S(1)}) custom-call(bf16[64,144]{1,0:T(8,128)(2,1)S(1)} %get-tuple-element.49.mine_ref, bf16[64,144]{1,0:T(8,128)(2,1)S(1)} %get-tuple-element.43.theirs_ref, bf16[144,12288]{1,0:T(8,128)(2,1)S(1)} %copy-done, bf16[144,12288]{1,0:T(8,128)(2,1)S(1)} %collective-permute-done.1.other_ref), custom_call_target="tpu_custom_call" | custom-call | tf_op jit(solution)/shard_map/partial_product/pallas_call | solution.py:339
  19.8 2.0 %collective-permute-start.3 = (s16[32,4224]{1,0:T(8,128)(2,1)S(1)}, s16[32,4224]{1,0:T(8,128)(2,1)S(1)}, u32[]{:S(2)}, u32[]{:S(2)}) collective-permute-start(s16[32,4224]{1,0:T(8,128)(2,1)S(1)} %get-tuple-element.51), channel_id=1, source_target_pairs={{0,2},{1,3},{2,0},{3,1},{4,6},{5,7},{6,4},{7,5},{8,10},{9,11},{10,... | collective-permute-start | bytes 811016 | tf_op jit(solution)/shard_map/ppermute | solution.py:396
  21.9 10.5 %collective-permute-done.5.got_ref = s16[32,4224]{1,0:T(8,128)(2,1)S(1)} collective-permute-done((s16[32,4224]{1,0:T(8,128)(2,1)S(1)}, s16[32,4224]{1,0:T(8,128)(2,1)S(1)}, u32[]{:S(2)}, u32[]{:S(2)}) %collective-permute-start.5) | collective-permute-done | bytes 270368 | tf_op jit(solution)/shard_map/ppermute | solution.py:396
  32.3 5.9 %collective-permute-done.6.refs_1_ = bf16[16,384]{1,0:T(8,128)(2,1)S(1)} collective-permute-done((bf16[16,384]{1,0:T(8,128)(2,1)S(1)}, bf16[16,384]{1,0:T(8,128)(2,1)S(1)}, u32[]{:S(2)}, u32[]{:S(2)}) %collective-permute-start.6) | collective-permute-done | bytes 12320 | tf_op jit(solution)/shard_map/ppermute | solution.py:396
  38.8 1.9 %collective-permute-start.7 = (bf16[32,384]{1,0:T(8,128)(2,1)S(1)}, bf16[32,384]{1,0:T(8,128)(2,1)S(1)}, u32[]{:S(2)}, u32[]{:S(2)}) collective-permute-start(bf16[32,384]{1,0:T(8,128)(2,1)S(1)} %get-tuple-element.59.refs_0_), channel_id=1, source_target_pairs={{0,4},{1,5},{2,6},{3,7},{4,0},{5,1},{6,2},{7,3},{8,12},{9,13},{10,... | collective-permute-start | bytes 73736 | tf_op jit(solution)/shard_map/ppermute | solution.py:396
  41.5 1.8 %collective-permute-start.10 = (s16[16,4224]{1,0:T(8,128)(2,1)S(1)}, s16[16,4224]{1,0:T(8,128)(2,1)S(1)}, u32[]{:S(2)}, u32[]{:S(2)}) collective-permute-start(s16[16,4224]{1,0:T(8,128)(2,1)S(1)} %get-tuple-element.54), channel_id=1, source_target_pairs={{0,4},{1,5},{2,6},{3,7},{4,0},{5,1},{6,2},{7,3},{8,12},{9,13},{10,... | collective-permute-start | bytes 405512 | tf_op jit(solution)/shard_map/ppermute | solution.py:396
  43.8 1.4 %collective-permute-start.8 = (s16[16,4224]{1,0:T(8,128)(2,1)S(1)}, s16[16,4224]{1,0:T(8,128)(2,1)S(1)}, u32[]{:S(2)}, u32[]{:S(2)}) collective-permute-start(s16[16,4224]{1,0:T(8,128)(2,1)S(1)} %get-tuple-element.61), channel_id=1, source_target_pairs={{0,4},{1,5},{2,6},{3,7},{4,0},{5,1},{6,2},{7,3},{8,12},{9,13},{10,... | collective-permute-start | bytes 405512 | tf_op jit(solution)/shard_map/ppermute | solution.py:396
  45.2 2.6 %collective-permute-start.14 = (bf16[64,384]{1,0:T(8,128)(2,1)S(1)}, bf16[64,384]{1,0:T(8,128)(2,1)S(1)}, u32[]{:S(2)}, u32[]{:S(2)}) collective-permute-start(bf16[64,384]{1,0:T(8,128)(2,1)S(1)} %get-tuple-element.70.near_ref), channel_id=1, source_target_pairs={{0,8},{1,9},{2,10},{3,11},{4,12},{5,13},{6,14},{7,15},{8,0},{9,1},... | collective-permute-start | bytes 147464 | tf_op jit(solution)/shard_map/ppermute | solution.py:396
  47.8 4.0 %collective-permute-done.10.got_ref = s16[16,4224]{1,0:T(8,128)(2,1)S(1)} collective-permute-done((s16[16,4224]{1,0:T(8,128)(2,1)S(1)}, s16[16,4224]{1,0:T(8,128)(2,1)S(1)}, u32[]{:S(2)}, u32[]{:S(2)}) %collective-permute-start.10) | collective-permute-done | bytes 135200 | tf_op jit(solution)/shard_map/ppermute | solution.py:396
  52.1 1.7 %collective-permute-start.12 = (s16[16,2176]{1,0:T(8,128)(2,1)S(1)}, s16[16,2176]{1,0:T(8,128)(2,1)S(1)}, u32[]{:S(2)}, u32[]{:S(2)}) collective-permute-start(s16[16,2176]{1,0:T(8,128)(2,1)S(1)} %get-tuple-element.63), channel_id=1, source_target_pairs={{0,8},{1,9},{2,10},{3,11},{4,12},{5,13},{6,14},{7,15},{8,0},{9,1},... | collective-permute-start | bytes 208904 | tf_op jit(solution)/shard_map/ppermute | solution.py:396
  54.3 1.3 %collective-permute-start.13 = (s16[16,2304]{1,0:T(8,128)(2,1)S(1)}, s16[16,2304]{1,0:T(8,128)(2,1)S(1)}, u32[]{:S(2)}, u32[]{:S(2)}) collective-permute-start(s16[16,2304]{1,0:T(8,128)(2,1)S(1)} %get-tuple-element.66), channel_id=1, source_target_pairs={{0,8},{1,9},{2,10},{3,11},{4,12},{5,13},{6,14},{7,15},{8,0},{9,1},... | collective-permute-start | bytes 221192 | tf_op jit(solution)/shard_map/ppermute | solution.py:396
  56.0 1.7 %collective-permute-start.11 = (s16[16,2176]{1,0:T(8,128)(2,1)S(1)}, s16[16,2176]{1,0:T(8,128)(2,1)S(1)}, u32[]{:S(2)}, u32[]{:S(2)}) collective-permute-start(s16[16,2176]{1,0:T(8,128)(2,1)S(1)} %get-tuple-element.69), channel_id=1, source_target_pairs={{0,8},{1,9},{2,10},{3,11},{4,12},{5,13},{6,14},{7,15},{8,0},{9,1},... | collective-permute-start | bytes 208904 | tf_op jit(solution)/shard_map/ppermute | solution.py:396
  57.8 3.7 %collective-permute-done.12.query_got_ref = s16[16,2176]{1,0:T(8,128)(2,1)S(1)} collective-permute-done((s16[16,2176]{1,0:T(8,128)(2,1)S(1)}, s16[16,2176]{1,0:T(8,128)(2,1)S(1)}, u32[]{:S(2)}, u32[]{:S(2)}) %collective-permute-start.12) | collective-permute-done | bytes 69664 | tf_op jit(solution)/shard_map/ppermute | solution.py:396
  61.4 0.8 collective-permute-done.13.key_got_ref
  62.2 3.4 %keys_part.1 = (f32[32,8,128]{2,1,0:T(8,128)S(1)}, f32[32,8,128]{2,1,0:T(8,128)S(1)}, f32[32,8,128]{2,1,0:T(8,128)S(1)}, f32[3,32,8,128]{3,2,1,0:T(8,128)S(1)}, ...) custom-call(s32[1]{0:T(128)} %bitcast.twist_ref, f32[8,4096]{1,0:T(8,128)S(1)} %get-tuple-element.62.query_ref, ...), custom_call_target="tpu_custom_call" | custom-call | flops 40000000 | bytes 9000000 | tf_op jit(solution)/shard_map/keys_part/pallas_call | solution.py:238
  65.6 1.8 %values_part.1 = bf16[16,16,128]{2,1,0:T(8,128)(2,1)} custom-call(s32[64]{0:T(128)S(1)} %select_reduce_fusion.slots_ref, s32[64]{0:T(128)S(1)} %get-tuple-element.85.halves_ref, s32[2]{0:T(128)S(1)} %fusion.4.lengths_ref, s32[1]{0:T(128)} %bitcast.twist_ref, f32[8,4096]{1,0:T(8,128)S(1)} %get-tuple-element.68.value_ref, ...), custom_call_target="tpu_custom_call" | custom-call | flops 4000000 | bytes 2000000 | tf_op jit(solution)/shard_map/values_part/pallas_call | solution.py:251
  67.4 4.2 %all-to-all-start = ((bf16[16,16,128]{2,1,0:T(8,128)(2,1)}), bf16[16,16,128]{2,1,0:T(8,128)(2,1)S(1)}, u32[]{:S(2)}, u32[]{:S(2)}) async-start(bf16[16,16,128]{2,1,0:T(8,128)(2,1)} %values_part.1), calls=%async_computation | async-start | bytes 131072 | tf_op jit(solution)/shard_map/all_to_all | solution.py:483
  71.8 6.7 %all-to-all-done = bf16[16,16,128]{2,1,0:T(8,128)(2,1)S(1)} async-done(((bf16[16,16,128]{2,1,0:T(8,128)(2,1)}), bf16[16,16,128]{2,1,0:T(8,128)(2,1)S(1)}, u32[]{:S(2)}, u32[]{:S(2)}) %all-to-all-start) | async-done | bytes 65568 | tf_op jit(solution)/shard_map/all_to_all | solution.py:483
  78.7 0.7 reshape.46
  (43 shorter events, 5.6 us)
Async XLA Ops:
  0.0 11.6 %collective-permute-start = (bf16[4,768]{1,0:T(4,128)(2,1)}, bf16[4,768]{1,0:T(4,128)(2,1)S(1)}, u32[]{:S(2)}, u32[]{:S(2)}) collective-permute-start(bf16[4,768]{1,0:T(4,128)(2,1)} %param.13), channel_id=1, source_target_pairs={{0,1},{1,0},{2,3},{3,2},{4,5},{5,4},{6,7},{7,6},{8,9},{9,8},{10,11... | collective-permute-start | bytes 18440 | tf_op jit(solution)/shard_map/ppermute | solution.py:396
  0.5 11.2 %collective-permute-start.1 = (bf16[144,12288]{1,0:T(8,128)(2,1)}, bf16[144,12288]{1,0:T(8,128)(2,1)S(1)}, u32[]{:S(2)}, u32[]{:S(2)}) collective-permute-start(bf16[144,12288]{1,0:T(8,128)(2,1)} %block_ref.5), channel_id=1, source_target_pairs={{0,1},{1,0},{2,3},{3,2},{4,5},{5,4},{6,7},{7,6},{8,9},{9,8},{10,11... | collective-permute-start | bytes 10616840 | tf_op jit(solution)/shard_map/ppermute | solution.py:396
  2.0 12.5 %collective-permute-start.2 = (bf16[144,64]{1,0:T(8,128)(2,1)}, bf16[144,64]{1,0:T(8,128)(2,1)}, u32[]{:S(2)}, u32[]{:S(2)}) collective-permute-start(bf16[144,64]{1,0:T(8,128)(2,1)} %copy.22.refs_0_), channel_id=1, source_target_pairs={{0,1},{1,0},{2,3},{3,2},{4,5},{5,4},{6,7},{7,6},{8,9},{9,8},{10,11... | collective-permute-start | bytes 55304 | tf_op jit(solution)/shard_map/ppermute | solution.py:396
  9.0 1.1 %copy-start.2 = (bf16[32,4,2304]{2,1,0:T(4,128)(2,1)S(1)}, bf16[32,4,2304]{2,1,0:T(4,128)(2,1)}, u32[]{:S(2)}) copy-start(bf16[32,4,2304]{2,1,0:T(4,128)(2,1)} %tokens_hbm.1) | copy-start | bytes 1769476
  10.1 0.7 copy-start.4
  11.7 2.0 %copy-start = (bf16[144,12288]{1,0:T(8,128)(2,1)S(1)}, bf16[144,12288]{1,0:T(8,128)(2,1)}, u32[]{:S(2)}) copy-start(bf16[144,12288]{1,0:T(8,128)(2,1)} %block_ref.5) | copy-start | bytes 10616836
  13.7 0.8 %copy-start.3 = (bf16[144,64]{1,0:T(8,128)(2,1)S(1)}, bf16[144,64]{1,0:T(8,128)(2,1)}, u32[]{:S(2)}) copy-start(bf16[144,64]{1,0:T(8,128)(2,1)} %copy.22.refs_0_) | copy-start | bytes 55300
  16.3 24.3 %collective-permute-start.4 = (s16[32,4480]{1,0:T(8,128)(2,1)S(1)}, s16[32,4480]{1,0:T(8,128)(2,1)S(1)}, u32[]{:S(2)}, u32[]{:S(2)}) collective-permute-start(s16[32,4480]{1,0:T(8,128)(2,1)S(1)} %get-tuple-element.48), channel_id=1, source_target_pairs={{0,2},{1,3},{2,0},{3,1},{4,6},{5,7},{6,4},{7,5},{8,10},{9,11},{10,... | collective-permute-start | bytes 860168 | tf_op jit(solution)/shard_map/ppermute | solution.py:396
  18.8 13.5 %collective-permute-start.5 = (s16[32,4224]{1,0:T(8,128)(2,1)S(1)}, s16[32,4224]{1,0:T(8,128)(2,1)S(1)}, u32[]{:S(2)}, u32[]{:S(2)}) collective-permute-start(s16[32,4224]{1,0:T(8,128)(2,1)S(1)} %get-tuple-element.45), channel_id=1, source_target_pairs={{0,2},{1,3},{2,0},{3,1},{4,6},{5,7},{6,4},{7,5},{8,10},{9,11},{10,... | collective-permute-start | bytes 811016 | tf_op jit(solution)/shard_map/ppermute | solution.py:396
  18.9 43.3 %copy-start.1 = (f32[2,32,128,128]{3,2,1,0:T(8,128)S(1)}, f32[2,32,128,128]{3,2,1,0:T(8,128)}, u32[]{:S(2)}) copy-start(f32[2,32,128,128]{3,2,1,0:T(8,128)} %state_hbm.1) | copy-start | bytes 12582916
  19.8 38.0 %copy-start.5 = (s32[32]{0:T(128)S(1)}, s32[32]{0:T(128)}, u32[]{:S(2)}) copy-start(s32[32]{0:T(128)} %param.18) | copy-start | bytes 388
  19.8 23.5 %collective-permute-start.3 = (s16[32,4224]{1,0:T(8,128)(2,1)S(1)}, s16[32,4224]{1,0:T(8,128)(2,1)S(1)}, u32[]{:S(2)}, u32[]{:S(2)}) collective-permute-start(s16[32,4224]{1,0:T(8,128)(2,1)S(1)} %get-tuple-element.51), channel_id=1, source_target_pairs={{0,2},{1,3},{2,0},{3,1},{4,6},{5,7},{6,4},{7,5},{8,10},{9,11},{10,... | collective-permute-start | bytes 811016 | tf_op jit(solution)/shard_map/ppermute | solution.py:396
  21.8 16.4 %collective-permute-start.6 = (bf16[16,384]{1,0:T(8,128)(2,1)S(1)}, bf16[16,384]{1,0:T(8,128)(2,1)S(1)}, u32[]{:S(2)}, u32[]{:S(2)}) collective-permute-start(bf16[16,384]{1,0:T(8,128)(2,1)S(1)} %pad_maximum_fusion.1.refs_0_), channel_id=1, source_target_pairs={{0,2},{1,3},{2,0},{3,1},{4,6},{5,7},{6,4},{7,5},{8,10},{9,11},{10,... | collective-permute-start | bytes 36872 | tf_op jit(solution)/shard_map/ppermute | solution.py:396
  38.8 4.5 %collective-permute-start.7 = (bf16[32,384]{1,0:T(8,128)(2,1)S(1)}, bf16[32,384]{1,0:T(8,128)(2,1)S(1)}, u32[]{:S(2)}, u32[]{:S(2)}) collective-permute-start(bf16[32,384]{1,0:T(8,128)(2,1)S(1)} %get-tuple-element.59.refs_0_), channel_id=1, source_target_pairs={{0,4},{1,5},{2,6},{3,7},{4,0},{5,1},{6,2},{7,3},{8,12},{9,13},{10,... | collective-permute-start | bytes 73736 | tf_op jit(solution)/shard_map/ppermute | solution.py:396
  41.2 12.7 %collective-permute-start.9 = (s16[16,4480]{1,0:T(8,128)(2,1)S(1)}, s16[16,4480]{1,0:T(8,128)(2,1)S(1)}, u32[]{:S(2)}, u32[]{:S(2)}) collective-permute-start(s16[16,4480]{1,0:T(8,128)(2,1)S(1)} %get-tuple-element.57), channel_id=1, source_target_pairs={{0,4},{1,5},{2,6},{3,7},{4,0},{5,1},{6,2},{7,3},{8,12},{9,13},{10,... | collective-permute-start | bytes 430088 | tf_op jit(solution)/shard_map/ppermute | solution.py:396
  41.5 10.3 %collective-permute-start.10 = (s16[16,4224]{1,0:T(8,128)(2,1)S(1)}, s16[16,4224]{1,0:T(8,128)(2,1)S(1)}, u32[]{:S(2)}, u32[]{:S(2)}) collective-permute-start(s16[16,4224]{1,0:T(8,128)(2,1)S(1)} %get-tuple-element.54), channel_id=1, source_target_pairs={{0,4},{1,5},{2,6},{3,7},{4,0},{5,1},{6,2},{7,3},{8,12},{9,13},{10,... | collective-permute-start | bytes 405512 | tf_op jit(solution)/shard_map/ppermute | solution.py:396
  43.8 11.8 %collective-permute-start.8 = (s16[16,4224]{1,0:T(8,128)(2,1)S(1)}, s16[16,4224]{1,0:T(8,128)(2,1)S(1)}, u32[]{:S(2)}, u32[]{:S(2)}) collective-permute-start(s16[16,4224]{1,0:T(8,128)(2,1)S(1)} %get-tuple-element.61), channel_id=1, source_target_pairs={{0,4},{1,5},{2,6},{3,7},{4,0},{5,1},{6,2},{7,3},{8,12},{9,13},{10,... | collective-permute-start | bytes 405512 | tf_op jit(solution)/shard_map/ppermute | solution.py:396
  45.2 12.5 %collective-permute-start.14 = (bf16[64,384]{1,0:T(8,128)(2,1)S(1)}, bf16[64,384]{1,0:T(8,128)(2,1)S(1)}, u32[]{:S(2)}, u32[]{:S(2)}) collective-permute-start(bf16[64,384]{1,0:T(8,128)(2,1)S(1)} %get-tuple-element.70.near_ref), channel_id=1, source_target_pairs={{0,8},{1,9},{2,10},{3,11},{4,12},{5,13},{6,14},{7,15},{8,0},{9,1},... | collective-permute-start | bytes 147464 | tf_op jit(solution)/shard_map/ppermute | solution.py:396
  52.1 9.3 %collective-permute-start.12 = (s16[16,2176]{1,0:T(8,128)(2,1)S(1)}, s16[16,2176]{1,0:T(8,128)(2,1)S(1)}, u32[]{:S(2)}, u32[]{:S(2)}) collective-permute-start(s16[16,2176]{1,0:T(8,128)(2,1)S(1)} %get-tuple-element.63), channel_id=1, source_target_pairs={{0,8},{1,9},{2,10},{3,11},{4,12},{5,13},{6,14},{7,15},{8,0},{9,1},... | collective-permute-start | bytes 208904 | tf_op jit(solution)/shard_map/ppermute | solution.py:396
  54.3 7.9 %collective-permute-start.13 = (s16[16,2304]{1,0:T(8,128)(2,1)S(1)}, s16[16,2304]{1,0:T(8,128)(2,1)S(1)}, u32[]{:S(2)}, u32[]{:S(2)}) collective-permute-start(s16[16,2304]{1,0:T(8,128)(2,1)S(1)} %get-tuple-element.66), channel_id=1, source_target_pairs={{0,8},{1,9},{2,10},{3,11},{4,12},{5,13},{6,14},{7,15},{8,0},{9,1},... | collective-permute-start | bytes 221192 | tf_op jit(solution)/shard_map/ppermute | solution.py:396
  56.0 9.6 %collective-permute-start.11 = (s16[16,2176]{1,0:T(8,128)(2,1)S(1)}, s16[16,2176]{1,0:T(8,128)(2,1)S(1)}, u32[]{:S(2)}, u32[]{:S(2)}) collective-permute-start(s16[16,2176]{1,0:T(8,128)(2,1)S(1)} %get-tuple-element.69), channel_id=1, source_target_pairs={{0,8},{1,9},{2,10},{3,11},{4,12},{5,13},{6,14},{7,15},{8,0},{9,1},... | collective-permute-start | bytes 208904 | tf_op jit(solution)/shard_map/ppermute | solution.py:396
  67.4 11.1 %all-to-all-start = ((bf16[16,16,128]{2,1,0:T(8,128)(2,1)}), bf16[16,16,128]{2,1,0:T(8,128)(2,1)S(1)}, u32[]{:S(2)}, u32[]{:S(2)}) async-start(bf16[16,16,128]{2,1,0:T(8,128)(2,1)} %values_part.1), calls=%async_computation | async-start | bytes 131072 | tf_op jit(solution)/shard_map/all_to_all | solution.py:483
where the time goes:
time: 79.9 us; the launch traced here: 79.4 us
  waiting for transfers between devices  31.5 us (39%)
  starting transfers between devices  22.7 us (28%)
  Pallas kernels  12.2 us (15%)
  local copies, waits for them, and re-layouts  10 us (13%)
  other arithmetic  2.64 us (3%)
    ppermute x15, waiting for transfers between devices, swap(): return lax.ppermute(value, 'heads', [(i, i ^ bit) for i in range(devices)])  24.8 us
    ppermute x15, starting transfers between devices, swap(): return lax.ppermute(value, 'heads', [(i, i ^ bit) for i in range(devices)])  18.4 us
    all_to_all x1, waiting for transfers between devices, on_device(): lax.all_to_all(sending, 'heads', split_axis=0, concat_axis=0, tiled=True)  6.72 us
    unnamed x13, local copies, waits for them, and re-layouts  5.2 us
    all_to_all x1, starting transfers between devices, on_device(): lax.all_to_all(sending, 'heads', split_axis=0, concat_axis=0, tiled=True)  4.24 us
    pallas_call x3, Pallas kernels, run_product(): pl.pallas_call(product_kernel, grid=(1,), out_shape=[jax.ShapeDtypeStruct...  3.4 us
    pallas_call x1, Pallas kernels, run_delta(): pl.pallas_call(keys_kernel, out_shape=[per_head] * 3 + lags + [tap_blocks...  3.37 us
    pallas_call x6, Pallas kernels, run_combine(): pl.pallas_call(combine_kernel, out_shape=wide + [jax.ShapeDtypeStruct((ha...  2.81 us
  transfers between devices with their start and end apart: 16, of which 6 were waited for; matrix products, arithmetic and copies ran while one was open for 10% of the time, Pallas kernels for 11%

commit v1 on v0

--- a/solution.py
+++ b/solution.py
@@ -18,9 +18,6 @@
 ROWS = LOCAL * STEPS
 HEADS_WIDTH = H * DK
 LEVELS = 32767.0
-SCALE_LANES = 128
-EXPONENT_AT = 64
-BLOCKS = HEADS_WIDTH // DK
 STATE_COPIES = 4
 TAP_WIDTH = 384
 TAP_BLOCKS = 3 * HEADS_WIDTH // TAP_WIDTH
@@ -57,11 +54,16 @@
     return value * lax.rsqrt(lane_sum(value * value) + norm_eps)
 
 
+def scale_lanes(blocks):
+    return -(-blocks // HALF) * DK
+
+
 def pack_rows(total, packed_ref):
     rows, width = total.shape
     blocks = width // DK
-    lane = lax.broadcasted_iota(jnp.int32, (rows, SCALE_LANES), 1)
-    scales = jnp.zeros((rows, SCALE_LANES), jnp.float32)
+    lanes = scale_lanes(blocks)
+    lane = lax.broadcasted_iota(jnp.int32, (rows, lanes), 1)
+    scales = jnp.zeros((rows, lanes), jnp.float32)
     for block in range(blocks):
         part = total[:, block * DK : (block + 1) * DK]
         top = jnp.max(jnp.abs(part), axis=-1, keepdims=True) + 1e-30
@@ -71,7 +73,7 @@
         coded = jnp.clip(jnp.floor(part * factor + 0.5), -LEVELS, LEVELS)
         packed_ref[:, block * DK : (block + 1) * DK] = coded.astype(jnp.int32).astype(jnp.int16)
         scales = jnp.where(lane == block, mantissa, scales)
-        scales = jnp.where(lane == EXPONENT_AT + block, exponent, scales)
+        scales = jnp.where(lane == lanes // 2 + block, exponent, scales)
     packed_ref[:, width:] = scales.astype(jnp.int32).astype(jnp.int16)
 
 
@@ -80,8 +82,9 @@
 
 
 def steps_of(packed_ref):
-    scales = to_float(packed_ref[:, packed_ref.shape[1] - SCALE_LANES :])
-    exponents = pltpu.roll(scales, EXPONENT_AT, 1)
+    lanes = DK if packed_ref.shape[1] <= (HALF + 1) * DK else 2 * DK
+    scales = to_float(packed_ref[:, packed_ref.shape[1] - lanes :])
+    exponents = pltpu.roll(scales, lanes // 2, 1)
     return scales * jnp.exp2(exponents) * (1.0 / (LEVELS * LEVELS))
 
 
@@ -101,8 +104,8 @@
     return kept_ref[:, block * DK : (block + 1) * DK] + rows
 
 
-def activate(kept_ref, got_ref, steps, part, head, history_ref, taps_ref, twist, row_step):
-    fresh = received(kept_ref, got_ref, steps, head)
+def activate(kept_ref, got_ref, steps, at, part, head, history_ref, taps_ref, twist, row_step):
+    fresh = received(kept_ref, got_ref, steps, at * H + head)
     column = part * HEADS_WIDTH + head * DK
     carried = history_ref[:, column : column + DK]
     taps = taps_ref[jnp.bitwise_xor(column // TAP_WIDTH, twist)]
@@ -116,7 +119,7 @@
 
 
 def keys_kernel(
-    twist_ref, query_ref, query_got_ref, key_ref, key_got_ref, history_ref, near_ref, far_ref,
+    twist_ref, kept_ref, got_ref, history_ref, near_ref, far_ref,
     state_hbm, beta_ref, key_seen_ref, query_seen_ref, pulls_ref, weights_ref, taps_ref,
     state_ref, sems,
 ):
@@ -137,18 +140,17 @@
         taps_ref[at] = some[at % 4 * TAPS : (at % 4 + 1) * TAPS]
     row = lax.broadcasted_iota(jnp.int32, (ROWS, DK), 0)
     row_step = row % STEPS
-    query_steps, key_steps = steps_of(query_got_ref), steps_of(key_got_ref)
-    gates = received(key_ref, key_got_ref, key_steps, BLOCKS)
+    steps = steps_of(got_ref)
+    gates = received(kept_ref, got_ref, steps, 2 * H)
     for head in range(H):
         key = unit_length(
             activate(
-                key_ref, key_got_ref, key_steps, 1, head, history_ref, taps_ref, twist, row_step
+                kept_ref, got_ref, steps, 1, 1, head, history_ref, taps_ref, twist, row_step
             )
         )
         query = unit_length(
             activate(
-                query_ref, query_got_ref, query_steps, 0, head, history_ref, taps_ref, twist,
-                row_step,
+                kept_ref, got_ref, steps, 0, 0, head, history_ref, taps_ref, twist, row_step
             )
         )
         beta_logit = jnp.broadcast_to(gates[:, head : head + 1], (ROWS, DK))
@@ -200,7 +202,7 @@
     value_steps = steps_of(value_got_ref)
     for head in range(H):
         value = activate(
-            value_ref, value_got_ref, value_steps, 2, head, history_ref, taps_ref, twist, row_step
+            value_ref, value_got_ref, value_steps, 0, 2, head, history_ref, taps_ref, twist, row_step
         )
         base = beta_ref[head] * value - key_seen_ref[head]
         solved = base
@@ -226,7 +228,7 @@
         out_ref[quad] = jnp.concatenate(joined, axis=0).astype(jnp.bfloat16)
 
 
-def run_delta(slots, halves, lengths, queries, keys, values, history, twist, taps, state):
+def run_delta(slots, halves, lengths, keys, values, history, twist, taps, state):
     smem = pl.BlockSpec(memory_space=pltpu.SMEM)
     vmem = pl.BlockSpec(memory_space=pltpu.VMEM)
     params = pltpu.CompilerParams(vmem_limit_bytes=32 * 1024 * 1024)
@@ -238,7 +240,7 @@
     prepared = pl.pallas_call(
         keys_kernel,
         out_shape=[per_head] * 3 + lags + [tap_blocks],
-        in_specs=[smem] + [vmem] * 7 + [pl.BlockSpec(memory_space=pl.ANY)],
+        in_specs=[smem] + [vmem] * 5 + [pl.BlockSpec(memory_space=pl.ANY)],
         out_specs=[vmem] * 6,
         scratch_shapes=[
             pltpu.VMEM(state.shape, jnp.float32),
@@ -247,7 +249,7 @@
         compiler_params=params,
         cost_estimate=pl.CostEstimate(flops=40_000_000, bytes_accessed=9_000_000, transcendentals=0),
         name="keys_part",
-    )(twist, *queries, *keys, history, *taps, state)
+    )(twist, *keys, history, *taps, state)
     return pl.pallas_call(
         values_kernel,
         out_shape=jax.ShapeDtypeStruct((UNITS // 4, 2 * ROWS, DK), jnp.bfloat16),
@@ -331,17 +333,17 @@
     pack_rows(total[half:], packed_ref)
 
 
-def run_product(mine, theirs, weights, part, gates=()):
+def run_product(mine, theirs, weights, first, parts, gates=()):
     vmem = pl.BlockSpec(memory_space=pltpu.VMEM)
-    block = pl.BlockSpec((mine.shape[1], HEADS_WIDTH), lambda i: (0, part))
+    block = pl.BlockSpec((mine.shape[1], parts * HEADS_WIDTH), lambda i: (0, first // parts))
     half = mine.shape[0] // 2
-    width = HEADS_WIDTH + len(gates) * DK
+    width = parts * HEADS_WIDTH + len(gates) * DK
     return pl.pallas_call(
         product_kernel,
         grid=(1,),
         out_shape=[
             jax.ShapeDtypeStruct((half, width), jnp.float32),
-            jax.ShapeDtypeStruct((half, width + SCALE_LANES), jnp.int16),
+            jax.ShapeDtypeStruct((half, width + scale_lanes(width // DK)), jnp.int16),
         ],
         in_specs=[vmem, vmem, block, block] + [vmem] * len(gates),
         out_specs=[vmem] * 2,
@@ -351,11 +353,7 @@
     )(mine, theirs, *weights, *gates)
 
 
-def combine_kernel(kept_ref, got_ref, *refs):
-    tap_refs, (still_ref, packed_ref), wide_refs = refs[:-2], refs[-2:], ()
-    if tap_refs:
-        tap_refs, wide_refs = refs[:2], refs[2:3]
-        still_ref, packed_ref = refs[3:]
+def combine_kernel(kept_ref, got_ref, still_ref, packed_ref):
     half = still_ref.shape[0]
     steps = steps_of(got_ref)
     sent = []
@@ -366,30 +364,25 @@
         sent.append(total[half:])
     sent = jnp.concatenate(sent, axis=1)
     pack_rows(fold_rows(sent) if half == ROWS else sent, packed_ref)
-    for wide_ref in wide_refs:
-        rows = tap_refs[0].shape[0]
-        wide_ref[:rows] = tap_refs[0][...]
-        wide_ref[rows:] = tap_refs[1][...]
-
-
-def run_combine(kept, got, taps=()):
+
+
+def run_combine(kept, got):
     vmem = pl.BlockSpec(memory_space=pltpu.VMEM)
     half, width = kept.shape[0] // 2, kept.shape[1]
-    packed = (2 * ROWS, width // 2 + SCALE_LANES) if half == ROWS else (half, width + SCALE_LANES)
-    wide = [jax.ShapeDtypeStruct((2 * taps[0].shape[0], TAP_WIDTH), jnp.bfloat16)] if taps else []
+    rows, packed = (2 * ROWS, width // 2) if half == ROWS else (half, width)
+    packed = (rows, packed + scale_lanes(packed // DK))
     return pl.pallas_call(
         combine_kernel,
-        out_shape=wide
-        + [
+        out_shape=[
             jax.ShapeDtypeStruct((half, width), jnp.float32),
             jax.ShapeDtypeStruct(packed, jnp.int16),
         ],
-        in_specs=[vmem] * (2 + len(taps)),
-        out_specs=[vmem] * (2 + len(wide)),
+        in_specs=[vmem] * 2,
+        out_specs=[vmem] * 2,
         compiler_params=pltpu.CompilerParams(vmem_limit_bytes=32 * 1024 * 1024),
         cost_estimate=pl.CostEstimate(flops=0, bytes_accessed=0, transcendentals=0),
         name="combine",
-    )(kept, got, *taps)
+    )(kept, got)
 
 
 def swap(value, bit, devices):
@@ -415,7 +408,6 @@
     row_count = tokens.shape[0]
     chips = devices // 2
 
-    old_slots, halves = unit_tables(old_heads, new_units)
     bits = [1 << b for b in range(1, devices.bit_length() - 1)]
     steps = jnp.arange(STEPS, dtype=jnp.int32)
     offered = (slot_of[:, None] * STEPS + steps[None, :]).reshape(-1)
@@ -431,47 +423,49 @@
     ride = conv_weight.shape[1] == 2 * TAP_WIDTH and len(bits) == 3
     taps = conv_weight
     if ride:
-        taps = jnp.concatenate([taps, swap(taps, 1, devices)], axis=1)
+        taps = jnp.concatenate([taps[:, :TAP_WIDTH], taps[:, TAP_WIDTH:]], axis=0)
+        for bit in (1, 2):
+            taps = jnp.concatenate([taps, swap(taps, bit, devices)], axis=0)
     else:
         taps = lax.all_gather(taps, "heads", axis=1, tiled=True)
-    blocks = range(0, taps.shape[1], TAP_WIDTH)
-    taps = jnp.concatenate([taps[:, at : at + TAP_WIDTH] for at in blocks], axis=0)
+        blocks = range(0, taps.shape[1], TAP_WIDTH)
+        taps = jnp.concatenate([taps[:, at : at + TAP_WIDTH] for at in blocks], axis=0)
+    mine = in_order(mine, taps)
+    keys = run_product(mine, theirs, weights, 0, 2, gates)
+    mine = in_order(mine, *keys)
+    values = run_product(mine, theirs, weights, 2, 1)
+
+    slot_of, lengths, old_heads, new_units, carried = lax.optimization_barrier(
+        (slot_of, lengths, old_heads, new_units, conv_state, *values)
+    )[:5]
+    old_slots, halves = unit_tables(old_heads, new_units)
     my_rows = me * LOCAL + jnp.arange(LOCAL, dtype=jnp.int32)
     my_lengths = jnp.sum(
         jnp.where(slot_of[None, :] == my_rows[:, None], lengths[None, :], 0), axis=1
     )
-    carried = conv_state.reshape(LOCAL, TAPS - 1, -1)
     blank = jnp.zeros((1, carried.shape[2]), jnp.float32)
     history = jnp.concatenate([blank, carried[1], blank, carried[0]], axis=0)
-    mine = in_order(mine, taps, history, my_lengths, old_slots, halves)
-    query = run_product(mine, theirs, weights, 0)
-    mine = in_order(mine, *query)
-    key = run_product(mine, theirs, weights, 1, gates)
-    mine = in_order(mine, *key)
-    value = run_product(mine, theirs, weights, 2)
-
-    chunks = [query, key, value]
-    got = [swap(packed, bits[0], devices) for _, packed in chunks]
-    got[0] = in_order(got[0], *value)
-    far = swap(taps, bits[0], devices) if ride else taps
-    for level, bit in enumerate(bits[1:]):
-        for at in range(len(chunks)):
-            arrived = in_order(got[at], *chunks[at - 1]) if at else got[at]
-            if ride and level == 0 and at != 1:
-                taps, *chunks[at] = run_combine(chunks[at][0], arrived, (taps, far))
-                far = swap(taps, bits[1 + at // 2], devices)
-            else:
-                chunks[at] = run_combine(chunks[at][0], arrived)
-            got[at] = swap(chunks[at][1], bit, devices)
-    queries, keys, values = [(kept, came) for (kept, _), came in zip(chunks, got)]
     if ride:
+        taps = in_order(taps, *values)
+        taps = jnp.concatenate([taps, swap(taps, 4, devices)], axis=0)
+        far = swap(taps, 8, devices)
         twist, taps = (2 * me).reshape(1), (taps, far)
     else:
         half = TAP_BLOCKS // 2 * TAPS
         twist, taps = jnp.zeros(1, jnp.int32), (taps[:half], taps[half:])
 
+    chunks = [keys, values]
+    got = [swap(packed, bits[0], devices) for _, packed in chunks]
+    got[0] = in_order(got[0], *taps, history, my_lengths, old_slots, halves)
+    for level, bit in enumerate(bits[1:]):
+        for at in range(len(chunks)):
+            arrived = in_order(got[at], *chunks[at - 1]) if at else got[at]
+            chunks[at] = run_combine(chunks[at][0], arrived)
+            got[at] = swap(chunks[at][1], bit, devices)
+    keys, values = [(kept, came) for (kept, _), came in zip(chunks, got)]
+
     local_out = run_delta(
-        old_slots, halves, my_lengths, queries, keys, values, history, twist, taps, delta_state
+        old_slots, halves, my_lengths, keys, values, history, twist, taps, delta_state
     )
 
     placer = (offered[:, None] == jnp.arange(row_count * STEPS, dtype=jnp.int32)[None, :]).astype(

time: 79.9 us -> 71.5 us (0.89)
  starting transfers between devices: 22.7 us -> 18.3 us
  local copies, waits for them, and re-layouts: 10 us -> 7.79 us
  other arithmetic: 2.64 us -> 1.26 us
    ppermute x15 -> x12, starting transfers between devices: 18.4 us -> 14.8 us  [swap(): return lax.ppermute(value, 'heads', [(i, i ^ bit) for i in range(devices)])]
    slice x3 -> x1, local copies, waits for them, and re-layouts: 2.82 us -> 0.7 us  [on_device(): taps = jnp.concatenate([taps[:, :TAP_WIDTH], taps[:, TAP_WIDTH:]], axis=0)]
    squeeze x1, local copies, waits for them, and re-layouts: 1.19 us -> 0.07 us  [on_device(): history = jnp.concatenate([blank, carried[1], blank, carried[0]], axis=0)]
    unnamed x13 -> x22, local copies, waits for them, and re-layouts: 5.2 us -> 6 us
    pallas_call x6 -> x4, Pallas kernels: 2.81 us -> 2.28 us  [run_combine(): pl.pallas_call(combine_kernel, out_shape=[jax.ShapeDtypeStruct((half, wid...]
    ppermute x15 -> x12, waiting for transfers between devices: 24.8 us -> 25 us  [swap(): return lax.ppermute(value, 'heads', [(i, i ^ bit) for i in range(devices)])]
    pallas_call x3 -> x2, Pallas kernels: 3.4 us -> 3.34 us  [run_product(): pl.pallas_call(product_kernel, grid=(1,), out_shape=[jax.ShapeDtypeStruct...]
  transfers between devices with their start and end apart: 16 -> 13, of which waited for: 6 -> 7; matrix products, arithmetic and copies ran while one was open for 10% -> 5% of each run, Pallas kernels for 11% -> 9%
where the time goes in v1:
time: 71.5 us; the launch traced here: 71 us
  waiting for transfers between devices  31.6 us (44%)
  starting transfers between devices  18.3 us (26%)
  Pallas kernels  11.6 us (16%)
  local copies, waits for them, and re-layouts  7.79 us (11%)
  other arithmetic  1.26 us (2%)
    ppermute x12, waiting for transfers between devices, swap(): return lax.ppermute(value, 'heads', [(i, i ^ bit) for i in range(devices)])  25 us
    ppermute x12, starting transfers between devices, swap(): return lax.ppermute(value, 'heads', [(i, i ^ bit) for i in range(devices)])  14.8 us
    all_to_all x1, waiting for transfers between devices, on_device(): lax.all_to_all(sending, 'heads', split_axis=0, concat_axis=0, tiled=True)  6.68 us
    unnamed x22, local copies, waits for them, and re-layouts  6 us
    all_to_all x1, starting transfers between devices, on_device(): lax.all_to_all(sending, 'heads', split_axis=0, concat_axis=0, tiled=True)  3.5 us
    pallas_call x1, Pallas kernels, run_delta(): pl.pallas_call(keys_kernel, out_shape=[per_head] * 3 + lags + [tap_blocks...  3.37 us
    pallas_call x2, Pallas kernels, run_product(): pl.pallas_call(product_kernel, grid=(1,), out_shape=[jax.ShapeDtypeStruct...  3.34 us
    pallas_call x4, Pallas kernels, run_combine(): pl.pallas_call(combine_kernel, out_shape=[jax.ShapeDtypeStruct((half, wid...  2.28 us
  transfers between devices with their start and end apart: 13, of which 7 were waited for; matrix products, arithmetic and copies ran while one was open for 5% of the time, Pallas kernels for 9%

profile of v1, /device:TPU:0, one launch (start us, length us, event | category | flops | bytes accessed | tf_op | source)
XLA Modules:
  0.0 71.0 jit_solution(6389804890591060766)
XLA Ops:
  0.5 0.7 fusion.6
  1.2 0.6 pad_maximum_fusion.3
  1.8 1.5 %copy.20.refs_0_ = bf16[144,64]{1,0:T(8,128)(2,1)} copy(bf16[144,64]{0,1:T(8,128)(2,1)} %param.12) | data formatting | bytes 36864 | tf_op args[2]
  3.7 2.8 %collective-permute-done = bf16[8,384]{1,0:T(8,128)(2,1)S(1)} collective-permute-done((bf16[8,384]{1,0:T(8,128)(2,1)}, bf16[8,384]{1,0:T(8,128)(2,1)S(1)}, u32[]{:S(2)}, u32[]{:S(2)}) %collective-permute-start) | collective-permute-done | bytes 6176 | tf_op jit(solution)/shard_map/ppermute | solution.py:389
  6.5 3.0 %collective-permute-start.1 = (bf16[16,384]{1,0:T(8,128)(2,1)S(1)}, bf16[16,384]{1,0:T(8,128)(2,1)S(1)}, u32[]{:S(2)}, u32[]{:S(2)}) collective-permute-start(bf16[16,384]{1,0:T(8,128)(2,1)S(1)} %pad_maximum_fusion.2), channel_id=1, source_target_pairs={{0,2},{1,3},{2,0},{3,1},{4,6},{5,7},{6,4},{7,5},{8,10},{9,11},{10,... | collective-permute-start | bytes 36872 | tf_op jit(solution)/shard_map/ppermute | solution.py:389
  9.5 1.1 %copy-done.2 = bf16[32,4,2304]{2,1,0:T(4,128)(2,1)S(1)} copy-done((bf16[32,4,2304]{2,1,0:T(4,128)(2,1)S(1)}, bf16[32,4,2304]{2,1,0:T(4,128)(2,1)}, u32[]{:S(2)}) %copy-start.2) | copy-done | bytes 589848
  10.6 0.7 copy-done.4
  11.2 0.8 %token_rows.1 = (bf16[64,144]{1,0:T(8,128)(2,1)S(1)}, bf16[64,144]{1,0:T(8,128)(2,1)S(1)}) custom-call(s32[1]{0:T(128)} %bitcast.me_ref, s32[1,32]{1,0:T(1,128)S(1)} %bitcast.12, bf16[32,4,2304]{2,1,0:T(4,128)(2,1)S(1)} %copy-done.2), custom_call_target="tpu_custom_call" | custom-call | tf_op jit(solution)/shard_map/token_rows/pallas_call | solution.py:302
  12.1 2.0 %copy-done = bf16[144,12288]{1,0:T(8,128)(2,1)S(1)} copy-done((bf16[144,12288]{1,0:T(8,128)(2,1)S(1)}, bf16[144,12288]{1,0:T(8,128)(2,1)}, u32[]{:S(2)}) %copy-start) | copy-done | bytes 3538968
  14.1 0.8 %copy-done.3 = bf16[144,64]{1,0:T(8,128)(2,1)S(1)} copy-done((bf16[144,64]{1,0:T(8,128)(2,1)S(1)}, bf16[144,64]{1,0:T(8,128)(2,1)}, u32[]{:S(2)}) %copy-start.3) | copy-done | bytes 18456
  14.9 2.5 %partial_product.2 = (f32[32,8448]{1,0:T(8,128)S(1)}, s16[32,8704]{1,0:T(8,128)(2,1)S(1)}) custom-call(bf16[64,144]{1,0:T(8,128)(2,1)S(1)} %get-tuple-element.41.mine_ref, bf16[64,144]{1,0:T(8,128)(2,1)S(1)} %get-tuple-element.38.theirs_ref, bf16[144,12288]{1,0:T(8,128)(2,1)S(1)} %copy-done, bf16[144,12288]{1,0:T(8,128)(2,1)S(1)} %collective-permute-done.2.other_ref, ...), custom_call_target="tpu_custom_call" | custom-call | tf_op jit(solution)/shard_map/partial_product/pallas_call | solution.py:341
  17.5 0.8 %partial_product.3 = (f32[32,4096]{1,0:T(8,128)S(1)}, s16[32,4224]{1,0:T(8,128)(2,1)S(1)}) custom-call(bf16[64,144]{1,0:T(8,128)(2,1)S(1)} %get-tuple-element.41.mine_ref, bf16[64,144]{1,0:T(8,128)(2,1)S(1)} %get-tuple-element.38.theirs_ref, bf16[144,12288]{1,0:T(8,128)(2,1)S(1)} %copy-done, bf16[144,12288]{1,0:T(8,128)(2,1)S(1)} %collective-permute-done.2.other_ref), custom_call_target="tpu_custom_call" | custom-call | tf_op jit(solution)/shard_map/partial_product/pallas_call | solution.py:341
  18.3 1.6 %collective-permute-start.6 = (bf16[32,384]{1,0:T(8,128)(2,1)S(1)}, bf16[32,384]{1,0:T(8,128)(2,1)S(1)}, u32[]{:S(2)}, u32[]{:S(2)}) collective-permute-start(bf16[32,384]{1,0:T(8,128)(2,1)S(1)} %pad_maximum_fusion.1), channel_id=1, source_target_pairs={{0,4},{1,5},{2,6},{3,7},{4,0},{5,1},{6,2},{7,3},{8,12},{9,13},{10,... | collective-permute-start | bytes 73736 | tf_op jit(solution)/shard_map/ppermute | solution.py:389
  20.0 1.1 %collective-permute-start.5 = (s16[32,8704]{1,0:T(8,128)(2,1)S(1)}, s16[32,8704]{1,0:T(8,128)(2,1)S(1)}, u32[]{:S(2)}, u32[]{:S(2)}) collective-permute-start(s16[32,8704]{1,0:T(8,128)(2,1)S(1)} %get-tuple-element.40), channel_id=1, source_target_pairs={{0,2},{1,3},{2,0},{3,1},{4,6},{5,7},{6,4},{7,5},{8,10},{9,11},{10,... | collective-permute-start | bytes 1671176 | tf_op jit(solution)/shard_map/ppermute | solution.py:389
  21.1 0.9 %collective-permute-start.4 = (s16[32,4224]{1,0:T(8,128)(2,1)S(1)}, s16[32,4224]{1,0:T(8,128)(2,1)S(1)}, u32[]{:S(2)}, u32[]{:S(2)}) collective-permute-start(s16[32,4224]{1,0:T(8,128)(2,1)S(1)} %get-tuple-element.43), channel_id=1, source_target_pairs={{0,2},{1,3},{2,0},{3,1},{4,6},{5,7},{6,4},{7,5},{8,10},{9,11},{10,... | collective-permute-start | bytes 811016 | tf_op jit(solution)/shard_map/ppermute | solution.py:389
  22.8 2.6 %collective-permute-start.7 = (bf16[64,384]{1,0:T(8,128)(2,1)S(1)}, bf16[64,384]{1,0:T(8,128)(2,1)S(1)}, u32[]{:S(2)}, u32[]{:S(2)}) collective-permute-start(bf16[64,384]{1,0:T(8,128)(2,1)S(1)} %constant_dynamic-update-slice_fusion.near_ref), channel_id=1, source_target_pairs={{0,8},{1,9},{2,10},{3,11},{4,12},{5,13},{6,14},{7,15},{8,0},{9,1},... | collective-permute-start | bytes 147464 | tf_op jit(solution)/shard_map/ppermute | solution.py:389
  25.6 2.8 %collective-permute-done.7.far_ref = bf16[64,384]{1,0:T(8,128)(2,1)S(1)} collective-permute-done((bf16[64,384]{1,0:T(8,128)(2,1)S(1)}, bf16[64,384]{1,0:T(8,128)(2,1)S(1)}, u32[]{:S(2)}, u32[]{:S(2)}) %collective-permute-start.7) | collective-permute-done | bytes 49184 | tf_op jit(solution)/shard_map/ppermute | solution.py:389
  28.4 7.1 %collective-permute-done.5.got_ref = s16[32,8704]{1,0:T(8,128)(2,1)S(1)} collective-permute-done((s16[32,8704]{1,0:T(8,128)(2,1)S(1)}, s16[32,8704]{1,0:T(8,128)(2,1)S(1)}, u32[]{:S(2)}, u32[]{:S(2)}) %collective-permute-start.5) | collective-permute-done | bytes 557088 | tf_op jit(solution)/shard_map/ppermute | solution.py:389
  35.5 0.9 %combine.4 = (f32[16,8448]{1,0:T(8,128)S(1)}, s16[16,8704]{1,0:T(8,128)(2,1)S(1)}) custom-call(f32[32,8448]{1,0:T(8,128)S(1)} %get-tuple-element.39.kept_ref, s16[32,8704]{1,0:T(8,128)(2,1)S(1)} %collective-permute-done.5.got_ref), custom_call_target="tpu_custom_call" | custom-call | tf_op jit(solution)/shard_map/combine/pallas_call | solution.py:374
  36.4 0.5 collective-permute-start.9
  36.9 3.0 %collective-permute-done.4.got_ref = s16[32,4224]{1,0:T(8,128)(2,1)S(1)} collective-permute-done((s16[32,4224]{1,0:T(8,128)(2,1)S(1)}, s16[32,4224]{1,0:T(8,128)(2,1)S(1)}, u32[]{:S(2)}, u32[]{:S(2)}) %collective-permute-start.4) | collective-permute-done | bytes 270368 | tf_op jit(solution)/shard_map/ppermute | solution.py:389
  39.9 0.5 combine.5
  40.4 0.5 collective-permute-start.8
  40.9 4.8 %collective-permute-done.9.got_ref = s16[16,8704]{1,0:T(8,128)(2,1)S(1)} collective-permute-done((s16[16,8704]{1,0:T(8,128)(2,1)S(1)}, s16[16,8704]{1,0:T(8,128)(2,1)S(1)}, u32[]{:S(2)}, u32[]{:S(2)}) %collective-permute-start.9) | collective-permute-done | bytes 278560 | tf_op jit(solution)/shard_map/ppermute | solution.py:389
  46.2 1.2 %collective-permute-start.11 = (s16[16,4352]{1,0:T(8,128)(2,1)S(1)}, s16[16,4352]{1,0:T(8,128)(2,1)S(1)}, u32[]{:S(2)}, u32[]{:S(2)}) collective-permute-start(s16[16,4352]{1,0:T(8,128)(2,1)S(1)} %get-tuple-element.57), channel_id=1, source_target_pairs={{0,8},{1,9},{2,10},{3,11},{4,12},{5,13},{6,14},{7,15},{8,0},{9,1},... | collective-permute-start | bytes 417800 | tf_op jit(solution)/shard_map/ppermute | solution.py:389
  47.8 2.4 %collective-permute-start.10 = (s16[16,2176]{1,0:T(8,128)(2,1)S(1)}, s16[16,2176]{1,0:T(8,128)(2,1)S(1)}, u32[]{:S(2)}, u32[]{:S(2)}) collective-permute-start(s16[16,2176]{1,0:T(8,128)(2,1)S(1)} %get-tuple-element.60), channel_id=1, source_target_pairs={{0,8},{1,9},{2,10},{3,11},{4,12},{5,13},{6,14},{7,15},{8,0},{9,1},... | collective-permute-start | bytes 208904 | tf_op jit(solution)/shard_map/ppermute | solution.py:389
  50.1 4.5 %collective-permute-done.11.got_ref = s16[16,4352]{1,0:T(8,128)(2,1)S(1)} collective-permute-done((s16[16,4352]{1,0:T(8,128)(2,1)S(1)}, s16[16,4352]{1,0:T(8,128)(2,1)S(1)}, u32[]{:S(2)}, u32[]{:S(2)}) %collective-permute-start.11) | collective-permute-done | bytes 139296 | tf_op jit(solution)/shard_map/ppermute | solution.py:389
  54.6 3.4 %keys_part.1 = (f32[32,8,128]{2,1,0:T(8,128)S(1)}, f32[32,8,128]{2,1,0:T(8,128)S(1)}, f32[32,8,128]{2,1,0:T(8,128)S(1)}, f32[3,32,8,128]{3,2,1,0:T(8,128)S(1)}, ...) custom-call(s32[1]{0:T(128)} %bitcast.2.twist_ref, f32[8,8448]{1,0:T(8,128)S(1)} %get-tuple-element.56.kept_ref, ...), custom_call_target="tpu_custom_call" | custom-call | flops 40000000 | bytes 9000000 | tf_op jit(solution)/shard_map/keys_part/pallas_call | solution.py:240
  58.0 1.8 %values_part.1 = bf16[16,16,128]{2,1,0:T(8,128)(2,1)} custom-call(s32[64]{0:T(128)S(1)} %select_reduce_fusion.slots_ref, s32[64]{0:T(128)S(1)} %get-tuple-element.73.halves_ref, s32[2]{0:T(128)S(1)} %fusion.4.lengths_ref, s32[1]{0:T(128)} %bitcast.2.twist_ref, f32[8,4096]{1,0:T(8,128)S(1)} %get-tuple-element.59.value_ref, ...), custom_call_target="tpu_custom_call" | custom-call | flops 4000000 | bytes 2000000 | tf_op jit(solution)/shard_map/values_part/pallas_call | solution.py:253
  59.8 3.5 %all-to-all-start = ((bf16[16,16,128]{2,1,0:T(8,128)(2,1)}), bf16[16,16,128]{2,1,0:T(8,128)(2,1)S(1)}, u32[]{:S(2)}, u32[]{:S(2)}) async-start(bf16[16,16,128]{2,1,0:T(8,128)(2,1)} %values_part.1), calls=%async_computation | async-start | bytes 131072 | tf_op jit(solution)/shard_map/all_to_all | solution.py:477
  63.5 6.7 %all-to-all-done = bf16[16,16,128]{2,1,0:T(8,128)(2,1)S(1)} async-done(((bf16[16,16,128]{2,1,0:T(8,128)(2,1)}), bf16[16,16,128]{2,1,0:T(8,128)(2,1)S(1)}, u32[]{:S(2)}, u32[]{:S(2)}) %all-to-all-start) | async-done | bytes 65568 | tf_op jit(solution)/shard_map/all_to_all | solution.py:477
  70.4 0.7 reshape.49
  (45 shorter events, 3.2 us)
Async XLA Ops:
  0.0 12.1 %collective-permute-start.2 = (bf16[144,12288]{1,0:T(8,128)(2,1)}, bf16[144,12288]{1,0:T(8,128)(2,1)S(1)}, u32[]{:S(2)}, u32[]{:S(2)}) collective-permute-start(bf16[144,12288]{1,0:T(8,128)(2,1)} %block_ref.3), channel_id=1, source_target_pairs={{0,1},{1,0},{2,3},{3,2},{4,5},{5,4},{6,7},{7,6},{8,9},{9,8},{10,11... | collective-permute-start | bytes 10616840 | tf_op jit(solution)/shard_map/ppermute | solution.py:389
  1.8 4.8 %collective-permute-start = (bf16[8,384]{1,0:T(8,128)(2,1)}, bf16[8,384]{1,0:T(8,128)(2,1)S(1)}, u32[]{:S(2)}, u32[]{:S(2)}) collective-permute-start(bf16[8,384]{1,0:T(8,128)(2,1)} %pad_maximum_fusion.3), channel_id=1, source_target_pairs={{0,1},{1,0},{2,3},{3,2},{4,5},{5,4},{6,7},{7,6},{8,9},{9,8},{10,11... | collective-permute-start | bytes 18440 | tf_op jit(solution)/shard_map/ppermute | solution.py:389
  3.3 8.8 %collective-permute-start.3 = (bf16[144,64]{1,0:T(8,128)(2,1)}, bf16[144,64]{1,0:T(8,128)(2,1)}, u32[]{:S(2)}, u32[]{:S(2)}) collective-permute-start(bf16[144,64]{1,0:T(8,128)(2,1)} %copy.20.refs_0_), channel_id=1, source_target_pairs={{0,1},{1,0},{2,3},{3,2},{4,5},{5,4},{6,7},{7,6},{8,9},{9,8},{10,11... | collective-permute-start | bytes 55304 | tf_op jit(solution)/shard_map/ppermute | solution.py:389
  6.5 5.5 %collective-permute-start.1 = (bf16[16,384]{1,0:T(8,128)(2,1)S(1)}, bf16[16,384]{1,0:T(8,128)(2,1)S(1)}, u32[]{:S(2)}, u32[]{:S(2)}) collective-permute-start(bf16[16,384]{1,0:T(8,128)(2,1)S(1)} %pad_maximum_fusion.2), channel_id=1, source_target_pairs={{0,2},{1,3},{2,0},{3,1},{4,6},{5,7},{6,4},{7,5},{8,10},{9,11},{10,... | collective-permute-start | bytes 36872 | tf_op jit(solution)/shard_map/ppermute | solution.py:389
  9.5 1.1 %copy-start.2 = (bf16[32,4,2304]{2,1,0:T(4,128)(2,1)S(1)}, bf16[32,4,2304]{2,1,0:T(4,128)(2,1)}, u32[]{:S(2)}) copy-start(bf16[32,4,2304]{2,1,0:T(4,128)(2,1)} %tokens_hbm.1) | copy-start | bytes 1769476
  10.6 0.7 copy-start.4
  12.1 2.0 %copy-start = (bf16[144,12288]{1,0:T(8,128)(2,1)S(1)}, bf16[144,12288]{1,0:T(8,128)(2,1)}, u32[]{:S(2)}) copy-start(bf16[144,12288]{1,0:T(8,128)(2,1)} %block_ref.3) | copy-start | bytes 10616836
  14.1 0.8 %copy-start.3 = (bf16[144,64]{1,0:T(8,128)(2,1)S(1)}, bf16[144,64]{1,0:T(8,128)(2,1)}, u32[]{:S(2)}) copy-start(bf16[144,64]{1,0:T(8,128)(2,1)} %copy.20.refs_0_) | copy-start | bytes 55300
  17.4 4.6 %copy-start.6 = (f32[2,3,12288]{2,0,1:T(2,128)S(1)}, f32[2,3,12288]{2,0,1:T(2,128)}, u32[]{:S(2)}) copy-start(f32[2,3,12288]{2,0,1:T(2,128)} %param.15) | copy-start | bytes 884740
  17.4 5.1 %copy-start.5 = (s32[32]{0:T(128)S(1)}, s32[32]{0:T(128)}, u32[]{:S(2)}) copy-start(s32[32]{0:T(128)} %param.18) | copy-start | bytes 388
  17.4 5.1 %copy-start.7 = (s32[32]{0:T(128)S(1)}, s32[32]{0:T(128)}, u32[]{:S(2)}) copy-start(s32[32]{0:T(128)} %param.19) | copy-start | bytes 388
  17.4 5.3 %copy-start.8 = (s32[64]{0:T(128)S(1)}, s32[64]{0:T(128)}, u32[]{:S(2)}) copy-start(s32[64]{0:T(128)} %param.17) | copy-start | bytes 772
  17.4 5.3 %copy-start.9 = (s32[32]{0:T(128)S(1)}, s32[32]{0:T(128)}, u32[]{:S(2)}) copy-start(s32[32]{0:T(128)} %param.16) | copy-start | bytes 388
  18.3 36.3 %copy-start.1 = (f32[2,32,128,128]{3,2,1,0:T(8,128)S(1)}, f32[2,32,128,128]{3,2,1,0:T(8,128)}, u32[]{:S(2)}) copy-start(f32[2,32,128,128]{3,2,1,0:T(8,128)} %state_hbm.1) | copy-start | bytes 12582916
  18.3 4.5 %collective-permute-start.6 = (bf16[32,384]{1,0:T(8,128)(2,1)S(1)}, bf16[32,384]{1,0:T(8,128)(2,1)S(1)}, u32[]{:S(2)}, u32[]{:S(2)}) collective-permute-start(bf16[32,384]{1,0:T(8,128)(2,1)S(1)} %pad_maximum_fusion.1), channel_id=1, source_target_pairs={{0,4},{1,5},{2,6},{3,7},{4,0},{5,1},{6,2},{7,3},{8,12},{9,13},{10,... | collective-permute-start | bytes 73736 | tf_op jit(solution)/shard_map/ppermute | solution.py:389
  20.0 15.6 %collective-permute-start.5 = (s16[32,8704]{1,0:T(8,128)(2,1)S(1)}, s16[32,8704]{1,0:T(8,128)(2,1)S(1)}, u32[]{:S(2)}, u32[]{:S(2)}) collective-permute-start(s16[32,8704]{1,0:T(8,128)(2,1)S(1)} %get-tuple-element.40), channel_id=1, source_target_pairs={{0,2},{1,3},{2,0},{3,1},{4,6},{5,7},{6,4},{7,5},{8,10},{9,11},{10,... | collective-permute-start | bytes 1671176 | tf_op jit(solution)/shard_map/ppermute | solution.py:389
  21.1 18.8 %collective-permute-start.4 = (s16[32,4224]{1,0:T(8,128)(2,1)S(1)}, s16[32,4224]{1,0:T(8,128)(2,1)S(1)}, u32[]{:S(2)}, u32[]{:S(2)}) collective-permute-start(s16[32,4224]{1,0:T(8,128)(2,1)S(1)} %get-tuple-element.43), channel_id=1, source_target_pairs={{0,2},{1,3},{2,0},{3,1},{4,6},{5,7},{6,4},{7,5},{8,10},{9,11},{10,... | collective-permute-start | bytes 811016 | tf_op jit(solution)/shard_map/ppermute | solution.py:389
  22.8 5.6 %collective-permute-start.7 = (bf16[64,384]{1,0:T(8,128)(2,1)S(1)}, bf16[64,384]{1,0:T(8,128)(2,1)S(1)}, u32[]{:S(2)}, u32[]{:S(2)}) collective-permute-start(bf16[64,384]{1,0:T(8,128)(2,1)S(1)} %constant_dynamic-update-slice_fusion.near_ref), channel_id=1, source_target_pairs={{0,8},{1,9},{2,10},{3,11},{4,12},{5,13},{6,14},{7,15},{8,0},{9,1},... | collective-permute-start | bytes 147464 | tf_op jit(solution)/shard_map/ppermute | solution.py:389
  36.4 9.3 %collective-permute-start.9 = (s16[16,8704]{1,0:T(8,128)(2,1)S(1)}, s16[16,8704]{1,0:T(8,128)(2,1)S(1)}, u32[]{:S(2)}, u32[]{:S(2)}) collective-permute-start(s16[16,8704]{1,0:T(8,128)(2,1)S(1)} %get-tuple-element.52), channel_id=1, source_target_pairs={{0,4},{1,5},{2,6},{3,7},{4,0},{5,1},{6,2},{7,3},{8,12},{9,13},{10,... | collective-permute-start | bytes 835592 | tf_op jit(solution)/shard_map/ppermute | solution.py:389
  40.4 7.0 %collective-permute-start.8 = (s16[16,4224]{1,0:T(8,128)(2,1)S(1)}, s16[16,4224]{1,0:T(8,128)(2,1)S(1)}, u32[]{:S(2)}, u32[]{:S(2)}) collective-permute-start(s16[16,4224]{1,0:T(8,128)(2,1)S(1)} %get-tuple-element.55), channel_id=1, source_target_pairs={{0,4},{1,5},{2,6},{3,7},{4,0},{5,1},{6,2},{7,3},{8,12},{9,13},{10,... | collective-permute-start | bytes 405512 | tf_op jit(solution)/shard_map/ppermute | solution.py:389
  46.2 8.4 %collective-permute-start.11 = (s16[16,4352]{1,0:T(8,128)(2,1)S(1)}, s16[16,4352]{1,0:T(8,128)(2,1)S(1)}, u32[]{:S(2)}, u32[]{:S(2)}) collective-permute-start(s16[16,4352]{1,0:T(8,128)(2,1)S(1)} %get-tuple-element.57), channel_id=1, source_target_pairs={{0,8},{1,9},{2,10},{3,11},{4,12},{5,13},{6,14},{7,15},{8,0},{9,1},... | collective-permute-start | bytes 417800 | tf_op jit(solution)/shard_map/ppermute | solution.py:389
  47.8 10.2 %collective-permute-start.10 = (s16[16,2176]{1,0:T(8,128)(2,1)S(1)}, s16[16,2176]{1,0:T(8,128)(2,1)S(1)}, u32[]{:S(2)}, u32[]{:S(2)}) collective-permute-start(s16[16,2176]{1,0:T(8,128)(2,1)S(1)} %get-tuple-element.60), channel_id=1, source_target_pairs={{0,8},{1,9},{2,10},{3,11},{4,12},{5,13},{6,14},{7,15},{8,0},{9,1},... | collective-permute-start | bytes 208904 | tf_op jit(solution)/shard_map/ppermute | solution.py:389
  59.8 10.4 %all-to-all-start = ((bf16[16,16,128]{2,1,0:T(8,128)(2,1)}), bf16[16,16,128]{2,1,0:T(8,128)(2,1)S(1)}, u32[]{:S(2)}, u32[]{:S(2)}) async-start(bf16[16,16,128]{2,1,0:T(8,128)(2,1)} %values_part.1), calls=%async_computation | async-start | bytes 131072 | tf_op jit(solution)/shard_map/all_to_all | solution.py:477

commit v2 on v1

--- a/solution.py
+++ b/solution.py
@@ -19,6 +19,7 @@
 HEADS_WIDTH = H * DK
 LEVELS = 32767.0
 STATE_COPIES = 4
+WEIGHT_COPIES = 2
 TAP_WIDTH = 384
 TAP_BLOCKS = 3 * HEADS_WIDTH // TAP_WIDTH
 
@@ -104,11 +105,17 @@
     return kept_ref[:, block * DK : (block + 1) * DK] + rows
 
 
-def activate(kept_ref, got_ref, steps, at, part, head, history_ref, taps_ref, twist, row_step):
-    fresh = received(kept_ref, got_ref, steps, at * H + head)
+def tap_block(block, me):
+    other = jnp.bitwise_xor(block // 2, me)
+    place = (other & 1) + ((other >> 2) & 3) * 2 + ((other >> 1) & 1) * 8
+    return place * 2 + block % 2
+
+
+def activate(kept_ref, got_ref, steps, part, head, history_ref, taps_ref, twist, row_step):
+    fresh = received(kept_ref, got_ref, steps, head)
     column = part * HEADS_WIDTH + head * DK
     carried = history_ref[:, column : column + DK]
-    taps = taps_ref[jnp.bitwise_xor(column // TAP_WIDTH, twist)]
+    taps = taps_ref[tap_block(column // TAP_WIDTH, twist)]
     inner = column % TAP_WIDTH
     total = taps[TAPS - 1 :, inner : inner + DK] * fresh
     for lag in range(1, TAPS):
@@ -119,7 +126,7 @@
 
 
 def keys_kernel(
-    twist_ref, kept_ref, got_ref, history_ref, near_ref, far_ref,
+    twist_ref, query_ref, query_got_ref, key_ref, key_got_ref, history_ref, near_ref, far_ref,
     state_hbm, beta_ref, key_seen_ref, query_seen_ref, pulls_ref, weights_ref, taps_ref,
     state_ref, sems,
 ):
@@ -140,17 +147,18 @@
         taps_ref[at] = some[at % 4 * TAPS : (at % 4 + 1) * TAPS]
     row = lax.broadcasted_iota(jnp.int32, (ROWS, DK), 0)
     row_step = row % STEPS
-    steps = steps_of(got_ref)
-    gates = received(kept_ref, got_ref, steps, 2 * H)
+    query_steps, key_steps = steps_of(query_got_ref), steps_of(key_got_ref)
+    gates = received(key_ref, key_got_ref, key_steps, H)
     for head in range(H):
         key = unit_length(
             activate(
-                kept_ref, got_ref, steps, 1, 1, head, history_ref, taps_ref, twist, row_step
+                key_ref, key_got_ref, key_steps, 1, head, history_ref, taps_ref, twist, row_step
             )
         )
         query = unit_length(
             activate(
-                kept_ref, got_ref, steps, 0, 0, head, history_ref, taps_ref, twist, row_step
+                query_ref, query_got_ref, query_steps, 0, head, history_ref, taps_ref, twist,
+                row_step,
             )
         )
         beta_logit = jnp.broadcast_to(gates[:, head : head + 1], (ROWS, DK))
@@ -202,7 +210,7 @@
     value_steps = steps_of(value_got_ref)
     for head in range(H):
         value = activate(
-            value_ref, value_got_ref, value_steps, 0, 2, head, history_ref, taps_ref, twist, row_step
+            value_ref, value_got_ref, value_steps, 2, head, history_ref, taps_ref, twist, row_step
         )
         base = beta_ref[head] * value - key_seen_ref[head]
         solved = base
@@ -228,7 +236,7 @@
         out_ref[quad] = jnp.concatenate(joined, axis=0).astype(jnp.bfloat16)
 
 
-def run_delta(slots, halves, lengths, keys, values, history, twist, taps, state):
+def run_delta(slots, halves, lengths, queries, keys, values, history, twist, taps, state):
     smem = pl.BlockSpec(memory_space=pltpu.SMEM)
     vmem = pl.BlockSpec(memory_space=pltpu.VMEM)
     params = pltpu.CompilerParams(vmem_limit_bytes=32 * 1024 * 1024)
@@ -240,7 +248,7 @@
     prepared = pl.pallas_call(
         keys_kernel,
         out_shape=[per_head] * 3 + lags + [tap_blocks],
-        in_specs=[smem] + [vmem] * 5 + [pl.BlockSpec(memory_space=pl.ANY)],
+        in_specs=[smem] + [vmem] * 7 + [pl.BlockSpec(memory_space=pl.ANY)],
         out_specs=[vmem] * 6,
         scratch_shapes=[
             pltpu.VMEM(state.shape, jnp.float32),
@@ -249,7 +257,7 @@
         compiler_params=params,
         cost_estimate=pl.CostEstimate(flops=40_000_000, bytes_accessed=9_000_000, transcendentals=0),
         name="keys_part",
-    )(twist, *keys, history, *taps, state)
+    )(twist, *queries, *keys, history, *taps, state)
     return pl.pallas_call(
         values_kernel,
         out_shape=jax.ShapeDtypeStruct((UNITS // 4, 2 * ROWS, DK), jnp.bfloat16),
@@ -316,41 +324,65 @@
     )(me.reshape(1), slot_of.reshape(1, -1), tokens)
 
 
-def product_kernel(mine_ref, theirs_ref, block_ref, other_ref, *refs):
-    gate_refs, (kept_ref, packed_ref) = refs[:-2], refs[-2:]
+def product_kernel(first, count, mine_ref, theirs_ref, own_hbm, other_hbm, *refs):
+    scratch, refs = refs[-3:], refs[:-3]
+    (own_ref, other_ref, sems), gate_refs, out_refs = scratch, refs[: -2 * count], refs[-2 * count :]
     half = mine_ref.shape[0] // 2
-
-    def product(own, other):
-        total = jnp.dot(mine_ref[...], own, preferred_element_type=jnp.float32)
-        return total + jnp.dot(theirs_ref[...], other, preferred_element_type=jnp.float32)
-
-    total = product(block_ref[...], other_ref[...])
-    if gate_refs:
-        gates = product(gate_refs[0][...], gate_refs[1][...])
-        zeros = jnp.zeros((gates.shape[0], 2 * DK - gates.shape[1]), jnp.float32)
-        total = jnp.concatenate([total, gates, zeros], axis=1)
-    kept_ref[...] = total[:half]
-    pack_rows(total[half:], packed_ref)
-
-
-def run_product(mine, theirs, weights, first, parts, gates=()):
-    vmem = pl.BlockSpec(memory_space=pltpu.VMEM)
-    block = pl.BlockSpec((mine.shape[1], parts * HEADS_WIDTH), lambda i: (0, first // parts))
+    step = HEADS_WIDTH // WEIGHT_COPIES
+    copies = []
+    for at in range(count * WEIGHT_COPIES):
+        source, target = pl.ds(first * HEADS_WIDTH + at * step, step), pl.ds(at * step, step)
+        pair = [
+            pltpu.make_async_copy(hbm.at[:, source], ref.at[:, target], sems.at[side, at])
+            for side, (hbm, ref) in enumerate(((own_hbm, own_ref), (other_hbm, other_ref)))
+        ]
+        for copy in pair:
+            copy.start()
+        copies.append(pair)
+
+    def product(own, other, dims):
+        total = lax.dot_general(mine_ref[...], own, dims, preferred_element_type=jnp.float32)
+        return total + lax.dot_general(
+            theirs_ref[...], other, dims, preferred_element_type=jnp.float32
+        )
+
+    for part in range(count):
+        totals = []
+        for at in range(part * WEIGHT_COPIES, (part + 1) * WEIGHT_COPIES):
+            for copy in copies[at]:
+                copy.wait()
+            columns = pl.ds(at * step, step)
+            totals.append(
+                product(own_ref[:, columns], other_ref[:, columns], (((1,), (0,)), ((), ())))
+            )
+        if gate_refs and part == 0:
+            gates = product(gate_refs[0][...], gate_refs[1][...], (((1,), (1,)), ((), ())))
+            totals += [gates, jnp.zeros((gates.shape[0], 2 * DK - gates.shape[1]), jnp.float32)]
+        total = jnp.concatenate(totals, axis=1)
+        out_refs[2 * part][...] = total[:half]
+        pack_rows(total[half:], out_refs[2 * part + 1])
+
+
+def run_product(mine, theirs, weights, first, count, gates=()):
+    vmem, hbm = pl.BlockSpec(memory_space=pltpu.VMEM), pl.BlockSpec(memory_space=pl.ANY)
     half = mine.shape[0] // 2
-    width = parts * HEADS_WIDTH + len(gates) * DK
-    return pl.pallas_call(
-        product_kernel,
-        grid=(1,),
-        out_shape=[
-            jax.ShapeDtypeStruct((half, width), jnp.float32),
-            jax.ShapeDtypeStruct((half, width + scale_lanes(width // DK)), jnp.int16),
-        ],
-        in_specs=[vmem, vmem, block, block] + [vmem] * len(gates),
-        out_specs=[vmem] * 2,
-        compiler_params=pltpu.CompilerParams(vmem_limit_bytes=32 * 1024 * 1024),
+    outs = []
+    for part in range(count):
+        width = HEADS_WIDTH + (len(gates) * DK if part == 0 else 0)
+        outs.append(jax.ShapeDtypeStruct((half, width), jnp.float32))
+        outs.append(jax.ShapeDtypeStruct((half, width + scale_lanes(width // DK)), jnp.int16))
+    outs = pl.pallas_call(
+        functools.partial(product_kernel, first, count),
+        out_shape=outs,
+        in_specs=[vmem, vmem, hbm, hbm] + [vmem] * len(gates),
+        out_specs=[vmem] * len(outs),
+        scratch_shapes=[pltpu.VMEM((mine.shape[1], count * HEADS_WIDTH), jnp.bfloat16)] * 2
+        + [pltpu.SemaphoreType.DMA((2, count * WEIGHT_COPIES))],
+        compiler_params=pltpu.CompilerParams(vmem_limit_bytes=56 * 1024 * 1024),
         cost_estimate=pl.CostEstimate(flops=0, bytes_accessed=0, transcendentals=0),
         name="partial_product",
     )(mine, theirs, *weights, *gates)
+    return [outs[2 * part : 2 * part + 2] for part in range(count)]
 
 
 def combine_kernel(kept_ref, got_ref, still_ref, packed_ref):
@@ -415,29 +447,27 @@
     mine, theirs = run_rows(me, slot_of, tokens, depth, chips)
 
     weights = (qkv_weight, swap(qkv_weight, 1, devices))
-    gates = (gate_weight, swap(gate_weight, 1, devices))
-
-    def in_order(value, *earlier):
-        return lax.optimization_barrier((value,) + earlier)[0]
+    gate_columns = gate_weight.T
+    gates = (gate_columns, swap(gate_columns, 1, devices))
+
+    tie = lambda *values: lax.optimization_barrier(values)
 
     ride = conv_weight.shape[1] == 2 * TAP_WIDTH and len(bits) == 3
-    taps = conv_weight
     if ride:
-        taps = jnp.concatenate([taps[:, :TAP_WIDTH], taps[:, TAP_WIDTH:]], axis=0)
-        for bit in (1, 2):
-            taps = jnp.concatenate([taps, swap(taps, bit, devices)], axis=0)
+        taps = jnp.concatenate([conv_weight[:, :TAP_WIDTH], conv_weight[:, TAP_WIDTH:]], axis=0)
+        taps = jnp.concatenate([taps, swap(taps, 1, devices)], axis=0)
     else:
-        taps = lax.all_gather(taps, "heads", axis=1, tiled=True)
-        blocks = range(0, taps.shape[1], TAP_WIDTH)
-        taps = jnp.concatenate([taps[:, at : at + TAP_WIDTH] for at in blocks], axis=0)
-    mine = in_order(mine, taps)
-    keys = run_product(mine, theirs, weights, 0, 2, gates)
-    mine = in_order(mine, *keys)
-    values = run_product(mine, theirs, weights, 2, 1)
-
-    slot_of, lengths, old_heads, new_units, carried = lax.optimization_barrier(
-        (slot_of, lengths, old_heads, new_units, conv_state, *values)
-    )[:5]
+        taps = lax.all_gather(conv_weight, "heads", axis=1, tiled=True)
+        blocks = [block for bit in (0, 4) for block in range(TAP_BLOCKS) if block & 4 == bit]
+        taps = [taps[:, block * TAP_WIDTH : (block + 1) * TAP_WIDTH] for block in blocks]
+        taps = jnp.concatenate(taps, axis=0)
+    (queries,) = run_product(mine, theirs, weights, 0, 1)
+    mine, *queries = tie(mine, *queries)
+    keys, values = run_product(mine, theirs, weights, 1, 2, gates)
+
+    lengths, old_heads, new_units, carried, *values = tie(
+        lengths, old_heads, new_units, conv_state, *values
+    )
     old_slots, halves = unit_tables(old_heads, new_units)
     my_rows = me * LOCAL + jnp.arange(LOCAL, dtype=jnp.int32)
     my_lengths = jnp.sum(
@@ -445,27 +475,32 @@
     )
     blank = jnp.zeros((1, carried.shape[2]), jnp.float32)
     history = jnp.concatenate([blank, carried[1], blank, carried[0]], axis=0)
+    got = [swap(queries[1], bits[0], devices), swap(keys[1], bits[0], devices)]
+    got[0], history, my_lengths, old_slots, halves = tie(
+        got[0], history, my_lengths, old_slots, halves
+    )
     if ride:
-        taps = in_order(taps, *values)
+        taps, *values = tie(taps, *values)
         taps = jnp.concatenate([taps, swap(taps, 4, devices)], axis=0)
-        far = swap(taps, 8, devices)
-        twist, taps = (2 * me).reshape(1), (taps, far)
+        got[0], values[1], taps = tie(got[0], values[1], taps)
+        taps = jnp.concatenate([taps, swap(taps, 8, devices)], axis=0)
+        got[1], taps = tie(got[1], taps)
+        twist, taps = me.reshape(1), (taps, swap(taps, 2, devices))
     else:
         half = TAP_BLOCKS // 2 * TAPS
         twist, taps = jnp.zeros(1, jnp.int32), (taps[:half], taps[half:])
-
-    chunks = [keys, values]
-    got = [swap(packed, bits[0], devices) for _, packed in chunks]
-    got[0] = in_order(got[0], *taps, history, my_lengths, old_slots, halves)
-    for level, bit in enumerate(bits[1:]):
-        for at in range(len(chunks)):
-            arrived = in_order(got[at], *chunks[at - 1]) if at else got[at]
-            chunks[at] = run_combine(chunks[at][0], arrived)
-            got[at] = swap(chunks[at][1], bit, devices)
-    keys, values = [(kept, came) for (kept, _), came in zip(chunks, got)]
+    got.append(swap(values[1], bits[0], devices))
+    kept = [queries[0], keys[0], values[0]]
+    for bit in bits[1:]:
+        for at in range(3):
+            if at:
+                got[at], kept[at - 1] = tie(got[at], kept[at - 1])
+            kept[at], packed = run_combine(kept[at], got[at])
+            got[at] = swap(packed, bit, devices)
+    queries, keys, values = zip(kept, got)
 
     local_out = run_delta(
-        old_slots, halves, my_lengths, keys, values, history, twist, taps, delta_state
+        old_slots, halves, my_lengths, queries, keys, values, history, twist, taps, delta_state
     )
 
     placer = (offered[:, None] == jnp.arange(row_count * STEPS, dtype=jnp.int32)[None, :]).astype(

time: 71.5 us -> 74 us (1.035)
  waiting for transfers between devices: 31.6 us -> 22.3 us
  Pallas kernels: 11.6 us -> 17.3 us
  starting transfers between devices: 18.3 us -> 23.4 us
  local copies, waits for them, and re-layouts: 7.79 us -> 8.57 us
    ppermute x12 -> x15, waiting for transfers between devices: 25 us -> 15.6 us  [swap(): return lax.ppermute(value, 'heads', [(i, i ^ bit) for i in range(devices)])]
    pallas_call x2, Pallas kernels: 3.34 us -> 8.56 us  [run_product(): pl.pallas_call(functools.partial(product_kernel, first, count), out_shape...]
    ppermute x12 -> x15, starting transfers between devices: 14.8 us -> 19.8 us  [swap(): return lax.ppermute(value, 'heads', [(i, i ^ bit) for i in range(devices)])]
    unnamed x22 -> x30, local copies, waits for them, and re-layouts: 6 us -> 6.8 us
    pallas_call x4 -> x6, Pallas kernels: 2.28 us -> 2.8 us  [run_combine(): pl.pallas_call(combine_kernel, out_shape=[jax.ShapeDtypeStruct((half, wid...]
  transfers between devices with their start and end apart: 13 -> 16, of which waited for: 7 -> 8; matrix products, arithmetic and copies ran while one was open for 5% -> 3% of each run, Pallas kernels for 9% -> 15%
where the time goes in v2:
time: 74 us; the launch traced here: 73.4 us
  starting transfers between devices  23.4 us (32%)
  waiting for transfers between devices  22.3 us (30%)
  Pallas kernels  17.3 us (23%)
  local copies, waits for them, and re-layouts  8.57 us (12%)
  other arithmetic  1.37 us (2%)
    ppermute x15, starting transfers between devices, swap(): return lax.ppermute(value, 'heads', [(i, i ^ bit) for i in range(devices)])  19.8 us
    ppermute x15, waiting for transfers between devices, swap(): return lax.ppermute(value, 'heads', [(i, i ^ bit) for i in range(devices)])  15.6 us
    pallas_call x2, Pallas kernels, run_product(): pl.pallas_call(functools.partial(product_kernel, first, count), out_shape...  8.56 us
    unnamed x30, local copies, waits for them, and re-layouts  6.8 us
    all_to_all x1, waiting for transfers between devices, on_device(): lax.all_to_all(sending, 'heads', split_axis=0, concat_axis=0, tiled=True)  6.72 us
    all_to_all x1, starting transfers between devices, on_device(): lax.all_to_all(sending, 'heads', split_axis=0, concat_axis=0, tiled=True)  3.57 us
    pallas_call x1, Pallas kernels, run_delta(): pl.pallas_call(keys_kernel, out_shape=[per_head] * 3 + lags + [tap_blocks...  3.37 us
    pallas_call x6, Pallas kernels, run_combine(): pl.pallas_call(combine_kernel, out_shape=[jax.ShapeDtypeStruct((half, wid...  2.8 us
  transfers between devices with their start and end apart: 16, of which 8 were waited for; matrix products, arithmetic and copies ran while one was open for 3% of the time, Pallas kernels for 15%

profile of v2, /device:TPU:0, one launch (start us, length us, event | category | flops | bytes accessed | tf_op | source)
XLA Modules:
  0.0 73.4 jit_solution(8382269741161909707)
XLA Ops:
  0.5 0.7 fusion.6
  1.8 1.1 %copy-done.1 = bf16[32,4,2304]{2,1,0:T(4,128)(2,1)S(1)} copy-done((bf16[32,4,2304]{2,1,0:T(4,128)(2,1)S(1)}, bf16[32,4,2304]{2,1,0:T(4,128)(2,1)}, u32[]{:S(2)}) %copy-start.1) | copy-done | bytes 589848
  2.8 0.7 copy-done.7
  3.5 0.8 %token_rows.1 = (bf16[64,144]{1,0:T(8,128)(2,1)S(1)}, bf16[64,144]{1,0:T(8,128)(2,1)S(1)}) custom-call(s32[1]{0:T(128)} %bitcast.me_ref.twist_ref, s32[1,32]{1,0:T(1,128)S(1)} %bitcast.12, bf16[32,4,2304]{2,1,0:T(4,128)(2,1)S(1)} %copy-done.1), custom_call_target="tpu_custom_call" | custom-call | tf_op jit(solution)/shard_map/token_rows/pallas_call | solution.py:310
  4.3 0.6 copy-done.5
  5.5 1.0 %collective-permute-done.3 = bf16[8,384]{1,0:T(8,128)(2,1)} collective-permute-done((bf16[8,384]{1,0:T(8,128)(2,1)S(1)}, bf16[8,384]{1,0:T(8,128)(2,1)}, u32[]{:S(2)}, u32[]{:S(2)}) %collective-permute-start.3) | collective-permute-done | bytes 6176 | tf_op jit(solution)/shard_map/ppermute | solution.py:421
  6.5 0.7 pad_maximum_fusion.3
  7.2 1.7 %copy-done.9 = bf16[144,12288]{1,0:T(8,128)(2,1)} copy-done((bf16[144,12288]{1,0:T(8,128)(2,1)}, bf16[144,12288]{1,0:T(8,128)(2,1)S(1)}, u32[]{:S(2)}) %copy-start.9) | copy-done | bytes 3538968
  8.9 3.7 %partial_product.2 = (f32[32,4096]{1,0:T(8,128)}, s16[32,4224]{1,0:T(8,128)(2,1)}) custom-call(bf16[64,144]{1,0:T(8,128)(2,1)} %copy-done.5, bf16[64,144]{1,0:T(8,128)(2,1)} %copy-done.6, bf16[144,12288]{1,0:T(8,128)(2,1)} %own_hbm.3, bf16[144,12288]{1,0:T(8,128)(2,1)} %copy-done.9), custom_call_target="tpu_custom_call" | custom-call | tf_op jit(solution)/shard_map/partial_product/pallas_call | solution.py:374
  12.7 4.9 %partial_product.3 = (f32[32,4352]{1,0:T(8,128)}, s16[32,4480]{1,0:T(8,128)(2,1)}, f32[32,4096]{1,0:T(8,128)}, s16[32,4224]{1,0:T(8,128)(2,1)}) custom-call(bf16[64,144]{1,0:T(8,128)(2,1)} %copy-done.5, bf16[64,144]{1,0:T(8,128)(2,1)} %copy-done.6, bf16[144,12288]{1,0:T(8,128)(2,1)} %own_hbm.3, bf16[144,12288]{1,0:T(8,128)(2,1)} %copy-done.9, ...), custom_call_target="tpu_custom_call" | custom-call | tf_op jit(solution)/shard_map/partial_product/pallas_call | solution.py:374
  17.6 3.0 %collective-permute-start.4 = (bf16[16,384]{1,0:T(8,128)(2,1)S(1)}, bf16[16,384]{1,0:T(8,128)(2,1)S(1)}, u32[]{:S(2)}, u32[]{:S(2)}) collective-permute-start(bf16[16,384]{1,0:T(8,128)(2,1)S(1)} %pad_maximum_fusion.3), channel_id=1, source_target_pairs={{0,4},{1,5},{2,6},{3,7},{4,0},{5,1},{6,2},{7,3},{8,12},{9,13},{10,... | collective-permute-start | bytes 36872 | tf_op jit(solution)/shard_map/ppermute | solution.py:421
  20.9 1.6 %collective-permute-start.1 = (s16[32,4224]{1,0:T(8,128)(2,1)S(1)}, s16[32,4224]{1,0:T(8,128)(2,1)S(1)}, u32[]{:S(2)}, u32[]{:S(2)}) collective-permute-start(s16[32,4224]{1,0:T(8,128)(2,1)S(1)} %copy-done.12), channel_id=1, source_target_pairs={{0,2},{1,3},{2,0},{3,1},{4,6},{5,7},{6,4},{7,5},{8,10},{9,11},{10,... | collective-permute-start | bytes 811016 | tf_op jit(solution)/shard_map/ppermute | solution.py:421
  23.7 6.7 %collective-permute-done.1.got_ref = s16[32,4224]{1,0:T(8,128)(2,1)S(1)} collective-permute-done((s16[32,4224]{1,0:T(8,128)(2,1)S(1)}, s16[32,4224]{1,0:T(8,128)(2,1)S(1)}, u32[]{:S(2)}, u32[]{:S(2)}) %collective-permute-start.1) | collective-permute-done | bytes 270368 | tf_op jit(solution)/shard_map/ppermute | solution.py:421
  30.4 1.5 %collective-permute-start.5 = (s16[32,4224]{1,0:T(8,128)(2,1)}, s16[32,4224]{1,0:T(8,128)(2,1)S(1)}, u32[]{:S(2)}, u32[]{:S(2)}) collective-permute-start(s16[32,4224]{1,0:T(8,128)(2,1)} %get-tuple-element.82), channel_id=1, source_target_pairs={{0,2},{1,3},{2,0},{3,1},{4,6},{5,7},{6,4},{7,5},{8,10},{9,11},{10,... | collective-permute-start | bytes 811016 | tf_op jit(solution)/shard_map/ppermute | solution.py:421
  31.9 2.6 %collective-permute-start.7 = (bf16[32,384]{1,0:T(8,128)(2,1)S(1)}, bf16[32,384]{1,0:T(8,128)(2,1)S(1)}, u32[]{:S(2)}, u32[]{:S(2)}) collective-permute-start(bf16[32,384]{1,0:T(8,128)(2,1)S(1)} %pad_maximum_fusion.2), channel_id=1, source_target_pairs={{0,8},{1,9},{2,10},{3,11},{4,12},{5,13},{6,14},{7,15},{8,0},{9,1},... | collective-permute-start | bytes 73736 | tf_op jit(solution)/shard_map/ppermute | solution.py:421
  35.0 1.7 %collective-permute-done.7 = bf16[32,384]{1,0:T(8,128)(2,1)S(1)} collective-permute-done((bf16[32,384]{1,0:T(8,128)(2,1)S(1)}, bf16[32,384]{1,0:T(8,128)(2,1)S(1)}, u32[]{:S(2)}, u32[]{:S(2)}) %collective-permute-start.7) | collective-permute-done | bytes 24608 | tf_op jit(solution)/shard_map/ppermute | solution.py:421
  36.8 1.0 %copy-done.2 = f32[32,4352]{1,0:T(8,128)S(1)} copy-done((f32[32,4352]{1,0:T(8,128)S(1)}, f32[32,4352]{1,0:T(8,128)}, u32[]{:S(2)}) %copy-start.2) | copy-done | bytes 557080
  38.8 1.7 %collective-permute-start.10 = (s16[16,4224]{1,0:T(8,128)(2,1)S(1)}, s16[16,4224]{1,0:T(8,128)(2,1)S(1)}, u32[]{:S(2)}, u32[]{:S(2)}) collective-permute-start(s16[16,4224]{1,0:T(8,128)(2,1)S(1)} %get-tuple-element.98), channel_id=1, source_target_pairs={{0,4},{1,5},{2,6},{3,7},{4,0},{5,1},{6,2},{7,3},{8,12},{9,13},{10,... | collective-permute-start | bytes 405512 | tf_op jit(solution)/shard_map/ppermute | solution.py:421
  40.5 0.7 collective-permute-done.5.got_ref
  41.2 1.0 %copy-done.3 = f32[32,4096]{1,0:T(8,128)S(1)} copy-done((f32[32,4096]{1,0:T(8,128)S(1)}, f32[32,4096]{1,0:T(8,128)}, u32[]{:S(2)}) %copy-start.3) | copy-done | bytes 524312
  43.2 1.7 %collective-permute-start.14 = (bf16[64,384]{1,0:T(8,128)(2,1)S(1)}, bf16[64,384]{1,0:T(8,128)(2,1)S(1)}, u32[]{:S(2)}, u32[]{:S(2)}) collective-permute-start(bf16[64,384]{1,0:T(8,128)(2,1)S(1)} %pad_maximum_fusion.1.near_ref), channel_id=1, source_target_pairs={{0,2},{1,3},{2,0},{3,1},{4,6},{5,7},{6,4},{7,5},{8,10},{9,11},{10,... | collective-permute-start | bytes 147464 | tf_op jit(solution)/shard_map/ppermute | solution.py:421
  44.8 0.7 collective-permute-done.10.got_ref
  45.9 2.4 %collective-permute-start.12 = (s16[16,2176]{1,0:T(8,128)(2,1)S(1)}, s16[16,2176]{1,0:T(8,128)(2,1)S(1)}, u32[]{:S(2)}, u32[]{:S(2)}) collective-permute-start(s16[16,2176]{1,0:T(8,128)(2,1)S(1)} %get-tuple-element.107), channel_id=1, source_target_pairs={{0,8},{1,9},{2,10},{3,11},{4,12},{5,13},{6,14},{7,15},{8,0},{9,1},... | collective-permute-start | bytes 208904 | tf_op jit(solution)/shard_map/ppermute | solution.py:421
  48.7 0.7 collective-permute-start.13
  49.8 2.4 %collective-permute-start.11 = (s16[16,2176]{1,0:T(8,128)(2,1)S(1)}, s16[16,2176]{1,0:T(8,128)(2,1)S(1)}, u32[]{:S(2)}, u32[]{:S(2)}) collective-permute-start(s16[16,2176]{1,0:T(8,128)(2,1)S(1)} %get-tuple-element.104), channel_id=1, source_target_pairs={{0,8},{1,9},{2,10},{3,11},{4,12},{5,13},{6,14},{7,15},{8,0},{9,1},... | collective-permute-start | bytes 208904 | tf_op jit(solution)/shard_map/ppermute | solution.py:421
  52.2 3.5 %collective-permute-done.12.query_got_ref = s16[16,2176]{1,0:T(8,128)(2,1)S(1)} collective-permute-done((s16[16,2176]{1,0:T(8,128)(2,1)S(1)}, s16[16,2176]{1,0:T(8,128)(2,1)S(1)}, u32[]{:S(2)}, u32[]{:S(2)}) %collective-permute-start.12) | collective-permute-done | bytes 69664 | tf_op jit(solution)/shard_map/ppermute | solution.py:421
  55.7 1.2 %collective-permute-done.13.key_got_ref = s16[16,2304]{1,0:T(8,128)(2,1)S(1)} collective-permute-done((s16[16,2304]{1,0:T(8,128)(2,1)S(1)}, s16[16,2304]{1,0:T(8,128)(2,1)S(1)}, u32[]{:S(2)}, u32[]{:S(2)}) %collective-permute-start.13) | collective-permute-done | bytes 73760 | tf_op jit(solution)/shard_map/ppermute | solution.py:421
  56.9 3.4 %keys_part.1 = (f32[32,8,128]{2,1,0:T(8,128)S(1)}, f32[32,8,128]{2,1,0:T(8,128)S(1)}, f32[32,8,128]{2,1,0:T(8,128)S(1)}, f32[3,32,8,128]{3,2,1,0:T(8,128)S(1)}, ...) custom-call(s32[1]{0:T(128)} %bitcast.me_ref.twist_ref, f32[8,4096]{1,0:T(8,128)S(1)} %get-tuple-element.106.query_ref, ...), custom_call_target="tpu_custom_call" | custom-call | flops 40000000 | bytes 9000000 | tf_op jit(solution)/shard_map/keys_part/pallas_call | solution.py:248
  60.3 1.8 %values_part.1 = bf16[16,16,128]{2,1,0:T(8,128)(2,1)} custom-call(s32[64]{0:T(128)S(1)} %select_reduce_fusion.slots_ref, s32[64]{0:T(128)S(1)} %get-tuple-element.74.halves_ref, s32[2]{0:T(128)S(1)} %fusion.4.lengths_ref, s32[1]{0:T(128)} %bitcast.me_ref.twist_ref, f32[8,4096]{1,0:T(8,128)S(1)} %get-tuple-element.103.value_ref, ...), custom_call_target="tpu_custom_call" | custom-call | flops 4000000 | bytes 2000000 | tf_op jit(solution)/shard_map/values_part/pallas_call | solution.py:261
  62.1 3.6 %all-to-all-start = ((bf16[16,16,128]{2,1,0:T(8,128)(2,1)}), bf16[16,16,128]{2,1,0:T(8,128)(2,1)S(1)}, u32[]{:S(2)}, u32[]{:S(2)}) async-start(bf16[16,16,128]{2,1,0:T(8,128)(2,1)} %values_part.1), calls=%async_computation | async-start | bytes 131072 | tf_op jit(solution)/shard_map/all_to_all | solution.py:512
  65.9 6.7 %all-to-all-done = bf16[16,16,128]{2,1,0:T(8,128)(2,1)S(1)} async-done(((bf16[16,16,128]{2,1,0:T(8,128)(2,1)}), bf16[16,16,128]{2,1,0:T(8,128)(2,1)S(1)}, u32[]{:S(2)}, u32[]{:S(2)}) %all-to-all-start) | async-done | bytes 65568 | tf_op jit(solution)/shard_map/all_to_all | solution.py:512
  72.8 0.7 reshape.46
  (61 shorter events, 7.0 us)
Async XLA Ops:
  0.0 7.2 %collective-permute-start = (bf16[144,12288]{1,0:T(8,128)(2,1)}, bf16[144,12288]{1,0:T(8,128)(2,1)S(1)}, u32[]{:S(2)}, u32[]{:S(2)}) collective-permute-start(bf16[144,12288]{1,0:T(8,128)(2,1)} %own_hbm.3), channel_id=1, source_target_pairs={{0,1},{1,0},{2,3},{3,2},{4,5},{5,4},{6,7},{7,6},{8,9},{9,8},{10,11... | collective-permute-start | bytes 10616840 | tf_op jit(solution)/shard_map/ppermute | solution.py:421
  0.5 12.3 %collective-permute-start.2 = (bf16[64,144]{1,0:T(8,128)(2,1)}, bf16[64,144]{1,0:T(8,128)(2,1)}, u32[]{:S(2)}, u32[]{:S(2)}) collective-permute-start(bf16[64,144]{1,0:T(8,128)(2,1)} %bitcast.14), channel_id=1, source_target_pairs={{0,1},{1,0},{2,3},{3,2},{4,5},{5,4},{6,7},{7,6},{8,9},{9,8},{10,11... | collective-permute-start | bytes 55304 | tf_op jit(solution)/shard_map/ppermute | solution.py:421
  1.2 5.3 %collective-permute-start.3 = (bf16[8,384]{1,0:T(8,128)(2,1)S(1)}, bf16[8,384]{1,0:T(8,128)(2,1)}, u32[]{:S(2)}, u32[]{:S(2)}) collective-permute-start(bf16[8,384]{1,0:T(8,128)(2,1)S(1)} %pad_maximum_fusion.4), channel_id=1, source_target_pairs={{0,1},{1,0},{2,3},{3,2},{4,5},{5,4},{6,7},{7,6},{8,9},{9,8},{10,11... | collective-permute-start | bytes 18440 | tf_op jit(solution)/shard_map/ppermute | solution.py:421
  1.7 1.1 %copy-start.1 = (bf16[32,4,2304]{2,1,0:T(4,128)(2,1)S(1)}, bf16[32,4,2304]{2,1,0:T(4,128)(2,1)}, u32[]{:S(2)}) copy-start(bf16[32,4,2304]{2,1,0:T(4,128)(2,1)} %tokens_hbm.1) | copy-start | bytes 1769476
  2.8 0.7 copy-start.7
  4.3 0.6 copy-start.5
  4.9 0.6 copy-start.6
  7.2 1.7 %copy-start.9 = (bf16[144,12288]{1,0:T(8,128)(2,1)}, bf16[144,12288]{1,0:T(8,128)(2,1)S(1)}, u32[]{:S(2)}) copy-start(bf16[144,12288]{1,0:T(8,128)(2,1)S(1)} %collective-permute-done.other_hbm) | copy-start | bytes 10616836
  12.7 8.0 %copy-start.13 = (s32[64]{0:T(128)S(1)}, s32[64]{0:T(128)}, u32[]{:S(2)}) copy-start(s32[64]{0:T(128)} %param.17) | copy-start | bytes 772
  12.7 8.0 %copy-start.10 = (f32[2,3,12288]{2,0,1:T(2,128)S(1)}, f32[2,3,12288]{2,0,1:T(2,128)}, u32[]{:S(2)}) copy-start(f32[2,3,12288]{2,0,1:T(2,128)} %param.15) | copy-start | bytes 884740
  12.7 8.3 %copy-start.12 = (s16[32,4224]{1,0:T(8,128)(2,1)S(1)}, s16[32,4224]{1,0:T(8,128)(2,1)}, u32[]{:S(2)}) copy-start(s16[32,4224]{1,0:T(8,128)(2,1)} %get-tuple-element.65) | copy-start | bytes 811012
  12.7 10.4 %copy-start.8 = (s32[32]{0:T(128)S(1)}, s32[32]{0:T(128)}, u32[]{:S(2)}) copy-start(s32[32]{0:T(128)} %param.18) | copy-start | bytes 388
  12.7 10.3 %copy-start.11 = (s32[32]{0:T(128)S(1)}, s32[32]{0:T(128)}, u32[]{:S(2)}) copy-start(s32[32]{0:T(128)} %param.19) | copy-start | bytes 388
  12.7 10.7 %copy-start.14 = (s32[32]{0:T(128)S(1)}, s32[32]{0:T(128)}, u32[]{:S(2)}) copy-start(s32[32]{0:T(128)} %param.16) | copy-start | bytes 388
  12.7 21.8 %copy-start.4 = (f32[32,4096]{1,0:T(8,128)S(1)}, f32[32,4096]{1,0:T(8,128)}, u32[]{:S(2)}) copy-start(f32[32,4096]{1,0:T(8,128)} %get-tuple-element.87.kept_ref) | copy-start | bytes 1572868
  17.6 39.3 %copy-start = (f32[2,32,128,128]{3,2,1,0:T(8,128)S(1)}, f32[2,32,128,128]{3,2,1,0:T(8,128)}, u32[]{:S(2)}) copy-start(f32[2,32,128,128]{3,2,1,0:T(8,128)} %state_hbm.1) | copy-start | bytes 12582916
  17.6 6.0 %collective-permute-start.4 = (bf16[16,384]{1,0:T(8,128)(2,1)S(1)}, bf16[16,384]{1,0:T(8,128)(2,1)S(1)}, u32[]{:S(2)}, u32[]{:S(2)}) collective-permute-start(bf16[16,384]{1,0:T(8,128)(2,1)S(1)} %pad_maximum_fusion.3), channel_id=1, source_target_pairs={{0,4},{1,5},{2,6},{3,7},{4,0},{5,1},{6,2},{7,3},{8,12},{9,13},{10,... | collective-permute-start | bytes 36872 | tf_op jit(solution)/shard_map/ppermute | solution.py:421
  20.9 9.4 %collective-permute-start.1 = (s16[32,4224]{1,0:T(8,128)(2,1)S(1)}, s16[32,4224]{1,0:T(8,128)(2,1)S(1)}, u32[]{:S(2)}, u32[]{:S(2)}) collective-permute-start(s16[32,4224]{1,0:T(8,128)(2,1)S(1)} %copy-done.12), channel_id=1, source_target_pairs={{0,2},{1,3},{2,0},{3,1},{4,6},{5,7},{6,4},{7,5},{8,10},{9,11},{10,... | collective-permute-start | bytes 811016 | tf_op jit(solution)/shard_map/ppermute | solution.py:421
  22.5 14.3 %collective-permute-start.6 = (s16[32,4480]{1,0:T(8,128)(2,1)}, s16[32,4480]{1,0:T(8,128)(2,1)S(1)}, u32[]{:S(2)}, u32[]{:S(2)}) collective-permute-start(s16[32,4480]{1,0:T(8,128)(2,1)} %get-tuple-element.84), channel_id=1, source_target_pairs={{0,2},{1,3},{2,0},{3,1},{4,6},{5,7},{6,4},{7,5},{8,10},{9,11},{10,... | collective-permute-start | bytes 860168 | tf_op jit(solution)/shard_map/ppermute | solution.py:421
  30.4 10.8 %collective-permute-start.5 = (s16[32,4224]{1,0:T(8,128)(2,1)}, s16[32,4224]{1,0:T(8,128)(2,1)S(1)}, u32[]{:S(2)}, u32[]{:S(2)}) collective-permute-start(s16[32,4224]{1,0:T(8,128)(2,1)} %get-tuple-element.82), channel_id=1, source_target_pairs={{0,2},{1,3},{2,0},{3,1},{4,6},{5,7},{6,4},{7,5},{8,10},{9,11},{10,... | collective-permute-start | bytes 811016 | tf_op jit(solution)/shard_map/ppermute | solution.py:421
  31.9 4.9 %collective-permute-start.7 = (bf16[32,384]{1,0:T(8,128)(2,1)S(1)}, bf16[32,384]{1,0:T(8,128)(2,1)S(1)}, u32[]{:S(2)}, u32[]{:S(2)}) collective-permute-start(bf16[32,384]{1,0:T(8,128)(2,1)S(1)} %pad_maximum_fusion.2), channel_id=1, source_target_pairs={{0,8},{1,9},{2,10},{3,11},{4,12},{5,13},{6,14},{7,15},{8,0},{9,1},... | collective-permute-start | bytes 73736 | tf_op jit(solution)/shard_map/ppermute | solution.py:421
  36.8 1.1 %copy-start.2 = (f32[32,4352]{1,0:T(8,128)S(1)}, f32[32,4352]{1,0:T(8,128)}, u32[]{:S(2)}) copy-start(f32[32,4352]{1,0:T(8,128)} %get-tuple-element.83.kept_ref) | copy-start | bytes 1671172
  38.4 9.9 %collective-permute-start.9 = (s16[16,4480]{1,0:T(8,128)(2,1)S(1)}, s16[16,4480]{1,0:T(8,128)(2,1)S(1)}, u32[]{:S(2)}, u32[]{:S(2)}) collective-permute-start(s16[16,4480]{1,0:T(8,128)(2,1)S(1)} %get-tuple-element.96), channel_id=1, source_target_pairs={{0,4},{1,5},{2,6},{3,7},{4,0},{5,1},{6,2},{7,3},{8,12},{9,13},{10,... | collective-permute-start | bytes 430088 | tf_op jit(solution)/shard_map/ppermute | solution.py:421
  38.8 6.7 %collective-permute-start.10 = (s16[16,4224]{1,0:T(8,128)(2,1)S(1)}, s16[16,4224]{1,0:T(8,128)(2,1)S(1)}, u32[]{:S(2)}, u32[]{:S(2)}) collective-permute-start(s16[16,4224]{1,0:T(8,128)(2,1)S(1)} %get-tuple-element.98), channel_id=1, source_target_pairs={{0,4},{1,5},{2,6},{3,7},{4,0},{5,1},{6,2},{7,3},{8,12},{9,13},{10,... | collective-permute-start | bytes 405512 | tf_op jit(solution)/shard_map/ppermute | solution.py:421
  41.2 1.0 %copy-start.3 = (f32[32,4096]{1,0:T(8,128)S(1)}, f32[32,4096]{1,0:T(8,128)}, u32[]{:S(2)}) copy-start(f32[32,4096]{1,0:T(8,128)} %get-tuple-element.78.kept_ref) | copy-start | bytes 1572868
  42.8 6.6 %collective-permute-start.8 = (s16[16,4224]{1,0:T(8,128)(2,1)S(1)}, s16[16,4224]{1,0:T(8,128)(2,1)S(1)}, u32[]{:S(2)}, u32[]{:S(2)}) collective-permute-start(s16[16,4224]{1,0:T(8,128)(2,1)S(1)} %get-tuple-element.94), channel_id=1, source_target_pairs={{0,4},{1,5},{2,6},{3,7},{4,0},{5,1},{6,2},{7,3},{8,12},{9,13},{10,... | collective-permute-start | bytes 405512 | tf_op jit(solution)/shard_map/ppermute | solution.py:421
  43.2 9.0 %collective-permute-start.14 = (bf16[64,384]{1,0:T(8,128)(2,1)S(1)}, bf16[64,384]{1,0:T(8,128)(2,1)S(1)}, u32[]{:S(2)}, u32[]{:S(2)}) collective-permute-start(bf16[64,384]{1,0:T(8,128)(2,1)S(1)} %pad_maximum_fusion.1.near_ref), channel_id=1, source_target_pairs={{0,2},{1,3},{2,0},{3,1},{4,6},{5,7},{6,4},{7,5},{8,10},{9,11},{10,... | collective-permute-start | bytes 147464 | tf_op jit(solution)/shard_map/ppermute | solution.py:421
  45.9 9.8 %collective-permute-start.12 = (s16[16,2176]{1,0:T(8,128)(2,1)S(1)}, s16[16,2176]{1,0:T(8,128)(2,1)S(1)}, u32[]{:S(2)}, u32[]{:S(2)}) collective-permute-start(s16[16,2176]{1,0:T(8,128)(2,1)S(1)} %get-tuple-element.107), channel_id=1, source_target_pairs={{0,8},{1,9},{2,10},{3,11},{4,12},{5,13},{6,14},{7,15},{8,0},{9,1},... | collective-permute-start | bytes 208904 | tf_op jit(solution)/shard_map/ppermute | solution.py:421
  48.7 8.2 %collective-permute-start.13 = (s16[16,2304]{1,0:T(8,128)(2,1)S(1)}, s16[16,2304]{1,0:T(8,128)(2,1)S(1)}, u32[]{:S(2)}, u32[]{:S(2)}) collective-permute-start(s16[16,2304]{1,0:T(8,128)(2,1)S(1)} %get-tuple-element.109), channel_id=1, source_target_pairs={{0,8},{1,9},{2,10},{3,11},{4,12},{5,13},{6,14},{7,15},{8,0},{9,1},... | collective-permute-start | bytes 221192 | tf_op jit(solution)/shard_map/ppermute | solution.py:421
  49.8 10.5 %collective-permute-start.11 = (s16[16,2176]{1,0:T(8,128)(2,1)S(1)}, s16[16,2176]{1,0:T(8,128)(2,1)S(1)}, u32[]{:S(2)}, u32[]{:S(2)}) collective-permute-start(s16[16,2176]{1,0:T(8,128)(2,1)S(1)} %get-tuple-element.104), channel_id=1, source_target_pairs={{0,8},{1,9},{2,10},{3,11},{4,12},{5,13},{6,14},{7,15},{8,0},{9,1},... | collective-permute-start | bytes 208904 | tf_op jit(solution)/shard_map/ppermute | solution.py:421
  62.1 10.5 %all-to-all-start = ((bf16[16,16,128]{2,1,0:T(8,128)(2,1)}), bf16[16,16,128]{2,1,0:T(8,128)(2,1)S(1)}, u32[]{:S(2)}, u32[]{:S(2)}) async-start(bf16[16,16,128]{2,1,0:T(8,128)(2,1)} %values_part.1), calls=%async_computation | async-start | bytes 131072 | tf_op jit(solution)/shard_map/all_to_all | solution.py:512

commit v3 on v2

--- a/solution.py
+++ b/solution.py
@@ -19,7 +19,6 @@
 HEADS_WIDTH = H * DK
 LEVELS = 32767.0
 STATE_COPIES = 4
-WEIGHT_COPIES = 2
 TAP_WIDTH = 384
 TAP_BLOCKS = 3 * HEADS_WIDTH // TAP_WIDTH
 
@@ -127,8 +126,7 @@
 
 def keys_kernel(
     twist_ref, query_ref, query_got_ref, key_ref, key_got_ref, history_ref, near_ref, far_ref,
-    state_hbm, beta_ref, key_seen_ref, query_seen_ref, pulls_ref, weights_ref, taps_ref,
-    state_ref, sems,
+    state_hbm, key_seen_ref, query_seen_ref, pulls_ref, weights_ref, taps_ref, state_ref, sems,
 ):
     per_copy = H // STATE_COPIES
     copies = []
@@ -148,7 +146,6 @@
     row = lax.broadcasted_iota(jnp.int32, (ROWS, DK), 0)
     row_step = row % STEPS
     query_steps, key_steps = steps_of(query_got_ref), steps_of(key_got_ref)
-    gates = received(key_ref, key_got_ref, key_steps, H)
     for head in range(H):
         key = unit_length(
             activate(
@@ -161,14 +158,6 @@
                 row_step,
             )
         )
-        beta_logit = jnp.broadcast_to(gates[:, head : head + 1], (ROWS, DK))
-        decay_logit = jnp.broadcast_to(gates[:, H + head : H + head + 1], (ROWS, DK))
-        beta = 1.0 / (1.0 + jnp.exp(-beta_logit))
-        decay = 1.0 / (1.0 + jnp.exp(decay_logit))
-        fades = [jnp.ones_like(decay), decay]
-        for lag in range(2, STEPS + 1):
-            earlier = pltpu.roll(decay, lag - 1, 0)
-            fades.append(jnp.where(row_step >= lag - 1, fades[-1] * earlier, fades[-1]))
         both = jnp.concatenate([key, query], axis=0)
         if head % per_copy == 0:
             copies[head // per_copy].wait()
@@ -183,23 +172,18 @@
             main = jnp.dot(stacked, high, preferred_element_type=jnp.float32)
             rest = jnp.dot(both_high, low, preferred_element_type=jnp.float32)
             seen.append(main[: 2 * ROWS] + main[2 * ROWS :] + rest)
-        beta_ref[head] = beta
-        key_seen_ref[head] = beta * fades[STEPS] * jnp.where(
-            row < STEPS, seen[0][:ROWS], seen[1][:ROWS]
-        )
-        query_seen_ref[head] = fades[STEPS] * jnp.where(
-            row < STEPS, seen[0][ROWS:], seen[1][ROWS:]
-        )
+        key_seen_ref[head] = jnp.where(row < STEPS, seen[0][:ROWS], seen[1][:ROWS])
+        query_seen_ref[head] = jnp.where(row < STEPS, seen[0][ROWS:], seen[1][ROWS:])
         for lag in range(STEPS):
             moved_key = shift_rows(key, lag, row_step)
             if lag:
-                pulls_ref[lag - 1, head] = beta * fades[lag] * lane_sum(key * moved_key)
-            weights_ref[lag, head] = fades[lag] * lane_sum(query * moved_key)
+                pulls_ref[lag - 1, head] = jnp.broadcast_to(lane_sum(key * moved_key), (ROWS, DK))
+            weights_ref[lag, head] = jnp.broadcast_to(lane_sum(query * moved_key), (ROWS, DK))
 
 
 def values_kernel(
     slots_ref, halves_ref, lengths_ref, twist_ref, value_ref, value_got_ref, history_ref,
-    beta_ref, key_seen_ref, query_seen_ref, pulls_ref, weights_ref, taps_ref, out_ref, heads_ref,
+    key_seen_ref, query_seen_ref, pulls_ref, weights_ref, taps_ref, out_ref, heads_ref,
 ):
     twist = twist_ref[0]
     row = lax.broadcasted_iota(jnp.int32, (ROWS, DK), 0)
@@ -208,22 +192,33 @@
     row_length = jnp.where(row < STEPS, lengths_ref[0], lengths_ref[1])
     live = row_step < row_length
     value_steps = steps_of(value_got_ref)
+    gates = received(value_ref, value_got_ref, value_steps, H)
     for head in range(H):
         value = activate(
             value_ref, value_got_ref, value_steps, 2, head, history_ref, taps_ref, twist, row_step
         )
-        base = beta_ref[head] * value - key_seen_ref[head]
+        beta_logit = jnp.broadcast_to(gates[:, head : head + 1], (ROWS, DK))
+        decay_logit = jnp.broadcast_to(gates[:, H + head : H + head + 1], (ROWS, DK))
+        beta = 1.0 / (1.0 + jnp.exp(-beta_logit))
+        decay = 1.0 / (1.0 + jnp.exp(decay_logit))
+        fades = [jnp.ones_like(decay), decay]
+        for lag in range(2, STEPS + 1):
+            earlier = pltpu.roll(decay, lag - 1, 0)
+            fades.append(jnp.where(row_step >= lag - 1, fades[-1] * earlier, fades[-1]))
+        base = beta * (value - fades[STEPS] * key_seen_ref[head])
+        pulls = [
+            beta * fades[lag] * pulls_ref[lag - 1, head] if lag else None for lag in range(STEPS)
+        ]
         solved = base
         for _ in range(STEPS - 1):
             following = base
             for lag in range(1, STEPS):
-                following = following - pulls_ref[lag - 1, head] * shift_rows(
-                    solved, lag, row_step
-                )
+                following = following - pulls[lag] * shift_rows(solved, lag, row_step)
             solved = following
-        out = query_seen_ref[head]
+        out = fades[STEPS] * query_seen_ref[head]
         for lag in range(STEPS):
-            out = out + weights_ref[lag, head] * shift_rows(solved, lag, row_step)
+            weight = fades[lag] * weights_ref[lag, head]
+            out = out + weight * shift_rows(solved, lag, row_step)
         heads_ref[head] = jnp.where(live, out, 0.0)
     for quad in range(UNITS // 4):
         joined = []
@@ -247,9 +242,9 @@
     tap_blocks = jax.ShapeDtypeStruct((TAP_BLOCKS, TAPS, TAP_WIDTH), jnp.float32)
     prepared = pl.pallas_call(
         keys_kernel,
-        out_shape=[per_head] * 3 + lags + [tap_blocks],
+        out_shape=[per_head] * 2 + lags + [tap_blocks],
         in_specs=[smem] + [vmem] * 7 + [pl.BlockSpec(memory_space=pl.ANY)],
-        out_specs=[vmem] * 6,
+        out_specs=[vmem] * 5,
         scratch_shapes=[
             pltpu.VMEM(state.shape, jnp.float32),
             pltpu.SemaphoreType.DMA((STATE_COPIES,)),
@@ -261,7 +256,7 @@
     return pl.pallas_call(
         values_kernel,
         out_shape=jax.ShapeDtypeStruct((UNITS // 4, 2 * ROWS, DK), jnp.bfloat16),
-        in_specs=[smem] * 4 + [vmem] * 9,
+        in_specs=[smem] * 4 + [vmem] * 8,
         out_specs=vmem,
         scratch_shapes=[pltpu.VMEM((H, ROWS, DK), jnp.float32)],
         compiler_params=params,
@@ -271,7 +266,8 @@
 
 
 def rows_kernel(
-    depth, me_ref, slot_of_ref, tokens_hbm, mine_ref, theirs_ref, window_ref, sem
+    depth, me_ref, slot_of_ref, tokens_hbm, weight_hbm, mine_ref, theirs_ref, weight_ref,
+    window_ref, sem, weight_sem,
 ):
     me = me_ref[0]
     width = window_ref.shape[2]
@@ -280,6 +276,8 @@
     columns = pl.ds(pl.multiple_of(start, DK), width)
     copy = pltpu.make_async_copy(tokens_hbm.at[:, :, columns], window_ref, sem)
     copy.start()
+    weight_copy = pltpu.make_async_copy(weight_hbm, weight_ref, weight_sem)
+    weight_copy.start()
     shape = (mine_ref.shape[0], slot_of_ref.shape[1])
     row = lax.broadcasted_iota(jnp.int32, shape, 0)
     place = row // ROWS
@@ -301,44 +299,37 @@
     first_core = me % 2 == 0
     mine_ref[...] = jnp.where(first_core, low, high).astype(jnp.bfloat16)
     theirs_ref[...] = jnp.where(first_core, high, low).astype(jnp.bfloat16)
-
-
-def run_rows(me, slot_of, tokens, depth, chips):
+    weight_copy.wait()
+
+
+def run_rows(me, slot_of, tokens, weight, chips):
+    depth = weight.shape[0]
     width = -(-(2 * depth + DK - 1) // DK) * DK
     out = jax.ShapeDtypeStruct((chips * ROWS, depth), jnp.bfloat16)
     vmem = pl.BlockSpec(memory_space=pltpu.VMEM)
     return pl.pallas_call(
         functools.partial(rows_kernel, depth),
-        out_shape=[out, out],
+        out_shape=[out, out, jax.ShapeDtypeStruct(weight.shape, weight.dtype)],
         in_specs=[
-            pl.BlockSpec(memory_space=pltpu.SMEM), vmem, pl.BlockSpec(memory_space=pltpu.HBM)
+            pl.BlockSpec(memory_space=pltpu.SMEM), vmem, pl.BlockSpec(memory_space=pl.ANY),
+            pl.BlockSpec(memory_space=pl.ANY),
         ],
-        out_specs=[vmem, vmem],
+        out_specs=[vmem] * 3,
         scratch_shapes=[
             pltpu.VMEM((tokens.shape[0], STEPS, width), jnp.bfloat16),
+            pltpu.SemaphoreType.DMA,
             pltpu.SemaphoreType.DMA,
         ],
         compiler_params=pltpu.CompilerParams(vmem_limit_bytes=32 * 1024 * 1024),
         cost_estimate=pl.CostEstimate(flops=0, bytes_accessed=0, transcendentals=0),
         name="token_rows",
-    )(me.reshape(1), slot_of.reshape(1, -1), tokens)
-
-
-def product_kernel(first, count, mine_ref, theirs_ref, own_hbm, other_hbm, *refs):
-    scratch, refs = refs[-3:], refs[:-3]
-    (own_ref, other_ref, sems), gate_refs, out_refs = scratch, refs[: -2 * count], refs[-2 * count :]
+    )(me.reshape(1), slot_of.reshape(1, -1), tokens, weight)
+
+
+def product_kernel(skipped, *refs):
+    mine_ref, theirs_ref, block_ref, other_ref, *refs = refs[skipped:]
+    gate_refs, (kept_ref, packed_ref) = refs[:-2], refs[-2:]
     half = mine_ref.shape[0] // 2
-    step = HEADS_WIDTH // WEIGHT_COPIES
-    copies = []
-    for at in range(count * WEIGHT_COPIES):
-        source, target = pl.ds(first * HEADS_WIDTH + at * step, step), pl.ds(at * step, step)
-        pair = [
-            pltpu.make_async_copy(hbm.at[:, source], ref.at[:, target], sems.at[side, at])
-            for side, (hbm, ref) in enumerate(((own_hbm, own_ref), (other_hbm, other_ref)))
-        ]
-        for copy in pair:
-            copy.start()
-        copies.append(pair)
 
     def product(own, other, dims):
         total = lax.dot_general(mine_ref[...], own, dims, preferred_element_type=jnp.float32)
@@ -346,43 +337,35 @@
             theirs_ref[...], other, dims, preferred_element_type=jnp.float32
         )
 
-    for part in range(count):
-        totals = []
-        for at in range(part * WEIGHT_COPIES, (part + 1) * WEIGHT_COPIES):
-            for copy in copies[at]:
-                copy.wait()
-            columns = pl.ds(at * step, step)
-            totals.append(
-                product(own_ref[:, columns], other_ref[:, columns], (((1,), (0,)), ((), ())))
-            )
-        if gate_refs and part == 0:
-            gates = product(gate_refs[0][...], gate_refs[1][...], (((1,), (1,)), ((), ())))
-            totals += [gates, jnp.zeros((gates.shape[0], 2 * DK - gates.shape[1]), jnp.float32)]
-        total = jnp.concatenate(totals, axis=1)
-        out_refs[2 * part][...] = total[:half]
-        pack_rows(total[half:], out_refs[2 * part + 1])
-
-
-def run_product(mine, theirs, weights, first, count, gates=()):
-    vmem, hbm = pl.BlockSpec(memory_space=pltpu.VMEM), pl.BlockSpec(memory_space=pl.ANY)
+    total = product(block_ref[...], other_ref[...], (((1,), (0,)), ((), ())))
+    if gate_refs:
+        gates = product(gate_refs[0][...], gate_refs[1][...], (((1,), (1,)), ((), ())))
+        zeros = jnp.zeros((gates.shape[0], 2 * DK - gates.shape[1]), jnp.float32)
+        total = jnp.concatenate([total, gates, zeros], axis=1)
+    kept_ref[...] = total[:half]
+    pack_rows(total[half:], packed_ref)
+
+
+def run_product(mine, theirs, weights, part, gates=(), earlier=()):
+    vmem = pl.BlockSpec(memory_space=pltpu.VMEM)
+    block = pl.BlockSpec((mine.shape[1], HEADS_WIDTH), lambda i: (0, part))
     half = mine.shape[0] // 2
-    outs = []
-    for part in range(count):
-        width = HEADS_WIDTH + (len(gates) * DK if part == 0 else 0)
-        outs.append(jax.ShapeDtypeStruct((half, width), jnp.float32))
-        outs.append(jax.ShapeDtypeStruct((half, width + scale_lanes(width // DK)), jnp.int16))
-    outs = pl.pallas_call(
-        functools.partial(product_kernel, first, count),
-        out_shape=outs,
-        in_specs=[vmem, vmem, hbm, hbm] + [vmem] * len(gates),
-        out_specs=[vmem] * len(outs),
-        scratch_shapes=[pltpu.VMEM((mine.shape[1], count * HEADS_WIDTH), jnp.bfloat16)] * 2
-        + [pltpu.SemaphoreType.DMA((2, count * WEIGHT_COPIES))],
-        compiler_params=pltpu.CompilerParams(vmem_limit_bytes=56 * 1024 * 1024),
+    width = HEADS_WIDTH + len(gates) * DK
+    return pl.pallas_call(
+        functools.partial(product_kernel, len(earlier)),
+        grid=(1,),
+        out_shape=[
+            jax.ShapeDtypeStruct((half, width), jnp.float32),
+            jax.ShapeDtypeStruct((half, width + scale_lanes(width // DK)), jnp.int16),
+        ],
+        in_specs=[pl.BlockSpec(memory_space=pl.ANY)] * len(earlier)
+        + [vmem, vmem, block, block]
+        + [vmem] * len(gates),
+        out_specs=[vmem] * 2,
+        compiler_params=pltpu.CompilerParams(vmem_limit_bytes=32 * 1024 * 1024),
         cost_estimate=pl.CostEstimate(flops=0, bytes_accessed=0, transcendentals=0),
         name="partial_product",
-    )(mine, theirs, *weights, *gates)
-    return [outs[2 * part : 2 * part + 2] for part in range(count)]
+    )(*earlier, mine, theirs, *weights, *gates)
 
 
 def combine_kernel(kept_ref, got_ref, still_ref, packed_ref):
@@ -436,7 +419,6 @@
     devices = lax.axis_size("heads")
     me = lax.axis_index("heads")
     per_device = UNITS // devices
-    depth = qkv_weight.shape[0]
     row_count = tokens.shape[0]
     chips = devices // 2
 
@@ -444,9 +426,9 @@
     steps = jnp.arange(STEPS, dtype=jnp.int32)
     offered = (slot_of[:, None] * STEPS + steps[None, :]).reshape(-1)
 
-    mine, theirs = run_rows(me, slot_of, tokens, depth, chips)
-
-    weights = (qkv_weight, swap(qkv_weight, 1, devices))
+    mine, theirs, near_weight = run_rows(me, slot_of, tokens, qkv_weight, chips)
+
+    weights = (near_weight, swap(qkv_weight, 1, devices))
     gate_columns = gate_weight.T
     gates = (gate_columns, swap(gate_columns, 1, devices))
 
@@ -455,15 +437,15 @@
     ride = conv_weight.shape[1] == 2 * TAP_WIDTH and len(bits) == 3
     if ride:
         taps = jnp.concatenate([conv_weight[:, :TAP_WIDTH], conv_weight[:, TAP_WIDTH:]], axis=0)
-        taps = jnp.concatenate([taps, swap(taps, 1, devices)], axis=0)
+        far = swap(taps, 1, devices)
     else:
         taps = lax.all_gather(conv_weight, "heads", axis=1, tiled=True)
         blocks = [block for bit in (0, 4) for block in range(TAP_BLOCKS) if block & 4 == bit]
         taps = [taps[:, block * TAP_WIDTH : (block + 1) * TAP_WIDTH] for block in blocks]
         taps = jnp.concatenate(taps, axis=0)
-    (queries,) = run_product(mine, theirs, weights, 0, 1)
-    mine, *queries = tie(mine, *queries)
-    keys, values = run_product(mine, theirs, weights, 1, 2, gates)
+    queries = run_product(mine, theirs, weights, 0)
+    keys = run_product(mine, theirs, weights, 1, earlier=queries[:1])
+    values = run_product(mine, theirs, weights, 2, gates, earlier=keys[:1])
 
     lengths, old_heads, new_units, carried, *values = tie(
         lengths, old_heads, new_units, conv_state, *values
@@ -475,28 +457,22 @@
     )
     blank = jnp.zeros((1, carried.shape[2]), jnp.float32)
     history = jnp.concatenate([blank, carried[1], blank, carried[0]], axis=0)
-    got = [swap(queries[1], bits[0], devices), swap(keys[1], bits[0], devices)]
-    got[0], history, my_lengths, old_slots, halves = tie(
-        got[0], history, my_lengths, old_slots, halves
-    )
+    kept = [chunk[0] for chunk in (queries, keys, values)]
+    got = [swap(chunk[1], bits[0], devices) for chunk in (queries, keys, values)]
+    for level, bit in enumerate(bits[1:]):
+        for at in range(3):
+            kept[at], packed = run_combine(kept[at], got[at])
+            got[at] = swap(packed, bit, devices)
+            if ride and level == 0 and at == 0:
+                kept[0], taps, far = tie(kept[0], taps, far)
+                taps = jnp.concatenate([taps, far], axis=0)
+                taps = jnp.concatenate([taps, swap(taps, 4, devices)], axis=0)
     if ride:
-        taps, *values = tie(taps, *values)
-        taps = jnp.concatenate([taps, swap(taps, 4, devices)], axis=0)
-        got[0], values[1], taps = tie(got[0], values[1], taps)
         taps = jnp.concatenate([taps, swap(taps, 8, devices)], axis=0)
-        got[1], taps = tie(got[1], taps)
         twist, taps = me.reshape(1), (taps, swap(taps, 2, devices))
     else:
         half = TAP_BLOCKS // 2 * TAPS
         twist, taps = jnp.zeros(1, jnp.int32), (taps[:half], taps[half:])
-    got.append(swap(values[1], bits[0], devices))
-    kept = [queries[0], keys[0], values[0]]
-    for bit in bits[1:]:
-        for at in range(3):
-            if at:
-                got[at], kept[at - 1] = tie(got[at], kept[at - 1])
-            kept[at], packed = run_combine(kept[at], got[at])
-            got[at] = swap(packed, bit, devices)
     queries, keys, values = zip(kept, got)
 
     local_out = run_delta(

time: 74 us -> 62.6 us (0.85)
  waiting for transfers between devices: 22.3 us -> 16.8 us
  Pallas kernels: 17.3 us -> 12.2 us
  local copies, waits for them, and re-layouts: 8.57 us -> 5.57 us
  starting transfers between devices: 23.4 us -> 25.4 us
    pallas_call x3 -> x4, Pallas kernels: 11.9 us -> 6.2 us  [the longest x3 3.39 us: run_product(): pl.pallas_call(functools.partial(product_kernel, len(earlier)), grid=(1,)...]
    ppermute x15, waiting for transfers between devices: 15.6 us -> 10.1 us  [swap(): return lax.ppermute(value, 'heads', [(i, i ^ bit) for i in range(devices)])]
    unnamed x30 -> x25, local copies, waits for them, and re-layouts: 6.8 us -> 3.78 us
    ppermute x15, starting transfers between devices: 19.8 us -> 21.8 us  [swap(): return lax.ppermute(value, 'heads', [(i, i ^ bit) for i in range(devices)])]
    mul x1, other arithmetic: 0.01 us -> 1.23 us  [on_device(): offered = (slot_of[:, None] * STEPS + steps[None, :]).reshape(-1)]
  transfers between devices with their start and end apart: 16 -> 16, of which waited for: 8 -> 6; matrix products, arithmetic and copies ran while one was open for 3% -> 5% of each run, Pallas kernels for 15% -> 16%
where the time goes in v3:
time: 62.6 us; the launch traced here: 62.3 us
  starting transfers between devices  25.4 us (41%)
  waiting for transfers between devices  16.8 us (27%)
  Pallas kernels  12.2 us (19%)
  local copies, waits for them, and re-layouts  5.57 us (9%)
  other arithmetic  1.89 us (3%)
    ppermute x15, starting transfers between devices, swap(): return lax.ppermute(value, 'heads', [(i, i ^ bit) for i in range(devices)])  21.8 us
    ppermute x15, waiting for transfers between devices, swap(): return lax.ppermute(value, 'heads', [(i, i ^ bit) for i in range(devices)])  10.1 us
    all_to_all x1, waiting for transfers between devices, on_device(): lax.all_to_all(sending, 'heads', split_axis=0, concat_axis=0, tiled=True)  6.71 us
    unnamed x25, local copies, waits for them, and re-layouts  3.78 us
    all_to_all x1, starting transfers between devices, on_device(): lax.all_to_all(sending, 'heads', split_axis=0, concat_axis=0, tiled=True)  3.65 us
    pallas_call x3, Pallas kernels, run_product(): pl.pallas_call(functools.partial(product_kernel, len(earlier)), grid=(1,)...  3.39 us
    pallas_call x1, Pallas kernels, run_delta(): pl.pallas_call(keys_kernel, out_shape=[per_head] * 2 + lags + [tap_blocks...  2.81 us
    pallas_call x6, Pallas kernels, run_combine(): pl.pallas_call(combine_kernel, out_shape=[jax.ShapeDtypeStruct((half, wid...  2.8 us
  transfers between devices with their start and end apart: 16, of which 6 were waited for; matrix products, arithmetic and copies ran while one was open for 5% of the time, Pallas kernels for 16%

profile of v3, /device:TPU:0, one launch (start us, length us, event | category | flops | bytes accessed | tf_op | source)
XLA Modules:
  0.0 62.3 jit_solution(2370110725205857430)
XLA Ops:
  0.0 0.5 collective-permute-start
  0.5 0.7 %fusion.6 = (bf16[4,384]{1,0:T(4,128)(2,1)S(1)}, bf16[4,384]{1,0:T(4,128)(2,1)S(1)}) fusion(bf16[4,768]{1,0:T(4,128)(2,1)} %param.13), kind=kLoop, calls=%fused_computation.33 | loop fusion | bytes 12288 | tf_op jit(solution)/shard_map/slice | solution.py:439
  1.7 1.2 %broadcast_multiply_fusion = s32[32]{0:T(128)} fusion(s32[32]{0:T(128)} %param.18), kind=kLoop, calls=%fused_computation.31 | loop fusion | flops 32 | bytes 256 | tf_op jit(solution)/shard_map/mul | solution.py:427
  3.0 2.0 %copy-done.1 = bf16[144,12288]{1,0:T(8,128)(2,1)S(1)} copy-done((bf16[144,12288]{1,0:T(8,128)(2,1)S(1)}, bf16[144,12288]{1,0:T(8,128)(2,1)}, u32[]{:S(2)}) %copy-start.1) | copy-done | bytes 3538968
  5.0 1.1 %copy-done.2 = bf16[32,4,2304]{2,1,0:T(4,128)(2,1)S(1)} copy-done((bf16[32,4,2304]{2,1,0:T(4,128)(2,1)S(1)}, bf16[32,4,2304]{2,1,0:T(4,128)(2,1)}, u32[]{:S(2)}) %copy-start.2) | copy-done | bytes 589848
  6.1 0.7 %copy-done.4 = s32[32]{0:T(128)S(1)} copy-done((s32[32]{0:T(128)S(1)}, s32[32]{0:T(128)}, u32[]{:S(2)}) %copy-start.4) | copy-done | bytes 152
  6.7 1.2 %token_rows.1 = (bf16[64,144]{1,0:T(8,128)(2,1)S(1)}, bf16[64,144]{1,0:T(8,128)(2,1)S(1)}, bf16[144,12288]{1,0:T(8,128)(2,1)S(1)}) custom-call(s32[1]{0:T(128)} %bitcast.me_ref.twist_ref, s32[1,32]{1,0:T(1,128)S(1)} %bitcast.14, bf16[32,4,2304]{2,1,0:T(4,128)(2,1)S(1)} %copy-done.2, bf16[144,12288]{1,0:T(8,128)(2,1)S(1)} %copy-done.1), custom_call_target="tpu_custom_call" | custom-call | tf_op jit(solution)/shard_map/token_rows/pallas_call | solution.py:310
  7.9 0.8 %partial_product.3 = (f32[32,4096]{1,0:T(8,128)S(1)}, s16[32,4224]{1,0:T(8,128)(2,1)S(1)}) custom-call(bf16[64,144]{1,0:T(8,128)(2,1)S(1)} %get-tuple-element.40.refs_0_.refs_1_, bf16[64,144]{1,0:T(8,128)(2,1)S(1)} %get-tuple-element.41.refs_1_.refs_2_, bf16[144,12288]{1,0:T(8,128)(2,1)S(1)} %get-tuple-element.42.refs_2_.refs_3_, ...), custom_call_target="tpu_custom_call" | custom-call | tf_op jit(solution)/shard_map/partial_product/pallas_call | solution.py:354
  8.8 2.7 %collective-permute-start.5 = (s16[32,4224]{1,0:T(8,128)(2,1)S(1)}, s16[32,4224]{1,0:T(8,128)(2,1)S(1)}, u32[]{:S(2)}, u32[]{:S(2)}) collective-permute-start(s16[32,4224]{1,0:T(8,128)(2,1)S(1)} %get-tuple-element.57), channel_id=1, source_target_pairs={{0,2},{1,3},{2,0},{3,1},{4,6},{5,7},{6,4},{7,5},{8,10},{9,11},{10,... | collective-permute-start | bytes 811016 | tf_op jit(solution)/shard_map/ppermute | solution.py:404
  11.4 0.8 %partial_product.4 = (f32[32,4096]{1,0:T(8,128)S(1)}, s16[32,4224]{1,0:T(8,128)(2,1)S(1)}) custom-call(f32[32,4096]{1,0:T(8,128)S(1)} %get-tuple-element.43.refs_0_.kept_ref, bf16[64,144]{1,0:T(8,128)(2,1)S(1)} %get-tuple-element.40.refs_0_.refs_1_, bf16[64,144]{1,0:T(8,128)(2,1)S(1)} %get-tuple-element.41.refs_1_.refs_2_, ...), custom_call_target="tpu_custom_call" | custom-call | tf_op jit(solution)/shard_map/partial_product/pallas_call | solution.py:354
  12.3 1.8 %partial_product.5 = (f32[32,4352]{1,0:T(8,128)S(1)}, s16[32,4480]{1,0:T(8,128)(2,1)S(1)}) custom-call(f32[32,4096]{1,0:T(8,128)S(1)} %get-tuple-element.44.refs_0_.kept_ref, bf16[64,144]{1,0:T(8,128)(2,1)S(1)} %get-tuple-element.40.refs_0_.refs_1_, bf16[64,144]{1,0:T(8,128)(2,1)S(1)} %get-tuple-element.41.refs_1_.refs_2_, ...), custom_call_target="tpu_custom_call" | custom-call | tf_op jit(solution)/shard_map/partial_product/pallas_call | solution.py:354
  14.4 2.0 %collective-permute-start.2 = (s16[32,4480]{1,0:T(8,128)(2,1)S(1)}, s16[32,4480]{1,0:T(8,128)(2,1)S(1)}, u32[]{:S(2)}, u32[]{:S(2)}) collective-permute-start(s16[32,4480]{1,0:T(8,128)(2,1)S(1)} %get-tuple-element.51), channel_id=1, source_target_pairs={{0,2},{1,3},{2,0},{3,1},{4,6},{5,7},{6,4},{7,5},{8,10},{9,11},{10,... | collective-permute-start | bytes 860168 | tf_op jit(solution)/shard_map/ppermute | solution.py:404
  17.1 1.7 %collective-permute-done.5.got_ref = s16[32,4224]{1,0:T(8,128)(2,1)S(1)} collective-permute-done((s16[32,4224]{1,0:T(8,128)(2,1)S(1)}, s16[32,4224]{1,0:T(8,128)(2,1)S(1)}, u32[]{:S(2)}, u32[]{:S(2)}) %collective-permute-start.5) | collective-permute-done | bytes 270368 | tf_op jit(solution)/shard_map/ppermute | solution.py:404
  18.8 0.5 combine.8
  19.3 2.1 %collective-permute-start.12 = (bf16[16,384]{1,0:T(8,128)(2,1)S(1)}, bf16[16,384]{1,0:T(8,128)(2,1)S(1)}, u32[]{:S(2)}, u32[]{:S(2)}) collective-permute-start(bf16[16,384]{1,0:T(8,128)(2,1)S(1)} %pad_maximum_fusion.2), channel_id=1, source_target_pairs={{0,4},{1,5},{2,6},{3,7},{4,0},{5,1},{6,2},{7,3},{8,12},{9,13},{10,... | collective-permute-start | bytes 36872 | tf_op jit(solution)/shard_map/ppermute | solution.py:404
  21.5 3.1 %collective-permute-done.9.got_ref = s16[32,4224]{1,0:T(8,128)(2,1)S(1)} collective-permute-done((s16[32,4224]{1,0:T(8,128)(2,1)S(1)}, s16[32,4224]{1,0:T(8,128)(2,1)S(1)}, u32[]{:S(2)}, u32[]{:S(2)}) %collective-permute-start.9) | collective-permute-done | bytes 270368 | tf_op jit(solution)/shard_map/ppermute | solution.py:404
  24.6 0.5 combine.10
  25.1 2.1 %collective-permute-start.10 = (s16[16,4224]{1,0:T(8,128)(2,1)S(1)}, s16[16,4224]{1,0:T(8,128)(2,1)S(1)}, u32[]{:S(2)}, u32[]{:S(2)}) collective-permute-start(s16[16,4224]{1,0:T(8,128)(2,1)S(1)} %get-tuple-element.65), channel_id=1, source_target_pairs={{0,4},{1,5},{2,6},{3,7},{4,0},{5,1},{6,2},{7,3},{8,12},{9,13},{10,... | collective-permute-start | bytes 405512 | tf_op jit(solution)/shard_map/ppermute | solution.py:404
  27.2 2.6 %collective-permute-start.13 = (bf16[32,384]{1,0:T(8,128)(2,1)S(1)}, bf16[32,384]{1,0:T(8,128)(2,1)S(1)}, u32[]{:S(2)}, u32[]{:S(2)}) collective-permute-start(bf16[32,384]{1,0:T(8,128)(2,1)S(1)} %pad_maximum_fusion.1), channel_id=1, source_target_pairs={{0,8},{1,9},{2,10},{3,11},{4,12},{5,13},{6,14},{7,15},{8,0},{9,1},... | collective-permute-start | bytes 73736 | tf_op jit(solution)/shard_map/ppermute | solution.py:404
  29.8 0.7 %collective-permute-done.2.got_ref = s16[32,4480]{1,0:T(8,128)(2,1)S(1)} collective-permute-done((s16[32,4480]{1,0:T(8,128)(2,1)S(1)}, s16[32,4480]{1,0:T(8,128)(2,1)S(1)}, u32[]{:S(2)}, u32[]{:S(2)}) %collective-permute-start.2) | collective-permute-done | bytes 286752 | tf_op jit(solution)/shard_map/ppermute | solution.py:404
  30.5 0.5 combine.6
  31.0 1.9 %collective-permute-start.3 = (s16[16,4480]{1,0:T(8,128)(2,1)S(1)}, s16[16,4480]{1,0:T(8,128)(2,1)S(1)}, u32[]{:S(2)}, u32[]{:S(2)}) collective-permute-start(s16[16,4480]{1,0:T(8,128)(2,1)S(1)} %get-tuple-element.53), channel_id=1, source_target_pairs={{0,4},{1,5},{2,6},{3,7},{4,0},{5,1},{6,2},{7,3},{8,12},{9,13},{10,... | collective-permute-start | bytes 430088 | tf_op jit(solution)/shard_map/ppermute | solution.py:404
  32.9 1.6 %collective-permute-start.14 = (bf16[64,384]{1,0:T(8,128)(2,1)S(1)}, bf16[64,384]{1,0:T(8,128)(2,1)S(1)}, u32[]{:S(2)}, u32[]{:S(2)}) collective-permute-start(bf16[64,384]{1,0:T(8,128)(2,1)S(1)} %constant_dynamic-update-slice_fusion.near_ref), channel_id=1, source_target_pairs={{0,2},{1,3},{2,0},{3,1},{4,6},{5,7},{6,4},{7,5},{8,10},{9,11},{10,... | collective-permute-start | bytes 147464 | tf_op jit(solution)/shard_map/ppermute | solution.py:404
  34.9 2.7 %collective-permute-start.8 = (s16[16,2176]{1,0:T(8,128)(2,1)S(1)}, s16[16,2176]{1,0:T(8,128)(2,1)S(1)}, u32[]{:S(2)}, u32[]{:S(2)}) collective-permute-start(s16[16,2176]{1,0:T(8,128)(2,1)S(1)} %get-tuple-element.62), channel_id=1, source_target_pairs={{0,8},{1,9},{2,10},{3,11},{4,12},{5,13},{6,14},{7,15},{8,0},{9,1},... | collective-permute-start | bytes 208904 | tf_op jit(solution)/shard_map/ppermute | solution.py:404
  38.8 2.7 %collective-permute-start.4 = (s16[16,2304]{1,0:T(8,128)(2,1)S(1)}, s16[16,2304]{1,0:T(8,128)(2,1)S(1)}, u32[]{:S(2)}, u32[]{:S(2)}) collective-permute-start(s16[16,2304]{1,0:T(8,128)(2,1)S(1)} %get-tuple-element.55), channel_id=1, source_target_pairs={{0,8},{1,9},{2,10},{3,11},{4,12},{5,13},{6,14},{7,15},{8,0},{9,1},... | collective-permute-start | bytes 221192 | tf_op jit(solution)/shard_map/ppermute | solution.py:404
  41.5 3.1 %collective-permute-done.8.query_got_ref = s16[16,2176]{1,0:T(8,128)(2,1)S(1)} collective-permute-done((s16[16,2176]{1,0:T(8,128)(2,1)S(1)}, s16[16,2176]{1,0:T(8,128)(2,1)S(1)}, u32[]{:S(2)}, u32[]{:S(2)}) %collective-permute-start.8) | collective-permute-done | bytes 69664 | tf_op jit(solution)/shard_map/ppermute | solution.py:404
  44.6 1.5 %collective-permute-done.11.key_got_ref = s16[16,2176]{1,0:T(8,128)(2,1)S(1)} collective-permute-done((s16[16,2176]{1,0:T(8,128)(2,1)S(1)}, s16[16,2176]{1,0:T(8,128)(2,1)S(1)}, u32[]{:S(2)}, u32[]{:S(2)}) %collective-permute-start.11) | collective-permute-done | bytes 69664 | tf_op jit(solution)/shard_map/ppermute | solution.py:404
  46.1 2.8 %keys_part.1 = (f32[32,8,128]{2,1,0:T(8,128)S(1)}, f32[32,8,128]{2,1,0:T(8,128)S(1)}, f32[3,32,8,128]{3,2,1,0:T(8,128)S(1)}, f32[4,32,8,128]{3,2,1,0:T(8,128)S(1)}, f32[32,4,384]{2,1,0:T(4,128)S(1)}) custom-call(s32[1]{0:T(128)} %bitcast.me_ref.twist_ref, f32[8,4096]{1,0:T(8,128)S(1)} %get-tuple-element.61.query_ref, ...), custom_call_target="tpu_custom_call" | custom-call | flops 40000000 | bytes 9000000 | tf_op jit(solution)/shard_map/keys_part/pallas_call | solution.py:243
  48.9 1.9 %values_part.1 = bf16[16,16,128]{2,1,0:T(8,128)(2,1)} custom-call(s32[64]{0:T(128)S(1)} %select_reduce_fusion.slots_ref, s32[64]{0:T(128)S(1)} %get-tuple-element.81.halves_ref, s32[2]{0:T(128)S(1)} %fusion.4.lengths_ref, s32[1]{0:T(128)} %bitcast.me_ref.twist_ref, f32[8,4352]{1,0:T(8,128)S(1)} %get-tuple-element.54.value_ref, ...), custom_call_target="tpu_custom_call" | custom-call | flops 4000000 | bytes 2000000 | tf_op jit(solution)/shard_map/values_part/pallas_call | solution.py:256
  50.9 3.6 %all-to-all-start = ((bf16[16,16,128]{2,1,0:T(8,128)(2,1)}), bf16[16,16,128]{2,1,0:T(8,128)(2,1)S(1)}, u32[]{:S(2)}, u32[]{:S(2)}) async-start(bf16[16,16,128]{2,1,0:T(8,128)(2,1)} %values_part.1), calls=%async_computation | async-start | bytes 131072 | tf_op jit(solution)/shard_map/all_to_all | solution.py:488
  54.7 6.7 %all-to-all-done = bf16[16,16,128]{2,1,0:T(8,128)(2,1)S(1)} async-done(((bf16[16,16,128]{2,1,0:T(8,128)(2,1)}), bf16[16,16,128]{2,1,0:T(8,128)(2,1)S(1)}, u32[]{:S(2)}, u32[]{:S(2)}) %all-to-all-start) | async-done | bytes 65568 | tf_op jit(solution)/shard_map/all_to_all | solution.py:488
  61.6 0.7 %reshape.46 = bf16[32,4,256]{2,1,0:T(4,128)(2,1)} reshape(bf16[128,256]{1,0:T(8,128)(2,1)S(1)} %convolution_convert_fusion) | data formatting | bytes 131072 | tf_op jit(solution)/shard_map/reshape | solution.py:499
  (57 shorter events, 3.7 us)
Async XLA Ops:
  0.0 7.9 %collective-permute-start = (bf16[144,12288]{1,0:T(8,128)(2,1)}, bf16[144,12288]{1,0:T(8,128)(2,1)S(1)}, u32[]{:S(2)}, u32[]{:S(2)}) collective-permute-start(bf16[144,12288]{1,0:T(8,128)(2,1)} %weight_hbm.1), channel_id=1, source_target_pairs={{0,1},{1,0},{2,3},{3,2},{4,5},{5,4},{6,7},{7,6},{8,9},{9,8},{10,11... | collective-permute-start | bytes 10616840 | tf_op jit(solution)/shard_map/ppermute | solution.py:404
  1.2 18.1 %collective-permute-start.6 = (bf16[8,384]{1,0:T(8,128)(2,1)S(1)}, bf16[8,384]{1,0:T(8,128)(2,1)S(1)}, u32[]{:S(2)}, u32[]{:S(2)}) collective-permute-start(bf16[8,384]{1,0:T(8,128)(2,1)S(1)} %pad_maximum_fusion.3), channel_id=1, source_target_pairs={{0,1},{1,0},{2,3},{3,2},{4,5},{5,4},{6,7},{7,6},{8,9},{9,8},{10,11... | collective-permute-start | bytes 18440 | tf_op jit(solution)/shard_map/ppermute | solution.py:404
  1.3 11.0 %collective-permute-start.1 = (bf16[64,144]{1,0:T(8,128)(2,1)}, bf16[64,144]{1,0:T(8,128)(2,1)}, u32[]{:S(2)}, u32[]{:S(2)}) collective-permute-start(bf16[64,144]{1,0:T(8,128)(2,1)} %bitcast.12), channel_id=1, source_target_pairs={{0,1},{1,0},{2,3},{3,2},{4,5},{5,4},{6,7},{7,6},{8,9},{9,8},{10,11... | collective-permute-start | bytes 55304 | tf_op jit(solution)/shard_map/ppermute | solution.py:404
  3.0 2.0 %copy-start.1 = (bf16[144,12288]{1,0:T(8,128)(2,1)S(1)}, bf16[144,12288]{1,0:T(8,128)(2,1)}, u32[]{:S(2)}) copy-start(bf16[144,12288]{1,0:T(8,128)(2,1)} %weight_hbm.1) | copy-start | bytes 10616836
  5.0 1.1 %copy-start.2 = (bf16[32,4,2304]{2,1,0:T(4,128)(2,1)S(1)}, bf16[32,4,2304]{2,1,0:T(4,128)(2,1)}, u32[]{:S(2)}) copy-start(bf16[32,4,2304]{2,1,0:T(4,128)(2,1)} %tokens_hbm.1) | copy-start | bytes 1769476
  6.0 0.7 %copy-start.4 = (s32[32]{0:T(128)S(1)}, s32[32]{0:T(128)}, u32[]{:S(2)}) copy-start(s32[32]{0:T(128)} %param.18) | copy-start | bytes 388
  8.8 10.0 %collective-permute-start.5 = (s16[32,4224]{1,0:T(8,128)(2,1)S(1)}, s16[32,4224]{1,0:T(8,128)(2,1)S(1)}, u32[]{:S(2)}, u32[]{:S(2)}) collective-permute-start(s16[32,4224]{1,0:T(8,128)(2,1)S(1)} %get-tuple-element.57), channel_id=1, source_target_pairs={{0,2},{1,3},{2,0},{3,1},{4,6},{5,7},{6,4},{7,5},{8,10},{9,11},{10,... | collective-permute-start | bytes 811016 | tf_op jit(solution)/shard_map/ppermute | solution.py:404
  11.4 0.8 %copy-start.3 = (bf16[144,64]{0,1:T(8,128)(2,1)S(1)}, bf16[144,64]{0,1:T(8,128)(2,1)}, u32[]{:S(2)}) copy-start(bf16[144,64]{0,1:T(8,128)(2,1)} %param.12) | copy-start | bytes 55300
  12.3 1.8 %copy-start.9 = (s32[32]{0:T(128)S(1)}, s32[32]{0:T(128)}, u32[]{:S(2)}) copy-start(s32[32]{0:T(128)} %param.16) | copy-start | bytes 388
  12.3 1.9 %copy-start.10 = (s32[64]{0:T(128)S(1)}, s32[64]{0:T(128)}, u32[]{:S(2)}) copy-start(s32[64]{0:T(128)} %param.17) | copy-start | bytes 772
  12.3 4.0 %copy-start.6 = (f32[2,3,12288]{2,0,1:T(2,128)S(1)}, f32[2,3,12288]{2,0,1:T(2,128)}, u32[]{:S(2)}) copy-start(f32[2,3,12288]{2,0,1:T(2,128)} %param.15) | copy-start | bytes 884740
  12.3 4.3 %copy-start.5 = (s32[32]{0:T(128)S(1)}, s32[32]{0:T(128)}, u32[]{:S(2)}) copy-start(s32[32]{0:T(128)} %param.18) | copy-start | bytes 388
  12.3 4.3 %copy-start.8 = (s32[32]{0:T(128)S(1)}, s32[32]{0:T(128)}, u32[]{:S(2)}) copy-start(s32[32]{0:T(128)} %param.19) | copy-start | bytes 388
  14.1 32.0 %copy-start = (f32[2,32,128,128]{3,2,1,0:T(8,128)S(1)}, f32[2,32,128,128]{3,2,1,0:T(8,128)}, u32[]{:S(2)}) copy-start(f32[2,32,128,128]{3,2,1,0:T(8,128)} %state_hbm.1) | copy-start | bytes 12582916
  14.3 10.3 %collective-permute-start.9 = (s16[32,4224]{1,0:T(8,128)(2,1)S(1)}, s16[32,4224]{1,0:T(8,128)(2,1)S(1)}, u32[]{:S(2)}, u32[]{:S(2)}) collective-permute-start(s16[32,4224]{1,0:T(8,128)(2,1)S(1)} %get-tuple-element.63), channel_id=1, source_target_pairs={{0,2},{1,3},{2,0},{3,1},{4,6},{5,7},{6,4},{7,5},{8,10},{9,11},{10,... | collective-permute-start | bytes 811016 | tf_op jit(solution)/shard_map/ppermute | solution.py:404
  14.4 16.1 %collective-permute-start.2 = (s16[32,4480]{1,0:T(8,128)(2,1)S(1)}, s16[32,4480]{1,0:T(8,128)(2,1)S(1)}, u32[]{:S(2)}, u32[]{:S(2)}) collective-permute-start(s16[32,4480]{1,0:T(8,128)(2,1)S(1)} %get-tuple-element.51), channel_id=1, source_target_pairs={{0,2},{1,3},{2,0},{3,1},{4,6},{5,7},{6,4},{7,5},{8,10},{9,11},{10,... | collective-permute-start | bytes 860168 | tf_op jit(solution)/shard_map/ppermute | solution.py:404
  19.3 7.9 %collective-permute-start.12 = (bf16[16,384]{1,0:T(8,128)(2,1)S(1)}, bf16[16,384]{1,0:T(8,128)(2,1)S(1)}, u32[]{:S(2)}, u32[]{:S(2)}) collective-permute-start(bf16[16,384]{1,0:T(8,128)(2,1)S(1)} %pad_maximum_fusion.2), channel_id=1, source_target_pairs={{0,4},{1,5},{2,6},{3,7},{4,0},{5,1},{6,2},{7,3},{8,12},{9,13},{10,... | collective-permute-start | bytes 36872 | tf_op jit(solution)/shard_map/ppermute | solution.py:404
  21.4 13.1 %collective-permute-start.7 = (s16[16,4224]{1,0:T(8,128)(2,1)S(1)}, s16[16,4224]{1,0:T(8,128)(2,1)S(1)}, u32[]{:S(2)}, u32[]{:S(2)}) collective-permute-start(s16[16,4224]{1,0:T(8,128)(2,1)S(1)} %get-tuple-element.60), channel_id=1, source_target_pairs={{0,4},{1,5},{2,6},{3,7},{4,0},{5,1},{6,2},{7,3},{8,12},{9,13},{10,... | collective-permute-start | bytes 405512 | tf_op jit(solution)/shard_map/ppermute | solution.py:404
  25.1 12.4 %collective-permute-start.10 = (s16[16,4224]{1,0:T(8,128)(2,1)S(1)}, s16[16,4224]{1,0:T(8,128)(2,1)S(1)}, u32[]{:S(2)}, u32[]{:S(2)}) collective-permute-start(s16[16,4224]{1,0:T(8,128)(2,1)S(1)} %get-tuple-element.65), channel_id=1, source_target_pairs={{0,4},{1,5},{2,6},{3,7},{4,0},{5,1},{6,2},{7,3},{8,12},{9,13},{10,... | collective-permute-start | bytes 405512 | tf_op jit(solution)/shard_map/ppermute | solution.py:404
  27.2 5.7 %collective-permute-start.13 = (bf16[32,384]{1,0:T(8,128)(2,1)S(1)}, bf16[32,384]{1,0:T(8,128)(2,1)S(1)}, u32[]{:S(2)}, u32[]{:S(2)}) collective-permute-start(bf16[32,384]{1,0:T(8,128)(2,1)S(1)} %pad_maximum_fusion.1), channel_id=1, source_target_pairs={{0,8},{1,9},{2,10},{3,11},{4,12},{5,13},{6,14},{7,15},{8,0},{9,1},... | collective-permute-start | bytes 73736 | tf_op jit(solution)/shard_map/ppermute | solution.py:404
  31.0 7.3 %collective-permute-start.3 = (s16[16,4480]{1,0:T(8,128)(2,1)S(1)}, s16[16,4480]{1,0:T(8,128)(2,1)S(1)}, u32[]{:S(2)}, u32[]{:S(2)}) collective-permute-start(s16[16,4480]{1,0:T(8,128)(2,1)S(1)} %get-tuple-element.53), channel_id=1, source_target_pairs={{0,4},{1,5},{2,6},{3,7},{4,0},{5,1},{6,2},{7,3},{8,12},{9,13},{10,... | collective-permute-start | bytes 430088 | tf_op jit(solution)/shard_map/ppermute | solution.py:404
  32.9 8.6 %collective-permute-start.14 = (bf16[64,384]{1,0:T(8,128)(2,1)S(1)}, bf16[64,384]{1,0:T(8,128)(2,1)S(1)}, u32[]{:S(2)}, u32[]{:S(2)}) collective-permute-start(bf16[64,384]{1,0:T(8,128)(2,1)S(1)} %constant_dynamic-update-slice_fusion.near_ref), channel_id=1, source_target_pairs={{0,2},{1,3},{2,0},{3,1},{4,6},{5,7},{6,4},{7,5},{8,10},{9,11},{10,... | collective-permute-start | bytes 147464 | tf_op jit(solution)/shard_map/ppermute | solution.py:404
  34.9 9.7 %collective-permute-start.8 = (s16[16,2176]{1,0:T(8,128)(2,1)S(1)}, s16[16,2176]{1,0:T(8,128)(2,1)S(1)}, u32[]{:S(2)}, u32[]{:S(2)}) collective-permute-start(s16[16,2176]{1,0:T(8,128)(2,1)S(1)} %get-tuple-element.62), channel_id=1, source_target_pairs={{0,8},{1,9},{2,10},{3,11},{4,12},{5,13},{6,14},{7,15},{8,0},{9,1},... | collective-permute-start | bytes 208904 | tf_op jit(solution)/shard_map/ppermute | solution.py:404
  37.9 8.2 %collective-permute-start.11 = (s16[16,2176]{1,0:T(8,128)(2,1)S(1)}, s16[16,2176]{1,0:T(8,128)(2,1)S(1)}, u32[]{:S(2)}, u32[]{:S(2)}) collective-permute-start(s16[16,2176]{1,0:T(8,128)(2,1)S(1)} %get-tuple-element.67), channel_id=1, source_target_pairs={{0,8},{1,9},{2,10},{3,11},{4,12},{5,13},{6,14},{7,15},{8,0},{9,1},... | collective-permute-start | bytes 208904 | tf_op jit(solution)/shard_map/ppermute | solution.py:404
  38.8 10.2 %collective-permute-start.4 = (s16[16,2304]{1,0:T(8,128)(2,1)S(1)}, s16[16,2304]{1,0:T(8,128)(2,1)S(1)}, u32[]{:S(2)}, u32[]{:S(2)}) collective-permute-start(s16[16,2304]{1,0:T(8,128)(2,1)S(1)} %get-tuple-element.55), channel_id=1, source_target_pairs={{0,8},{1,9},{2,10},{3,11},{4,12},{5,13},{6,14},{7,15},{8,0},{9,1},... | collective-permute-start | bytes 221192 | tf_op jit(solution)/shard_map/ppermute | solution.py:404
  46.1 8.4 %copy-start.7 = (s32[32]{0:T(128)S(1)}, s32[32]{0:T(128)}, u32[]{:S(2)}) copy-start(s32[32]{0:T(128)} %broadcast_multiply_fusion) | copy-start | bytes 388
  50.9 10.6 %all-to-all-start = ((bf16[16,16,128]{2,1,0:T(8,128)(2,1)}), bf16[16,16,128]{2,1,0:T(8,128)(2,1)S(1)}, u32[]{:S(2)}, u32[]{:S(2)}) async-start(bf16[16,16,128]{2,1,0:T(8,128)(2,1)} %values_part.1), calls=%async_computation | async-start | bytes 131072 | tf_op jit(solution)/shard_map/all_to_all | solution.py:488

commit v4 on v3

--- a/solution.py
+++ b/solution.py
@@ -326,7 +326,7 @@
     )(me.reshape(1), slot_of.reshape(1, -1), tokens, weight)
 
 
-def product_kernel(skipped, *refs):
+def product_kernel(skipped, crossed, *refs):
     mine_ref, theirs_ref, block_ref, other_ref, *refs = refs[skipped:]
     gate_refs, (kept_ref, packed_ref) = refs[:-2], refs[-2:]
     half = mine_ref.shape[0] // 2
@@ -342,17 +342,24 @@
         gates = product(gate_refs[0][...], gate_refs[1][...], (((1,), (1,)), ((), ())))
         zeros = jnp.zeros((gates.shape[0], 2 * DK - gates.shape[1]), jnp.float32)
         total = jnp.concatenate([total, gates, zeros], axis=1)
-    kept_ref[...] = total[:half]
-    pack_rows(total[half:], packed_ref)
-
-
-def run_product(mine, theirs, weights, part, gates=(), earlier=()):
+    kept, sent = total[:half], total[half:]
+    if crossed:
+        quarter = half // 2
+        kept, sent = (
+            jnp.concatenate([kept[:quarter], sent[:quarter]], axis=0),
+            jnp.concatenate([kept[quarter:], sent[quarter:]], axis=0),
+        )
+    kept_ref[...] = kept
+    pack_rows(sent, packed_ref)
+
+
+def run_product(mine, theirs, weights, part, gates=(), earlier=(), crossed=False):
     vmem = pl.BlockSpec(memory_space=pltpu.VMEM)
     block = pl.BlockSpec((mine.shape[1], HEADS_WIDTH), lambda i: (0, part))
     half = mine.shape[0] // 2
     width = HEADS_WIDTH + len(gates) * DK
     return pl.pallas_call(
-        functools.partial(product_kernel, len(earlier)),
+        functools.partial(product_kernel, len(earlier), crossed),
         grid=(1,),
         out_shape=[
             jax.ShapeDtypeStruct((half, width), jnp.float32),
@@ -443,7 +450,7 @@
         blocks = [block for bit in (0, 4) for block in range(TAP_BLOCKS) if block & 4 == bit]
         taps = [taps[:, block * TAP_WIDTH : (block + 1) * TAP_WIDTH] for block in blocks]
         taps = jnp.concatenate(taps, axis=0)
-    queries = run_product(mine, theirs, weights, 0)
+    queries = run_product(mine, theirs, weights, 0, crossed=True)
     keys = run_product(mine, theirs, weights, 1, earlier=queries[:1])
     values = run_product(mine, theirs, weights, 2, gates, earlier=keys[:1])
 
@@ -457,13 +464,17 @@
     )
     blank = jnp.zeros((1, carried.shape[2]), jnp.float32)
     history = jnp.concatenate([blank, carried[1], blank, carried[0]], axis=0)
+    routes = [[bits[1], bits[0]] + bits[2:], bits, bits]
     kept = [chunk[0] for chunk in (queries, keys, values)]
-    got = [swap(chunk[1], bits[0], devices) for chunk in (queries, keys, values)]
-    for level, bit in enumerate(bits[1:]):
+    got = [
+        swap(chunk[1], route[0], devices)
+        for chunk, route in zip((queries, keys, values), routes)
+    ]
+    for level in range(1, len(bits)):
         for at in range(3):
             kept[at], packed = run_combine(kept[at], got[at])
-            got[at] = swap(packed, bit, devices)
-            if ride and level == 0 and at == 0:
+            got[at] = swap(packed, routes[at][level], devices)
+            if ride and level == 1 and at == 0:
                 kept[0], taps, far = tie(kept[0], taps, far)
                 taps = jnp.concatenate([taps, far], axis=0)
                 taps = jnp.concatenate([taps, swap(taps, 4, devices)], axis=0)

time: 62.6 us -> 61.3 us (0.979)
  starting transfers between devices: 25.4 us -> 24.7 us
  waiting for transfers between devices: 16.8 us -> 16.1 us
    ppermute x15, starting transfers between devices: 21.8 us -> 20.1 us  [swap(): return lax.ppermute(value, 'heads', [(i, i ^ bit) for i in range(devices)])]
    all_to_all x1, starting transfers between devices: 3.65 us -> 4.67 us  [on_device(): lax.all_to_all(sending, 'heads', split_axis=0, concat_axis=0, tiled=True)]
    ppermute x15, waiting for transfers between devices: 10.1 us -> 9.36 us  [swap(): return lax.ppermute(value, 'heads', [(i, i ^ bit) for i in range(devices)])]
  transfers between devices with their start and end apart: 16 -> 16, of which waited for: 6 -> 6; matrix products, arithmetic and copies ran while one was open for 5% -> 5% of each run, Pallas kernels for 16% -> 17%
where the time goes in v4:
time: 61.3 us; the launch traced here: 61 us
  starting transfers between devices  24.7 us (40%)
  waiting for transfers between devices  16.1 us (26%)
  Pallas kernels  12.2 us (20%)
  local copies, waits for them, and re-layouts  5.57 us (9%)
  other arithmetic  1.89 us (3%)
    ppermute x15, starting transfers between devices, swap(): return lax.ppermute(value, 'heads', [(i, i ^ bit) for i in range(devices)])  20.1 us
    ppermute x15, waiting for transfers between devices, swap(): return lax.ppermute(value, 'heads', [(i, i ^ bit) for i in range(devices)])  9.36 us
    all_to_all x1, waiting for transfers between devices, on_device(): lax.all_to_all(sending, 'heads', split_axis=0, concat_axis=0, tiled=True)  6.71 us
    all_to_all x1, starting transfers between devices, on_device(): lax.all_to_all(sending, 'heads', split_axis=0, concat_axis=0, tiled=True)  4.67 us
    unnamed x25, local copies, waits for them, and re-layouts  3.78 us
    pallas_call x3, Pallas kernels, run_product(): pl.pallas_call(functools.partial(product_kernel, len(earlier), crossed),...  3.4 us
    pallas_call x1, Pallas kernels, run_delta(): pl.pallas_call(keys_kernel, out_shape=[per_head] * 2 + lags + [tap_blocks...  2.81 us
    pallas_call x6, Pallas kernels, run_combine(): pl.pallas_call(combine_kernel, out_shape=[jax.ShapeDtypeStruct((half, wid...  2.8 us
  transfers between devices with their start and end apart: 16, of which 6 were waited for; matrix products, arithmetic and copies ran while one was open for 5% of the time, Pallas kernels for 17%

profile of v4, /device:TPU:0, one launch (start us, length us, event | category | flops | bytes accessed | tf_op | source)
XLA Modules:
  0.0 61.0 jit_solution(4257070383147739163)
XLA Ops:
  0.0 0.5 collective-permute-start
  0.5 0.7 %fusion.6 = (bf16[4,384]{1,0:T(4,128)(2,1)S(1)}, bf16[4,384]{1,0:T(4,128)(2,1)S(1)}) fusion(bf16[4,768]{1,0:T(4,128)(2,1)} %param.13), kind=kLoop, calls=%fused_computation.33 | loop fusion | bytes 12288 | tf_op jit(solution)/shard_map/slice | solution.py:446
  1.7 1.2 %broadcast_multiply_fusion = s32[32]{0:T(128)} fusion(s32[32]{0:T(128)} %param.18), kind=kLoop, calls=%fused_computation.31 | loop fusion | flops 32 | bytes 256 | tf_op jit(solution)/shard_map/mul | solution.py:434
  3.0 2.0 %copy-done.1 = bf16[144,12288]{1,0:T(8,128)(2,1)S(1)} copy-done((bf16[144,12288]{1,0:T(8,128)(2,1)S(1)}, bf16[144,12288]{1,0:T(8,128)(2,1)}, u32[]{:S(2)}) %copy-start.1) | copy-done | bytes 3538968
  5.0 1.1 %copy-done.2 = bf16[32,4,2304]{2,1,0:T(4,128)(2,1)S(1)} copy-done((bf16[32,4,2304]{2,1,0:T(4,128)(2,1)S(1)}, bf16[32,4,2304]{2,1,0:T(4,128)(2,1)}, u32[]{:S(2)}) %copy-start.2) | copy-done | bytes 589848
  6.1 0.7 %copy-done.4 = s32[32]{0:T(128)S(1)} copy-done((s32[32]{0:T(128)S(1)}, s32[32]{0:T(128)}, u32[]{:S(2)}) %copy-start.4) | copy-done | bytes 152
  6.7 1.2 %token_rows.1 = (bf16[64,144]{1,0:T(8,128)(2,1)S(1)}, bf16[64,144]{1,0:T(8,128)(2,1)S(1)}, bf16[144,12288]{1,0:T(8,128)(2,1)S(1)}) custom-call(s32[1]{0:T(128)} %bitcast.me_ref.twist_ref, s32[1,32]{1,0:T(1,128)S(1)} %bitcast.14, bf16[32,4,2304]{2,1,0:T(4,128)(2,1)S(1)} %copy-done.2, bf16[144,12288]{1,0:T(8,128)(2,1)S(1)} %copy-done.1), custom_call_target="tpu_custom_call" | custom-call | tf_op jit(solution)/shard_map/token_rows/pallas_call | solution.py:310
  7.9 0.8 %partial_product.3 = (f32[32,4096]{1,0:T(8,128)S(1)}, s16[32,4224]{1,0:T(8,128)(2,1)S(1)}) custom-call(bf16[64,144]{1,0:T(8,128)(2,1)S(1)} %get-tuple-element.40.refs_0_.refs_1_, bf16[64,144]{1,0:T(8,128)(2,1)S(1)} %get-tuple-element.41.refs_1_.refs_2_, bf16[144,12288]{1,0:T(8,128)(2,1)S(1)} %get-tuple-element.42.refs_2_.refs_3_, ...), custom_call_target="tpu_custom_call" | custom-call | tf_op jit(solution)/shard_map/partial_product/pallas_call | solution.py:361
  8.8 2.7 %collective-permute-start.5 = (s16[32,4224]{1,0:T(8,128)(2,1)S(1)}, s16[32,4224]{1,0:T(8,128)(2,1)S(1)}, u32[]{:S(2)}, u32[]{:S(2)}) collective-permute-start(s16[32,4224]{1,0:T(8,128)(2,1)S(1)} %get-tuple-element.57), channel_id=1, source_target_pairs={{0,4},{1,5},{2,6},{3,7},{4,0},{5,1},{6,2},{7,3},{8,12},{9,13},{10,... | collective-permute-start | bytes 811016 | tf_op jit(solution)/shard_map/ppermute | solution.py:411
  11.5 0.8 %partial_product.4 = (f32[32,4096]{1,0:T(8,128)S(1)}, s16[32,4224]{1,0:T(8,128)(2,1)S(1)}) custom-call(f32[32,4096]{1,0:T(8,128)S(1)} %get-tuple-element.43.refs_0_.kept_ref, bf16[64,144]{1,0:T(8,128)(2,1)S(1)} %get-tuple-element.40.refs_0_.refs_1_, bf16[64,144]{1,0:T(8,128)(2,1)S(1)} %get-tuple-element.41.refs_1_.refs_2_, ...), custom_call_target="tpu_custom_call" | custom-call | tf_op jit(solution)/shard_map/partial_product/pallas_call | solution.py:361
  12.4 1.8 %partial_product.5 = (f32[32,4352]{1,0:T(8,128)S(1)}, s16[32,4480]{1,0:T(8,128)(2,1)S(1)}) custom-call(f32[32,4096]{1,0:T(8,128)S(1)} %get-tuple-element.44.refs_0_.kept_ref, bf16[64,144]{1,0:T(8,128)(2,1)S(1)} %get-tuple-element.40.refs_0_.refs_1_, bf16[64,144]{1,0:T(8,128)(2,1)S(1)} %get-tuple-element.41.refs_1_.refs_2_, ...), custom_call_target="tpu_custom_call" | custom-call | tf_op jit(solution)/shard_map/partial_product/pallas_call | solution.py:361
  14.3 1.6 %collective-permute-start.9 = (s16[32,4224]{1,0:T(8,128)(2,1)S(1)}, s16[32,4224]{1,0:T(8,128)(2,1)S(1)}, u32[]{:S(2)}, u32[]{:S(2)}) collective-permute-start(s16[32,4224]{1,0:T(8,128)(2,1)S(1)} %get-tuple-element.63), channel_id=1, source_target_pairs={{0,2},{1,3},{2,0},{3,1},{4,6},{5,7},{6,4},{7,5},{8,10},{9,11},{10,... | collective-permute-start | bytes 811016 | tf_op jit(solution)/shard_map/ppermute | solution.py:411
  15.9 0.5 collective-permute-start.2
  17.1 1.5 %collective-permute-done.5.got_ref = s16[32,4224]{1,0:T(8,128)(2,1)S(1)} collective-permute-done((s16[32,4224]{1,0:T(8,128)(2,1)S(1)}, s16[32,4224]{1,0:T(8,128)(2,1)S(1)}, u32[]{:S(2)}, u32[]{:S(2)}) %collective-permute-start.5) | collective-permute-done | bytes 270368 | tf_op jit(solution)/shard_map/ppermute | solution.py:411
  18.6 0.5 combine.8
  19.1 1.8 %collective-permute-start.12 = (bf16[16,384]{1,0:T(8,128)(2,1)S(1)}, bf16[16,384]{1,0:T(8,128)(2,1)S(1)}, u32[]{:S(2)}, u32[]{:S(2)}) collective-permute-start(bf16[16,384]{1,0:T(8,128)(2,1)S(1)} %pad_maximum_fusion.2), channel_id=1, source_target_pairs={{0,4},{1,5},{2,6},{3,7},{4,0},{5,1},{6,2},{7,3},{8,12},{9,13},{10,... | collective-permute-start | bytes 36872 | tf_op jit(solution)/shard_map/ppermute | solution.py:411
  20.9 1.5 %collective-permute-start.7 = (s16[16,4224]{1,0:T(8,128)(2,1)S(1)}, s16[16,4224]{1,0:T(8,128)(2,1)S(1)}, u32[]{:S(2)}, u32[]{:S(2)}) collective-permute-start(s16[16,4224]{1,0:T(8,128)(2,1)S(1)} %get-tuple-element.60), channel_id=1, source_target_pairs={{0,2},{1,3},{2,0},{3,1},{4,6},{5,7},{6,4},{7,5},{8,10},{9,11},{10,... | collective-permute-start | bytes 405512 | tf_op jit(solution)/shard_map/ppermute | solution.py:411
  22.5 1.2 %collective-permute-done.9.got_ref = s16[32,4224]{1,0:T(8,128)(2,1)S(1)} collective-permute-done((s16[32,4224]{1,0:T(8,128)(2,1)S(1)}, s16[32,4224]{1,0:T(8,128)(2,1)S(1)}, u32[]{:S(2)}, u32[]{:S(2)}) %collective-permute-start.9) | collective-permute-done | bytes 270368 | tf_op jit(solution)/shard_map/ppermute | solution.py:411
  23.7 0.5 combine.10
  24.4 3.0 %collective-permute-start.13 = (bf16[32,384]{1,0:T(8,128)(2,1)S(1)}, bf16[32,384]{1,0:T(8,128)(2,1)S(1)}, u32[]{:S(2)}, u32[]{:S(2)}) collective-permute-start(bf16[32,384]{1,0:T(8,128)(2,1)S(1)} %pad_maximum_fusion.1), channel_id=1, source_target_pairs={{0,8},{1,9},{2,10},{3,11},{4,12},{5,13},{6,14},{7,15},{8,0},{9,1},... | collective-permute-start | bytes 73736 | tf_op jit(solution)/shard_map/ppermute | solution.py:411
  27.4 2.5 %collective-permute-done.2.got_ref = s16[32,4480]{1,0:T(8,128)(2,1)S(1)} collective-permute-done((s16[32,4480]{1,0:T(8,128)(2,1)S(1)}, s16[32,4480]{1,0:T(8,128)(2,1)S(1)}, u32[]{:S(2)}, u32[]{:S(2)}) %collective-permute-start.2) | collective-permute-done | bytes 286752 | tf_op jit(solution)/shard_map/ppermute | solution.py:411
  29.9 0.5 combine.6
  30.5 2.0 %collective-permute-start.14 = (bf16[64,384]{1,0:T(8,128)(2,1)S(1)}, bf16[64,384]{1,0:T(8,128)(2,1)S(1)}, u32[]{:S(2)}, u32[]{:S(2)}) collective-permute-start(bf16[64,384]{1,0:T(8,128)(2,1)S(1)} %constant_dynamic-update-slice_fusion.near_ref), channel_id=1, source_target_pairs={{0,2},{1,3},{2,0},{3,1},{4,6},{5,7},{6,4},{7,5},{8,10},{9,11},{10,... | collective-permute-start | bytes 147464 | tf_op jit(solution)/shard_map/ppermute | solution.py:411
  32.9 2.7 %collective-permute-start.8 = (s16[16,2176]{1,0:T(8,128)(2,1)S(1)}, s16[16,2176]{1,0:T(8,128)(2,1)S(1)}, u32[]{:S(2)}, u32[]{:S(2)}) collective-permute-start(s16[16,2176]{1,0:T(8,128)(2,1)S(1)} %get-tuple-element.62), channel_id=1, source_target_pairs={{0,8},{1,9},{2,10},{3,11},{4,12},{5,13},{6,14},{7,15},{8,0},{9,1},... | collective-permute-start | bytes 208904 | tf_op jit(solution)/shard_map/ppermute | solution.py:411
  36.8 2.7 %collective-permute-start.4 = (s16[16,2304]{1,0:T(8,128)(2,1)S(1)}, s16[16,2304]{1,0:T(8,128)(2,1)S(1)}, u32[]{:S(2)}, u32[]{:S(2)}) collective-permute-start(s16[16,2304]{1,0:T(8,128)(2,1)S(1)} %get-tuple-element.55), channel_id=1, source_target_pairs={{0,8},{1,9},{2,10},{3,11},{4,12},{5,13},{6,14},{7,15},{8,0},{9,1},... | collective-permute-start | bytes 221192 | tf_op jit(solution)/shard_map/ppermute | solution.py:411
  39.6 1.1 %collective-permute-done.8.query_got_ref = s16[16,2176]{1,0:T(8,128)(2,1)S(1)} collective-permute-done((s16[16,2176]{1,0:T(8,128)(2,1)S(1)}, s16[16,2176]{1,0:T(8,128)(2,1)S(1)}, u32[]{:S(2)}, u32[]{:S(2)}) %collective-permute-start.8) | collective-permute-done | bytes 69664 | tf_op jit(solution)/shard_map/ppermute | solution.py:411
  40.7 3.0 %collective-permute-done.11.key_got_ref = s16[16,2176]{1,0:T(8,128)(2,1)S(1)} collective-permute-done((s16[16,2176]{1,0:T(8,128)(2,1)S(1)}, s16[16,2176]{1,0:T(8,128)(2,1)S(1)}, u32[]{:S(2)}, u32[]{:S(2)}) %collective-permute-start.11) | collective-permute-done | bytes 69664 | tf_op jit(solution)/shard_map/ppermute | solution.py:411
  43.7 2.8 %keys_part.1 = (f32[32,8,128]{2,1,0:T(8,128)S(1)}, f32[32,8,128]{2,1,0:T(8,128)S(1)}, f32[3,32,8,128]{3,2,1,0:T(8,128)S(1)}, f32[4,32,8,128]{3,2,1,0:T(8,128)S(1)}, f32[32,4,384]{2,1,0:T(4,128)S(1)}) custom-call(s32[1]{0:T(128)} %bitcast.me_ref.twist_ref, f32[8,4096]{1,0:T(8,128)S(1)} %get-tuple-element.61.query_ref, ...), custom_call_target="tpu_custom_call" | custom-call | flops 40000000 | bytes 9000000 | tf_op jit(solution)/shard_map/keys_part/pallas_call | solution.py:243
  46.6 1.9 %values_part.1 = bf16[16,16,128]{2,1,0:T(8,128)(2,1)} custom-call(s32[64]{0:T(128)S(1)} %select_reduce_fusion.slots_ref, s32[64]{0:T(128)S(1)} %get-tuple-element.81.halves_ref, s32[2]{0:T(128)S(1)} %fusion.4.lengths_ref, s32[1]{0:T(128)} %bitcast.me_ref.twist_ref, f32[8,4352]{1,0:T(8,128)S(1)} %get-tuple-element.54.value_ref, ...), custom_call_target="tpu_custom_call" | custom-call | flops 4000000 | bytes 2000000 | tf_op jit(solution)/shard_map/values_part/pallas_call | solution.py:256
  48.5 4.7 %all-to-all-start = ((bf16[16,16,128]{2,1,0:T(8,128)(2,1)}), bf16[16,16,128]{2,1,0:T(8,128)(2,1)S(1)}, u32[]{:S(2)}, u32[]{:S(2)}) async-start(bf16[16,16,128]{2,1,0:T(8,128)(2,1)} %values_part.1), calls=%async_computation | async-start | bytes 131072 | tf_op jit(solution)/shard_map/all_to_all | solution.py:499
  53.4 6.7 %all-to-all-done = bf16[16,16,128]{2,1,0:T(8,128)(2,1)S(1)} async-done(((bf16[16,16,128]{2,1,0:T(8,128)(2,1)}), bf16[16,16,128]{2,1,0:T(8,128)(2,1)S(1)}, u32[]{:S(2)}, u32[]{:S(2)}) %all-to-all-start) | async-done | bytes 65568 | tf_op jit(solution)/shard_map/all_to_all | solution.py:499
  60.3 0.7 %reshape.46 = bf16[32,4,256]{2,1,0:T(4,128)(2,1)} reshape(bf16[128,256]{1,0:T(8,128)(2,1)S(1)} %convolution_convert_fusion) | data formatting | bytes 131072 | tf_op jit(solution)/shard_map/reshape | solution.py:510
  (57 shorter events, 3.7 us)
Async XLA Ops:
  0.0 7.9 %collective-permute-start = (bf16[144,12288]{1,0:T(8,128)(2,1)}, bf16[144,12288]{1,0:T(8,128)(2,1)S(1)}, u32[]{:S(2)}, u32[]{:S(2)}) collective-permute-start(bf16[144,12288]{1,0:T(8,128)(2,1)} %weight_hbm.1), channel_id=1, source_target_pairs={{0,1},{1,0},{2,3},{3,2},{4,5},{5,4},{6,7},{7,6},{8,9},{9,8},{10,11... | collective-permute-start | bytes 10616840 | tf_op jit(solution)/shard_map/ppermute | solution.py:411
  1.2 17.9 %collective-permute-start.6 = (bf16[8,384]{1,0:T(8,128)(2,1)S(1)}, bf16[8,384]{1,0:T(8,128)(2,1)S(1)}, u32[]{:S(2)}, u32[]{:S(2)}) collective-permute-start(bf16[8,384]{1,0:T(8,128)(2,1)S(1)} %pad_maximum_fusion.3), channel_id=1, source_target_pairs={{0,1},{1,0},{2,3},{3,2},{4,5},{5,4},{6,7},{7,6},{8,9},{9,8},{10,11... | collective-permute-start | bytes 18440 | tf_op jit(solution)/shard_map/ppermute | solution.py:411
  1.3 11.0 %collective-permute-start.1 = (bf16[64,144]{1,0:T(8,128)(2,1)}, bf16[64,144]{1,0:T(8,128)(2,1)}, u32[]{:S(2)}, u32[]{:S(2)}) collective-permute-start(bf16[64,144]{1,0:T(8,128)(2,1)} %bitcast.12), channel_id=1, source_target_pairs={{0,1},{1,0},{2,3},{3,2},{4,5},{5,4},{6,7},{7,6},{8,9},{9,8},{10,11... | collective-permute-start | bytes 55304 | tf_op jit(solution)/shard_map/ppermute | solution.py:411
  3.0 2.0 %copy-start.1 = (bf16[144,12288]{1,0:T(8,128)(2,1)S(1)}, bf16[144,12288]{1,0:T(8,128)(2,1)}, u32[]{:S(2)}) copy-start(bf16[144,12288]{1,0:T(8,128)(2,1)} %weight_hbm.1) | copy-start | bytes 10616836
  5.0 1.1 %copy-start.2 = (bf16[32,4,2304]{2,1,0:T(4,128)(2,1)S(1)}, bf16[32,4,2304]{2,1,0:T(4,128)(2,1)}, u32[]{:S(2)}) copy-start(bf16[32,4,2304]{2,1,0:T(4,128)(2,1)} %tokens_hbm.1) | copy-start | bytes 1769476
  6.0 0.7 %copy-start.4 = (s32[32]{0:T(128)S(1)}, s32[32]{0:T(128)}, u32[]{:S(2)}) copy-start(s32[32]{0:T(128)} %param.18) | copy-start | bytes 388
  8.8 9.8 %collective-permute-start.5 = (s16[32,4224]{1,0:T(8,128)(2,1)S(1)}, s16[32,4224]{1,0:T(8,128)(2,1)S(1)}, u32[]{:S(2)}, u32[]{:S(2)}) collective-permute-start(s16[32,4224]{1,0:T(8,128)(2,1)S(1)} %get-tuple-element.57), channel_id=1, source_target_pairs={{0,4},{1,5},{2,6},{3,7},{4,0},{5,1},{6,2},{7,3},{8,12},{9,13},{10,... | collective-permute-start | bytes 811016 | tf_op jit(solution)/shard_map/ppermute | solution.py:411
  11.5 0.8 %copy-start.3 = (bf16[144,64]{0,1:T(8,128)(2,1)S(1)}, bf16[144,64]{0,1:T(8,128)(2,1)}, u32[]{:S(2)}) copy-start(bf16[144,64]{0,1:T(8,128)(2,1)} %param.12) | copy-start | bytes 55300
  12.3 1.8 %copy-start.9 = (s32[32]{0:T(128)S(1)}, s32[32]{0:T(128)}, u32[]{:S(2)}) copy-start(s32[32]{0:T(128)} %param.16) | copy-start | bytes 388
  12.4 1.9 %copy-start.10 = (s32[64]{0:T(128)S(1)}, s32[64]{0:T(128)}, u32[]{:S(2)}) copy-start(s32[64]{0:T(128)} %param.17) | copy-start | bytes 772
  12.4 4.0 %copy-start.6 = (f32[2,3,12288]{2,0,1:T(2,128)S(1)}, f32[2,3,12288]{2,0,1:T(2,128)}, u32[]{:S(2)}) copy-start(f32[2,3,12288]{2,0,1:T(2,128)} %param.15) | copy-start | bytes 884740
  12.4 4.3 %copy-start.5 = (s32[32]{0:T(128)S(1)}, s32[32]{0:T(128)}, u32[]{:S(2)}) copy-start(s32[32]{0:T(128)} %param.18) | copy-start | bytes 388
  12.4 4.3 %copy-start.8 = (s32[32]{0:T(128)S(1)}, s32[32]{0:T(128)}, u32[]{:S(2)}) copy-start(s32[32]{0:T(128)} %param.19) | copy-start | bytes 388
  14.2 29.6 %copy-start = (f32[2,32,128,128]{3,2,1,0:T(8,128)S(1)}, f32[2,32,128,128]{3,2,1,0:T(8,128)}, u32[]{:S(2)}) copy-start(f32[2,32,128,128]{3,2,1,0:T(8,128)} %state_hbm.1) | copy-start | bytes 12582916
  14.3 9.4 %collective-permute-start.9 = (s16[32,4224]{1,0:T(8,128)(2,1)S(1)}, s16[32,4224]{1,0:T(8,128)(2,1)S(1)}, u32[]{:S(2)}, u32[]{:S(2)}) collective-permute-start(s16[32,4224]{1,0:T(8,128)(2,1)S(1)} %get-tuple-element.63), channel_id=1, source_target_pairs={{0,2},{1,3},{2,0},{3,1},{4,6},{5,7},{6,4},{7,5},{8,10},{9,11},{10,... | collective-permute-start | bytes 811016 | tf_op jit(solution)/shard_map/ppermute | solution.py:411
  15.9 13.9 %collective-permute-start.2 = (s16[32,4480]{1,0:T(8,128)(2,1)S(1)}, s16[32,4480]{1,0:T(8,128)(2,1)S(1)}, u32[]{:S(2)}, u32[]{:S(2)}) collective-permute-start(s16[32,4480]{1,0:T(8,128)(2,1)S(1)} %get-tuple-element.51), channel_id=1, source_target_pairs={{0,2},{1,3},{2,0},{3,1},{4,6},{5,7},{6,4},{7,5},{8,10},{9,11},{10,... | collective-permute-start | bytes 860168 | tf_op jit(solution)/shard_map/ppermute | solution.py:411
  19.1 5.2 %collective-permute-start.12 = (bf16[16,384]{1,0:T(8,128)(2,1)S(1)}, bf16[16,384]{1,0:T(8,128)(2,1)S(1)}, u32[]{:S(2)}, u32[]{:S(2)}) collective-permute-start(bf16[16,384]{1,0:T(8,128)(2,1)S(1)} %pad_maximum_fusion.2), channel_id=1, source_target_pairs={{0,4},{1,5},{2,6},{3,7},{4,0},{5,1},{6,2},{7,3},{8,12},{9,13},{10,... | collective-permute-start | bytes 36872 | tf_op jit(solution)/shard_map/ppermute | solution.py:411
  20.9 11.6 %collective-permute-start.7 = (s16[16,4224]{1,0:T(8,128)(2,1)S(1)}, s16[16,4224]{1,0:T(8,128)(2,1)S(1)}, u32[]{:S(2)}, u32[]{:S(2)}) collective-permute-start(s16[16,4224]{1,0:T(8,128)(2,1)S(1)} %get-tuple-element.60), channel_id=1, source_target_pairs={{0,2},{1,3},{2,0},{3,1},{4,6},{5,7},{6,4},{7,5},{8,10},{9,11},{10,... | collective-permute-start | bytes 405512 | tf_op jit(solution)/shard_map/ppermute | solution.py:411
  24.2 11.4 %collective-permute-start.10 = (s16[16,4224]{1,0:T(8,128)(2,1)S(1)}, s16[16,4224]{1,0:T(8,128)(2,1)S(1)}, u32[]{:S(2)}, u32[]{:S(2)}) collective-permute-start(s16[16,4224]{1,0:T(8,128)(2,1)S(1)} %get-tuple-element.65), channel_id=1, source_target_pairs={{0,4},{1,5},{2,6},{3,7},{4,0},{5,1},{6,2},{7,3},{8,12},{9,13},{10,... | collective-permute-start | bytes 405512 | tf_op jit(solution)/shard_map/ppermute | solution.py:411
  24.4 6.2 %collective-permute-start.13 = (bf16[32,384]{1,0:T(8,128)(2,1)S(1)}, bf16[32,384]{1,0:T(8,128)(2,1)S(1)}, u32[]{:S(2)}, u32[]{:S(2)}) collective-permute-start(bf16[32,384]{1,0:T(8,128)(2,1)S(1)} %pad_maximum_fusion.1), channel_id=1, source_target_pairs={{0,8},{1,9},{2,10},{3,11},{4,12},{5,13},{6,14},{7,15},{8,0},{9,1},... | collective-permute-start | bytes 73736 | tf_op jit(solution)/shard_map/ppermute | solution.py:411
  30.4 6.0 %collective-permute-start.3 = (s16[16,4480]{1,0:T(8,128)(2,1)S(1)}, s16[16,4480]{1,0:T(8,128)(2,1)S(1)}, u32[]{:S(2)}, u32[]{:S(2)}) collective-permute-start(s16[16,4480]{1,0:T(8,128)(2,1)S(1)} %get-tuple-element.53), channel_id=1, source_target_pairs={{0,4},{1,5},{2,6},{3,7},{4,0},{5,1},{6,2},{7,3},{8,12},{9,13},{10,... | collective-permute-start | bytes 430088 | tf_op jit(solution)/shard_map/ppermute | solution.py:411
  30.5 9.1 %collective-permute-start.14 = (bf16[64,384]{1,0:T(8,128)(2,1)S(1)}, bf16[64,384]{1,0:T(8,128)(2,1)S(1)}, u32[]{:S(2)}, u32[]{:S(2)}) collective-permute-start(bf16[64,384]{1,0:T(8,128)(2,1)S(1)} %constant_dynamic-update-slice_fusion.near_ref), channel_id=1, source_target_pairs={{0,2},{1,3},{2,0},{3,1},{4,6},{5,7},{6,4},{7,5},{8,10},{9,11},{10,... | collective-permute-start | bytes 147464 | tf_op jit(solution)/shard_map/ppermute | solution.py:411
  32.9 7.8 %collective-permute-start.8 = (s16[16,2176]{1,0:T(8,128)(2,1)S(1)}, s16[16,2176]{1,0:T(8,128)(2,1)S(1)}, u32[]{:S(2)}, u32[]{:S(2)}) collective-permute-start(s16[16,2176]{1,0:T(8,128)(2,1)S(1)} %get-tuple-element.62), channel_id=1, source_target_pairs={{0,8},{1,9},{2,10},{3,11},{4,12},{5,13},{6,14},{7,15},{8,0},{9,1},... | collective-permute-start | bytes 208904 | tf_op jit(solution)/shard_map/ppermute | solution.py:411
  36.0 7.7 %collective-permute-start.11 = (s16[16,2176]{1,0:T(8,128)(2,1)S(1)}, s16[16,2176]{1,0:T(8,128)(2,1)S(1)}, u32[]{:S(2)}, u32[]{:S(2)}) collective-permute-start(s16[16,2176]{1,0:T(8,128)(2,1)S(1)} %get-tuple-element.67), channel_id=1, source_target_pairs={{0,8},{1,9},{2,10},{3,11},{4,12},{5,13},{6,14},{7,15},{8,0},{9,1},... | collective-permute-start | bytes 208904 | tf_op jit(solution)/shard_map/ppermute | solution.py:411
  36.8 9.7 %collective-permute-start.4 = (s16[16,2304]{1,0:T(8,128)(2,1)S(1)}, s16[16,2304]{1,0:T(8,128)(2,1)S(1)}, u32[]{:S(2)}, u32[]{:S(2)}) collective-permute-start(s16[16,2304]{1,0:T(8,128)(2,1)S(1)} %get-tuple-element.55), channel_id=1, source_target_pairs={{0,8},{1,9},{2,10},{3,11},{4,12},{5,13},{6,14},{7,15},{8,0},{9,1},... | collective-permute-start | bytes 221192 | tf_op jit(solution)/shard_map/ppermute | solution.py:411
  43.7 9.4 %copy-start.7 = (s32[32]{0:T(128)S(1)}, s32[32]{0:T(128)}, u32[]{:S(2)}) copy-start(s32[32]{0:T(128)} %broadcast_multiply_fusion) | copy-start | bytes 388
  48.5 11.6 %all-to-all-start = ((bf16[16,16,128]{2,1,0:T(8,128)(2,1)}), bf16[16,16,128]{2,1,0:T(8,128)(2,1)S(1)}, u32[]{:S(2)}, u32[]{:S(2)}) async-start(bf16[16,16,128]{2,1,0:T(8,128)(2,1)} %values_part.1), calls=%async_computation | async-start | bytes 131072 | tf_op jit(solution)/shard_map/all_to_all | solution.py:499

commit v5 on v4

--- a/solution.py
+++ b/solution.py
@@ -450,9 +450,9 @@
         blocks = [block for bit in (0, 4) for block in range(TAP_BLOCKS) if block & 4 == bit]
         taps = [taps[:, block * TAP_WIDTH : (block + 1) * TAP_WIDTH] for block in blocks]
         taps = jnp.concatenate(taps, axis=0)
-    queries = run_product(mine, theirs, weights, 0, crossed=True)
-    keys = run_product(mine, theirs, weights, 1, earlier=queries[:1])
+    keys = run_product(mine, theirs, weights, 1)
     values = run_product(mine, theirs, weights, 2, gates, earlier=keys[:1])
+    queries = run_product(mine, theirs, weights, 0, earlier=values[:1], crossed=True)
 
     lengths, old_heads, new_units, carried, *values = tie(
         lengths, old_heads, new_units, conv_state, *values

time: 61.3 us -> 60.2 us (0.982)
  starting transfers between devices: 24.7 us -> 23.5 us
    ppermute x15, starting transfers between devices: 20.1 us -> 19 us  [swap(): return lax.ppermute(value, 'heads', [(i, i ^ bit) for i in range(devices)])]
  transfers between devices with their start and end apart: 16 -> 16, of which waited for: 6 -> 7; matrix products, arithmetic and copies ran while one was open for 5% -> 5% of each run, Pallas kernels for 17% -> 17%
where the time goes in v5:
time: 60.2 us; the launch traced here: 59.8 us
  starting transfers between devices  23.5 us (39%)
  waiting for transfers between devices  16.2 us (27%)
  Pallas kernels  12.2 us (20%)
  local copies, waits for them, and re-layouts  5.57 us (9%)
  other arithmetic  1.89 us (3%)
    ppermute x15, starting transfers between devices, swap(): return lax.ppermute(value, 'heads', [(i, i ^ bit) for i in range(devices)])  19 us
    ppermute x15, waiting for transfers between devices, swap(): return lax.ppermute(value, 'heads', [(i, i ^ bit) for i in range(devices)])  9.47 us
    all_to_all x1, waiting for transfers between devices, on_device(): lax.all_to_all(sending, 'heads', split_axis=0, concat_axis=0, tiled=True)  6.71 us
    all_to_all x1, starting transfers between devices, on_device(): lax.all_to_all(sending, 'heads', split_axis=0, concat_axis=0, tiled=True)  4.46 us
    unnamed x25, local copies, waits for them, and re-layouts  3.78 us
    pallas_call x3, Pallas kernels, run_product(): pl.pallas_call(functools.partial(product_kernel, len(earlier), crossed),...  3.4 us
    pallas_call x1, Pallas kernels, run_delta(): pl.pallas_call(keys_kernel, out_shape=[per_head] * 2 + lags + [tap_blocks...  2.81 us
    pallas_call x6, Pallas kernels, run_combine(): pl.pallas_call(combine_kernel, out_shape=[jax.ShapeDtypeStruct((half, wid...  2.8 us
  transfers between devices with their start and end apart: 16, of which 7 were waited for; matrix products, arithmetic and copies ran while one was open for 5% of the time, Pallas kernels for 17%

profile of v5, /device:TPU:0, one launch (start us, length us, event | category | flops | bytes accessed | tf_op | source)
XLA Modules:
  0.0 59.8 jit_solution(358942098273656544)
XLA Ops:
  0.5 0.7 %fusion.6 = (bf16[4,384]{1,0:T(4,128)(2,1)S(1)}, bf16[4,384]{1,0:T(4,128)(2,1)S(1)}) fusion(bf16[4,768]{1,0:T(4,128)(2,1)} %param.13), kind=kLoop, calls=%fused_computation.33 | loop fusion | bytes 12288 | tf_op jit(solution)/shard_map/slice | solution.py:446
  1.7 1.2 %broadcast_multiply_fusion = s32[32]{0:T(128)} fusion(s32[32]{0:T(128)} %param.18), kind=kLoop, calls=%fused_computation.31 | loop fusion | flops 32 | bytes 256 | tf_op jit(solution)/shard_map/mul | solution.py:434
  3.0 2.0 %copy-done.1 = bf16[144,12288]{1,0:T(8,128)(2,1)S(1)} copy-done((bf16[144,12288]{1,0:T(8,128)(2,1)S(1)}, bf16[144,12288]{1,0:T(8,128)(2,1)}, u32[]{:S(2)}) %copy-start.1) | copy-done | bytes 3538968
  5.0 1.1 %copy-done.2 = bf16[32,4,2304]{2,1,0:T(4,128)(2,1)S(1)} copy-done((bf16[32,4,2304]{2,1,0:T(4,128)(2,1)S(1)}, bf16[32,4,2304]{2,1,0:T(4,128)(2,1)}, u32[]{:S(2)}) %copy-start.2) | copy-done | bytes 589848
  6.1 0.7 %copy-done.4 = s32[32]{0:T(128)S(1)} copy-done((s32[32]{0:T(128)S(1)}, s32[32]{0:T(128)}, u32[]{:S(2)}) %copy-start.4) | copy-done | bytes 152
  6.7 1.2 %token_rows.1 = (bf16[64,144]{1,0:T(8,128)(2,1)S(1)}, bf16[64,144]{1,0:T(8,128)(2,1)S(1)}, bf16[144,12288]{1,0:T(8,128)(2,1)S(1)}) custom-call(s32[1]{0:T(128)} %bitcast.me_ref.twist_ref, s32[1,32]{1,0:T(1,128)S(1)} %bitcast.14, bf16[32,4,2304]{2,1,0:T(4,128)(2,1)S(1)} %copy-done.2, bf16[144,12288]{1,0:T(8,128)(2,1)S(1)} %copy-done.1), custom_call_target="tpu_custom_call" | custom-call | tf_op jit(solution)/shard_map/token_rows/pallas_call | solution.py:310
  8.0 0.8 %partial_product.3 = (f32[32,4096]{1,0:T(8,128)S(1)}, s16[32,4224]{1,0:T(8,128)(2,1)S(1)}) custom-call(bf16[64,144]{1,0:T(8,128)(2,1)S(1)} %get-tuple-element.40.refs_0_.refs_1_, bf16[64,144]{1,0:T(8,128)(2,1)S(1)} %get-tuple-element.41.refs_1_.refs_2_, bf16[144,12288]{1,0:T(8,128)(2,1)S(1)} %get-tuple-element.42.refs_2_.refs_3_, ...), custom_call_target="tpu_custom_call" | custom-call | tf_op jit(solution)/shard_map/partial_product/pallas_call | solution.py:361
  8.8 2.7 %collective-permute-start.9 = (s16[32,4224]{1,0:T(8,128)(2,1)S(1)}, s16[32,4224]{1,0:T(8,128)(2,1)S(1)}, u32[]{:S(2)}, u32[]{:S(2)}) collective-permute-start(s16[32,4224]{1,0:T(8,128)(2,1)S(1)} %get-tuple-element.63), channel_id=1, source_target_pairs={{0,2},{1,3},{2,0},{3,1},{4,6},{5,7},{6,4},{7,5},{8,10},{9,11},{10,... | collective-permute-start | bytes 811016 | tf_op jit(solution)/shard_map/ppermute | solution.py:411
  11.5 1.7 %partial_product.4 = (f32[32,4352]{1,0:T(8,128)S(1)}, s16[32,4480]{1,0:T(8,128)(2,1)S(1)}) custom-call(f32[32,4096]{1,0:T(8,128)S(1)} %get-tuple-element.43.refs_0_.kept_ref, bf16[64,144]{1,0:T(8,128)(2,1)S(1)} %get-tuple-element.40.refs_0_.refs_1_, bf16[64,144]{1,0:T(8,128)(2,1)S(1)} %get-tuple-element.41.refs_1_.refs_2_, ...), custom_call_target="tpu_custom_call" | custom-call | tf_op jit(solution)/shard_map/partial_product/pallas_call | solution.py:361
  13.3 0.8 %partial_product.5 = (f32[32,4096]{1,0:T(8,128)S(1)}, s16[32,4224]{1,0:T(8,128)(2,1)S(1)}) custom-call(f32[32,4352]{1,0:T(8,128)S(1)} %get-tuple-element.49.kept_ref.refs_0_, bf16[64,144]{1,0:T(8,128)(2,1)S(1)} %get-tuple-element.40.refs_0_.refs_1_, bf16[64,144]{1,0:T(8,128)(2,1)S(1)} %get-tuple-element.41.refs_1_.refs_2_, ...), custom_call_target="tpu_custom_call" | custom-call | tf_op jit(solution)/shard_map/partial_product/pallas_call | solution.py:361
  14.1 1.6 %collective-permute-start.5 = (s16[32,4224]{1,0:T(8,128)(2,1)S(1)}, s16[32,4224]{1,0:T(8,128)(2,1)S(1)}, u32[]{:S(2)}, u32[]{:S(2)}) collective-permute-start(s16[32,4224]{1,0:T(8,128)(2,1)S(1)} %get-tuple-element.57), channel_id=1, source_target_pairs={{0,4},{1,5},{2,6},{3,7},{4,0},{5,1},{6,2},{7,3},{8,12},{9,13},{10,... | collective-permute-start | bytes 811016 | tf_op jit(solution)/shard_map/ppermute | solution.py:411
  15.8 0.5 collective-permute-start.2
  17.1 1.7 %collective-permute-done.9.got_ref = s16[32,4224]{1,0:T(8,128)(2,1)S(1)} collective-permute-done((s16[32,4224]{1,0:T(8,128)(2,1)S(1)}, s16[32,4224]{1,0:T(8,128)(2,1)S(1)}, u32[]{:S(2)}, u32[]{:S(2)}) %collective-permute-start.9) | collective-permute-done | bytes 270368 | tf_op jit(solution)/shard_map/ppermute | solution.py:411
  18.8 0.5 combine.10
  19.3 2.1 %collective-permute-start.10 = (s16[16,4224]{1,0:T(8,128)(2,1)S(1)}, s16[16,4224]{1,0:T(8,128)(2,1)S(1)}, u32[]{:S(2)}, u32[]{:S(2)}) collective-permute-start(s16[16,4224]{1,0:T(8,128)(2,1)S(1)} %get-tuple-element.65), channel_id=1, source_target_pairs={{0,4},{1,5},{2,6},{3,7},{4,0},{5,1},{6,2},{7,3},{8,12},{9,13},{10,... | collective-permute-start | bytes 405512 | tf_op jit(solution)/shard_map/ppermute | solution.py:411
  21.4 2.1 %collective-permute-done.5.got_ref = s16[32,4224]{1,0:T(8,128)(2,1)S(1)} collective-permute-done((s16[32,4224]{1,0:T(8,128)(2,1)S(1)}, s16[32,4224]{1,0:T(8,128)(2,1)S(1)}, u32[]{:S(2)}, u32[]{:S(2)}) %collective-permute-start.5) | collective-permute-done | bytes 270368 | tf_op jit(solution)/shard_map/ppermute | solution.py:411
  23.5 0.5 combine.8
  24.1 1.6 %collective-permute-start.12 = (bf16[16,384]{1,0:T(8,128)(2,1)S(1)}, bf16[16,384]{1,0:T(8,128)(2,1)S(1)}, u32[]{:S(2)}, u32[]{:S(2)}) collective-permute-start(bf16[16,384]{1,0:T(8,128)(2,1)S(1)} %pad_maximum_fusion.2), channel_id=1, source_target_pairs={{0,4},{1,5},{2,6},{3,7},{4,0},{5,1},{6,2},{7,3},{8,12},{9,13},{10,... | collective-permute-start | bytes 36872 | tf_op jit(solution)/shard_map/ppermute | solution.py:411
  25.7 2.1 %collective-permute-done.12 = bf16[16,384]{1,0:T(8,128)(2,1)S(1)} collective-permute-done((bf16[16,384]{1,0:T(8,128)(2,1)S(1)}, bf16[16,384]{1,0:T(8,128)(2,1)S(1)}, u32[]{:S(2)}, u32[]{:S(2)}) %collective-permute-start.12) | collective-permute-done | bytes 12320 | tf_op jit(solution)/shard_map/ppermute | solution.py:411
  27.8 2.6 %collective-permute-start.13 = (bf16[32,384]{1,0:T(8,128)(2,1)S(1)}, bf16[32,384]{1,0:T(8,128)(2,1)S(1)}, u32[]{:S(2)}, u32[]{:S(2)}) collective-permute-start(bf16[32,384]{1,0:T(8,128)(2,1)S(1)} %pad_maximum_fusion.1), channel_id=1, source_target_pairs={{0,8},{1,9},{2,10},{3,11},{4,12},{5,13},{6,14},{7,15},{8,0},{9,1},... | collective-permute-start | bytes 73736 | tf_op jit(solution)/shard_map/ppermute | solution.py:411
  30.4 0.5 combine.6
  31.0 1.6 %collective-permute-start.3 = (s16[16,4480]{1,0:T(8,128)(2,1)S(1)}, s16[16,4480]{1,0:T(8,128)(2,1)S(1)}, u32[]{:S(2)}, u32[]{:S(2)}) collective-permute-start(s16[16,4480]{1,0:T(8,128)(2,1)S(1)} %get-tuple-element.52), channel_id=1, source_target_pairs={{0,4},{1,5},{2,6},{3,7},{4,0},{5,1},{6,2},{7,3},{8,12},{9,13},{10,... | collective-permute-start | bytes 430088 | tf_op jit(solution)/shard_map/ppermute | solution.py:411
  33.2 2.8 %collective-permute-start.11 = (s16[16,2176]{1,0:T(8,128)(2,1)S(1)}, s16[16,2176]{1,0:T(8,128)(2,1)S(1)}, u32[]{:S(2)}, u32[]{:S(2)}) collective-permute-start(s16[16,2176]{1,0:T(8,128)(2,1)S(1)} %get-tuple-element.67), channel_id=1, source_target_pairs={{0,8},{1,9},{2,10},{3,11},{4,12},{5,13},{6,14},{7,15},{8,0},{9,1},... | collective-permute-start | bytes 208904 | tf_op jit(solution)/shard_map/ppermute | solution.py:411
  36.6 0.6 %collective-permute-done.3.got_ref = s16[16,4480]{1,0:T(8,128)(2,1)S(1)} collective-permute-done((s16[16,4480]{1,0:T(8,128)(2,1)S(1)}, s16[16,4480]{1,0:T(8,128)(2,1)S(1)}, u32[]{:S(2)}, u32[]{:S(2)}) %collective-permute-start.3) | collective-permute-done | bytes 143392 | tf_op jit(solution)/shard_map/ppermute | solution.py:411
  37.6 2.2 %collective-permute-start.4 = (s16[16,2304]{1,0:T(8,128)(2,1)S(1)}, s16[16,2304]{1,0:T(8,128)(2,1)S(1)}, u32[]{:S(2)}, u32[]{:S(2)}) collective-permute-start(s16[16,2304]{1,0:T(8,128)(2,1)S(1)} %get-tuple-element.54), channel_id=1, source_target_pairs={{0,8},{1,9},{2,10},{3,11},{4,12},{5,13},{6,14},{7,15},{8,0},{9,1},... | collective-permute-start | bytes 221192 | tf_op jit(solution)/shard_map/ppermute | solution.py:411
  39.9 1.4 %collective-permute-done.11.key_got_ref = s16[16,2176]{1,0:T(8,128)(2,1)S(1)} collective-permute-done((s16[16,2176]{1,0:T(8,128)(2,1)S(1)}, s16[16,2176]{1,0:T(8,128)(2,1)S(1)}, u32[]{:S(2)}, u32[]{:S(2)}) %collective-permute-start.11) | collective-permute-done | bytes 69664 | tf_op jit(solution)/shard_map/ppermute | solution.py:411
  41.3 1.5 %collective-permute-done.8.query_got_ref = s16[16,2176]{1,0:T(8,128)(2,1)S(1)} collective-permute-done((s16[16,2176]{1,0:T(8,128)(2,1)S(1)}, s16[16,2176]{1,0:T(8,128)(2,1)S(1)}, u32[]{:S(2)}, u32[]{:S(2)}) %collective-permute-start.8) | collective-permute-done | bytes 69664 | tf_op jit(solution)/shard_map/ppermute | solution.py:411
  42.8 2.8 %keys_part.1 = (f32[32,8,128]{2,1,0:T(8,128)S(1)}, f32[32,8,128]{2,1,0:T(8,128)S(1)}, f32[3,32,8,128]{3,2,1,0:T(8,128)S(1)}, f32[4,32,8,128]{3,2,1,0:T(8,128)S(1)}, f32[32,4,384]{2,1,0:T(4,128)S(1)}) custom-call(s32[1]{0:T(128)} %bitcast.me_ref.twist_ref, f32[8,4096]{1,0:T(8,128)S(1)} %get-tuple-element.61.query_ref, ...), custom_call_target="tpu_custom_call" | custom-call | flops 40000000 | bytes 9000000 | tf_op jit(solution)/shard_map/keys_part/pallas_call | solution.py:243
  45.6 1.9 %values_part.1 = bf16[16,16,128]{2,1,0:T(8,128)(2,1)} custom-call(s32[64]{0:T(128)S(1)} %select_reduce_fusion.slots_ref, s32[64]{0:T(128)S(1)} %get-tuple-element.81.halves_ref, s32[2]{0:T(128)S(1)} %fusion.4.lengths_ref, s32[1]{0:T(128)} %bitcast.me_ref.twist_ref, f32[8,4352]{1,0:T(8,128)S(1)} %get-tuple-element.53.value_ref, ...), custom_call_target="tpu_custom_call" | custom-call | flops 4000000 | bytes 2000000 | tf_op jit(solution)/shard_map/values_part/pallas_call | solution.py:256
  47.6 4.5 %all-to-all-start = ((bf16[16,16,128]{2,1,0:T(8,128)(2,1)}), bf16[16,16,128]{2,1,0:T(8,128)(2,1)S(1)}, u32[]{:S(2)}, u32[]{:S(2)}) async-start(bf16[16,16,128]{2,1,0:T(8,128)(2,1)} %values_part.1), calls=%async_computation | async-start | bytes 131072 | tf_op jit(solution)/shard_map/all_to_all | solution.py:499
  52.2 6.7 %all-to-all-done = bf16[16,16,128]{2,1,0:T(8,128)(2,1)S(1)} async-done(((bf16[16,16,128]{2,1,0:T(8,128)(2,1)}), bf16[16,16,128]{2,1,0:T(8,128)(2,1)S(1)}, u32[]{:S(2)}, u32[]{:S(2)}) %all-to-all-start) | async-done | bytes 65568 | tf_op jit(solution)/shard_map/all_to_all | solution.py:499
  59.1 0.7 %reshape.46 = bf16[32,4,256]{2,1,0:T(4,128)(2,1)} reshape(bf16[128,256]{1,0:T(8,128)(2,1)S(1)} %convolution_convert_fusion) | data formatting | bytes 131072 | tf_op jit(solution)/shard_map/reshape | solution.py:510
  (57 shorter events, 4.0 us)
Async XLA Ops:
  0.0 7.9 %collective-permute-start = (bf16[144,12288]{1,0:T(8,128)(2,1)}, bf16[144,12288]{1,0:T(8,128)(2,1)S(1)}, u32[]{:S(2)}, u32[]{:S(2)}) collective-permute-start(bf16[144,12288]{1,0:T(8,128)(2,1)} %weight_hbm.1), channel_id=1, source_target_pairs={{0,1},{1,0},{2,3},{3,2},{4,5},{5,4},{6,7},{7,6},{8,9},{9,8},{10,11... | collective-permute-start | bytes 10616840 | tf_op jit(solution)/shard_map/ppermute | solution.py:411
  1.2 22.9 %collective-permute-start.6 = (bf16[8,384]{1,0:T(8,128)(2,1)S(1)}, bf16[8,384]{1,0:T(8,128)(2,1)S(1)}, u32[]{:S(2)}, u32[]{:S(2)}) collective-permute-start(bf16[8,384]{1,0:T(8,128)(2,1)S(1)} %pad_maximum_fusion.3), channel_id=1, source_target_pairs={{0,1},{1,0},{2,3},{3,2},{4,5},{5,4},{6,7},{7,6},{8,9},{9,8},{10,11... | collective-permute-start | bytes 18440 | tf_op jit(solution)/shard_map/ppermute | solution.py:411
  1.3 10.2 %collective-permute-start.1 = (bf16[64,144]{1,0:T(8,128)(2,1)}, bf16[64,144]{1,0:T(8,128)(2,1)}, u32[]{:S(2)}, u32[]{:S(2)}) collective-permute-start(bf16[64,144]{1,0:T(8,128)(2,1)} %bitcast.12), channel_id=1, source_target_pairs={{0,1},{1,0},{2,3},{3,2},{4,5},{5,4},{6,7},{7,6},{8,9},{9,8},{10,11... | collective-permute-start | bytes 55304 | tf_op jit(solution)/shard_map/ppermute | solution.py:411
  3.0 2.0 %copy-start.1 = (bf16[144,12288]{1,0:T(8,128)(2,1)S(1)}, bf16[144,12288]{1,0:T(8,128)(2,1)}, u32[]{:S(2)}) copy-start(bf16[144,12288]{1,0:T(8,128)(2,1)} %weight_hbm.1) | copy-start | bytes 10616836
  5.0 1.1 %copy-start.2 = (bf16[32,4,2304]{2,1,0:T(4,128)(2,1)S(1)}, bf16[32,4,2304]{2,1,0:T(4,128)(2,1)}, u32[]{:S(2)}) copy-start(bf16[32,4,2304]{2,1,0:T(4,128)(2,1)} %tokens_hbm.1) | copy-start | bytes 1769476
  6.0 0.7 %copy-start.4 = (s32[32]{0:T(128)S(1)}, s32[32]{0:T(128)}, u32[]{:S(2)}) copy-start(s32[32]{0:T(128)} %param.18) | copy-start | bytes 388
  7.9 3.5 %copy-start.3 = (bf16[144,64]{0,1:T(8,128)(2,1)S(1)}, bf16[144,64]{0,1:T(8,128)(2,1)}, u32[]{:S(2)}) copy-start(bf16[144,64]{0,1:T(8,128)(2,1)} %param.12) | copy-start | bytes 55300
  8.8 10.0 %collective-permute-start.9 = (s16[32,4224]{1,0:T(8,128)(2,1)S(1)}, s16[32,4224]{1,0:T(8,128)(2,1)S(1)}, u32[]{:S(2)}, u32[]{:S(2)}) collective-permute-start(s16[32,4224]{1,0:T(8,128)(2,1)S(1)} %get-tuple-element.63), channel_id=1, source_target_pairs={{0,2},{1,3},{2,0},{3,1},{4,6},{5,7},{6,4},{7,5},{8,10},{9,11},{10,... | collective-permute-start | bytes 811016 | tf_op jit(solution)/shard_map/ppermute | solution.py:411
  11.5 1.8 %copy-start.9 = (s32[64]{0:T(128)S(1)}, s32[64]{0:T(128)}, u32[]{:S(2)}) copy-start(s32[64]{0:T(128)} %param.17) | copy-start | bytes 772
  13.2 3.0 %copy-start.6 = (f32[2,3,12288]{2,0,1:T(2,128)S(1)}, f32[2,3,12288]{2,0,1:T(2,128)}, u32[]{:S(2)}) copy-start(f32[2,3,12288]{2,0,1:T(2,128)} %param.15) | copy-start | bytes 884740
  13.2 3.5 %copy-start.5 = (s32[32]{0:T(128)S(1)}, s32[32]{0:T(128)}, u32[]{:S(2)}) copy-start(s32[32]{0:T(128)} %param.18) | copy-start | bytes 388
  13.3 3.5 %copy-start.8 = (s32[32]{0:T(128)S(1)}, s32[32]{0:T(128)}, u32[]{:S(2)}) copy-start(s32[32]{0:T(128)} %param.19) | copy-start | bytes 388
  13.3 3.7 %copy-start.10 = (s32[32]{0:T(128)S(1)}, s32[32]{0:T(128)}, u32[]{:S(2)}) copy-start(s32[32]{0:T(128)} %param.16) | copy-start | bytes 388
  14.1 28.7 %copy-start = (f32[2,32,128,128]{3,2,1,0:T(8,128)S(1)}, f32[2,32,128,128]{3,2,1,0:T(8,128)}, u32[]{:S(2)}) copy-start(f32[2,32,128,128]{3,2,1,0:T(8,128)} %state_hbm.1) | copy-start | bytes 12582916
  14.1 9.4 %collective-permute-start.5 = (s16[32,4224]{1,0:T(8,128)(2,1)S(1)}, s16[32,4224]{1,0:T(8,128)(2,1)S(1)}, u32[]{:S(2)}, u32[]{:S(2)}) collective-permute-start(s16[32,4224]{1,0:T(8,128)(2,1)S(1)} %get-tuple-element.57), channel_id=1, source_target_pairs={{0,4},{1,5},{2,6},{3,7},{4,0},{5,1},{6,2},{7,3},{8,12},{9,13},{10,... | collective-permute-start | bytes 811016 | tf_op jit(solution)/shard_map/ppermute | solution.py:411
  15.8 14.7 %collective-permute-start.2 = (s16[32,4480]{1,0:T(8,128)(2,1)S(1)}, s16[32,4480]{1,0:T(8,128)(2,1)S(1)}, u32[]{:S(2)}, u32[]{:S(2)}) collective-permute-start(s16[32,4480]{1,0:T(8,128)(2,1)S(1)} %get-tuple-element.50), channel_id=1, source_target_pairs={{0,2},{1,3},{2,0},{3,1},{4,6},{5,7},{6,4},{7,5},{8,10},{9,11},{10,... | collective-permute-start | bytes 860168 | tf_op jit(solution)/shard_map/ppermute | solution.py:411
  19.3 13.4 %collective-permute-start.10 = (s16[16,4224]{1,0:T(8,128)(2,1)S(1)}, s16[16,4224]{1,0:T(8,128)(2,1)S(1)}, u32[]{:S(2)}, u32[]{:S(2)}) collective-permute-start(s16[16,4224]{1,0:T(8,128)(2,1)S(1)} %get-tuple-element.65), channel_id=1, source_target_pairs={{0,4},{1,5},{2,6},{3,7},{4,0},{5,1},{6,2},{7,3},{8,12},{9,13},{10,... | collective-permute-start | bytes 405512 | tf_op jit(solution)/shard_map/ppermute | solution.py:411
  24.1 3.8 %collective-permute-start.12 = (bf16[16,384]{1,0:T(8,128)(2,1)S(1)}, bf16[16,384]{1,0:T(8,128)(2,1)S(1)}, u32[]{:S(2)}, u32[]{:S(2)}) collective-permute-start(bf16[16,384]{1,0:T(8,128)(2,1)S(1)} %pad_maximum_fusion.2), channel_id=1, source_target_pairs={{0,4},{1,5},{2,6},{3,7},{4,0},{5,1},{6,2},{7,3},{8,12},{9,13},{10,... | collective-permute-start | bytes 36872 | tf_op jit(solution)/shard_map/ppermute | solution.py:411
  25.7 10.2 %collective-permute-start.7 = (s16[16,4224]{1,0:T(8,128)(2,1)S(1)}, s16[16,4224]{1,0:T(8,128)(2,1)S(1)}, u32[]{:S(2)}, u32[]{:S(2)}) collective-permute-start(s16[16,4224]{1,0:T(8,128)(2,1)S(1)} %get-tuple-element.60), channel_id=1, source_target_pairs={{0,2},{1,3},{2,0},{3,1},{4,6},{5,7},{6,4},{7,5},{8,10},{9,11},{10,... | collective-permute-start | bytes 405512 | tf_op jit(solution)/shard_map/ppermute | solution.py:411
  27.8 4.8 %collective-permute-start.13 = (bf16[32,384]{1,0:T(8,128)(2,1)S(1)}, bf16[32,384]{1,0:T(8,128)(2,1)S(1)}, u32[]{:S(2)}, u32[]{:S(2)}) collective-permute-start(bf16[32,384]{1,0:T(8,128)(2,1)S(1)} %pad_maximum_fusion.1), channel_id=1, source_target_pairs={{0,8},{1,9},{2,10},{3,11},{4,12},{5,13},{6,14},{7,15},{8,0},{9,1},... | collective-permute-start | bytes 73736 | tf_op jit(solution)/shard_map/ppermute | solution.py:411
  31.0 6.2 %collective-permute-start.3 = (s16[16,4480]{1,0:T(8,128)(2,1)S(1)}, s16[16,4480]{1,0:T(8,128)(2,1)S(1)}, u32[]{:S(2)}, u32[]{:S(2)}) collective-permute-start(s16[16,4480]{1,0:T(8,128)(2,1)S(1)} %get-tuple-element.52), channel_id=1, source_target_pairs={{0,4},{1,5},{2,6},{3,7},{4,0},{5,1},{6,2},{7,3},{8,12},{9,13},{10,... | collective-permute-start | bytes 430088 | tf_op jit(solution)/shard_map/ppermute | solution.py:411
  32.7 7.2 %collective-permute-start.14 = (bf16[64,384]{1,0:T(8,128)(2,1)S(1)}, bf16[64,384]{1,0:T(8,128)(2,1)S(1)}, u32[]{:S(2)}, u32[]{:S(2)}) collective-permute-start(bf16[64,384]{1,0:T(8,128)(2,1)S(1)} %constant_dynamic-update-slice_fusion.near_ref), channel_id=1, source_target_pairs={{0,2},{1,3},{2,0},{3,1},{4,6},{5,7},{6,4},{7,5},{8,10},{9,11},{10,... | collective-permute-start | bytes 147464 | tf_op jit(solution)/shard_map/ppermute | solution.py:411
  33.2 8.1 %collective-permute-start.11 = (s16[16,2176]{1,0:T(8,128)(2,1)S(1)}, s16[16,2176]{1,0:T(8,128)(2,1)S(1)}, u32[]{:S(2)}, u32[]{:S(2)}) collective-permute-start(s16[16,2176]{1,0:T(8,128)(2,1)S(1)} %get-tuple-element.67), channel_id=1, source_target_pairs={{0,8},{1,9},{2,10},{3,11},{4,12},{5,13},{6,14},{7,15},{8,0},{9,1},... | collective-permute-start | bytes 208904 | tf_op jit(solution)/shard_map/ppermute | solution.py:411
  36.3 6.4 %collective-permute-start.8 = (s16[16,2176]{1,0:T(8,128)(2,1)S(1)}, s16[16,2176]{1,0:T(8,128)(2,1)S(1)}, u32[]{:S(2)}, u32[]{:S(2)}) collective-permute-start(s16[16,2176]{1,0:T(8,128)(2,1)S(1)} %get-tuple-element.62), channel_id=1, source_target_pairs={{0,8},{1,9},{2,10},{3,11},{4,12},{5,13},{6,14},{7,15},{8,0},{9,1},... | collective-permute-start | bytes 208904 | tf_op jit(solution)/shard_map/ppermute | solution.py:411
  37.6 8.0 %collective-permute-start.4 = (s16[16,2304]{1,0:T(8,128)(2,1)S(1)}, s16[16,2304]{1,0:T(8,128)(2,1)S(1)}, u32[]{:S(2)}, u32[]{:S(2)}) collective-permute-start(s16[16,2304]{1,0:T(8,128)(2,1)S(1)} %get-tuple-element.54), channel_id=1, source_target_pairs={{0,8},{1,9},{2,10},{3,11},{4,12},{5,13},{6,14},{7,15},{8,0},{9,1},... | collective-permute-start | bytes 221192 | tf_op jit(solution)/shard_map/ppermute | solution.py:411
  42.8 9.2 %copy-start.7 = (s32[32]{0:T(128)S(1)}, s32[32]{0:T(128)}, u32[]{:S(2)}) copy-start(s32[32]{0:T(128)} %broadcast_multiply_fusion) | copy-start | bytes 388
  47.6 11.4 %all-to-all-start = ((bf16[16,16,128]{2,1,0:T(8,128)(2,1)}), bf16[16,16,128]{2,1,0:T(8,128)(2,1)S(1)}, u32[]{:S(2)}, u32[]{:S(2)}) async-start(bf16[16,16,128]{2,1,0:T(8,128)(2,1)} %values_part.1), calls=%async_computation | async-start | bytes 131072 | tf_op jit(solution)/shard_map/all_to_all | solution.py:499

commit v6 on v5

--- a/solution.py
+++ b/solution.py
@@ -375,7 +375,8 @@
     )(*earlier, mine, theirs, *weights, *gates)
 
 
-def combine_kernel(kept_ref, got_ref, still_ref, packed_ref):
+def combine_kernel(kept_ref, got_ref, *refs):
+    still_ref, packed_ref = refs[-2:]
     half = still_ref.shape[0]
     steps = steps_of(got_ref)
     sent = []
@@ -388,7 +389,7 @@
     pack_rows(fold_rows(sent) if half == ROWS else sent, packed_ref)
 
 
-def run_combine(kept, got):
+def run_combine(kept, got, earlier):
     vmem = pl.BlockSpec(memory_space=pltpu.VMEM)
     half, width = kept.shape[0] // 2, kept.shape[1]
     rows, packed = (2 * ROWS, width // 2) if half == ROWS else (half, width)
@@ -399,12 +400,12 @@
             jax.ShapeDtypeStruct((half, width), jnp.float32),
             jax.ShapeDtypeStruct(packed, jnp.int16),
         ],
-        in_specs=[vmem] * 2,
+        in_specs=[vmem] * 2 + [pl.BlockSpec(memory_space=pl.ANY)] * len(earlier),
         out_specs=[vmem] * 2,
         compiler_params=pltpu.CompilerParams(vmem_limit_bytes=32 * 1024 * 1024),
         cost_estimate=pl.CostEstimate(flops=0, bytes_accessed=0, transcendentals=0),
         name="combine",
-    )(kept, got)
+    )(kept, got, *earlier)
 
 
 def swap(value, bit, devices):
@@ -430,8 +431,6 @@
     chips = devices // 2
 
     bits = [1 << b for b in range(1, devices.bit_length() - 1)]
-    steps = jnp.arange(STEPS, dtype=jnp.int32)
-    offered = (slot_of[:, None] * STEPS + steps[None, :]).reshape(-1)
 
     mine, theirs, near_weight = run_rows(me, slot_of, tokens, qkv_weight, chips)
 
@@ -443,8 +442,10 @@
 
     ride = conv_weight.shape[1] == 2 * TAP_WIDTH and len(bits) == 3
     if ride:
-        taps = jnp.concatenate([conv_weight[:, :TAP_WIDTH], conv_weight[:, TAP_WIDTH:]], axis=0)
-        far = swap(taps, 1, devices)
+        taps = jnp.concatenate([conv_weight, swap(conv_weight, 1, devices)], axis=1)
+        blocks = range(0, taps.shape[1], TAP_WIDTH)
+        taps = jnp.concatenate([taps[:, at : at + TAP_WIDTH] for at in blocks], axis=0)
+        taps = jnp.concatenate([taps, swap(taps, 4, devices)], axis=0)
     else:
         taps = lax.all_gather(conv_weight, "heads", axis=1, tiled=True)
         blocks = [block for bit in (0, 4) for block in range(TAP_BLOCKS) if block & 4 == bit]
@@ -452,11 +453,13 @@
         taps = jnp.concatenate(taps, axis=0)
     keys = run_product(mine, theirs, weights, 1)
     values = run_product(mine, theirs, weights, 2, gates, earlier=keys[:1])
-    queries = run_product(mine, theirs, weights, 0, earlier=values[:1], crossed=True)
-
-    lengths, old_heads, new_units, carried, *values = tie(
-        lengths, old_heads, new_units, conv_state, *values
-    )
+    queries = run_product(mine, theirs, weights, 0, earlier=(values[0], taps), crossed=True)
+
+    slot_of, lengths, old_heads, new_units, carried, *values = tie(
+        slot_of, lengths, old_heads, new_units, conv_state, *values
+    )
+    steps = jnp.arange(STEPS, dtype=jnp.int32)
+    offered = (slot_of[:, None] * STEPS + steps[None, :]).reshape(-1)
     old_slots, halves = unit_tables(old_heads, new_units)
     my_rows = me * LOCAL + jnp.arange(LOCAL, dtype=jnp.int32)
     my_lengths = jnp.sum(
@@ -472,14 +475,12 @@
     ]
     for level in range(1, len(bits)):
         for at in range(3):
-            kept[at], packed = run_combine(kept[at], got[at])
+            if ride and level == 1 and at == 0:
+                taps = jnp.concatenate([taps, swap(taps, 8, devices)], axis=0)
+            earlier = (taps,) if level == 1 and at == 0 else ()
+            kept[at], packed = run_combine(kept[at], got[at], earlier)
             got[at] = swap(packed, routes[at][level], devices)
-            if ride and level == 1 and at == 0:
-                kept[0], taps, far = tie(kept[0], taps, far)
-                taps = jnp.concatenate([taps, far], axis=0)
-                taps = jnp.concatenate([taps, swap(taps, 4, devices)], axis=0)
     if ride:
-        taps = jnp.concatenate([taps, swap(taps, 8, devices)], axis=0)
         twist, taps = me.reshape(1), (taps, swap(taps, 2, devices))
     else:
         half = TAP_BLOCKS // 2 * TAPS

time: 60.2 us -> 78.1 us (1.30)
  local copies, waits for them, and re-layouts: 5.57 us -> 18.4 us
  waiting for transfers between devices: 16.2 us -> 20.4 us
    unnamed x25 -> x40, local copies, waits for them, and re-layouts: 3.78 us -> 10.2 us
    ppermute x15, waiting for transfers between devices: 9.47 us -> 13.7 us  [swap(): return lax.ppermute(value, 'heads', [(i, i ^ bit) for i in range(devices)])]
    concatenate x1, local copies, waits for them, and re-layouts: 0.01 us -> 3.88 us  [on_device(): taps = jnp.concatenate([taps, swap(taps, 8, devices)], axis=0)]
    concatenate x0 -> x1, local copies, waits for them, and re-layouts: none -> 2.53 us  [on_device(): taps = jnp.concatenate([taps, swap(taps, 4, devices)], axis=0)]
    ppermute x15, starting transfers between devices: 19 us -> 20.6 us  [swap(): return lax.ppermute(value, 'heads', [(i, i ^ bit) for i in range(devices)])]
    mul x1, other arithmetic: 1.23 us -> 0.01 us  [on_device(): offered = (slot_of[:, None] * STEPS + steps[None, :]).reshape(-1)]
    all_to_all x1, starting transfers between devices: 4.46 us -> 3.5 us  [on_device(): lax.all_to_all(sending, 'heads', split_axis=0, concat_axis=0, tiled=True)]
  transfers between devices with their start and end apart: 16 -> 16, of which waited for: 7 -> 8; matrix products, arithmetic and copies ran while one was open for 5% -> 12% of each run, Pallas kernels for 17% -> 13%
where the time goes in v6:
time: 78.1 us; the launch traced here: 77.4 us
  starting transfers between devices  24.1 us (31%)
  waiting for transfers between devices  20.4 us (26%)
  local copies, waits for them, and re-layouts  18.4 us (24%)
  Pallas kernels  12.2 us (16%)
  other arithmetic  1.85 us (2%)
    ppermute x15, starting transfers between devices, swap(): return lax.ppermute(value, 'heads', [(i, i ^ bit) for i in range(devices)])  20.6 us
    ppermute x15, waiting for transfers between devices, swap(): return lax.ppermute(value, 'heads', [(i, i ^ bit) for i in range(devices)])  13.7 us
    unnamed x40, local copies, waits for them, and re-layouts  10.2 us
    all_to_all x1, waiting for transfers between devices, on_device(): lax.all_to_all(sending, 'heads', split_axis=0, concat_axis=0, tiled=True)  6.68 us
    concatenate x1, local copies, waits for them, and re-layouts, on_device(): taps = jnp.concatenate([taps, swap(taps, 8, devices)], axis=0)  3.88 us
    all_to_all x1, starting transfers between devices, on_device(): lax.all_to_all(sending, 'heads', split_axis=0, concat_axis=0, tiled=True)  3.5 us
    pallas_call x3, Pallas kernels, run_product(): pl.pallas_call(functools.partial(product_kernel, len(earlier), crossed),...  3.38 us
    pallas_call x1, Pallas kernels, run_delta(): pl.pallas_call(keys_kernel, out_shape=[per_head] * 2 + lags + [tap_blocks...  2.81 us
  transfers between devices with their start and end apart: 16, of which 8 were waited for; matrix products, arithmetic and copies ran while one was open for 12% of the time, Pallas kernels for 13%

profile of v6, /device:TPU:0, one launch (start us, length us, event | category | flops | bytes accessed | tf_op | source)
XLA Modules:
  0.0 77.4 jit_solution(18410101776607072623)
XLA Ops:
  0.5 0.7 fusion.7
  1.2 5.3 %collective-permute-done.5 = bf16[4,768]{1,0:T(4,128)(2,1)S(1)} collective-permute-done((bf16[4,768]{1,0:T(4,128)(2,1)}, bf16[4,768]{1,0:T(4,128)(2,1)S(1)}, u32[]{:S(2)}, u32[]{:S(2)}) %collective-permute-start.5) | collective-permute-done | bytes 6176 | tf_op jit(solution)/shard_map/ppermute | solution.py:412
  7.1 2.9 %collective-permute-start.6 = (bf16[16,384]{1,0:T(8,128)(2,1)}, bf16[16,384]{1,0:T(8,128)(2,1)}, u32[]{:S(2)}, u32[]{:S(2)}) collective-permute-start(bf16[16,384]{1,0:T(8,128)(2,1)} %pad_maximum_fusion.1), channel_id=1, source_target_pairs={{0,4},{1,5},{2,6},{3,7},{4,0},{5,1},{6,2},{7,3},{8,12},{9,13},{10,... | collective-permute-start | bytes 36872 | tf_op jit(solution)/shard_map/ppermute | solution.py:412
  10.1 2.0 %collective-permute-done.6 = bf16[16,384]{1,0:T(8,128)(2,1)} collective-permute-done((bf16[16,384]{1,0:T(8,128)(2,1)}, bf16[16,384]{1,0:T(8,128)(2,1)}, u32[]{:S(2)}, u32[]{:S(2)}) %collective-permute-start.6) | collective-permute-done | bytes 12320 | tf_op jit(solution)/shard_map/ppermute | solution.py:412
  12.1 2.5 %concatenate.24.refs_1_ = bf16[32,384]{1,0:T(8,128)(2,1)} concatenate(bf16[4,384]{1,0:T(4,128)(2,1)S(1)} %get-tuple-element.78, bf16[4,384]{1,0:T(4,128)(2,1)S(1)} %get-tuple-element.77, bf16[4,384]{1,0:T(4,128)(2,1)S(1)} %get-tuple-element.76, bf16[4,384]{1,0:T(4,128)(2,1)S(1)} %get-tuple-element.75, bf16[16,384]{1,0:T(8,128)(2,1)} %collective-permute-done.6), dimensions={0} | concatenate | bytes 49152 | tf_op jit(solution)/shard_map/concatenate | solution.py:448
  14.6 3.0 %collective-permute-start.8 = (bf16[32,384]{1,0:T(8,128)(2,1)}, bf16[32,384]{1,0:T(8,128)(2,1)}, u32[]{:S(2)}, u32[]{:S(2)}) collective-permute-start(bf16[32,384]{1,0:T(8,128)(2,1)} %concatenate.24.refs_1_), channel_id=1, source_target_pairs={{0,8},{1,9},{2,10},{3,11},{4,12},{5,13},{6,14},{7,15},{8,0},{9,1},... | collective-permute-start | bytes 73736 | tf_op jit(solution)/shard_map/ppermute | solution.py:412
  18.2 2.0 %copy-done.3 = bf16[144,12288]{1,0:T(8,128)(2,1)S(1)} copy-done((bf16[144,12288]{1,0:T(8,128)(2,1)S(1)}, bf16[144,12288]{1,0:T(8,128)(2,1)}, u32[]{:S(2)}) %copy-start.3) | copy-done | bytes 3538968
  20.2 1.1 %copy-done.4 = bf16[32,4,2304]{2,1,0:T(4,128)(2,1)S(1)} copy-done((bf16[32,4,2304]{2,1,0:T(4,128)(2,1)S(1)}, bf16[32,4,2304]{2,1,0:T(4,128)(2,1)}, u32[]{:S(2)}) %copy-start.4) | copy-done | bytes 589848
  22.0 1.2 %token_rows.1 = (bf16[64,144]{1,0:T(8,128)(2,1)S(1)}, bf16[64,144]{1,0:T(8,128)(2,1)S(1)}, bf16[144,12288]{1,0:T(8,128)(2,1)S(1)}) custom-call(s32[1]{0:T(128)} %bitcast.me_ref.twist_ref, s32[1,32]{1,0:T(1,128)S(1)} %bitcast.14, bf16[32,4,2304]{2,1,0:T(4,128)(2,1)S(1)} %copy-done.4, bf16[144,12288]{1,0:T(8,128)(2,1)S(1)} %copy-done.3), custom_call_target="tpu_custom_call" | custom-call | tf_op jit(solution)/shard_map/token_rows/pallas_call | solution.py:310
  23.2 1.7 %copy-done = bf16[144,12288]{1,0:T(8,128)(2,1)} copy-done((bf16[144,12288]{1,0:T(8,128)(2,1)}, bf16[144,12288]{1,0:T(8,128)(2,1)S(1)}, u32[]{:S(2)}) %copy-start) | copy-done | bytes 3538968
  26.2 3.9 %concatenate.25.refs_0_.near_ref = bf16[64,384]{1,0:T(8,128)(2,1)} concatenate(bf16[4,384]{1,0:T(4,128)(2,1)S(1)} %get-tuple-element.78, bf16[4,384]{1,0:T(4,128)(2,1)S(1)} %get-tuple-element.77, bf16[4,384]{1,0:T(4,128)(2,1)S(1)} %get-tuple-element.76, bf16[4,384]{1,0:T(4,128)(2,1)S(1)} %get-tuple-element.75, bf16[16,384]{1,0:T(8,128)(2,1)} %collective-permute-done.6, ...), dimensions={0} | concatenate | bytes 98304 | tf_op jit(solution)/shard_map/concatenate | solution.py:479
  30.0 1.5 %collective-permute-start.14 = (bf16[64,384]{1,0:T(8,128)(2,1)}, bf16[64,384]{1,0:T(8,128)(2,1)S(1)}, u32[]{:S(2)}, u32[]{:S(2)}) collective-permute-start(bf16[64,384]{1,0:T(8,128)(2,1)} %concatenate.25.refs_0_.near_ref), channel_id=1, source_target_pairs={{0,2},{1,3},{2,0},{3,1},{4,6},{5,7},{6,4},{7,5},{8,10},{9,11},{10,... | collective-permute-start | bytes 147464 | tf_op jit(solution)/shard_map/ppermute | solution.py:412
  31.6 2.0 %copy-done.1 = bf16[144,12288]{1,0:T(8,128)(2,1)S(1)} copy-done((bf16[144,12288]{1,0:T(8,128)(2,1)S(1)}, bf16[144,12288]{1,0:T(8,128)(2,1)}, u32[]{:S(2)}) %copy-start.1) | copy-done | bytes 3538968
  33.6 0.8 copy-done.7
  34.3 0.8 copy-done.10
  35.1 0.8 %partial_product.3 = (f32[32,4096]{1,0:T(8,128)S(1)}, s16[32,4224]{1,0:T(8,128)(2,1)S(1)}) custom-call(bf16[64,144]{1,0:T(8,128)(2,1)S(1)} %copy-done.7, bf16[64,144]{1,0:T(8,128)(2,1)S(1)} %copy-done.10, bf16[144,12288]{1,0:T(8,128)(2,1)S(1)} %copy-done.1, bf16[144,12288]{1,0:T(8,128)(2,1)S(1)} %collective-permute-done.refs_3_.refs_4_.refs_5_), custom_call_target="tpu_custom_call" | custom-call | tf_op jit(solution)/shard_map/partial_product/pallas_call | solution.py:361
  36.5 1.7 %partial_product.4 = (f32[32,4352]{1,0:T(8,128)S(1)}, s16[32,4480]{1,0:T(8,128)(2,1)S(1)}) custom-call(f32[32,4096]{1,0:T(8,128)S(1)} %get-tuple-element.41.refs_0_.kept_ref, bf16[64,144]{1,0:T(8,128)(2,1)S(1)} %copy-done.8, bf16[64,144]{1,0:T(8,128)(2,1)S(1)} %copy-done.10, bf16[144,12288]{1,0:T(8,128)(2,1)S(1)} %copy-done.1, ...), custom_call_target="tpu_custom_call" | custom-call | tf_op jit(solution)/shard_map/partial_product/pallas_call | solution.py:361
  38.3 0.8 %partial_product.5 = (f32[32,4096]{1,0:T(8,128)S(1)}, s16[32,4224]{1,0:T(8,128)(2,1)S(1)}) custom-call(f32[32,4352]{1,0:T(8,128)S(1)} %get-tuple-element.48.kept_ref.refs_0_, bf16[32,384]{1,0:T(8,128)(2,1)S(1)} %copy-done.11, bf16[64,144]{1,0:T(8,128)(2,1)S(1)} %copy-done.8, bf16[64,144]{1,0:T(8,128)(2,1)S(1)} %copy-done.10, ...), custom_call_target="tpu_custom_call" | custom-call | tf_op jit(solution)/shard_map/partial_product/pallas_call | solution.py:361
  39.2 1.6 %collective-permute-start.7 = (s16[32,4224]{1,0:T(8,128)(2,1)S(1)}, s16[32,4224]{1,0:T(8,128)(2,1)S(1)}, u32[]{:S(2)}, u32[]{:S(2)}) collective-permute-start(s16[32,4224]{1,0:T(8,128)(2,1)S(1)} %get-tuple-element.56), channel_id=1, source_target_pairs={{0,4},{1,5},{2,6},{3,7},{4,0},{5,1},{6,2},{7,3},{8,12},{9,13},{10,... | collective-permute-start | bytes 811016 | tf_op jit(solution)/shard_map/ppermute | solution.py:412
  40.8 1.5 %collective-permute-start.2 = (s16[32,4480]{1,0:T(8,128)(2,1)S(1)}, s16[32,4480]{1,0:T(8,128)(2,1)S(1)}, u32[]{:S(2)}, u32[]{:S(2)}) collective-permute-start(s16[32,4480]{1,0:T(8,128)(2,1)S(1)} %get-tuple-element.49), channel_id=1, source_target_pairs={{0,2},{1,3},{2,0},{3,1},{4,6},{5,7},{6,4},{7,5},{8,10},{9,11},{10,... | collective-permute-start | bytes 860168 | tf_op jit(solution)/shard_map/ppermute | solution.py:412
  42.9 1.3 %collective-permute-done.11.got_ref = s16[32,4224]{1,0:T(8,128)(2,1)S(1)} collective-permute-done((s16[32,4224]{1,0:T(8,128)(2,1)S(1)}, s16[32,4224]{1,0:T(8,128)(2,1)S(1)}, u32[]{:S(2)}, u32[]{:S(2)}) %collective-permute-start.11) | collective-permute-done | bytes 270368 | tf_op jit(solution)/shard_map/ppermute | solution.py:412
  44.8 2.8 %collective-permute-start.12 = (s16[16,4224]{1,0:T(8,128)(2,1)S(1)}, s16[16,4224]{1,0:T(8,128)(2,1)S(1)}, u32[]{:S(2)}, u32[]{:S(2)}) collective-permute-start(s16[16,4224]{1,0:T(8,128)(2,1)S(1)} %get-tuple-element.63), channel_id=1, source_target_pairs={{0,4},{1,5},{2,6},{3,7},{4,0},{5,1},{6,2},{7,3},{8,12},{9,13},{10,... | collective-permute-start | bytes 405512 | tf_op jit(solution)/shard_map/ppermute | solution.py:412
  48.1 1.3 %collective-permute-start.9 = (s16[16,4224]{1,0:T(8,128)(2,1)S(1)}, s16[16,4224]{1,0:T(8,128)(2,1)S(1)}, u32[]{:S(2)}, u32[]{:S(2)}) collective-permute-start(s16[16,4224]{1,0:T(8,128)(2,1)S(1)} %get-tuple-element.58), channel_id=1, source_target_pairs={{0,2},{1,3},{2,0},{3,1},{4,6},{5,7},{6,4},{7,5},{8,10},{9,11},{10,... | collective-permute-start | bytes 405512 | tf_op jit(solution)/shard_map/ppermute | solution.py:412
  49.4 1.0 %collective-permute-done.2.got_ref = s16[32,4480]{1,0:T(8,128)(2,1)S(1)} collective-permute-done((s16[32,4480]{1,0:T(8,128)(2,1)S(1)}, s16[32,4480]{1,0:T(8,128)(2,1)S(1)}, u32[]{:S(2)}, u32[]{:S(2)}) %collective-permute-start.2) | collective-permute-done | bytes 286752 | tf_op jit(solution)/shard_map/ppermute | solution.py:412
  50.9 1.6 %collective-permute-start.3 = (s16[16,4480]{1,0:T(8,128)(2,1)S(1)}, s16[16,4480]{1,0:T(8,128)(2,1)S(1)}, u32[]{:S(2)}, u32[]{:S(2)}) collective-permute-start(s16[16,4480]{1,0:T(8,128)(2,1)S(1)} %get-tuple-element.51), channel_id=1, source_target_pairs={{0,4},{1,5},{2,6},{3,7},{4,0},{5,1},{6,2},{7,3},{8,12},{9,13},{10,... | collective-permute-start | bytes 430088 | tf_op jit(solution)/shard_map/ppermute | solution.py:412
  54.1 2.6 %collective-permute-start.10 = (s16[16,2176]{1,0:T(8,128)(2,1)S(1)}, s16[16,2176]{1,0:T(8,128)(2,1)S(1)}, u32[]{:S(2)}, u32[]{:S(2)}) collective-permute-start(s16[16,2176]{1,0:T(8,128)(2,1)S(1)} %get-tuple-element.60), channel_id=1, source_target_pairs={{0,8},{1,9},{2,10},{3,11},{4,12},{5,13},{6,14},{7,15},{8,0},{9,1},... | collective-permute-start | bytes 208904 | tf_op jit(solution)/shard_map/ppermute | solution.py:412
  58.1 2.6 %collective-permute-done.13.key_got_ref = s16[16,2176]{1,0:T(8,128)(2,1)S(1)} collective-permute-done((s16[16,2176]{1,0:T(8,128)(2,1)S(1)}, s16[16,2176]{1,0:T(8,128)(2,1)S(1)}, u32[]{:S(2)}, u32[]{:S(2)}) %collective-permute-start.13) | collective-permute-done | bytes 69664 | tf_op jit(solution)/shard_map/ppermute | solution.py:412
  60.7 0.7 collective-permute-done.10.query_got_ref
  61.4 2.8 %keys_part.1 = (f32[32,8,128]{2,1,0:T(8,128)S(1)}, f32[32,8,128]{2,1,0:T(8,128)S(1)}, f32[3,32,8,128]{3,2,1,0:T(8,128)S(1)}, f32[4,32,8,128]{3,2,1,0:T(8,128)S(1)}, f32[32,4,384]{2,1,0:T(4,128)S(1)}) custom-call(s32[1]{0:T(128)} %bitcast.me_ref.twist_ref, f32[8,4096]{1,0:T(8,128)S(1)} %get-tuple-element.59.query_ref, ...), custom_call_target="tpu_custom_call" | custom-call | flops 40000000 | bytes 9000000 | tf_op jit(solution)/shard_map/keys_part/pallas_call | solution.py:243
  64.3 1.9 %values_part.1 = bf16[16,16,128]{2,1,0:T(8,128)(2,1)} custom-call(s32[64]{0:T(128)S(1)} %select_reduce_fusion.slots_ref, s32[64]{0:T(128)S(1)} %get-tuple-element.79.halves_ref, s32[2]{0:T(128)S(1)} %fusion.4.lengths_ref, s32[1]{0:T(128)} %bitcast.me_ref.twist_ref, f32[8,4352]{1,0:T(8,128)S(1)} %get-tuple-element.52.value_ref, ...), custom_call_target="tpu_custom_call" | custom-call | flops 4000000 | bytes 2000000 | tf_op jit(solution)/shard_map/values_part/pallas_call | solution.py:256
  66.2 3.5 %all-to-all-start = ((bf16[16,16,128]{2,1,0:T(8,128)(2,1)}), bf16[16,16,128]{2,1,0:T(8,128)(2,1)S(1)}, u32[]{:S(2)}, u32[]{:S(2)}) async-start(bf16[16,16,128]{2,1,0:T(8,128)(2,1)} %values_part.1), calls=%async_computation | async-start | bytes 131072 | tf_op jit(solution)/shard_map/all_to_all | solution.py:500
  69.9 6.7 %all-to-all-done = bf16[16,16,128]{2,1,0:T(8,128)(2,1)S(1)} async-done(((bf16[16,16,128]{2,1,0:T(8,128)(2,1)}), bf16[16,16,128]{2,1,0:T(8,128)(2,1)S(1)}, u32[]{:S(2)}, u32[]{:S(2)}) %all-to-all-start) | async-done | bytes 65568 | tf_op jit(solution)/shard_map/all_to_all | solution.py:500
  (72 shorter events, 10.2 us)
Async XLA Ops:
  0.0 31.6 %collective-permute-start = (bf16[144,12288]{1,0:T(8,128)(2,1)}, bf16[144,12288]{1,0:T(8,128)(2,1)S(1)}, u32[]{:S(2)}, u32[]{:S(2)}) collective-permute-start(bf16[144,12288]{1,0:T(8,128)(2,1)} %weight_hbm.1), channel_id=1, source_target_pairs={{0,1},{1,0},{2,3},{3,2},{4,5},{5,4},{6,7},{7,6},{8,9},{9,8},{10,11... | collective-permute-start | bytes 10616840 | tf_op jit(solution)/shard_map/ppermute | solution.py:412
  0.5 6.1 %collective-permute-start.5 = (bf16[4,768]{1,0:T(4,128)(2,1)}, bf16[4,768]{1,0:T(4,128)(2,1)S(1)}, u32[]{:S(2)}, u32[]{:S(2)}) collective-permute-start(bf16[4,768]{1,0:T(4,128)(2,1)} %param.13), channel_id=1, source_target_pairs={{0,1},{1,0},{2,3},{3,2},{4,5},{5,4},{6,7},{7,6},{8,9},{9,8},{10,11... | collective-permute-start | bytes 18440 | tf_op jit(solution)/shard_map/ppermute | solution.py:412
  7.1 4.9 %collective-permute-start.6 = (bf16[16,384]{1,0:T(8,128)(2,1)}, bf16[16,384]{1,0:T(8,128)(2,1)}, u32[]{:S(2)}, u32[]{:S(2)}) collective-permute-start(bf16[16,384]{1,0:T(8,128)(2,1)} %pad_maximum_fusion.1), channel_id=1, source_target_pairs={{0,4},{1,5},{2,6},{3,7},{4,0},{5,1},{6,2},{7,3},{8,12},{9,13},{10,... | collective-permute-start | bytes 36872 | tf_op jit(solution)/shard_map/ppermute | solution.py:412
  10.1 26.4 %collective-permute-start.1 = (bf16[64,144]{1,0:T(8,128)(2,1)}, bf16[64,144]{1,0:T(8,128)(2,1)}, u32[]{:S(2)}, u32[]{:S(2)}) collective-permute-start(bf16[64,144]{1,0:T(8,128)(2,1)} %bitcast.12), channel_id=1, source_target_pairs={{0,1},{1,0},{2,3},{3,2},{4,5},{5,4},{6,7},{7,6},{8,9},{9,8},{10,11... | collective-permute-start | bytes 55304 | tf_op jit(solution)/shard_map/ppermute | solution.py:412
  14.6 11.6 %collective-permute-start.8 = (bf16[32,384]{1,0:T(8,128)(2,1)}, bf16[32,384]{1,0:T(8,128)(2,1)}, u32[]{:S(2)}, u32[]{:S(2)}) collective-permute-start(bf16[32,384]{1,0:T(8,128)(2,1)} %concatenate.24.refs_1_), channel_id=1, source_target_pairs={{0,8},{1,9},{2,10},{3,11},{4,12},{5,13},{6,14},{7,15},{8,0},{9,1},... | collective-permute-start | bytes 73736 | tf_op jit(solution)/shard_map/ppermute | solution.py:412
  18.2 2.0 %copy-start.3 = (bf16[144,12288]{1,0:T(8,128)(2,1)S(1)}, bf16[144,12288]{1,0:T(8,128)(2,1)}, u32[]{:S(2)}) copy-start(bf16[144,12288]{1,0:T(8,128)(2,1)} %weight_hbm.1) | copy-start | bytes 10616836
  20.2 1.1 %copy-start.4 = (bf16[32,4,2304]{2,1,0:T(4,128)(2,1)S(1)}, bf16[32,4,2304]{2,1,0:T(4,128)(2,1)}, u32[]{:S(2)}) copy-start(bf16[32,4,2304]{2,1,0:T(4,128)(2,1)} %tokens_hbm.1) | copy-start | bytes 1769476
  23.2 1.7 %copy-start = (bf16[144,12288]{1,0:T(8,128)(2,1)}, bf16[144,12288]{1,0:T(8,128)(2,1)S(1)}, u32[]{:S(2)}) copy-start(bf16[144,12288]{1,0:T(8,128)(2,1)S(1)} %get-tuple-element.40.refs_2_.refs_3_.refs_4_) | copy-start | bytes 10616836
  30.0 28.0 %collective-permute-start.14 = (bf16[64,384]{1,0:T(8,128)(2,1)}, bf16[64,384]{1,0:T(8,128)(2,1)S(1)}, u32[]{:S(2)}, u32[]{:S(2)}) collective-permute-start(bf16[64,384]{1,0:T(8,128)(2,1)} %concatenate.25.refs_0_.near_ref), channel_id=1, source_target_pairs={{0,2},{1,3},{2,0},{3,1},{4,6},{5,7},{6,4},{7,5},{8,10},{9,11},{10,... | collective-permute-start | bytes 147464 | tf_op jit(solution)/shard_map/ppermute | solution.py:412
  31.6 2.0 %copy-start.1 = (bf16[144,12288]{1,0:T(8,128)(2,1)S(1)}, bf16[144,12288]{1,0:T(8,128)(2,1)}, u32[]{:S(2)}) copy-start(bf16[144,12288]{1,0:T(8,128)(2,1)} %copy-done) | copy-start | bytes 10616836
  33.6 0.8 copy-start.7
  35.1 1.4 %copy-start.8 = (bf16[64,144]{1,0:T(8,128)(2,1)S(1)}, bf16[64,144]{1,0:T(8,128)(2,1)}, u32[]{:S(2)}) copy-start(bf16[64,144]{1,0:T(8,128)(2,1)} %copy-done.6) | copy-start | bytes 55300
  35.1 1.4 %copy-start.12 = (bf16[144,64]{0,1:T(8,128)(2,1)S(1)}, bf16[144,64]{0,1:T(8,128)(2,1)}, u32[]{:S(2)}) copy-start(bf16[144,64]{0,1:T(8,128)(2,1)} %param.12) | copy-start | bytes 55300
  35.9 8.3 %collective-permute-start.11 = (s16[32,4224]{1,0:T(8,128)(2,1)S(1)}, s16[32,4224]{1,0:T(8,128)(2,1)S(1)}, u32[]{:S(2)}, u32[]{:S(2)}) collective-permute-start(s16[32,4224]{1,0:T(8,128)(2,1)S(1)} %get-tuple-element.61), channel_id=1, source_target_pairs={{0,2},{1,3},{2,0},{3,1},{4,6},{5,7},{6,4},{7,5},{8,10},{9,11},{10,... | collective-permute-start | bytes 811016 | tf_op jit(solution)/shard_map/ppermute | solution.py:412
  36.5 1.8 %copy-start.11 = (bf16[32,384]{1,0:T(8,128)(2,1)S(1)}, bf16[32,384]{1,0:T(8,128)(2,1)}, u32[]{:S(2)}) copy-start(bf16[32,384]{1,0:T(8,128)(2,1)} %concatenate.24.refs_1_) | copy-start | bytes 73732
  38.3 4.1 %copy-start.15 = (f32[2,3,12288]{2,0,1:T(2,128)S(1)}, f32[2,3,12288]{2,0,1:T(2,128)}, u32[]{:S(2)}) copy-start(f32[2,3,12288]{2,0,1:T(2,128)} %param.15) | copy-start | bytes 884740
  38.3 4.6 %copy-start.14 = (s32[32]{0:T(128)S(1)}, s32[32]{0:T(128)}, u32[]{:S(2)}) copy-start(s32[32]{0:T(128)} %param.18) | copy-start | bytes 388
  38.3 4.6 %copy-start.18 = (s32[64]{0:T(128)S(1)}, s32[64]{0:T(128)}, u32[]{:S(2)}) copy-start(s32[64]{0:T(128)} %param.17) | copy-start | bytes 772
  38.3 9.3 %copy-start.5 = (bf16[64,384]{1,0:T(8,128)(2,1)S(1)}, bf16[64,384]{1,0:T(8,128)(2,1)}, u32[]{:S(2)}) copy-start(bf16[64,384]{1,0:T(8,128)(2,1)} %concatenate.25.refs_0_.near_ref) | copy-start | bytes 147460
  39.1 13.4 %copy-start.19 = (s32[32]{0:T(128)S(1)}, s32[32]{0:T(128)}, u32[]{:S(2)}) copy-start(s32[32]{0:T(128)} %param.16) | copy-start | bytes 388
  39.2 13.5 %copy-start.16 = (s32[32]{0:T(128)S(1)}, s32[32]{0:T(128)}, u32[]{:S(2)}) copy-start(s32[32]{0:T(128)} %param.19) | copy-start | bytes 388
  39.2 13.5 %copy-start.17 = (s32[2]{0:T(128)S(1)}, s32[2]{0:T(128)}, u32[]{:S(2)}) copy-start(s32[2]{0:T(128)} %iota_add_fusion.1) | copy-start | bytes 28
  39.2 22.2 %copy-start.2 = (f32[2,32,128,128]{3,2,1,0:T(8,128)S(1)}, f32[2,32,128,128]{3,2,1,0:T(8,128)}, u32[]{:S(2)}) copy-start(f32[2,32,128,128]{3,2,1,0:T(8,128)} %state_hbm.1) | copy-start | bytes 12582916
  39.2 8.4 %collective-permute-start.7 = (s16[32,4224]{1,0:T(8,128)(2,1)S(1)}, s16[32,4224]{1,0:T(8,128)(2,1)S(1)}, u32[]{:S(2)}, u32[]{:S(2)}) collective-permute-start(s16[32,4224]{1,0:T(8,128)(2,1)S(1)} %get-tuple-element.56), channel_id=1, source_target_pairs={{0,4},{1,5},{2,6},{3,7},{4,0},{5,1},{6,2},{7,3},{8,12},{9,13},{10,... | collective-permute-start | bytes 811016 | tf_op jit(solution)/shard_map/ppermute | solution.py:412
  40.8 9.6 %collective-permute-start.2 = (s16[32,4480]{1,0:T(8,128)(2,1)S(1)}, s16[32,4480]{1,0:T(8,128)(2,1)S(1)}, u32[]{:S(2)}, u32[]{:S(2)}) collective-permute-start(s16[32,4480]{1,0:T(8,128)(2,1)S(1)} %get-tuple-element.49), channel_id=1, source_target_pairs={{0,2},{1,3},{2,0},{3,1},{4,6},{5,7},{6,4},{7,5},{8,10},{9,11},{10,... | collective-permute-start | bytes 860168 | tf_op jit(solution)/shard_map/ppermute | solution.py:412
  44.8 8.1 %collective-permute-start.12 = (s16[16,4224]{1,0:T(8,128)(2,1)S(1)}, s16[16,4224]{1,0:T(8,128)(2,1)S(1)}, u32[]{:S(2)}, u32[]{:S(2)}) collective-permute-start(s16[16,4224]{1,0:T(8,128)(2,1)S(1)} %get-tuple-element.63), channel_id=1, source_target_pairs={{0,4},{1,5},{2,6},{3,7},{4,0},{5,1},{6,2},{7,3},{8,12},{9,13},{10,... | collective-permute-start | bytes 405512 | tf_op jit(solution)/shard_map/ppermute | solution.py:412
  48.1 5.6 %collective-permute-start.9 = (s16[16,4224]{1,0:T(8,128)(2,1)S(1)}, s16[16,4224]{1,0:T(8,128)(2,1)S(1)}, u32[]{:S(2)}, u32[]{:S(2)}) collective-permute-start(s16[16,4224]{1,0:T(8,128)(2,1)S(1)} %get-tuple-element.58), channel_id=1, source_target_pairs={{0,2},{1,3},{2,0},{3,1},{4,6},{5,7},{6,4},{7,5},{8,10},{9,11},{10,... | collective-permute-start | bytes 405512 | tf_op jit(solution)/shard_map/ppermute | solution.py:412
  50.9 6.5 %collective-permute-start.3 = (s16[16,4480]{1,0:T(8,128)(2,1)S(1)}, s16[16,4480]{1,0:T(8,128)(2,1)S(1)}, u32[]{:S(2)}, u32[]{:S(2)}) collective-permute-start(s16[16,4480]{1,0:T(8,128)(2,1)S(1)} %get-tuple-element.51), channel_id=1, source_target_pairs={{0,4},{1,5},{2,6},{3,7},{4,0},{5,1},{6,2},{7,3},{8,12},{9,13},{10,... | collective-permute-start | bytes 430088 | tf_op jit(solution)/shard_map/ppermute | solution.py:412
  53.3 7.4 %collective-permute-start.13 = (s16[16,2176]{1,0:T(8,128)(2,1)S(1)}, s16[16,2176]{1,0:T(8,128)(2,1)S(1)}, u32[]{:S(2)}, u32[]{:S(2)}) collective-permute-start(s16[16,2176]{1,0:T(8,128)(2,1)S(1)} %get-tuple-element.65), channel_id=1, source_target_pairs={{0,8},{1,9},{2,10},{3,11},{4,12},{5,13},{6,14},{7,15},{8,0},{9,1},... | collective-permute-start | bytes 208904 | tf_op jit(solution)/shard_map/ppermute | solution.py:412
  54.1 7.3 %collective-permute-start.10 = (s16[16,2176]{1,0:T(8,128)(2,1)S(1)}, s16[16,2176]{1,0:T(8,128)(2,1)S(1)}, u32[]{:S(2)}, u32[]{:S(2)}) collective-permute-start(s16[16,2176]{1,0:T(8,128)(2,1)S(1)} %get-tuple-element.60), channel_id=1, source_target_pairs={{0,8},{1,9},{2,10},{3,11},{4,12},{5,13},{6,14},{7,15},{8,0},{9,1},... | collective-permute-start | bytes 208904 | tf_op jit(solution)/shard_map/ppermute | solution.py:412
  57.9 6.4 %collective-permute-start.4 = (s16[16,2304]{1,0:T(8,128)(2,1)S(1)}, s16[16,2304]{1,0:T(8,128)(2,1)S(1)}, u32[]{:S(2)}, u32[]{:S(2)}) collective-permute-start(s16[16,2304]{1,0:T(8,128)(2,1)S(1)} %get-tuple-element.53), channel_id=1, source_target_pairs={{0,8},{1,9},{2,10},{3,11},{4,12},{5,13},{6,14},{7,15},{8,0},{9,1},... | collective-permute-start | bytes 221192 | tf_op jit(solution)/shard_map/ppermute | solution.py:412
  66.2 10.4 %all-to-all-start = ((bf16[16,16,128]{2,1,0:T(8,128)(2,1)}), bf16[16,16,128]{2,1,0:T(8,128)(2,1)S(1)}, u32[]{:S(2)}, u32[]{:S(2)}) async-start(bf16[16,16,128]{2,1,0:T(8,128)(2,1)} %values_part.1), calls=%async_computation | async-start | bytes 131072 | tf_op jit(solution)/shard_map/all_to_all | solution.py:500
  (4 other events, 2.6 us)

commit v7 on v5

--- a/solution.py
+++ b/solution.py
@@ -106,7 +106,7 @@
 
 def tap_block(block, me):
     other = jnp.bitwise_xor(block // 2, me)
-    place = (other & 1) + ((other >> 2) & 3) * 2 + ((other >> 1) & 1) * 8
+    place = ((other >> 2) & 3) + ((other >> 1) & 1) * 4 + (other & 1) * 8
     return place * 2 + block % 2
 
 
@@ -266,8 +266,8 @@
 
 
 def rows_kernel(
-    depth, me_ref, slot_of_ref, tokens_hbm, weight_hbm, mine_ref, theirs_ref, weight_ref,
-    window_ref, sem, weight_sem,
+    depth, me_ref, slot_of_ref, tokens_hbm, weight_hbm, mine_ref, theirs_ref,
+    weight_ref, window_ref, sem, weight_sem,
 ):
     me = me_ref[0]
     width = window_ref.shape[2]
@@ -407,6 +407,25 @@
     )(kept, got)
 
 
+def join_kernel(first_ref, second_ref, earlier_ref, out_ref):
+    both = [ref[...].astype(jnp.float32) for ref in (first_ref, second_ref)]
+    out_ref[...] = jnp.concatenate(both, axis=0).astype(out_ref.dtype)
+
+
+def join(first, second, earlier):
+    vmem = pl.BlockSpec(memory_space=pltpu.VMEM)
+    rows, width = first.shape
+    return pl.pallas_call(
+        join_kernel,
+        out_shape=jax.ShapeDtypeStruct((2 * rows, width), first.dtype),
+        in_specs=[vmem, vmem, pl.BlockSpec(memory_space=pl.ANY)],
+        out_specs=vmem,
+        compiler_params=pltpu.CompilerParams(vmem_limit_bytes=32 * 1024 * 1024),
+        cost_estimate=pl.CostEstimate(flops=0, bytes_accessed=0, transcendentals=0),
+        name="join_taps",
+    )(first, second, earlier)
+
+
 def swap(value, bit, devices):
     return lax.ppermute(value, "heads", [(i, i ^ bit) for i in range(devices)])
 
@@ -430,8 +449,19 @@
     chips = devices // 2
 
     bits = [1 << b for b in range(1, devices.bit_length() - 1)]
-    steps = jnp.arange(STEPS, dtype=jnp.int32)
-    offered = (slot_of[:, None] * STEPS + steps[None, :]).reshape(-1)
+
+    ride = conv_weight.shape[1] == 2 * TAP_WIDTH and len(bits) == 3
+    if ride:
+        taps = jnp.concatenate([conv_weight[:, :TAP_WIDTH], conv_weight[:, TAP_WIDTH:]], axis=0)
+        far = swap(taps, 4, devices)
+    else:
+        taps = lax.all_gather(conv_weight, "heads", axis=1, tiled=True)
+        order = [
+            2 * (at >> 4 & 1) + 4 * (at >> 3 & 1) + 8 * (at >> 1 & 1) + 16 * (at >> 2 & 1) + (at & 1)
+            for at in range(TAP_BLOCKS)
+        ]
+        taps = [taps[:, block * TAP_WIDTH : (block + 1) * TAP_WIDTH] for block in order]
+        taps = jnp.concatenate(taps, axis=0)
 
     mine, theirs, near_weight = run_rows(me, slot_of, tokens, qkv_weight, chips)
 
@@ -441,22 +471,21 @@
 
     tie = lambda *values: lax.optimization_barrier(values)
 
-    ride = conv_weight.shape[1] == 2 * TAP_WIDTH and len(bits) == 3
     if ride:
-        taps = jnp.concatenate([conv_weight[:, :TAP_WIDTH], conv_weight[:, TAP_WIDTH:]], axis=0)
-        far = swap(taps, 1, devices)
-    else:
-        taps = lax.all_gather(conv_weight, "heads", axis=1, tiled=True)
-        blocks = [block for bit in (0, 4) for block in range(TAP_BLOCKS) if block & 4 == bit]
-        taps = [taps[:, block * TAP_WIDTH : (block + 1) * TAP_WIDTH] for block in blocks]
-        taps = jnp.concatenate(taps, axis=0)
+        taps = join(taps, far, mine)
+        far = swap(taps, 8, devices)
     keys = run_product(mine, theirs, weights, 1)
     values = run_product(mine, theirs, weights, 2, gates, earlier=keys[:1])
-    queries = run_product(mine, theirs, weights, 0, earlier=values[:1], crossed=True)
-
-    lengths, old_heads, new_units, carried, *values = tie(
-        lengths, old_heads, new_units, conv_state, *values
-    )
+    if ride:
+        taps = join(taps, far, values[0])
+        far = swap(taps, 2, devices)
+    queries = run_product(mine, theirs, weights, 0, earlier=(values[0], taps), crossed=True)
+
+    slot_of, lengths, old_heads, new_units, carried, *values = tie(
+        slot_of, lengths, old_heads, new_units, conv_state, *values
+    )
+    steps = jnp.arange(STEPS, dtype=jnp.int32)
+    offered = (slot_of[:, None] * STEPS + steps[None, :]).reshape(-1)
     old_slots, halves = unit_tables(old_heads, new_units)
     my_rows = me * LOCAL + jnp.arange(LOCAL, dtype=jnp.int32)
     my_lengths = jnp.sum(
@@ -474,13 +503,11 @@
         for at in range(3):
             kept[at], packed = run_combine(kept[at], got[at])
             got[at] = swap(packed, routes[at][level], devices)
-            if ride and level == 1 and at == 0:
-                kept[0], taps, far = tie(kept[0], taps, far)
-                taps = jnp.concatenate([taps, far], axis=0)
-                taps = jnp.concatenate([taps, swap(taps, 4, devices)], axis=0)
+        if ride and level == 1:
+            taps = join(taps, far, kept[2])
+            far = swap(taps, 1, devices)
     if ride:
-        taps = jnp.concatenate([taps, swap(taps, 8, devices)], axis=0)
-        twist, taps = me.reshape(1), (taps, swap(taps, 2, devices))
+        twist, taps = me.reshape(1), (taps, far)
     else:
         half = TAP_BLOCKS // 2 * TAPS
         twist, taps = jnp.zeros(1, jnp.int32), (taps[:half], taps[half:])

time: 60.2 us -> 59.1 us (0.982)
  waiting for transfers between devices: 16.2 us -> 20.7 us
  starting transfers between devices: 23.5 us -> 19.1 us
  other arithmetic: 1.89 us -> 0.65 us
    ppermute x15, waiting for transfers between devices: 9.47 us -> 14 us  [swap(): return lax.ppermute(value, 'heads', [(i, i ^ bit) for i in range(devices)])]
    ppermute x15, starting transfers between devices: 19 us -> 15.6 us  [swap(): return lax.ppermute(value, 'heads', [(i, i ^ bit) for i in range(devices)])]
    mul x1, other arithmetic: 1.23 us -> 0.01 us  [on_device(): offered = (slot_of[:, None] * STEPS + steps[None, :]).reshape(-1)]
    all_to_all x1, starting transfers between devices: 4.46 us -> 3.5 us  [on_device(): lax.all_to_all(sending, 'heads', split_axis=0, concat_axis=0, tiled=True)]
    unnamed x25 -> x20, local copies, waits for them, and re-layouts: 3.78 us -> 3.76 us
  transfers between devices with their start and end apart: 16 -> 16, of which waited for: 7 -> 7; matrix products, arithmetic and copies ran while one was open for 5% -> 3% of each run, Pallas kernels for 17% -> 17%
where the time goes in v7:
time: 59.1 us; the launch traced here: 58.7 us
  waiting for transfers between devices  20.7 us (35%)
  starting transfers between devices  19.1 us (32%)
  Pallas kernels  12.2 us (21%)
  local copies, waits for them, and re-layouts  5.54 us (9%)
  other arithmetic  0.65 us (1%)
    ppermute x15, starting transfers between devices, swap(): return lax.ppermute(value, 'heads', [(i, i ^ bit) for i in range(devices)])  15.6 us
    ppermute x15, waiting for transfers between devices, swap(): return lax.ppermute(value, 'heads', [(i, i ^ bit) for i in range(devices)])  14 us
    all_to_all x1, waiting for transfers between devices, on_device(): lax.all_to_all(sending, 'heads', split_axis=0, concat_axis=0, tiled=True)  6.68 us
    unnamed x20, local copies, waits for them, and re-layouts  3.76 us
    all_to_all x1, starting transfers between devices, on_device(): lax.all_to_all(sending, 'heads', split_axis=0, concat_axis=0, tiled=True)  3.5 us
    pallas_call x3, Pallas kernels, run_product(): pl.pallas_call(functools.partial(product_kernel, len(earlier), crossed),...  3.4 us
    pallas_call x1, Pallas kernels, run_delta(): pl.pallas_call(keys_kernel, out_shape=[per_head] * 2 + lags + [tap_blocks...  2.81 us
    pallas_call x6, Pallas kernels, run_combine(): pl.pallas_call(combine_kernel, out_shape=[jax.ShapeDtypeStruct((half, wid...  2.8 us
  transfers between devices with their start and end apart: 16, of which 7 were waited for; matrix products, arithmetic and copies ran while one was open for 3% of the time, Pallas kernels for 17%

profile of v7, /device:TPU:0, one launch (start us, length us, event | category | flops | bytes accessed | tf_op | source)
XLA Modules:
  0.0 58.7 jit_solution(13058783324107749061)
XLA Ops:
  0.0 0.5 collective-permute-start
  0.5 0.7 %fusion.6 = (bf16[4,384]{1,0:T(4,128)(2,1)S(1)}, bf16[4,384]{1,0:T(4,128)(2,1)S(1)}) fusion(bf16[4,768]{1,0:T(4,128)(2,1)} %param.13), kind=kLoop, calls=%fused_computation.27 | loop fusion | bytes 12288 | tf_op jit(solution)/shard_map/slice | solution.py:455
  1.2 2.6 %collective-permute-start.5 = (bf16[8,384]{1,0:T(8,128)(2,1)S(1)}, bf16[8,384]{1,0:T(8,128)(2,1)S(1)}, u32[]{:S(2)}, u32[]{:S(2)}) collective-permute-start(bf16[8,384]{1,0:T(8,128)(2,1)S(1)} %pad_maximum_fusion.1.first_ref), channel_id=1, source_target_pairs={{0,4},{1,5},{2,6},{3,7},{4,0},{5,1},{6,2},{7,3},{8,12},{9,13},{10,... | collective-permute-start | bytes 18440 | tf_op jit(solution)/shard_map/ppermute | solution.py:430
  4.0 2.0 %copy-done.1 = bf16[144,12288]{1,0:T(8,128)(2,1)S(1)} copy-done((bf16[144,12288]{1,0:T(8,128)(2,1)S(1)}, bf16[144,12288]{1,0:T(8,128)(2,1)}, u32[]{:S(2)}) %copy-start.1) | copy-done | bytes 3538968
  6.0 1.1 %copy-done.2 = bf16[32,4,2304]{2,1,0:T(4,128)(2,1)S(1)} copy-done((bf16[32,4,2304]{2,1,0:T(4,128)(2,1)S(1)}, bf16[32,4,2304]{2,1,0:T(4,128)(2,1)}, u32[]{:S(2)}) %copy-start.2) | copy-done | bytes 589848
  7.1 0.7 %copy-done.4 = s32[32]{0:T(128)S(1)} copy-done((s32[32]{0:T(128)S(1)}, s32[32]{0:T(128)}, u32[]{:S(2)}) %copy-start.4) | copy-done | bytes 152
  7.8 1.2 %token_rows.1 = (bf16[64,144]{1,0:T(8,128)(2,1)S(1)}, bf16[64,144]{1,0:T(8,128)(2,1)S(1)}, bf16[144,12288]{1,0:T(8,128)(2,1)S(1)}) custom-call(s32[1]{0:T(128)} %bitcast.me_ref.twist_ref, s32[1,32]{1,0:T(1,128)S(1)} %bitcast.14, bf16[32,4,2304]{2,1,0:T(4,128)(2,1)S(1)} %copy-done.2, bf16[144,12288]{1,0:T(8,128)(2,1)S(1)} %copy-done.1), custom_call_target="tpu_custom_call" | custom-call | tf_op jit(solution)/shard_map/token_rows/pallas_call | solution.py:310
  9.0 2.7 %collective-permute-start.6 = (bf16[16,384]{1,0:T(8,128)(2,1)S(1)}, bf16[16,384]{1,0:T(8,128)(2,1)S(1)}, u32[]{:S(2)}, u32[]{:S(2)}) collective-permute-start(bf16[16,384]{1,0:T(8,128)(2,1)S(1)} %join_taps.3.first_ref), channel_id=1, source_target_pairs={{0,8},{1,9},{2,10},{3,11},{4,12},{5,13},{6,14},{7,15},{8,0},{9,1},... | collective-permute-start | bytes 36872 | tf_op jit(solution)/shard_map/ppermute | solution.py:430
  11.7 0.8 %partial_product.3 = (f32[32,4096]{1,0:T(8,128)S(1)}, s16[32,4224]{1,0:T(8,128)(2,1)S(1)}) custom-call(bf16[64,144]{1,0:T(8,128)(2,1)S(1)} %get-tuple-element.38.refs_0_.refs_1_.earlier_ref.refs_2_, bf16[64,144]{1,0:T(8,128)(2,1)S(1)} %get-tuple-element.39.refs_1_.refs_2_.refs_3_, bf16[144,12288]{1,0:T(8,128)(2,1)S(1)} %get-tuple-element.40.refs_2_.refs_3_.refs_4_, ...), custom_call_target="tpu_custom_call" | custom-call | tf_op jit(solution)/shard_map/partial_product/pallas_call | solution.py:361
  12.5 1.6 %collective-permute-start.10 = (s16[32,4224]{1,0:T(8,128)(2,1)S(1)}, s16[32,4224]{1,0:T(8,128)(2,1)S(1)}, u32[]{:S(2)}, u32[]{:S(2)}) collective-permute-start(s16[32,4224]{1,0:T(8,128)(2,1)S(1)} %get-tuple-element.61), channel_id=1, source_target_pairs={{0,2},{1,3},{2,0},{3,1},{4,6},{5,7},{6,4},{7,5},{8,10},{9,11},{10,... | collective-permute-start | bytes 811016 | tf_op jit(solution)/shard_map/ppermute | solution.py:430
  14.1 1.7 %partial_product.4 = (f32[32,4352]{1,0:T(8,128)S(1)}, s16[32,4480]{1,0:T(8,128)(2,1)S(1)}) custom-call(f32[32,4096]{1,0:T(8,128)S(1)} %get-tuple-element.41.refs_0_.kept_ref, bf16[64,144]{1,0:T(8,128)(2,1)S(1)} %get-tuple-element.38.refs_0_.refs_1_.earlier_ref.refs_2_, bf16[64,144]{1,0:T(8,128)(2,1)S(1)} %get-tuple-element.39.refs_1_.refs_2_.refs_3_, ...), custom_call_target="tpu_custom_call" | custom-call | tf_op jit(solution)/shard_map/partial_product/pallas_call | solution.py:361
  15.9 0.6 collective-permute-start.13
  16.5 0.8 %partial_product.5 = (f32[32,4096]{1,0:T(8,128)S(1)}, s16[32,4224]{1,0:T(8,128)(2,1)S(1)}) custom-call(f32[32,4352]{1,0:T(8,128)S(1)} %get-tuple-element.48.kept_ref.earlier_ref.refs_0_, bf16[32,384]{1,0:T(8,128)(2,1)S(1)} %join_taps.4.refs_1_.first_ref, bf16[64,144]{1,0:T(8,128)(2,1)S(1)} %get-tuple-element.38.refs_0_.refs_1_.earlier_ref.refs_2_, ...), custom_call_target="tpu_custom_call" | custom-call | tf_op jit(solution)/shard_map/partial_product/pallas_call | solution.py:361
  17.4 0.5 collective-permute-start.7
  17.9 1.5 %collective-permute-start.2 = (s16[32,4480]{1,0:T(8,128)(2,1)S(1)}, s16[32,4480]{1,0:T(8,128)(2,1)S(1)}, u32[]{:S(2)}, u32[]{:S(2)}) collective-permute-start(s16[32,4480]{1,0:T(8,128)(2,1)S(1)} %get-tuple-element.49), channel_id=1, source_target_pairs={{0,2},{1,3},{2,0},{3,1},{4,6},{5,7},{6,4},{7,5},{8,10},{9,11},{10,... | collective-permute-start | bytes 860168 | tf_op jit(solution)/shard_map/ppermute | solution.py:430
  19.9 2.0 %collective-permute-done.10.got_ref = s16[32,4224]{1,0:T(8,128)(2,1)S(1)} collective-permute-done((s16[32,4224]{1,0:T(8,128)(2,1)S(1)}, s16[32,4224]{1,0:T(8,128)(2,1)S(1)}, u32[]{:S(2)}, u32[]{:S(2)}) %collective-permute-start.10) | collective-permute-done | bytes 270368 | tf_op jit(solution)/shard_map/ppermute | solution.py:430
  21.9 0.5 combine.10
  22.7 4.0 %collective-permute-done.7.got_ref = s16[32,4224]{1,0:T(8,128)(2,1)S(1)} collective-permute-done((s16[32,4224]{1,0:T(8,128)(2,1)S(1)}, s16[32,4224]{1,0:T(8,128)(2,1)S(1)}, u32[]{:S(2)}, u32[]{:S(2)}) %collective-permute-start.7) | collective-permute-done | bytes 270368 | tf_op jit(solution)/shard_map/ppermute | solution.py:430
  26.7 0.5 combine.8
  27.2 1.6 %collective-permute-start.8 = (s16[16,4224]{1,0:T(8,128)(2,1)S(1)}, s16[16,4224]{1,0:T(8,128)(2,1)S(1)}, u32[]{:S(2)}, u32[]{:S(2)}) collective-permute-start(s16[16,4224]{1,0:T(8,128)(2,1)S(1)} %get-tuple-element.58), channel_id=1, source_target_pairs={{0,2},{1,3},{2,0},{3,1},{4,6},{5,7},{6,4},{7,5},{8,10},{9,11},{10,... | collective-permute-start | bytes 405512 | tf_op jit(solution)/shard_map/ppermute | solution.py:430
  28.8 0.5 combine.6
  29.4 0.5 collective-permute-start.3
  31.1 1.2 %collective-permute-done.8.got_ref = s16[16,4224]{1,0:T(8,128)(2,1)S(1)} collective-permute-done((s16[16,4224]{1,0:T(8,128)(2,1)S(1)}, s16[16,4224]{1,0:T(8,128)(2,1)S(1)}, u32[]{:S(2)}, u32[]{:S(2)}) %collective-permute-start.8) | collective-permute-done | bytes 135200 | tf_op jit(solution)/shard_map/ppermute | solution.py:430
  32.7 1.4 %collective-permute-start.9 = (s16[16,2176]{1,0:T(8,128)(2,1)S(1)}, s16[16,2176]{1,0:T(8,128)(2,1)S(1)}, u32[]{:S(2)}, u32[]{:S(2)}) collective-permute-start(s16[16,2176]{1,0:T(8,128)(2,1)S(1)} %get-tuple-element.60), channel_id=1, source_target_pairs={{0,8},{1,9},{2,10},{3,11},{4,12},{5,13},{6,14},{7,15},{8,0},{9,1},... | collective-permute-start | bytes 208904 | tf_op jit(solution)/shard_map/ppermute | solution.py:430
  35.0 1.2 %collective-permute-start.4 = (s16[16,2304]{1,0:T(8,128)(2,1)S(1)}, s16[16,2304]{1,0:T(8,128)(2,1)S(1)}, u32[]{:S(2)}, u32[]{:S(2)}) collective-permute-start(s16[16,2304]{1,0:T(8,128)(2,1)S(1)} %get-tuple-element.53), channel_id=1, source_target_pairs={{0,8},{1,9},{2,10},{3,11},{4,12},{5,13},{6,14},{7,15},{8,0},{9,1},... | collective-permute-start | bytes 221192 | tf_op jit(solution)/shard_map/ppermute | solution.py:430
  36.3 4.9 %collective-permute-done.12.key_got_ref = s16[16,2176]{1,0:T(8,128)(2,1)S(1)} collective-permute-done((s16[16,2176]{1,0:T(8,128)(2,1)S(1)}, s16[16,2176]{1,0:T(8,128)(2,1)S(1)}, u32[]{:S(2)}, u32[]{:S(2)}) %collective-permute-start.12) | collective-permute-done | bytes 69664 | tf_op jit(solution)/shard_map/ppermute | solution.py:430
  41.2 1.5 %collective-permute-done.9.query_got_ref = s16[16,2176]{1,0:T(8,128)(2,1)S(1)} collective-permute-done((s16[16,2176]{1,0:T(8,128)(2,1)S(1)}, s16[16,2176]{1,0:T(8,128)(2,1)S(1)}, u32[]{:S(2)}, u32[]{:S(2)}) %collective-permute-start.9) | collective-permute-done | bytes 69664 | tf_op jit(solution)/shard_map/ppermute | solution.py:430
  42.7 2.8 %keys_part.1 = (f32[32,8,128]{2,1,0:T(8,128)S(1)}, f32[32,8,128]{2,1,0:T(8,128)S(1)}, f32[3,32,8,128]{3,2,1,0:T(8,128)S(1)}, f32[4,32,8,128]{3,2,1,0:T(8,128)S(1)}, f32[32,4,384]{2,1,0:T(4,128)S(1)}) custom-call(s32[1]{0:T(128)} %bitcast.me_ref.twist_ref, f32[8,4096]{1,0:T(8,128)S(1)} %get-tuple-element.59.query_ref, ...), custom_call_target="tpu_custom_call" | custom-call | flops 40000000 | bytes 9000000 | tf_op jit(solution)/shard_map/keys_part/pallas_call | solution.py:243
  45.5 1.9 %values_part.1 = bf16[16,16,128]{2,1,0:T(8,128)(2,1)} custom-call(s32[64]{0:T(128)S(1)} %select_reduce_fusion.slots_ref, s32[64]{0:T(128)S(1)} %get-tuple-element.77.halves_ref, s32[2]{0:T(128)S(1)} %fusion.4.lengths_ref, s32[1]{0:T(128)} %bitcast.me_ref.twist_ref, f32[8,4352]{1,0:T(8,128)S(1)} %get-tuple-element.52.value_ref, ...), custom_call_target="tpu_custom_call" | custom-call | flops 4000000 | bytes 2000000 | tf_op jit(solution)/shard_map/values_part/pallas_call | solution.py:256
  47.5 3.5 %all-to-all-start = ((bf16[16,16,128]{2,1,0:T(8,128)(2,1)}), bf16[16,16,128]{2,1,0:T(8,128)(2,1)S(1)}, u32[]{:S(2)}, u32[]{:S(2)}) async-start(bf16[16,16,128]{2,1,0:T(8,128)(2,1)} %values_part.1), calls=%async_computation | async-start | bytes 131072 | tf_op jit(solution)/shard_map/all_to_all | solution.py:526
  51.2 6.7 %all-to-all-done = bf16[16,16,128]{2,1,0:T(8,128)(2,1)S(1)} async-done(((bf16[16,16,128]{2,1,0:T(8,128)(2,1)}), bf16[16,16,128]{2,1,0:T(8,128)(2,1)S(1)}, u32[]{:S(2)}, u32[]{:S(2)}) %all-to-all-start) | async-done | bytes 65568 | tf_op jit(solution)/shard_map/all_to_all | solution.py:526
  58.0 0.7 %reshape.46 = bf16[32,4,256]{2,1,0:T(4,128)(2,1)} reshape(bf16[128,256]{1,0:T(8,128)(2,1)S(1)} %convolution_convert_fusion) | data formatting | bytes 131072 | tf_op jit(solution)/shard_map/reshape | solution.py:537
  (52 shorter events, 3.9 us)
Async XLA Ops:
  0.0 11.7 %collective-permute-start = (bf16[144,12288]{1,0:T(8,128)(2,1)}, bf16[144,12288]{1,0:T(8,128)(2,1)S(1)}, u32[]{:S(2)}, u32[]{:S(2)}) collective-permute-start(bf16[144,12288]{1,0:T(8,128)(2,1)} %weight_hbm.1), channel_id=1, source_target_pairs={{0,1},{1,0},{2,3},{3,2},{4,5},{5,4},{6,7},{7,6},{8,9},{9,8},{10,11... | collective-permute-start | bytes 10616840 | tf_op jit(solution)/shard_map/ppermute | solution.py:430
  1.2 7.8 %collective-permute-start.5 = (bf16[8,384]{1,0:T(8,128)(2,1)S(1)}, bf16[8,384]{1,0:T(8,128)(2,1)S(1)}, u32[]{:S(2)}, u32[]{:S(2)}) collective-permute-start(bf16[8,384]{1,0:T(8,128)(2,1)S(1)} %pad_maximum_fusion.1.first_ref), channel_id=1, source_target_pairs={{0,4},{1,5},{2,6},{3,7},{4,0},{5,1},{6,2},{7,3},{8,12},{9,13},{10,... | collective-permute-start | bytes 18440 | tf_op jit(solution)/shard_map/ppermute | solution.py:430
  3.8 10.3 %collective-permute-start.1 = (bf16[64,144]{1,0:T(8,128)(2,1)}, bf16[64,144]{1,0:T(8,128)(2,1)}, u32[]{:S(2)}, u32[]{:S(2)}) collective-permute-start(bf16[64,144]{1,0:T(8,128)(2,1)} %bitcast.12), channel_id=1, source_target_pairs={{0,1},{1,0},{2,3},{3,2},{4,5},{5,4},{6,7},{7,6},{8,9},{9,8},{10,11... | collective-permute-start | bytes 55304 | tf_op jit(solution)/shard_map/ppermute | solution.py:430
  4.0 2.0 %copy-start.1 = (bf16[144,12288]{1,0:T(8,128)(2,1)S(1)}, bf16[144,12288]{1,0:T(8,128)(2,1)}, u32[]{:S(2)}) copy-start(bf16[144,12288]{1,0:T(8,128)(2,1)} %weight_hbm.1) | copy-start | bytes 10616836
  6.0 1.1 %copy-start.2 = (bf16[32,4,2304]{2,1,0:T(4,128)(2,1)S(1)}, bf16[32,4,2304]{2,1,0:T(4,128)(2,1)}, u32[]{:S(2)}) copy-start(bf16[32,4,2304]{2,1,0:T(4,128)(2,1)} %tokens_hbm.1) | copy-start | bytes 1769476
  7.1 0.7 %copy-start.4 = (s32[32]{0:T(128)S(1)}, s32[32]{0:T(128)}, u32[]{:S(2)}) copy-start(s32[32]{0:T(128)} %param.18) | copy-start | bytes 388
  9.0 6.8 %collective-permute-start.6 = (bf16[16,384]{1,0:T(8,128)(2,1)S(1)}, bf16[16,384]{1,0:T(8,128)(2,1)S(1)}, u32[]{:S(2)}, u32[]{:S(2)}) collective-permute-start(bf16[16,384]{1,0:T(8,128)(2,1)S(1)} %join_taps.3.first_ref), channel_id=1, source_target_pairs={{0,8},{1,9},{2,10},{3,11},{4,12},{5,13},{6,14},{7,15},{8,0},{9,1},... | collective-permute-start | bytes 36872 | tf_op jit(solution)/shard_map/ppermute | solution.py:430
  11.7 2.4 %copy-start.3 = (bf16[144,64]{0,1:T(8,128)(2,1)S(1)}, bf16[144,64]{0,1:T(8,128)(2,1)}, u32[]{:S(2)}) copy-start(bf16[144,64]{0,1:T(8,128)(2,1)} %param.12) | copy-start | bytes 55300
  12.5 9.4 %collective-permute-start.10 = (s16[32,4224]{1,0:T(8,128)(2,1)S(1)}, s16[32,4224]{1,0:T(8,128)(2,1)S(1)}, u32[]{:S(2)}, u32[]{:S(2)}) collective-permute-start(s16[32,4224]{1,0:T(8,128)(2,1)S(1)} %get-tuple-element.61), channel_id=1, source_target_pairs={{0,2},{1,3},{2,0},{3,1},{4,6},{5,7},{6,4},{7,5},{8,10},{9,11},{10,... | collective-permute-start | bytes 811016 | tf_op jit(solution)/shard_map/ppermute | solution.py:430
  15.9 3.5 %copy-start.6 = (f32[2,3,12288]{2,0,1:T(2,128)S(1)}, f32[2,3,12288]{2,0,1:T(2,128)}, u32[]{:S(2)}) copy-start(f32[2,3,12288]{2,0,1:T(2,128)} %param.15) | copy-start | bytes 884740
  15.9 4.0 %copy-start.5 = (s32[32]{0:T(128)S(1)}, s32[32]{0:T(128)}, u32[]{:S(2)}) copy-start(s32[32]{0:T(128)} %param.18) | copy-start | bytes 388
  15.9 4.0 %copy-start.8 = (s32[64]{0:T(128)S(1)}, s32[64]{0:T(128)}, u32[]{:S(2)}) copy-start(s32[64]{0:T(128)} %param.17) | copy-start | bytes 772
  15.9 14.3 %collective-permute-start.13 = (bf16[32,384]{1,0:T(8,128)(2,1)S(1)}, bf16[32,384]{1,0:T(8,128)(2,1)S(1)}, u32[]{:S(2)}, u32[]{:S(2)}) collective-permute-start(bf16[32,384]{1,0:T(8,128)(2,1)S(1)} %join_taps.4.refs_1_.first_ref), channel_id=1, source_target_pairs={{0,2},{1,3},{2,0},{3,1},{4,6},{5,7},{6,4},{7,5},{8,10},{9,11},{10,... | collective-permute-start | bytes 73736 | tf_op jit(solution)/shard_map/ppermute | solution.py:430
  17.3 12.6 %copy-start.7 = (s32[32]{0:T(128)S(1)}, s32[32]{0:T(128)}, u32[]{:S(2)}) copy-start(s32[32]{0:T(128)} %param.19) | copy-start | bytes 388
  17.3 12.7 %copy-start.9 = (s32[32]{0:T(128)S(1)}, s32[32]{0:T(128)}, u32[]{:S(2)}) copy-start(s32[32]{0:T(128)} %param.16) | copy-start | bytes 388
  17.3 25.4 %copy-start = (f32[2,32,128,128]{3,2,1,0:T(8,128)S(1)}, f32[2,32,128,128]{3,2,1,0:T(8,128)}, u32[]{:S(2)}) copy-start(f32[2,32,128,128]{3,2,1,0:T(8,128)} %state_hbm.1) | copy-start | bytes 12582916
  17.4 9.3 %collective-permute-start.7 = (s16[32,4224]{1,0:T(8,128)(2,1)S(1)}, s16[32,4224]{1,0:T(8,128)(2,1)S(1)}, u32[]{:S(2)}, u32[]{:S(2)}) collective-permute-start(s16[32,4224]{1,0:T(8,128)(2,1)S(1)} %get-tuple-element.56), channel_id=1, source_target_pairs={{0,4},{1,5},{2,6},{3,7},{4,0},{5,1},{6,2},{7,3},{8,12},{9,13},{10,... | collective-permute-start | bytes 811016 | tf_op jit(solution)/shard_map/ppermute | solution.py:430
  17.9 10.9 %collective-permute-start.2 = (s16[32,4480]{1,0:T(8,128)(2,1)S(1)}, s16[32,4480]{1,0:T(8,128)(2,1)S(1)}, u32[]{:S(2)}, u32[]{:S(2)}) collective-permute-start(s16[32,4480]{1,0:T(8,128)(2,1)S(1)} %get-tuple-element.49), channel_id=1, source_target_pairs={{0,2},{1,3},{2,0},{3,1},{4,6},{5,7},{6,4},{7,5},{8,10},{9,11},{10,... | collective-permute-start | bytes 860168 | tf_op jit(solution)/shard_map/ppermute | solution.py:430
  22.5 7.8 %collective-permute-start.11 = (s16[16,4224]{1,0:T(8,128)(2,1)S(1)}, s16[16,4224]{1,0:T(8,128)(2,1)S(1)}, u32[]{:S(2)}, u32[]{:S(2)}) collective-permute-start(s16[16,4224]{1,0:T(8,128)(2,1)S(1)} %get-tuple-element.63), channel_id=1, source_target_pairs={{0,4},{1,5},{2,6},{3,7},{4,0},{5,1},{6,2},{7,3},{8,12},{9,13},{10,... | collective-permute-start | bytes 405512 | tf_op jit(solution)/shard_map/ppermute | solution.py:430
  27.2 5.1 %collective-permute-start.8 = (s16[16,4224]{1,0:T(8,128)(2,1)S(1)}, s16[16,4224]{1,0:T(8,128)(2,1)S(1)}, u32[]{:S(2)}, u32[]{:S(2)}) collective-permute-start(s16[16,4224]{1,0:T(8,128)(2,1)S(1)} %get-tuple-element.58), channel_id=1, source_target_pairs={{0,2},{1,3},{2,0},{3,1},{4,6},{5,7},{6,4},{7,5},{8,10},{9,11},{10,... | collective-permute-start | bytes 405512 | tf_op jit(solution)/shard_map/ppermute | solution.py:430
  29.4 5.2 %collective-permute-start.3 = (s16[16,4480]{1,0:T(8,128)(2,1)S(1)}, s16[16,4480]{1,0:T(8,128)(2,1)S(1)}, u32[]{:S(2)}, u32[]{:S(2)}) collective-permute-start(s16[16,4480]{1,0:T(8,128)(2,1)S(1)} %get-tuple-element.51), channel_id=1, source_target_pairs={{0,4},{1,5},{2,6},{3,7},{4,0},{5,1},{6,2},{7,3},{8,12},{9,13},{10,... | collective-permute-start | bytes 430088 | tf_op jit(solution)/shard_map/ppermute | solution.py:430
  30.2 6.1 %collective-permute-start.14 = (bf16[64,384]{1,0:T(8,128)(2,1)S(1)}, bf16[64,384]{1,0:T(8,128)(2,1)S(1)}, u32[]{:S(2)}, u32[]{:S(2)}) collective-permute-start(bf16[64,384]{1,0:T(8,128)(2,1)S(1)} %join_taps.5.near_ref), channel_id=1, source_target_pairs={{0,1},{1,0},{2,3},{3,2},{4,5},{5,4},{6,7},{7,6},{8,9},{9,8},{10,11... | collective-permute-start | bytes 147464 | tf_op jit(solution)/shard_map/ppermute | solution.py:430
  30.7 10.5 %collective-permute-start.12 = (s16[16,2176]{1,0:T(8,128)(2,1)S(1)}, s16[16,2176]{1,0:T(8,128)(2,1)S(1)}, u32[]{:S(2)}, u32[]{:S(2)}) collective-permute-start(s16[16,2176]{1,0:T(8,128)(2,1)S(1)} %get-tuple-element.65), channel_id=1, source_target_pairs={{0,8},{1,9},{2,10},{3,11},{4,12},{5,13},{6,14},{7,15},{8,0},{9,1},... | collective-permute-start | bytes 208904 | tf_op jit(solution)/shard_map/ppermute | solution.py:430
  32.7 10.0 %collective-permute-start.9 = (s16[16,2176]{1,0:T(8,128)(2,1)S(1)}, s16[16,2176]{1,0:T(8,128)(2,1)S(1)}, u32[]{:S(2)}, u32[]{:S(2)}) collective-permute-start(s16[16,2176]{1,0:T(8,128)(2,1)S(1)} %get-tuple-element.60), channel_id=1, source_target_pairs={{0,8},{1,9},{2,10},{3,11},{4,12},{5,13},{6,14},{7,15},{8,0},{9,1},... | collective-permute-start | bytes 208904 | tf_op jit(solution)/shard_map/ppermute | solution.py:430
  35.0 10.6 %collective-permute-start.4 = (s16[16,2304]{1,0:T(8,128)(2,1)S(1)}, s16[16,2304]{1,0:T(8,128)(2,1)S(1)}, u32[]{:S(2)}, u32[]{:S(2)}) collective-permute-start(s16[16,2304]{1,0:T(8,128)(2,1)S(1)} %get-tuple-element.53), channel_id=1, source_target_pairs={{0,8},{1,9},{2,10},{3,11},{4,12},{5,13},{6,14},{7,15},{8,0},{9,1},... | collective-permute-start | bytes 221192 | tf_op jit(solution)/shard_map/ppermute | solution.py:430
  47.5 10.4 %all-to-all-start = ((bf16[16,16,128]{2,1,0:T(8,128)(2,1)}), bf16[16,16,128]{2,1,0:T(8,128)(2,1)S(1)}, u32[]{:S(2)}, u32[]{:S(2)}) async-start(bf16[16,16,128]{2,1,0:T(8,128)(2,1)} %values_part.1), calls=%async_computation | async-start | bytes 131072 | tf_op jit(solution)/shard_map/all_to_all | solution.py:526

commit v8 on v7

--- a/solution.py
+++ b/solution.py
@@ -342,13 +342,10 @@
         gates = product(gate_refs[0][...], gate_refs[1][...], (((1,), (1,)), ((), ())))
         zeros = jnp.zeros((gates.shape[0], 2 * DK - gates.shape[1]), jnp.float32)
         total = jnp.concatenate([total, gates, zeros], axis=1)
+    if crossed:
+        starts = [start for at in range(0, half, ROWS) for start in (at, half + at)]
+        total = jnp.concatenate([total[start : start + ROWS] for start in starts], axis=0)
     kept, sent = total[:half], total[half:]
-    if crossed:
-        quarter = half // 2
-        kept, sent = (
-            jnp.concatenate([kept[:quarter], sent[:quarter]], axis=0),
-            jnp.concatenate([kept[quarter:], sent[quarter:]], axis=0),
-        )
     kept_ref[...] = kept
     pack_rows(sent, packed_ref)
 
@@ -493,7 +490,7 @@
     )
     blank = jnp.zeros((1, carried.shape[2]), jnp.float32)
     history = jnp.concatenate([blank, carried[1], blank, carried[0]], axis=0)
-    routes = [[bits[1], bits[0]] + bits[2:], bits, bits]
+    routes = [bits[1:] + bits[:1], bits, bits]
     kept = [chunk[0] for chunk in (queries, keys, values)]
     got = [
         swap(chunk[1], route[0], devices)

time: 59.1 us -> 57.3 us (0.970)
  waiting for transfers between devices: 20.7 us -> 17.9 us
  starting transfers between devices: 19.1 us -> 20.2 us
    ppermute x15, waiting for transfers between devices: 14 us -> 11.2 us  [swap(): return lax.ppermute(value, 'heads', [(i, i ^ bit) for i in range(devices)])]
    ppermute x15, starting transfers between devices: 15.6 us -> 16.7 us  [swap(): return lax.ppermute(value, 'heads', [(i, i ^ bit) for i in range(devices)])]
  transfers between devices with their start and end apart: 16 -> 16, of which waited for: 7 -> 6; matrix products, arithmetic and copies ran while one was open for 3% -> 3% of each run, Pallas kernels for 17% -> 18%
where the time goes in v8:
time: 57.3 us; the launch traced here: 57 us
  starting transfers between devices  20.2 us (35%)
  waiting for transfers between devices  17.9 us (31%)
  Pallas kernels  12.2 us (21%)
  local copies, waits for them, and re-layouts  5.54 us (10%)
  other arithmetic  0.66 us (1%)
    ppermute x15, starting transfers between devices, swap(): return lax.ppermute(value, 'heads', [(i, i ^ bit) for i in range(devices)])  16.7 us
    ppermute x15, waiting for transfers between devices, swap(): return lax.ppermute(value, 'heads', [(i, i ^ bit) for i in range(devices)])  11.2 us
    all_to_all x1, waiting for transfers between devices, on_device(): lax.all_to_all(sending, 'heads', split_axis=0, concat_axis=0, tiled=True)  6.68 us
    unnamed x20, local copies, waits for them, and re-layouts  3.76 us
    all_to_all x1, starting transfers between devices, on_device(): lax.all_to_all(sending, 'heads', split_axis=0, concat_axis=0, tiled=True)  3.5 us
    pallas_call x3, Pallas kernels, run_product(): pl.pallas_call(functools.partial(product_kernel, len(earlier), crossed),...  3.39 us
    pallas_call x1, Pallas kernels, run_delta(): pl.pallas_call(keys_kernel, out_shape=[per_head] * 2 + lags + [tap_blocks...  2.81 us
    pallas_call x6, Pallas kernels, run_combine(): pl.pallas_call(combine_kernel, out_shape=[jax.ShapeDtypeStruct((half, wid...  2.8 us
  transfers between devices with their start and end apart: 16, of which 6 were waited for; matrix products, arithmetic and copies ran while one was open for 3% of the time, Pallas kernels for 18%

profile of v8, /device:TPU:0, one launch (start us, length us, event | category | flops | bytes accessed | tf_op | source)
XLA Modules:
  0.0 57.0 jit_solution(4734068621876680554)
XLA Ops:
  0.0 0.5 collective-permute-start
  0.5 0.7 %fusion.6 = (bf16[4,384]{1,0:T(4,128)(2,1)S(1)}, bf16[4,384]{1,0:T(4,128)(2,1)S(1)}) fusion(bf16[4,768]{1,0:T(4,128)(2,1)} %param.13), kind=kLoop, calls=%fused_computation.27 | loop fusion | bytes 12288 | tf_op jit(solution)/shard_map/slice | solution.py:452
  1.2 2.6 %collective-permute-start.5 = (bf16[8,384]{1,0:T(8,128)(2,1)S(1)}, bf16[8,384]{1,0:T(8,128)(2,1)S(1)}, u32[]{:S(2)}, u32[]{:S(2)}) collective-permute-start(bf16[8,384]{1,0:T(8,128)(2,1)S(1)} %pad_maximum_fusion.1.first_ref), channel_id=1, source_target_pairs={{0,4},{1,5},{2,6},{3,7},{4,0},{5,1},{6,2},{7,3},{8,12},{9,13},{10,... | collective-permute-start | bytes 18440 | tf_op jit(solution)/shard_map/ppermute | solution.py:427
  4.0 2.0 %copy-done.1 = bf16[144,12288]{1,0:T(8,128)(2,1)S(1)} copy-done((bf16[144,12288]{1,0:T(8,128)(2,1)S(1)}, bf16[144,12288]{1,0:T(8,128)(2,1)}, u32[]{:S(2)}) %copy-start.1) | copy-done | bytes 3538968
  6.0 1.1 %copy-done.2 = bf16[32,4,2304]{2,1,0:T(4,128)(2,1)S(1)} copy-done((bf16[32,4,2304]{2,1,0:T(4,128)(2,1)S(1)}, bf16[32,4,2304]{2,1,0:T(4,128)(2,1)}, u32[]{:S(2)}) %copy-start.2) | copy-done | bytes 589848
  7.1 0.7 %copy-done.4 = s32[32]{0:T(128)S(1)} copy-done((s32[32]{0:T(128)S(1)}, s32[32]{0:T(128)}, u32[]{:S(2)}) %copy-start.4) | copy-done | bytes 152
  7.8 1.2 %token_rows.1 = (bf16[64,144]{1,0:T(8,128)(2,1)S(1)}, bf16[64,144]{1,0:T(8,128)(2,1)S(1)}, bf16[144,12288]{1,0:T(8,128)(2,1)S(1)}) custom-call(s32[1]{0:T(128)} %bitcast.me_ref.twist_ref, s32[1,32]{1,0:T(1,128)S(1)} %bitcast.14, bf16[32,4,2304]{2,1,0:T(4,128)(2,1)S(1)} %copy-done.2, bf16[144,12288]{1,0:T(8,128)(2,1)S(1)} %copy-done.1), custom_call_target="tpu_custom_call" | custom-call | tf_op jit(solution)/shard_map/token_rows/pallas_call | solution.py:310
  9.0 2.7 %collective-permute-start.6 = (bf16[16,384]{1,0:T(8,128)(2,1)S(1)}, bf16[16,384]{1,0:T(8,128)(2,1)S(1)}, u32[]{:S(2)}, u32[]{:S(2)}) collective-permute-start(bf16[16,384]{1,0:T(8,128)(2,1)S(1)} %join_taps.3.first_ref), channel_id=1, source_target_pairs={{0,8},{1,9},{2,10},{3,11},{4,12},{5,13},{6,14},{7,15},{8,0},{9,1},... | collective-permute-start | bytes 36872 | tf_op jit(solution)/shard_map/ppermute | solution.py:427
  11.7 0.8 %partial_product.3 = (f32[32,4096]{1,0:T(8,128)S(1)}, s16[32,4224]{1,0:T(8,128)(2,1)S(1)}) custom-call(bf16[64,144]{1,0:T(8,128)(2,1)S(1)} %get-tuple-element.38.refs_0_.refs_1_.earlier_ref.refs_2_, bf16[64,144]{1,0:T(8,128)(2,1)S(1)} %get-tuple-element.39.refs_1_.refs_2_.refs_3_, bf16[144,12288]{1,0:T(8,128)(2,1)S(1)} %get-tuple-element.40.refs_2_.refs_3_.refs_4_, ...), custom_call_target="tpu_custom_call" | custom-call | tf_op jit(solution)/shard_map/partial_product/pallas_call | solution.py:358
  12.5 1.6 %collective-permute-start.10 = (s16[32,4224]{1,0:T(8,128)(2,1)S(1)}, s16[32,4224]{1,0:T(8,128)(2,1)S(1)}, u32[]{:S(2)}, u32[]{:S(2)}) collective-permute-start(s16[32,4224]{1,0:T(8,128)(2,1)S(1)} %get-tuple-element.61), channel_id=1, source_target_pairs={{0,2},{1,3},{2,0},{3,1},{4,6},{5,7},{6,4},{7,5},{8,10},{9,11},{10,... | collective-permute-start | bytes 811016 | tf_op jit(solution)/shard_map/ppermute | solution.py:427
  14.1 1.7 %partial_product.4 = (f32[32,4352]{1,0:T(8,128)S(1)}, s16[32,4480]{1,0:T(8,128)(2,1)S(1)}) custom-call(f32[32,4096]{1,0:T(8,128)S(1)} %get-tuple-element.41.refs_0_.kept_ref, bf16[64,144]{1,0:T(8,128)(2,1)S(1)} %get-tuple-element.38.refs_0_.refs_1_.earlier_ref.refs_2_, bf16[64,144]{1,0:T(8,128)(2,1)S(1)} %get-tuple-element.39.refs_1_.refs_2_.refs_3_, ...), custom_call_target="tpu_custom_call" | custom-call | tf_op jit(solution)/shard_map/partial_product/pallas_call | solution.py:358
  15.9 0.6 collective-permute-start.13
  16.5 0.8 %partial_product.5 = (f32[32,4096]{1,0:T(8,128)S(1)}, s16[32,4224]{1,0:T(8,128)(2,1)S(1)}) custom-call(f32[32,4352]{1,0:T(8,128)S(1)} %get-tuple-element.48.kept_ref.earlier_ref.refs_0_, bf16[32,384]{1,0:T(8,128)(2,1)S(1)} %join_taps.4.refs_1_.first_ref, bf16[64,144]{1,0:T(8,128)(2,1)S(1)} %get-tuple-element.38.refs_0_.refs_1_.earlier_ref.refs_2_, ...), custom_call_target="tpu_custom_call" | custom-call | tf_op jit(solution)/shard_map/partial_product/pallas_call | solution.py:358
  17.4 0.5 collective-permute-start.7
  17.9 1.5 %collective-permute-start.2 = (s16[32,4480]{1,0:T(8,128)(2,1)S(1)}, s16[32,4480]{1,0:T(8,128)(2,1)S(1)}, u32[]{:S(2)}, u32[]{:S(2)}) collective-permute-start(s16[32,4480]{1,0:T(8,128)(2,1)S(1)} %get-tuple-element.49), channel_id=1, source_target_pairs={{0,2},{1,3},{2,0},{3,1},{4,6},{5,7},{6,4},{7,5},{8,10},{9,11},{10,... | collective-permute-start | bytes 860168 | tf_op jit(solution)/shard_map/ppermute | solution.py:427
  19.9 2.0 %collective-permute-done.10.got_ref = s16[32,4224]{1,0:T(8,128)(2,1)S(1)} collective-permute-done((s16[32,4224]{1,0:T(8,128)(2,1)S(1)}, s16[32,4224]{1,0:T(8,128)(2,1)S(1)}, u32[]{:S(2)}, u32[]{:S(2)}) %collective-permute-start.10) | collective-permute-done | bytes 270368 | tf_op jit(solution)/shard_map/ppermute | solution.py:427
  21.9 0.5 combine.10
  22.7 4.0 %collective-permute-done.7.got_ref = s16[32,4224]{1,0:T(8,128)(2,1)S(1)} collective-permute-done((s16[32,4224]{1,0:T(8,128)(2,1)S(1)}, s16[32,4224]{1,0:T(8,128)(2,1)S(1)}, u32[]{:S(2)}, u32[]{:S(2)}) %collective-permute-start.7) | collective-permute-done | bytes 270368 | tf_op jit(solution)/shard_map/ppermute | solution.py:427
  26.7 0.5 combine.8
  27.2 0.9 %collective-permute-start.8 = (s16[16,4224]{1,0:T(8,128)(2,1)S(1)}, s16[16,4224]{1,0:T(8,128)(2,1)S(1)}, u32[]{:S(2)}, u32[]{:S(2)}) collective-permute-start(s16[16,4224]{1,0:T(8,128)(2,1)S(1)} %get-tuple-element.58), channel_id=1, source_target_pairs={{0,8},{1,9},{2,10},{3,11},{4,12},{5,13},{6,14},{7,15},{8,0},{9,1},... | collective-permute-start | bytes 405512 | tf_op jit(solution)/shard_map/ppermute | solution.py:427
  28.1 0.5 combine.6
  28.6 0.5 collective-permute-start.3
  30.0 2.2 %collective-permute-start.12 = (s16[16,2176]{1,0:T(8,128)(2,1)S(1)}, s16[16,2176]{1,0:T(8,128)(2,1)S(1)}, u32[]{:S(2)}, u32[]{:S(2)}) collective-permute-start(s16[16,2176]{1,0:T(8,128)(2,1)S(1)} %get-tuple-element.65), channel_id=1, source_target_pairs={{0,8},{1,9},{2,10},{3,11},{4,12},{5,13},{6,14},{7,15},{8,0},{9,1},... | collective-permute-start | bytes 208904 | tf_op jit(solution)/shard_map/ppermute | solution.py:427
  32.2 2.9 %collective-permute-done.8.got_ref = s16[16,4224]{1,0:T(8,128)(2,1)S(1)} collective-permute-done((s16[16,4224]{1,0:T(8,128)(2,1)S(1)}, s16[16,4224]{1,0:T(8,128)(2,1)S(1)}, u32[]{:S(2)}, u32[]{:S(2)}) %collective-permute-start.8) | collective-permute-done | bytes 135200 | tf_op jit(solution)/shard_map/ppermute | solution.py:427
  35.5 2.6 %collective-permute-start.9 = (s16[16,2176]{1,0:T(8,128)(2,1)S(1)}, s16[16,2176]{1,0:T(8,128)(2,1)S(1)}, u32[]{:S(2)}, u32[]{:S(2)}) collective-permute-start(s16[16,2176]{1,0:T(8,128)(2,1)S(1)} %get-tuple-element.60), channel_id=1, source_target_pairs={{0,2},{1,3},{2,0},{3,1},{4,6},{5,7},{6,4},{7,5},{8,10},{9,11},{10,... | collective-permute-start | bytes 208904 | tf_op jit(solution)/shard_map/ppermute | solution.py:427
  38.7 1.7 %collective-permute-done.9.query_got_ref = s16[16,2176]{1,0:T(8,128)(2,1)S(1)} collective-permute-done((s16[16,2176]{1,0:T(8,128)(2,1)S(1)}, s16[16,2176]{1,0:T(8,128)(2,1)S(1)}, u32[]{:S(2)}, u32[]{:S(2)}) %collective-permute-start.9) | collective-permute-done | bytes 69664 | tf_op jit(solution)/shard_map/ppermute | solution.py:427
  40.4 2.8 %keys_part.1 = (f32[32,8,128]{2,1,0:T(8,128)S(1)}, f32[32,8,128]{2,1,0:T(8,128)S(1)}, f32[3,32,8,128]{3,2,1,0:T(8,128)S(1)}, f32[4,32,8,128]{3,2,1,0:T(8,128)S(1)}, f32[32,4,384]{2,1,0:T(4,128)S(1)}) custom-call(s32[1]{0:T(128)} %bitcast.me_ref.twist_ref, f32[8,4096]{1,0:T(8,128)S(1)} %get-tuple-element.59.query_ref, ...), custom_call_target="tpu_custom_call" | custom-call | flops 40000000 | bytes 9000000 | tf_op jit(solution)/shard_map/keys_part/pallas_call | solution.py:243
  43.2 0.6 %collective-permute-done.4.value_got_ref = s16[16,2304]{1,0:T(8,128)(2,1)S(1)} collective-permute-done((s16[16,2304]{1,0:T(8,128)(2,1)S(1)}, s16[16,2304]{1,0:T(8,128)(2,1)S(1)}, u32[]{:S(2)}, u32[]{:S(2)}) %collective-permute-start.4) | collective-permute-done | bytes 73760 | tf_op jit(solution)/shard_map/ppermute | solution.py:427
  43.8 1.9 %values_part.1 = bf16[16,16,128]{2,1,0:T(8,128)(2,1)} custom-call(s32[64]{0:T(128)S(1)} %select_reduce_fusion.slots_ref, s32[64]{0:T(128)S(1)} %get-tuple-element.77.halves_ref, s32[2]{0:T(128)S(1)} %fusion.4.lengths_ref, s32[1]{0:T(128)} %bitcast.me_ref.twist_ref, f32[8,4352]{1,0:T(8,128)S(1)} %get-tuple-element.52.value_ref, ...), custom_call_target="tpu_custom_call" | custom-call | flops 4000000 | bytes 2000000 | tf_op jit(solution)/shard_map/values_part/pallas_call | solution.py:256
  45.7 3.5 %all-to-all-start = ((bf16[16,16,128]{2,1,0:T(8,128)(2,1)}), bf16[16,16,128]{2,1,0:T(8,128)(2,1)S(1)}, u32[]{:S(2)}, u32[]{:S(2)}) async-start(bf16[16,16,128]{2,1,0:T(8,128)(2,1)} %values_part.1), calls=%async_computation | async-start | bytes 131072 | tf_op jit(solution)/shard_map/all_to_all | solution.py:523
  49.4 6.7 %all-to-all-done = bf16[16,16,128]{2,1,0:T(8,128)(2,1)S(1)} async-done(((bf16[16,16,128]{2,1,0:T(8,128)(2,1)}), bf16[16,16,128]{2,1,0:T(8,128)(2,1)S(1)}, u32[]{:S(2)}, u32[]{:S(2)}) %all-to-all-start) | async-done | bytes 65568 | tf_op jit(solution)/shard_map/all_to_all | solution.py:523
  56.3 0.7 %reshape.46 = bf16[32,4,256]{2,1,0:T(4,128)(2,1)} reshape(bf16[128,256]{1,0:T(8,128)(2,1)S(1)} %convolution_convert_fusion) | data formatting | bytes 131072 | tf_op jit(solution)/shard_map/reshape | solution.py:534
  (52 shorter events, 3.2 us)
Async XLA Ops:
  0.0 11.7 %collective-permute-start = (bf16[144,12288]{1,0:T(8,128)(2,1)}, bf16[144,12288]{1,0:T(8,128)(2,1)S(1)}, u32[]{:S(2)}, u32[]{:S(2)}) collective-permute-start(bf16[144,12288]{1,0:T(8,128)(2,1)} %weight_hbm.1), channel_id=1, source_target_pairs={{0,1},{1,0},{2,3},{3,2},{4,5},{5,4},{6,7},{7,6},{8,9},{9,8},{10,11... | collective-permute-start | bytes 10616840 | tf_op jit(solution)/shard_map/ppermute | solution.py:427
  1.2 7.8 %collective-permute-start.5 = (bf16[8,384]{1,0:T(8,128)(2,1)S(1)}, bf16[8,384]{1,0:T(8,128)(2,1)S(1)}, u32[]{:S(2)}, u32[]{:S(2)}) collective-permute-start(bf16[8,384]{1,0:T(8,128)(2,1)S(1)} %pad_maximum_fusion.1.first_ref), channel_id=1, source_target_pairs={{0,4},{1,5},{2,6},{3,7},{4,0},{5,1},{6,2},{7,3},{8,12},{9,13},{10,... | collective-permute-start | bytes 18440 | tf_op jit(solution)/shard_map/ppermute | solution.py:427
  3.8 10.3 %collective-permute-start.1 = (bf16[64,144]{1,0:T(8,128)(2,1)}, bf16[64,144]{1,0:T(8,128)(2,1)}, u32[]{:S(2)}, u32[]{:S(2)}) collective-permute-start(bf16[64,144]{1,0:T(8,128)(2,1)} %bitcast.12), channel_id=1, source_target_pairs={{0,1},{1,0},{2,3},{3,2},{4,5},{5,4},{6,7},{7,6},{8,9},{9,8},{10,11... | collective-permute-start | bytes 55304 | tf_op jit(solution)/shard_map/ppermute | solution.py:427
  4.0 2.0 %copy-start.1 = (bf16[144,12288]{1,0:T(8,128)(2,1)S(1)}, bf16[144,12288]{1,0:T(8,128)(2,1)}, u32[]{:S(2)}) copy-start(bf16[144,12288]{1,0:T(8,128)(2,1)} %weight_hbm.1) | copy-start | bytes 10616836
  6.0 1.1 %copy-start.2 = (bf16[32,4,2304]{2,1,0:T(4,128)(2,1)S(1)}, bf16[32,4,2304]{2,1,0:T(4,128)(2,1)}, u32[]{:S(2)}) copy-start(bf16[32,4,2304]{2,1,0:T(4,128)(2,1)} %tokens_hbm.1) | copy-start | bytes 1769476
  7.1 0.7 %copy-start.4 = (s32[32]{0:T(128)S(1)}, s32[32]{0:T(128)}, u32[]{:S(2)}) copy-start(s32[32]{0:T(128)} %param.18) | copy-start | bytes 388
  9.0 6.8 %collective-permute-start.6 = (bf16[16,384]{1,0:T(8,128)(2,1)S(1)}, bf16[16,384]{1,0:T(8,128)(2,1)S(1)}, u32[]{:S(2)}, u32[]{:S(2)}) collective-permute-start(bf16[16,384]{1,0:T(8,128)(2,1)S(1)} %join_taps.3.first_ref), channel_id=1, source_target_pairs={{0,8},{1,9},{2,10},{3,11},{4,12},{5,13},{6,14},{7,15},{8,0},{9,1},... | collective-permute-start | bytes 36872 | tf_op jit(solution)/shard_map/ppermute | solution.py:427
  11.7 2.4 %copy-start.3 = (bf16[144,64]{0,1:T(8,128)(2,1)S(1)}, bf16[144,64]{0,1:T(8,128)(2,1)}, u32[]{:S(2)}) copy-start(bf16[144,64]{0,1:T(8,128)(2,1)} %param.12) | copy-start | bytes 55300
  12.5 9.4 %collective-permute-start.10 = (s16[32,4224]{1,0:T(8,128)(2,1)S(1)}, s16[32,4224]{1,0:T(8,128)(2,1)S(1)}, u32[]{:S(2)}, u32[]{:S(2)}) collective-permute-start(s16[32,4224]{1,0:T(8,128)(2,1)S(1)} %get-tuple-element.61), channel_id=1, source_target_pairs={{0,2},{1,3},{2,0},{3,1},{4,6},{5,7},{6,4},{7,5},{8,10},{9,11},{10,... | collective-permute-start | bytes 811016 | tf_op jit(solution)/shard_map/ppermute | solution.py:427
  15.9 3.5 %copy-start.6 = (f32[2,3,12288]{2,0,1:T(2,128)S(1)}, f32[2,3,12288]{2,0,1:T(2,128)}, u32[]{:S(2)}) copy-start(f32[2,3,12288]{2,0,1:T(2,128)} %param.15) | copy-start | bytes 884740
  15.9 4.0 %copy-start.5 = (s32[32]{0:T(128)S(1)}, s32[32]{0:T(128)}, u32[]{:S(2)}) copy-start(s32[32]{0:T(128)} %param.18) | copy-start | bytes 388
  15.9 4.0 %copy-start.8 = (s32[64]{0:T(128)S(1)}, s32[64]{0:T(128)}, u32[]{:S(2)}) copy-start(s32[64]{0:T(128)} %param.17) | copy-start | bytes 772
  15.9 13.5 %collective-permute-start.13 = (bf16[32,384]{1,0:T(8,128)(2,1)S(1)}, bf16[32,384]{1,0:T(8,128)(2,1)S(1)}, u32[]{:S(2)}, u32[]{:S(2)}) collective-permute-start(bf16[32,384]{1,0:T(8,128)(2,1)S(1)} %join_taps.4.refs_1_.first_ref), channel_id=1, source_target_pairs={{0,2},{1,3},{2,0},{3,1},{4,6},{5,7},{6,4},{7,5},{8,10},{9,11},{10,... | collective-permute-start | bytes 73736 | tf_op jit(solution)/shard_map/ppermute | solution.py:427
  17.3 11.8 %copy-start.7 = (s32[32]{0:T(128)S(1)}, s32[32]{0:T(128)}, u32[]{:S(2)}) copy-start(s32[32]{0:T(128)} %param.19) | copy-start | bytes 388
  17.3 12.0 %copy-start.9 = (s32[32]{0:T(128)S(1)}, s32[32]{0:T(128)}, u32[]{:S(2)}) copy-start(s32[32]{0:T(128)} %param.16) | copy-start | bytes 388
  17.3 23.0 %copy-start = (f32[2,32,128,128]{3,2,1,0:T(8,128)S(1)}, f32[2,32,128,128]{3,2,1,0:T(8,128)}, u32[]{:S(2)}) copy-start(f32[2,32,128,128]{3,2,1,0:T(8,128)} %state_hbm.1) | copy-start | bytes 12582916
  17.4 9.3 %collective-permute-start.7 = (s16[32,4224]{1,0:T(8,128)(2,1)S(1)}, s16[32,4224]{1,0:T(8,128)(2,1)S(1)}, u32[]{:S(2)}, u32[]{:S(2)}) collective-permute-start(s16[32,4224]{1,0:T(8,128)(2,1)S(1)} %get-tuple-element.56), channel_id=1, source_target_pairs={{0,4},{1,5},{2,6},{3,7},{4,0},{5,1},{6,2},{7,3},{8,12},{9,13},{10,... | collective-permute-start | bytes 811016 | tf_op jit(solution)/shard_map/ppermute | solution.py:427
  17.9 10.2 %collective-permute-start.2 = (s16[32,4480]{1,0:T(8,128)(2,1)S(1)}, s16[32,4480]{1,0:T(8,128)(2,1)S(1)}, u32[]{:S(2)}, u32[]{:S(2)}) collective-permute-start(s16[32,4480]{1,0:T(8,128)(2,1)S(1)} %get-tuple-element.49), channel_id=1, source_target_pairs={{0,2},{1,3},{2,0},{3,1},{4,6},{5,7},{6,4},{7,5},{8,10},{9,11},{10,... | collective-permute-start | bytes 860168 | tf_op jit(solution)/shard_map/ppermute | solution.py:427
  22.5 7.1 %collective-permute-start.11 = (s16[16,4224]{1,0:T(8,128)(2,1)S(1)}, s16[16,4224]{1,0:T(8,128)(2,1)S(1)}, u32[]{:S(2)}, u32[]{:S(2)}) collective-permute-start(s16[16,4224]{1,0:T(8,128)(2,1)S(1)} %get-tuple-element.63), channel_id=1, source_target_pairs={{0,4},{1,5},{2,6},{3,7},{4,0},{5,1},{6,2},{7,3},{8,12},{9,13},{10,... | collective-permute-start | bytes 405512 | tf_op jit(solution)/shard_map/ppermute | solution.py:427
  27.2 7.9 %collective-permute-start.8 = (s16[16,4224]{1,0:T(8,128)(2,1)S(1)}, s16[16,4224]{1,0:T(8,128)(2,1)S(1)}, u32[]{:S(2)}, u32[]{:S(2)}) collective-permute-start(s16[16,4224]{1,0:T(8,128)(2,1)S(1)} %get-tuple-element.58), channel_id=1, source_target_pairs={{0,8},{1,9},{2,10},{3,11},{4,12},{5,13},{6,14},{7,15},{8,0},{9,1},... | collective-permute-start | bytes 405512 | tf_op jit(solution)/shard_map/ppermute | solution.py:427
  28.6 9.4 %collective-permute-start.3 = (s16[16,4480]{1,0:T(8,128)(2,1)S(1)}, s16[16,4480]{1,0:T(8,128)(2,1)S(1)}, u32[]{:S(2)}, u32[]{:S(2)}) collective-permute-start(s16[16,4480]{1,0:T(8,128)(2,1)S(1)} %get-tuple-element.51), channel_id=1, source_target_pairs={{0,4},{1,5},{2,6},{3,7},{4,0},{5,1},{6,2},{7,3},{8,12},{9,13},{10,... | collective-permute-start | bytes 430088 | tf_op jit(solution)/shard_map/ppermute | solution.py:427
  29.5 9.2 %collective-permute-start.14 = (bf16[64,384]{1,0:T(8,128)(2,1)S(1)}, bf16[64,384]{1,0:T(8,128)(2,1)S(1)}, u32[]{:S(2)}, u32[]{:S(2)}) collective-permute-start(bf16[64,384]{1,0:T(8,128)(2,1)S(1)} %join_taps.5.near_ref), channel_id=1, source_target_pairs={{0,1},{1,0},{2,3},{3,2},{4,5},{5,4},{6,7},{7,6},{8,9},{9,8},{10,11... | collective-permute-start | bytes 147464 | tf_op jit(solution)/shard_map/ppermute | solution.py:427
  30.0 8.7 %collective-permute-start.12 = (s16[16,2176]{1,0:T(8,128)(2,1)S(1)}, s16[16,2176]{1,0:T(8,128)(2,1)S(1)}, u32[]{:S(2)}, u32[]{:S(2)}) collective-permute-start(s16[16,2176]{1,0:T(8,128)(2,1)S(1)} %get-tuple-element.65), channel_id=1, source_target_pairs={{0,8},{1,9},{2,10},{3,11},{4,12},{5,13},{6,14},{7,15},{8,0},{9,1},... | collective-permute-start | bytes 208904 | tf_op jit(solution)/shard_map/ppermute | solution.py:427
  35.5 4.8 %collective-permute-start.9 = (s16[16,2176]{1,0:T(8,128)(2,1)S(1)}, s16[16,2176]{1,0:T(8,128)(2,1)S(1)}, u32[]{:S(2)}, u32[]{:S(2)}) collective-permute-start(s16[16,2176]{1,0:T(8,128)(2,1)S(1)} %get-tuple-element.60), channel_id=1, source_target_pairs={{0,2},{1,3},{2,0},{3,1},{4,6},{5,7},{6,4},{7,5},{8,10},{9,11},{10,... | collective-permute-start | bytes 208904 | tf_op jit(solution)/shard_map/ppermute | solution.py:427
  38.5 5.3 %collective-permute-start.4 = (s16[16,2304]{1,0:T(8,128)(2,1)S(1)}, s16[16,2304]{1,0:T(8,128)(2,1)S(1)}, u32[]{:S(2)}, u32[]{:S(2)}) collective-permute-start(s16[16,2304]{1,0:T(8,128)(2,1)S(1)} %get-tuple-element.53), channel_id=1, source_target_pairs={{0,8},{1,9},{2,10},{3,11},{4,12},{5,13},{6,14},{7,15},{8,0},{9,1},... | collective-permute-start | bytes 221192 | tf_op jit(solution)/shard_map/ppermute | solution.py:427
  45.7 10.4 %all-to-all-start = ((bf16[16,16,128]{2,1,0:T(8,128)(2,1)}), bf16[16,16,128]{2,1,0:T(8,128)(2,1)S(1)}, u32[]{:S(2)}, u32[]{:S(2)}) async-start(bf16[16,16,128]{2,1,0:T(8,128)(2,1)} %values_part.1), calls=%async_computation | async-start | bytes 131072 | tf_op jit(solution)/shard_map/all_to_all | solution.py:523

commit v9 on v8

--- a/solution.py
+++ b/solution.py
@@ -473,10 +473,7 @@
         far = swap(taps, 8, devices)
     keys = run_product(mine, theirs, weights, 1)
     values = run_product(mine, theirs, weights, 2, gates, earlier=keys[:1])
-    if ride:
-        taps = join(taps, far, values[0])
-        far = swap(taps, 2, devices)
-    queries = run_product(mine, theirs, weights, 0, earlier=(values[0], taps), crossed=True)
+    queries = run_product(mine, theirs, weights, 0, earlier=values[:1], crossed=True)
 
     slot_of, lengths, old_heads, new_units, carried, *values = tie(
         slot_of, lengths, old_heads, new_units, conv_state, *values
@@ -500,9 +497,9 @@
         for at in range(3):
             kept[at], packed = run_combine(kept[at], got[at])
             got[at] = swap(packed, routes[at][level], devices)
-        if ride and level == 1:
-            taps = join(taps, far, kept[2])
-            far = swap(taps, 1, devices)
+            if ride and at == 2 - level:
+                taps = join(taps, far, kept[at])
+                far = swap(taps, 3 - level, devices)
     if ride:
         twist, taps = me.reshape(1), (taps, far)
     else:

time: 57.3 us -> 57.1 us (level)
  starting transfers between devices: 20.2 us -> 16 us
  waiting for transfers between devices: 17.9 us -> 21.8 us
    ppermute x15, starting transfers between devices: 16.7 us -> 12.5 us  [swap(): return lax.ppermute(value, 'heads', [(i, i ^ bit) for i in range(devices)])]
    ppermute x15, waiting for transfers between devices: 11.2 us -> 15.2 us  [swap(): return lax.ppermute(value, 'heads', [(i, i ^ bit) for i in range(devices)])]
  transfers between devices with their start and end apart: 16 -> 16, of which waited for: 6 -> 7; matrix products, arithmetic and copies ran while one was open for 3% -> 3% of each run, Pallas kernels for 18% -> 18%
where the time goes in v9:
time: 57.1 us; the launch traced here: 56.7 us
  waiting for transfers between devices  21.8 us (38%)
  starting transfers between devices  16 us (28%)
  Pallas kernels  12.2 us (21%)
  local copies, waits for them, and re-layouts  5.54 us (10%)
  other arithmetic  0.66 us (1%)
    ppermute x15, waiting for transfers between devices, swap(): return lax.ppermute(value, 'heads', [(i, i ^ bit) for i in range(devices)])  15.2 us
    ppermute x15, starting transfers between devices, swap(): return lax.ppermute(value, 'heads', [(i, i ^ bit) for i in range(devices)])  12.5 us
    all_to_all x1, waiting for transfers between devices, on_device(): lax.all_to_all(sending, 'heads', split_axis=0, concat_axis=0, tiled=True)  6.68 us
    unnamed x20, local copies, waits for them, and re-layouts  3.76 us
    all_to_all x1, starting transfers between devices, on_device(): lax.all_to_all(sending, 'heads', split_axis=0, concat_axis=0, tiled=True)  3.5 us
    pallas_call x3, Pallas kernels, run_product(): pl.pallas_call(functools.partial(product_kernel, len(earlier), crossed),...  3.39 us
    pallas_call x1, Pallas kernels, run_delta(): pl.pallas_call(keys_kernel, out_shape=[per_head] * 2 + lags + [tap_blocks...  2.81 us
    pallas_call x6, Pallas kernels, run_combine(): pl.pallas_call(combine_kernel, out_shape=[jax.ShapeDtypeStruct((half, wid...  2.8 us
  transfers between devices with their start and end apart: 16, of which 7 were waited for; matrix products, arithmetic and copies ran while one was open for 3% of the time, Pallas kernels for 18%

profile of v9, /device:TPU:0, one launch (start us, length us, event | category | flops | bytes accessed | tf_op | source)
XLA Modules:
  0.0 56.7 jit_solution(4090864111734353466)
XLA Ops:
  0.0 0.5 collective-permute-start
  0.5 0.7 %fusion.6 = (bf16[4,384]{1,0:T(4,128)(2,1)S(1)}, bf16[4,384]{1,0:T(4,128)(2,1)S(1)}) fusion(bf16[4,768]{1,0:T(4,128)(2,1)} %param.13), kind=kLoop, calls=%fused_computation.27 | loop fusion | bytes 12288 | tf_op jit(solution)/shard_map/slice | solution.py:452
  1.2 2.6 %collective-permute-start.11 = (bf16[8,384]{1,0:T(8,128)(2,1)S(1)}, bf16[8,384]{1,0:T(8,128)(2,1)S(1)}, u32[]{:S(2)}, u32[]{:S(2)}) collective-permute-start(bf16[8,384]{1,0:T(8,128)(2,1)S(1)} %pad_maximum_fusion.1.first_ref), channel_id=1, source_target_pairs={{0,4},{1,5},{2,6},{3,7},{4,0},{5,1},{6,2},{7,3},{8,12},{9,13},{10,... | collective-permute-start | bytes 18440 | tf_op jit(solution)/shard_map/ppermute | solution.py:427
  4.0 2.0 %copy-done.1 = bf16[144,12288]{1,0:T(8,128)(2,1)S(1)} copy-done((bf16[144,12288]{1,0:T(8,128)(2,1)S(1)}, bf16[144,12288]{1,0:T(8,128)(2,1)}, u32[]{:S(2)}) %copy-start.1) | copy-done | bytes 3538968
  6.0 1.1 %copy-done.2 = bf16[32,4,2304]{2,1,0:T(4,128)(2,1)S(1)} copy-done((bf16[32,4,2304]{2,1,0:T(4,128)(2,1)S(1)}, bf16[32,4,2304]{2,1,0:T(4,128)(2,1)}, u32[]{:S(2)}) %copy-start.2) | copy-done | bytes 589848
  7.1 0.7 %copy-done.4 = s32[32]{0:T(128)S(1)} copy-done((s32[32]{0:T(128)S(1)}, s32[32]{0:T(128)}, u32[]{:S(2)}) %copy-start.4) | copy-done | bytes 152
  7.8 1.2 %token_rows.1 = (bf16[64,144]{1,0:T(8,128)(2,1)S(1)}, bf16[64,144]{1,0:T(8,128)(2,1)S(1)}, bf16[144,12288]{1,0:T(8,128)(2,1)S(1)}) custom-call(s32[1]{0:T(128)} %bitcast.me_ref.twist_ref, s32[1,32]{1,0:T(1,128)S(1)} %bitcast.14, bf16[32,4,2304]{2,1,0:T(4,128)(2,1)S(1)} %copy-done.2, bf16[144,12288]{1,0:T(8,128)(2,1)S(1)} %copy-done.1), custom_call_target="tpu_custom_call" | custom-call | tf_op jit(solution)/shard_map/token_rows/pallas_call | solution.py:310
  9.0 2.7 %collective-permute-start.12 = (bf16[16,384]{1,0:T(8,128)(2,1)S(1)}, bf16[16,384]{1,0:T(8,128)(2,1)S(1)}, u32[]{:S(2)}, u32[]{:S(2)}) collective-permute-start(bf16[16,384]{1,0:T(8,128)(2,1)S(1)} %join_taps.3.first_ref), channel_id=1, source_target_pairs={{0,8},{1,9},{2,10},{3,11},{4,12},{5,13},{6,14},{7,15},{8,0},{9,1},... | collective-permute-start | bytes 36872 | tf_op jit(solution)/shard_map/ppermute | solution.py:427
  11.7 0.8 %partial_product.3 = (f32[32,4096]{1,0:T(8,128)S(1)}, s16[32,4224]{1,0:T(8,128)(2,1)S(1)}) custom-call(bf16[64,144]{1,0:T(8,128)(2,1)S(1)} %get-tuple-element.38.refs_0_.refs_1_.earlier_ref, bf16[64,144]{1,0:T(8,128)(2,1)S(1)} %get-tuple-element.39.refs_1_.refs_2_, bf16[144,12288]{1,0:T(8,128)(2,1)S(1)} %get-tuple-element.40.refs_2_.refs_3_, ...), custom_call_target="tpu_custom_call" | custom-call | tf_op jit(solution)/shard_map/partial_product/pallas_call | solution.py:358
  12.5 1.6 %collective-permute-start.8 = (s16[32,4224]{1,0:T(8,128)(2,1)S(1)}, s16[32,4224]{1,0:T(8,128)(2,1)S(1)}, u32[]{:S(2)}, u32[]{:S(2)}) collective-permute-start(s16[32,4224]{1,0:T(8,128)(2,1)S(1)} %get-tuple-element.61), channel_id=1, source_target_pairs={{0,2},{1,3},{2,0},{3,1},{4,6},{5,7},{6,4},{7,5},{8,10},{9,11},{10,... | collective-permute-start | bytes 811016 | tf_op jit(solution)/shard_map/ppermute | solution.py:427
  14.1 1.7 %partial_product.4 = (f32[32,4352]{1,0:T(8,128)S(1)}, s16[32,4480]{1,0:T(8,128)(2,1)S(1)}) custom-call(f32[32,4096]{1,0:T(8,128)S(1)} %get-tuple-element.41.refs_0_.kept_ref, bf16[64,144]{1,0:T(8,128)(2,1)S(1)} %get-tuple-element.38.refs_0_.refs_1_.earlier_ref, bf16[64,144]{1,0:T(8,128)(2,1)S(1)} %get-tuple-element.39.refs_1_.refs_2_, ...), custom_call_target="tpu_custom_call" | custom-call | tf_op jit(solution)/shard_map/partial_product/pallas_call | solution.py:358
  15.9 0.8 %partial_product.5 = (f32[32,4096]{1,0:T(8,128)S(1)}, s16[32,4224]{1,0:T(8,128)(2,1)S(1)}) custom-call(f32[32,4352]{1,0:T(8,128)S(1)} %get-tuple-element.48.kept_ref.refs_0_, bf16[64,144]{1,0:T(8,128)(2,1)S(1)} %get-tuple-element.38.refs_0_.refs_1_.earlier_ref, bf16[64,144]{1,0:T(8,128)(2,1)S(1)} %get-tuple-element.39.refs_1_.refs_2_, ...), custom_call_target="tpu_custom_call" | custom-call | tf_op jit(solution)/shard_map/partial_product/pallas_call | solution.py:358
  16.8 0.5 collective-permute-start.5
  17.3 0.5 collective-permute-start.2
  18.3 3.6 %collective-permute-done.8.got_ref = s16[32,4224]{1,0:T(8,128)(2,1)S(1)} collective-permute-done((s16[32,4224]{1,0:T(8,128)(2,1)S(1)}, s16[32,4224]{1,0:T(8,128)(2,1)S(1)}, u32[]{:S(2)}, u32[]{:S(2)}) %collective-permute-start.8) | collective-permute-done | bytes 270368 | tf_op jit(solution)/shard_map/ppermute | solution.py:427
  21.9 0.5 combine.10
  22.5 3.7 %collective-permute-done.5.got_ref = s16[32,4224]{1,0:T(8,128)(2,1)S(1)} collective-permute-done((s16[32,4224]{1,0:T(8,128)(2,1)S(1)}, s16[32,4224]{1,0:T(8,128)(2,1)S(1)}, u32[]{:S(2)}, u32[]{:S(2)}) %collective-permute-start.5) | collective-permute-done | bytes 270368 | tf_op jit(solution)/shard_map/ppermute | solution.py:427
  26.2 0.5 combine.8
  26.7 0.4 collective-permute-start.6
  27.1 0.5 combine.6
  27.7 0.5 collective-permute-start.3
  28.4 1.5 %collective-permute-start.13 = (bf16[32,384]{1,0:T(8,128)(2,1)S(1)}, bf16[32,384]{1,0:T(8,128)(2,1)S(1)}, u32[]{:S(2)}, u32[]{:S(2)}) collective-permute-start(bf16[32,384]{1,0:T(8,128)(2,1)S(1)} %join_taps.4.first_ref), channel_id=1, source_target_pairs={{0,2},{1,3},{2,0},{3,1},{4,6},{5,7},{6,4},{7,5},{8,10},{9,11},{10,... | collective-permute-start | bytes 73736 | tf_op jit(solution)/shard_map/ppermute | solution.py:427
  30.1 0.4 combine.11
  30.5 1.2 %collective-permute-start.10 = (s16[16,2176]{1,0:T(8,128)(2,1)S(1)}, s16[16,2176]{1,0:T(8,128)(2,1)S(1)}, u32[]{:S(2)}, u32[]{:S(2)}) collective-permute-start(s16[16,2176]{1,0:T(8,128)(2,1)S(1)} %get-tuple-element.65), channel_id=1, source_target_pairs={{0,8},{1,9},{2,10},{3,11},{4,12},{5,13},{6,14},{7,15},{8,0},{9,1},... | collective-permute-start | bytes 208904 | tf_op jit(solution)/shard_map/ppermute | solution.py:427
  31.7 3.9 %collective-permute-done.6.got_ref = s16[16,4224]{1,0:T(8,128)(2,1)S(1)} collective-permute-done((s16[16,4224]{1,0:T(8,128)(2,1)S(1)}, s16[16,4224]{1,0:T(8,128)(2,1)S(1)}, u32[]{:S(2)}, u32[]{:S(2)}) %collective-permute-start.6) | collective-permute-done | bytes 135200 | tf_op jit(solution)/shard_map/ppermute | solution.py:427
  36.5 0.4 combine.7
  37.4 3.4 %collective-permute-done.7.query_got_ref = s16[16,2176]{1,0:T(8,128)(2,1)S(1)} collective-permute-done((s16[16,2176]{1,0:T(8,128)(2,1)S(1)}, s16[16,2176]{1,0:T(8,128)(2,1)S(1)}, u32[]{:S(2)}, u32[]{:S(2)}) %collective-permute-start.7) | collective-permute-done | bytes 69664 | tf_op jit(solution)/shard_map/ppermute | solution.py:427
  40.7 2.8 %keys_part.1 = (f32[32,8,128]{2,1,0:T(8,128)S(1)}, f32[32,8,128]{2,1,0:T(8,128)S(1)}, f32[3,32,8,128]{3,2,1,0:T(8,128)S(1)}, f32[4,32,8,128]{3,2,1,0:T(8,128)S(1)}, f32[32,4,384]{2,1,0:T(4,128)S(1)}) custom-call(s32[1]{0:T(128)} %bitcast.me_ref.twist_ref, f32[8,4096]{1,0:T(8,128)S(1)} %get-tuple-element.59.earlier_ref.query_ref, ...), custom_call_target="tpu_custom_call" | custom-call | flops 40000000 | bytes 9000000 | tf_op jit(solution)/shard_map/keys_part/pallas_call | solution.py:243
  43.6 1.9 %values_part.1 = bf16[16,16,128]{2,1,0:T(8,128)(2,1)} custom-call(s32[64]{0:T(128)S(1)} %select_reduce_fusion.slots_ref, s32[64]{0:T(128)S(1)} %get-tuple-element.77.halves_ref, s32[2]{0:T(128)S(1)} %fusion.4.lengths_ref, s32[1]{0:T(128)} %bitcast.me_ref.twist_ref, f32[8,4352]{1,0:T(8,128)S(1)} %get-tuple-element.52.value_ref, ...), custom_call_target="tpu_custom_call" | custom-call | flops 4000000 | bytes 2000000 | tf_op jit(solution)/shard_map/values_part/pallas_call | solution.py:256
  45.5 3.5 %all-to-all-start = ((bf16[16,16,128]{2,1,0:T(8,128)(2,1)}), bf16[16,16,128]{2,1,0:T(8,128)(2,1)S(1)}, u32[]{:S(2)}, u32[]{:S(2)}) async-start(bf16[16,16,128]{2,1,0:T(8,128)(2,1)} %values_part.1), calls=%async_computation | async-start | bytes 131072 | tf_op jit(solution)/shard_map/all_to_all | solution.py:520
  49.2 6.7 %all-to-all-done = bf16[16,16,128]{2,1,0:T(8,128)(2,1)S(1)} async-done(((bf16[16,16,128]{2,1,0:T(8,128)(2,1)}), bf16[16,16,128]{2,1,0:T(8,128)(2,1)S(1)}, u32[]{:S(2)}, u32[]{:S(2)}) %all-to-all-start) | async-done | bytes 65568 | tf_op jit(solution)/shard_map/all_to_all | solution.py:520
  56.1 0.7 %reshape.46 = bf16[32,4,256]{2,1,0:T(4,128)(2,1)} reshape(bf16[128,256]{1,0:T(8,128)(2,1)S(1)} %convolution_convert_fusion) | data formatting | bytes 131072 | tf_op jit(solution)/shard_map/reshape | solution.py:531
  (52 shorter events, 2.8 us)
Async XLA Ops:
  0.0 11.7 %collective-permute-start = (bf16[144,12288]{1,0:T(8,128)(2,1)}, bf16[144,12288]{1,0:T(8,128)(2,1)S(1)}, u32[]{:S(2)}, u32[]{:S(2)}) collective-permute-start(bf16[144,12288]{1,0:T(8,128)(2,1)} %weight_hbm.1), channel_id=1, source_target_pairs={{0,1},{1,0},{2,3},{3,2},{4,5},{5,4},{6,7},{7,6},{8,9},{9,8},{10,11... | collective-permute-start | bytes 10616840 | tf_op jit(solution)/shard_map/ppermute | solution.py:427
  1.2 7.8 %collective-permute-start.11 = (bf16[8,384]{1,0:T(8,128)(2,1)S(1)}, bf16[8,384]{1,0:T(8,128)(2,1)S(1)}, u32[]{:S(2)}, u32[]{:S(2)}) collective-permute-start(bf16[8,384]{1,0:T(8,128)(2,1)S(1)} %pad_maximum_fusion.1.first_ref), channel_id=1, source_target_pairs={{0,4},{1,5},{2,6},{3,7},{4,0},{5,1},{6,2},{7,3},{8,12},{9,13},{10,... | collective-permute-start | bytes 18440 | tf_op jit(solution)/shard_map/ppermute | solution.py:427
  3.8 10.3 %collective-permute-start.1 = (bf16[64,144]{1,0:T(8,128)(2,1)}, bf16[64,144]{1,0:T(8,128)(2,1)}, u32[]{:S(2)}, u32[]{:S(2)}) collective-permute-start(bf16[64,144]{1,0:T(8,128)(2,1)} %bitcast.12), channel_id=1, source_target_pairs={{0,1},{1,0},{2,3},{3,2},{4,5},{5,4},{6,7},{7,6},{8,9},{9,8},{10,11... | collective-permute-start | bytes 55304 | tf_op jit(solution)/shard_map/ppermute | solution.py:427
  4.0 2.0 %copy-start.1 = (bf16[144,12288]{1,0:T(8,128)(2,1)S(1)}, bf16[144,12288]{1,0:T(8,128)(2,1)}, u32[]{:S(2)}) copy-start(bf16[144,12288]{1,0:T(8,128)(2,1)} %weight_hbm.1) | copy-start | bytes 10616836
  6.0 1.1 %copy-start.2 = (bf16[32,4,2304]{2,1,0:T(4,128)(2,1)S(1)}, bf16[32,4,2304]{2,1,0:T(4,128)(2,1)}, u32[]{:S(2)}) copy-start(bf16[32,4,2304]{2,1,0:T(4,128)(2,1)} %tokens_hbm.1) | copy-start | bytes 1769476
  7.1 0.7 %copy-start.4 = (s32[32]{0:T(128)S(1)}, s32[32]{0:T(128)}, u32[]{:S(2)}) copy-start(s32[32]{0:T(128)} %param.18) | copy-start | bytes 388
  9.0 19.4 %collective-permute-start.12 = (bf16[16,384]{1,0:T(8,128)(2,1)S(1)}, bf16[16,384]{1,0:T(8,128)(2,1)S(1)}, u32[]{:S(2)}, u32[]{:S(2)}) collective-permute-start(bf16[16,384]{1,0:T(8,128)(2,1)S(1)} %join_taps.3.first_ref), channel_id=1, source_target_pairs={{0,8},{1,9},{2,10},{3,11},{4,12},{5,13},{6,14},{7,15},{8,0},{9,1},... | collective-permute-start | bytes 36872 | tf_op jit(solution)/shard_map/ppermute | solution.py:427
  11.7 2.4 %copy-start.3 = (bf16[144,64]{0,1:T(8,128)(2,1)S(1)}, bf16[144,64]{0,1:T(8,128)(2,1)}, u32[]{:S(2)}) copy-start(bf16[144,64]{0,1:T(8,128)(2,1)} %param.12) | copy-start | bytes 55300
  12.5 9.4 %collective-permute-start.8 = (s16[32,4224]{1,0:T(8,128)(2,1)S(1)}, s16[32,4224]{1,0:T(8,128)(2,1)S(1)}, u32[]{:S(2)}, u32[]{:S(2)}) collective-permute-start(s16[32,4224]{1,0:T(8,128)(2,1)S(1)} %get-tuple-element.61), channel_id=1, source_target_pairs={{0,2},{1,3},{2,0},{3,1},{4,6},{5,7},{6,4},{7,5},{8,10},{9,11},{10,... | collective-permute-start | bytes 811016 | tf_op jit(solution)/shard_map/ppermute | solution.py:427
  15.9 1.9 %copy-start.6 = (f32[2,3,12288]{2,0,1:T(2,128)S(1)}, f32[2,3,12288]{2,0,1:T(2,128)}, u32[]{:S(2)}) copy-start(f32[2,3,12288]{2,0,1:T(2,128)} %param.15) | copy-start | bytes 884740
  15.9 2.4 %copy-start.5 = (s32[32]{0:T(128)S(1)}, s32[32]{0:T(128)}, u32[]{:S(2)}) copy-start(s32[32]{0:T(128)} %param.18) | copy-start | bytes 388
  15.9 2.4 %copy-start.8 = (s32[64]{0:T(128)S(1)}, s32[64]{0:T(128)}, u32[]{:S(2)}) copy-start(s32[64]{0:T(128)} %param.17) | copy-start | bytes 772
  16.7 11.5 %copy-start.7 = (s32[32]{0:T(128)S(1)}, s32[32]{0:T(128)}, u32[]{:S(2)}) copy-start(s32[32]{0:T(128)} %param.19) | copy-start | bytes 388
  16.7 13.2 %copy-start.9 = (s32[32]{0:T(128)S(1)}, s32[32]{0:T(128)}, u32[]{:S(2)}) copy-start(s32[32]{0:T(128)} %param.16) | copy-start | bytes 388
  16.7 24.0 %copy-start = (f32[2,32,128,128]{3,2,1,0:T(8,128)S(1)}, f32[2,32,128,128]{3,2,1,0:T(8,128)}, u32[]{:S(2)}) copy-start(f32[2,32,128,128]{3,2,1,0:T(8,128)} %state_hbm.1) | copy-start | bytes 12582916
  16.8 9.5 %collective-permute-start.5 = (s16[32,4224]{1,0:T(8,128)(2,1)S(1)}, s16[32,4224]{1,0:T(8,128)(2,1)S(1)}, u32[]{:S(2)}, u32[]{:S(2)}) collective-permute-start(s16[32,4224]{1,0:T(8,128)(2,1)S(1)} %get-tuple-element.56), channel_id=1, source_target_pairs={{0,4},{1,5},{2,6},{3,7},{4,0},{5,1},{6,2},{7,3},{8,12},{9,13},{10,... | collective-permute-start | bytes 811016 | tf_op jit(solution)/shard_map/ppermute | solution.py:427
  17.3 9.9 %collective-permute-start.2 = (s16[32,4480]{1,0:T(8,128)(2,1)S(1)}, s16[32,4480]{1,0:T(8,128)(2,1)S(1)}, u32[]{:S(2)}, u32[]{:S(2)}) collective-permute-start(s16[32,4480]{1,0:T(8,128)(2,1)S(1)} %get-tuple-element.49), channel_id=1, source_target_pairs={{0,2},{1,3},{2,0},{3,1},{4,6},{5,7},{6,4},{7,5},{8,10},{9,11},{10,... | collective-permute-start | bytes 860168 | tf_op jit(solution)/shard_map/ppermute | solution.py:427
  22.5 7.6 %collective-permute-start.9 = (s16[16,4224]{1,0:T(8,128)(2,1)S(1)}, s16[16,4224]{1,0:T(8,128)(2,1)S(1)}, u32[]{:S(2)}, u32[]{:S(2)}) collective-permute-start(s16[16,4224]{1,0:T(8,128)(2,1)S(1)} %get-tuple-element.63), channel_id=1, source_target_pairs={{0,4},{1,5},{2,6},{3,7},{4,0},{5,1},{6,2},{7,3},{8,12},{9,13},{10,... | collective-permute-start | bytes 405512 | tf_op jit(solution)/shard_map/ppermute | solution.py:427
  26.7 8.9 %collective-permute-start.6 = (s16[16,4224]{1,0:T(8,128)(2,1)S(1)}, s16[16,4224]{1,0:T(8,128)(2,1)S(1)}, u32[]{:S(2)}, u32[]{:S(2)}) collective-permute-start(s16[16,4224]{1,0:T(8,128)(2,1)S(1)} %get-tuple-element.58), channel_id=1, source_target_pairs={{0,8},{1,9},{2,10},{3,11},{4,12},{5,13},{6,14},{7,15},{8,0},{9,1},... | collective-permute-start | bytes 405512 | tf_op jit(solution)/shard_map/ppermute | solution.py:427
  27.7 8.7 %collective-permute-start.3 = (s16[16,4480]{1,0:T(8,128)(2,1)S(1)}, s16[16,4480]{1,0:T(8,128)(2,1)S(1)}, u32[]{:S(2)}, u32[]{:S(2)}) collective-permute-start(s16[16,4480]{1,0:T(8,128)(2,1)S(1)} %get-tuple-element.51), channel_id=1, source_target_pairs={{0,4},{1,5},{2,6},{3,7},{4,0},{5,1},{6,2},{7,3},{8,12},{9,13},{10,... | collective-permute-start | bytes 430088 | tf_op jit(solution)/shard_map/ppermute | solution.py:427
  28.4 7.6 %collective-permute-start.13 = (bf16[32,384]{1,0:T(8,128)(2,1)S(1)}, bf16[32,384]{1,0:T(8,128)(2,1)S(1)}, u32[]{:S(2)}, u32[]{:S(2)}) collective-permute-start(bf16[32,384]{1,0:T(8,128)(2,1)S(1)} %join_taps.4.first_ref), channel_id=1, source_target_pairs={{0,2},{1,3},{2,0},{3,1},{4,6},{5,7},{6,4},{7,5},{8,10},{9,11},{10,... | collective-permute-start | bytes 73736 | tf_op jit(solution)/shard_map/ppermute | solution.py:427
  30.5 6.9 %collective-permute-start.10 = (s16[16,2176]{1,0:T(8,128)(2,1)S(1)}, s16[16,2176]{1,0:T(8,128)(2,1)S(1)}, u32[]{:S(2)}, u32[]{:S(2)}) collective-permute-start(s16[16,2176]{1,0:T(8,128)(2,1)S(1)} %get-tuple-element.65), channel_id=1, source_target_pairs={{0,8},{1,9},{2,10},{3,11},{4,12},{5,13},{6,14},{7,15},{8,0},{9,1},... | collective-permute-start | bytes 208904 | tf_op jit(solution)/shard_map/ppermute | solution.py:427
  36.1 1.3 %collective-permute-start.14 = (bf16[64,384]{1,0:T(8,128)(2,1)S(1)}, bf16[64,384]{1,0:T(8,128)(2,1)S(1)}, u32[]{:S(2)}, u32[]{:S(2)}) collective-permute-start(bf16[64,384]{1,0:T(8,128)(2,1)S(1)} %join_taps.5.near_ref), channel_id=1, source_target_pairs={{0,1},{1,0},{2,3},{3,2},{4,5},{5,4},{6,7},{7,6},{8,9},{9,8},{10,11... | collective-permute-start | bytes 147464 | tf_op jit(solution)/shard_map/ppermute | solution.py:427
  36.1 4.6 %collective-permute-start.7 = (s16[16,2176]{1,0:T(8,128)(2,1)S(1)}, s16[16,2176]{1,0:T(8,128)(2,1)S(1)}, u32[]{:S(2)}, u32[]{:S(2)}) collective-permute-start(s16[16,2176]{1,0:T(8,128)(2,1)S(1)} %get-tuple-element.60), channel_id=1, source_target_pairs={{0,2},{1,3},{2,0},{3,1},{4,6},{5,7},{6,4},{7,5},{8,10},{9,11},{10,... | collective-permute-start | bytes 208904 | tf_op jit(solution)/shard_map/ppermute | solution.py:427
  36.9 6.7 %collective-permute-start.4 = (s16[16,2304]{1,0:T(8,128)(2,1)S(1)}, s16[16,2304]{1,0:T(8,128)(2,1)S(1)}, u32[]{:S(2)}, u32[]{:S(2)}) collective-permute-start(s16[16,2304]{1,0:T(8,128)(2,1)S(1)} %get-tuple-element.53), channel_id=1, source_target_pairs={{0,8},{1,9},{2,10},{3,11},{4,12},{5,13},{6,14},{7,15},{8,0},{9,1},... | collective-permute-start | bytes 221192 | tf_op jit(solution)/shard_map/ppermute | solution.py:427
  45.5 10.4 %all-to-all-start = ((bf16[16,16,128]{2,1,0:T(8,128)(2,1)}), bf16[16,16,128]{2,1,0:T(8,128)(2,1)S(1)}, u32[]{:S(2)}, u32[]{:S(2)}) async-start(bf16[16,16,128]{2,1,0:T(8,128)(2,1)} %values_part.1), calls=%async_computation | async-start | bytes 131072 | tf_op jit(solution)/shard_map/all_to_all | solution.py:520

commit v10 on v9

--- a/solution.py
+++ b/solution.py
@@ -471,9 +471,9 @@
     if ride:
         taps = join(taps, far, mine)
         far = swap(taps, 8, devices)
-    keys = run_product(mine, theirs, weights, 1)
+    queries = run_product(mine, theirs, weights, 0, crossed=True)
+    keys = run_product(mine, theirs, weights, 1, earlier=queries[:1])
     values = run_product(mine, theirs, weights, 2, gates, earlier=keys[:1])
-    queries = run_product(mine, theirs, weights, 0, earlier=values[:1], crossed=True)
 
     slot_of, lengths, old_heads, new_units, carried, *values = tie(
         slot_of, lengths, old_heads, new_units, conv_state, *values

time: 57.1 us -> 61.7 us (1.081)
  starting transfers between devices: 16 us -> 21 us
    ppermute x15, starting transfers between devices: 12.5 us -> 17.5 us  [swap(): return lax.ppermute(value, 'heads', [(i, i ^ bit) for i in range(devices)])]
  transfers between devices with their start and end apart: 16 -> 16, of which waited for: 7 -> 6; matrix products, arithmetic and copies ran while one was open for 3% -> 3% of each run, Pallas kernels for 18% -> 17%
where the time goes in v10:
time: 61.7 us; the launch traced here: 61.4 us
  waiting for transfers between devices  21.6 us (35%)
  starting transfers between devices  21 us (34%)
  Pallas kernels  12.2 us (20%)
  local copies, waits for them, and re-layouts  5.54 us (9%)
  other arithmetic  0.65 us (1%)
    ppermute x15, starting transfers between devices, swap(): return lax.ppermute(value, 'heads', [(i, i ^ bit) for i in range(devices)])  17.5 us
    ppermute x15, waiting for transfers between devices, swap(): return lax.ppermute(value, 'heads', [(i, i ^ bit) for i in range(devices)])  14.9 us
    all_to_all x1, waiting for transfers between devices, on_device(): lax.all_to_all(sending, 'heads', split_axis=0, concat_axis=0, tiled=True)  6.68 us
    unnamed x20, local copies, waits for them, and re-layouts  3.76 us
    all_to_all x1, starting transfers between devices, on_device(): lax.all_to_all(sending, 'heads', split_axis=0, concat_axis=0, tiled=True)  3.5 us
    pallas_call x3, Pallas kernels, run_product(): pl.pallas_call(functools.partial(product_kernel, len(earlier), crossed),...  3.39 us
    pallas_call x1, Pallas kernels, run_delta(): pl.pallas_call(keys_kernel, out_shape=[per_head] * 2 + lags + [tap_blocks...  2.81 us
    pallas_call x6, Pallas kernels, run_combine(): pl.pallas_call(combine_kernel, out_shape=[jax.ShapeDtypeStruct((half, wid...  2.81 us
  transfers between devices with their start and end apart: 16, of which 6 were waited for; matrix products, arithmetic and copies ran while one was open for 3% of the time, Pallas kernels for 17%

profile of v10, /device:TPU:0, one launch (start us, length us, event | category | flops | bytes accessed | tf_op | source)
XLA Modules:
  0.0 61.4 jit_solution(6995661420070675675)
XLA Ops:
  0.0 0.5 collective-permute-start
  0.5 0.7 %fusion.6 = (bf16[4,384]{1,0:T(4,128)(2,1)S(1)}, bf16[4,384]{1,0:T(4,128)(2,1)S(1)}) fusion(bf16[4,768]{1,0:T(4,128)(2,1)} %param.13), kind=kLoop, calls=%fused_computation.27 | loop fusion | bytes 12288 | tf_op jit(solution)/shard_map/slice | solution.py:452
  1.2 2.6 %collective-permute-start.11 = (bf16[8,384]{1,0:T(8,128)(2,1)S(1)}, bf16[8,384]{1,0:T(8,128)(2,1)S(1)}, u32[]{:S(2)}, u32[]{:S(2)}) collective-permute-start(bf16[8,384]{1,0:T(8,128)(2,1)S(1)} %pad_maximum_fusion.1.first_ref), channel_id=1, source_target_pairs={{0,4},{1,5},{2,6},{3,7},{4,0},{5,1},{6,2},{7,3},{8,12},{9,13},{10,... | collective-permute-start | bytes 18440 | tf_op jit(solution)/shard_map/ppermute | solution.py:427
  4.0 2.0 %copy-done.1 = bf16[144,12288]{1,0:T(8,128)(2,1)S(1)} copy-done((bf16[144,12288]{1,0:T(8,128)(2,1)S(1)}, bf16[144,12288]{1,0:T(8,128)(2,1)}, u32[]{:S(2)}) %copy-start.1) | copy-done | bytes 3538968
  6.0 1.1 %copy-done.2 = bf16[32,4,2304]{2,1,0:T(4,128)(2,1)S(1)} copy-done((bf16[32,4,2304]{2,1,0:T(4,128)(2,1)S(1)}, bf16[32,4,2304]{2,1,0:T(4,128)(2,1)}, u32[]{:S(2)}) %copy-start.2) | copy-done | bytes 589848
  7.1 0.7 %copy-done.4 = s32[32]{0:T(128)S(1)} copy-done((s32[32]{0:T(128)S(1)}, s32[32]{0:T(128)}, u32[]{:S(2)}) %copy-start.4) | copy-done | bytes 152
  7.8 1.2 %token_rows.1 = (bf16[64,144]{1,0:T(8,128)(2,1)S(1)}, bf16[64,144]{1,0:T(8,128)(2,1)S(1)}, bf16[144,12288]{1,0:T(8,128)(2,1)S(1)}) custom-call(s32[1]{0:T(128)} %bitcast.me_ref.twist_ref, s32[1,32]{1,0:T(1,128)S(1)} %bitcast.14, bf16[32,4,2304]{2,1,0:T(4,128)(2,1)S(1)} %copy-done.2, bf16[144,12288]{1,0:T(8,128)(2,1)S(1)} %copy-done.1), custom_call_target="tpu_custom_call" | custom-call | tf_op jit(solution)/shard_map/token_rows/pallas_call | solution.py:310
  9.0 2.7 %collective-permute-start.12 = (bf16[16,384]{1,0:T(8,128)(2,1)S(1)}, bf16[16,384]{1,0:T(8,128)(2,1)S(1)}, u32[]{:S(2)}, u32[]{:S(2)}) collective-permute-start(bf16[16,384]{1,0:T(8,128)(2,1)S(1)} %join_taps.3.first_ref), channel_id=1, source_target_pairs={{0,8},{1,9},{2,10},{3,11},{4,12},{5,13},{6,14},{7,15},{8,0},{9,1},... | collective-permute-start | bytes 36872 | tf_op jit(solution)/shard_map/ppermute | solution.py:427
  11.7 0.8 %partial_product.3 = (f32[32,4096]{1,0:T(8,128)S(1)}, s16[32,4224]{1,0:T(8,128)(2,1)S(1)}) custom-call(bf16[64,144]{1,0:T(8,128)(2,1)S(1)} %get-tuple-element.38.refs_0_.refs_1_.earlier_ref, bf16[64,144]{1,0:T(8,128)(2,1)S(1)} %get-tuple-element.39.refs_1_.refs_2_, bf16[144,12288]{1,0:T(8,128)(2,1)S(1)} %get-tuple-element.40.refs_2_.refs_3_, ...), custom_call_target="tpu_custom_call" | custom-call | tf_op jit(solution)/shard_map/partial_product/pallas_call | solution.py:358
  12.5 0.5 collective-permute-start.5
  13.0 0.8 %partial_product.4 = (f32[32,4096]{1,0:T(8,128)S(1)}, s16[32,4224]{1,0:T(8,128)(2,1)S(1)}) custom-call(f32[32,4096]{1,0:T(8,128)S(1)} %get-tuple-element.41.refs_0_.kept_ref, bf16[64,144]{1,0:T(8,128)(2,1)S(1)} %get-tuple-element.38.refs_0_.refs_1_.earlier_ref, bf16[64,144]{1,0:T(8,128)(2,1)S(1)} %get-tuple-element.39.refs_1_.refs_2_, ...), custom_call_target="tpu_custom_call" | custom-call | tf_op jit(solution)/shard_map/partial_product/pallas_call | solution.py:358
  13.9 1.7 %partial_product.5 = (f32[32,4352]{1,0:T(8,128)S(1)}, s16[32,4480]{1,0:T(8,128)(2,1)S(1)}) custom-call(f32[32,4096]{1,0:T(8,128)S(1)} %get-tuple-element.42.refs_0_.kept_ref, bf16[64,144]{1,0:T(8,128)(2,1)S(1)} %get-tuple-element.38.refs_0_.refs_1_.earlier_ref, bf16[64,144]{1,0:T(8,128)(2,1)S(1)} %get-tuple-element.39.refs_1_.refs_2_, ...), custom_call_target="tpu_custom_call" | custom-call | tf_op jit(solution)/shard_map/partial_product/pallas_call | solution.py:358
  15.7 1.6 %collective-permute-start.8 = (s16[32,4224]{1,0:T(8,128)(2,1)S(1)}, s16[32,4224]{1,0:T(8,128)(2,1)S(1)}, u32[]{:S(2)}, u32[]{:S(2)}) collective-permute-start(s16[32,4224]{1,0:T(8,128)(2,1)S(1)} %get-tuple-element.61), channel_id=1, source_target_pairs={{0,2},{1,3},{2,0},{3,1},{4,6},{5,7},{6,4},{7,5},{8,10},{9,11},{10,... | collective-permute-start | bytes 811016 | tf_op jit(solution)/shard_map/ppermute | solution.py:427
  17.3 0.5 collective-permute-start.2
  18.3 2.6 %collective-permute-done.5.got_ref = s16[32,4224]{1,0:T(8,128)(2,1)S(1)} collective-permute-done((s16[32,4224]{1,0:T(8,128)(2,1)S(1)}, s16[32,4224]{1,0:T(8,128)(2,1)S(1)}, u32[]{:S(2)}, u32[]{:S(2)}) %collective-permute-start.5) | collective-permute-done | bytes 270368 | tf_op jit(solution)/shard_map/ppermute | solution.py:427
  21.0 0.5 combine.8
  21.9 3.3 %collective-permute-done.8.got_ref = s16[32,4224]{1,0:T(8,128)(2,1)S(1)} collective-permute-done((s16[32,4224]{1,0:T(8,128)(2,1)S(1)}, s16[32,4224]{1,0:T(8,128)(2,1)S(1)}, u32[]{:S(2)}, u32[]{:S(2)}) %collective-permute-start.8) | collective-permute-done | bytes 270368 | tf_op jit(solution)/shard_map/ppermute | solution.py:427
  25.2 0.5 combine.10
  25.7 1.6 %collective-permute-start.9 = (s16[16,4224]{1,0:T(8,128)(2,1)S(1)}, s16[16,4224]{1,0:T(8,128)(2,1)S(1)}, u32[]{:S(2)}, u32[]{:S(2)}) collective-permute-start(s16[16,4224]{1,0:T(8,128)(2,1)S(1)} %get-tuple-element.63), channel_id=1, source_target_pairs={{0,4},{1,5},{2,6},{3,7},{4,0},{5,1},{6,2},{7,3},{8,12},{9,13},{10,... | collective-permute-start | bytes 405512 | tf_op jit(solution)/shard_map/ppermute | solution.py:427
  27.3 2.7 %collective-permute-done.2.got_ref = s16[32,4480]{1,0:T(8,128)(2,1)S(1)} collective-permute-done((s16[32,4480]{1,0:T(8,128)(2,1)S(1)}, s16[32,4480]{1,0:T(8,128)(2,1)S(1)}, u32[]{:S(2)}, u32[]{:S(2)}) %collective-permute-start.2) | collective-permute-done | bytes 286752 | tf_op jit(solution)/shard_map/ppermute | solution.py:427
  30.0 0.5 combine.6
  30.6 1.6 %collective-permute-start.3 = (s16[16,4480]{1,0:T(8,128)(2,1)S(1)}, s16[16,4480]{1,0:T(8,128)(2,1)S(1)}, u32[]{:S(2)}, u32[]{:S(2)}) collective-permute-start(s16[16,4480]{1,0:T(8,128)(2,1)S(1)} %get-tuple-element.52), channel_id=1, source_target_pairs={{0,4},{1,5},{2,6},{3,7},{4,0},{5,1},{6,2},{7,3},{8,12},{9,13},{10,... | collective-permute-start | bytes 430088 | tf_op jit(solution)/shard_map/ppermute | solution.py:427
  32.4 1.6 %collective-permute-start.13 = (bf16[32,384]{1,0:T(8,128)(2,1)S(1)}, bf16[32,384]{1,0:T(8,128)(2,1)S(1)}, u32[]{:S(2)}, u32[]{:S(2)}) collective-permute-start(bf16[32,384]{1,0:T(8,128)(2,1)S(1)} %join_taps.4.first_ref), channel_id=1, source_target_pairs={{0,2},{1,3},{2,0},{3,1},{4,6},{5,7},{6,4},{7,5},{8,10},{9,11},{10,... | collective-permute-start | bytes 73736 | tf_op jit(solution)/shard_map/ppermute | solution.py:427
  34.5 0.6 collective-permute-start.7
  35.1 1.3 %collective-permute-done.13.second_ref = bf16[32,384]{1,0:T(8,128)(2,1)S(1)} collective-permute-done((bf16[32,384]{1,0:T(8,128)(2,1)S(1)}, bf16[32,384]{1,0:T(8,128)(2,1)S(1)}, u32[]{:S(2)}, u32[]{:S(2)}) %collective-permute-start.13) | collective-permute-done | bytes 24608 | tf_op jit(solution)/shard_map/ppermute | solution.py:427
  37.7 2.6 %collective-permute-start.4 = (s16[16,2304]{1,0:T(8,128)(2,1)S(1)}, s16[16,2304]{1,0:T(8,128)(2,1)S(1)}, u32[]{:S(2)}, u32[]{:S(2)}) collective-permute-start(s16[16,2304]{1,0:T(8,128)(2,1)S(1)} %get-tuple-element.54), channel_id=1, source_target_pairs={{0,8},{1,9},{2,10},{3,11},{4,12},{5,13},{6,14},{7,15},{8,0},{9,1},... | collective-permute-start | bytes 221192 | tf_op jit(solution)/shard_map/ppermute | solution.py:427
  40.5 5.0 %collective-permute-done.10.key_got_ref = s16[16,2176]{1,0:T(8,128)(2,1)S(1)} collective-permute-done((s16[16,2176]{1,0:T(8,128)(2,1)S(1)}, s16[16,2176]{1,0:T(8,128)(2,1)S(1)}, u32[]{:S(2)}, u32[]{:S(2)}) %collective-permute-start.10) | collective-permute-done | bytes 69664 | tf_op jit(solution)/shard_map/ppermute | solution.py:427
  45.4 2.8 %keys_part.1 = (f32[32,8,128]{2,1,0:T(8,128)S(1)}, f32[32,8,128]{2,1,0:T(8,128)S(1)}, f32[3,32,8,128]{3,2,1,0:T(8,128)S(1)}, f32[4,32,8,128]{3,2,1,0:T(8,128)S(1)}, f32[32,4,384]{2,1,0:T(4,128)S(1)}) custom-call(s32[1]{0:T(128)} %bitcast.me_ref.twist_ref, f32[8,4096]{1,0:T(8,128)S(1)} %get-tuple-element.59.earlier_ref.query_ref, ...), custom_call_target="tpu_custom_call" | custom-call | flops 40000000 | bytes 9000000 | tf_op jit(solution)/shard_map/keys_part/pallas_call | solution.py:243
  48.3 1.9 %values_part.1 = bf16[16,16,128]{2,1,0:T(8,128)(2,1)} custom-call(s32[64]{0:T(128)S(1)} %select_reduce_fusion.slots_ref, s32[64]{0:T(128)S(1)} %get-tuple-element.77.halves_ref, s32[2]{0:T(128)S(1)} %fusion.4.lengths_ref, s32[1]{0:T(128)} %bitcast.me_ref.twist_ref, f32[8,4352]{1,0:T(8,128)S(1)} %get-tuple-element.53.value_ref, ...), custom_call_target="tpu_custom_call" | custom-call | flops 4000000 | bytes 2000000 | tf_op jit(solution)/shard_map/values_part/pallas_call | solution.py:256
  50.2 3.5 %all-to-all-start = ((bf16[16,16,128]{2,1,0:T(8,128)(2,1)}), bf16[16,16,128]{2,1,0:T(8,128)(2,1)S(1)}, u32[]{:S(2)}, u32[]{:S(2)}) async-start(bf16[16,16,128]{2,1,0:T(8,128)(2,1)} %values_part.1), calls=%async_computation | async-start | bytes 131072 | tf_op jit(solution)/shard_map/all_to_all | solution.py:520
  53.9 6.7 %all-to-all-done = bf16[16,16,128]{2,1,0:T(8,128)(2,1)S(1)} async-done(((bf16[16,16,128]{2,1,0:T(8,128)(2,1)}), bf16[16,16,128]{2,1,0:T(8,128)(2,1)S(1)}, u32[]{:S(2)}, u32[]{:S(2)}) %all-to-all-start) | async-done | bytes 65568 | tf_op jit(solution)/shard_map/all_to_all | solution.py:520
  60.8 0.7 %reshape.46 = bf16[32,4,256]{2,1,0:T(4,128)(2,1)} reshape(bf16[128,256]{1,0:T(8,128)(2,1)S(1)} %convolution_convert_fusion) | data formatting | bytes 131072 | tf_op jit(solution)/shard_map/reshape | solution.py:531
  (52 shorter events, 3.6 us)
Async XLA Ops:
  0.0 11.7 %collective-permute-start = (bf16[144,12288]{1,0:T(8,128)(2,1)}, bf16[144,12288]{1,0:T(8,128)(2,1)S(1)}, u32[]{:S(2)}, u32[]{:S(2)}) collective-permute-start(bf16[144,12288]{1,0:T(8,128)(2,1)} %weight_hbm.1), channel_id=1, source_target_pairs={{0,1},{1,0},{2,3},{3,2},{4,5},{5,4},{6,7},{7,6},{8,9},{9,8},{10,11... | collective-permute-start | bytes 10616840 | tf_op jit(solution)/shard_map/ppermute | solution.py:427
  1.2 7.8 %collective-permute-start.11 = (bf16[8,384]{1,0:T(8,128)(2,1)S(1)}, bf16[8,384]{1,0:T(8,128)(2,1)S(1)}, u32[]{:S(2)}, u32[]{:S(2)}) collective-permute-start(bf16[8,384]{1,0:T(8,128)(2,1)S(1)} %pad_maximum_fusion.1.first_ref), channel_id=1, source_target_pairs={{0,4},{1,5},{2,6},{3,7},{4,0},{5,1},{6,2},{7,3},{8,12},{9,13},{10,... | collective-permute-start | bytes 18440 | tf_op jit(solution)/shard_map/ppermute | solution.py:427
  3.8 10.0 %collective-permute-start.1 = (bf16[64,144]{1,0:T(8,128)(2,1)}, bf16[64,144]{1,0:T(8,128)(2,1)}, u32[]{:S(2)}, u32[]{:S(2)}) collective-permute-start(bf16[64,144]{1,0:T(8,128)(2,1)} %bitcast.12), channel_id=1, source_target_pairs={{0,1},{1,0},{2,3},{3,2},{4,5},{5,4},{6,7},{7,6},{8,9},{9,8},{10,11... | collective-permute-start | bytes 55304 | tf_op jit(solution)/shard_map/ppermute | solution.py:427
  4.0 2.0 %copy-start.1 = (bf16[144,12288]{1,0:T(8,128)(2,1)S(1)}, bf16[144,12288]{1,0:T(8,128)(2,1)}, u32[]{:S(2)}) copy-start(bf16[144,12288]{1,0:T(8,128)(2,1)} %weight_hbm.1) | copy-start | bytes 10616836
  6.0 1.1 %copy-start.2 = (bf16[32,4,2304]{2,1,0:T(4,128)(2,1)S(1)}, bf16[32,4,2304]{2,1,0:T(4,128)(2,1)}, u32[]{:S(2)}) copy-start(bf16[32,4,2304]{2,1,0:T(4,128)(2,1)} %tokens_hbm.1) | copy-start | bytes 1769476
  7.1 0.7 %copy-start.4 = (s32[32]{0:T(128)S(1)}, s32[32]{0:T(128)}, u32[]{:S(2)}) copy-start(s32[32]{0:T(128)} %param.18) | copy-start | bytes 388
  9.0 23.4 %collective-permute-start.12 = (bf16[16,384]{1,0:T(8,128)(2,1)S(1)}, bf16[16,384]{1,0:T(8,128)(2,1)S(1)}, u32[]{:S(2)}, u32[]{:S(2)}) collective-permute-start(bf16[16,384]{1,0:T(8,128)(2,1)S(1)} %join_taps.3.first_ref), channel_id=1, source_target_pairs={{0,8},{1,9},{2,10},{3,11},{4,12},{5,13},{6,14},{7,15},{8,0},{9,1},... | collective-permute-start | bytes 36872 | tf_op jit(solution)/shard_map/ppermute | solution.py:427
  12.5 8.5 %collective-permute-start.5 = (s16[32,4224]{1,0:T(8,128)(2,1)S(1)}, s16[32,4224]{1,0:T(8,128)(2,1)S(1)}, u32[]{:S(2)}, u32[]{:S(2)}) collective-permute-start(s16[32,4224]{1,0:T(8,128)(2,1)S(1)} %get-tuple-element.56), channel_id=1, source_target_pairs={{0,4},{1,5},{2,6},{3,7},{4,0},{5,1},{6,2},{7,3},{8,12},{9,13},{10,... | collective-permute-start | bytes 811016 | tf_op jit(solution)/shard_map/ppermute | solution.py:427
  13.0 0.8 %copy-start.3 = (bf16[144,64]{0,1:T(8,128)(2,1)S(1)}, bf16[144,64]{0,1:T(8,128)(2,1)}, u32[]{:S(2)}) copy-start(bf16[144,64]{0,1:T(8,128)(2,1)} %param.12) | copy-start | bytes 55300
  13.9 3.9 %copy-start.6 = (f32[2,3,12288]{2,0,1:T(2,128)S(1)}, f32[2,3,12288]{2,0,1:T(2,128)}, u32[]{:S(2)}) copy-start(f32[2,3,12288]{2,0,1:T(2,128)} %param.15) | copy-start | bytes 884740
  13.9 4.4 %copy-start.5 = (s32[32]{0:T(128)S(1)}, s32[32]{0:T(128)}, u32[]{:S(2)}) copy-start(s32[32]{0:T(128)} %param.18) | copy-start | bytes 388
  13.9 4.4 %copy-start.8 = (s32[64]{0:T(128)S(1)}, s32[64]{0:T(128)}, u32[]{:S(2)}) copy-start(s32[64]{0:T(128)} %param.17) | copy-start | bytes 772
  15.7 16.5 %copy-start.7 = (s32[32]{0:T(128)S(1)}, s32[32]{0:T(128)}, u32[]{:S(2)}) copy-start(s32[32]{0:T(128)} %param.19) | copy-start | bytes 388
  15.7 18.3 %copy-start.9 = (s32[32]{0:T(128)S(1)}, s32[32]{0:T(128)}, u32[]{:S(2)}) copy-start(s32[32]{0:T(128)} %param.16) | copy-start | bytes 388
  15.7 29.7 %copy-start = (f32[2,32,128,128]{3,2,1,0:T(8,128)S(1)}, f32[2,32,128,128]{3,2,1,0:T(8,128)}, u32[]{:S(2)}) copy-start(f32[2,32,128,128]{3,2,1,0:T(8,128)} %state_hbm.1) | copy-start | bytes 12582916
  15.7 9.5 %collective-permute-start.8 = (s16[32,4224]{1,0:T(8,128)(2,1)S(1)}, s16[32,4224]{1,0:T(8,128)(2,1)S(1)}, u32[]{:S(2)}, u32[]{:S(2)}) collective-permute-start(s16[32,4224]{1,0:T(8,128)(2,1)S(1)} %get-tuple-element.61), channel_id=1, source_target_pairs={{0,2},{1,3},{2,0},{3,1},{4,6},{5,7},{6,4},{7,5},{8,10},{9,11},{10,... | collective-permute-start | bytes 811016 | tf_op jit(solution)/shard_map/ppermute | solution.py:427
  17.3 12.7 %collective-permute-start.2 = (s16[32,4480]{1,0:T(8,128)(2,1)S(1)}, s16[32,4480]{1,0:T(8,128)(2,1)S(1)}, u32[]{:S(2)}, u32[]{:S(2)}) collective-permute-start(s16[32,4480]{1,0:T(8,128)(2,1)S(1)} %get-tuple-element.50), channel_id=1, source_target_pairs={{0,2},{1,3},{2,0},{3,1},{4,6},{5,7},{6,4},{7,5},{8,10},{9,11},{10,... | collective-permute-start | bytes 860168 | tf_op jit(solution)/shard_map/ppermute | solution.py:427
  21.5 12.6 %collective-permute-start.6 = (s16[16,4224]{1,0:T(8,128)(2,1)S(1)}, s16[16,4224]{1,0:T(8,128)(2,1)S(1)}, u32[]{:S(2)}, u32[]{:S(2)}) collective-permute-start(s16[16,4224]{1,0:T(8,128)(2,1)S(1)} %get-tuple-element.58), channel_id=1, source_target_pairs={{0,8},{1,9},{2,10},{3,11},{4,12},{5,13},{6,14},{7,15},{8,0},{9,1},... | collective-permute-start | bytes 405512 | tf_op jit(solution)/shard_map/ppermute | solution.py:427
  25.7 10.8 %collective-permute-start.9 = (s16[16,4224]{1,0:T(8,128)(2,1)S(1)}, s16[16,4224]{1,0:T(8,128)(2,1)S(1)}, u32[]{:S(2)}, u32[]{:S(2)}) collective-permute-start(s16[16,4224]{1,0:T(8,128)(2,1)S(1)} %get-tuple-element.63), channel_id=1, source_target_pairs={{0,4},{1,5},{2,6},{3,7},{4,0},{5,1},{6,2},{7,3},{8,12},{9,13},{10,... | collective-permute-start | bytes 405512 | tf_op jit(solution)/shard_map/ppermute | solution.py:427
  30.6 6.7 %collective-permute-start.3 = (s16[16,4480]{1,0:T(8,128)(2,1)S(1)}, s16[16,4480]{1,0:T(8,128)(2,1)S(1)}, u32[]{:S(2)}, u32[]{:S(2)}) collective-permute-start(s16[16,4480]{1,0:T(8,128)(2,1)S(1)} %get-tuple-element.52), channel_id=1, source_target_pairs={{0,4},{1,5},{2,6},{3,7},{4,0},{5,1},{6,2},{7,3},{8,12},{9,13},{10,... | collective-permute-start | bytes 430088 | tf_op jit(solution)/shard_map/ppermute | solution.py:427
  32.4 4.0 %collective-permute-start.13 = (bf16[32,384]{1,0:T(8,128)(2,1)S(1)}, bf16[32,384]{1,0:T(8,128)(2,1)S(1)}, u32[]{:S(2)}, u32[]{:S(2)}) collective-permute-start(bf16[32,384]{1,0:T(8,128)(2,1)S(1)} %join_taps.4.first_ref), channel_id=1, source_target_pairs={{0,2},{1,3},{2,0},{3,1},{4,6},{5,7},{6,4},{7,5},{8,10},{9,11},{10,... | collective-permute-start | bytes 73736 | tf_op jit(solution)/shard_map/ppermute | solution.py:427
  34.5 5.9 %collective-permute-start.7 = (s16[16,2176]{1,0:T(8,128)(2,1)S(1)}, s16[16,2176]{1,0:T(8,128)(2,1)S(1)}, u32[]{:S(2)}, u32[]{:S(2)}) collective-permute-start(s16[16,2176]{1,0:T(8,128)(2,1)S(1)} %get-tuple-element.60), channel_id=1, source_target_pairs={{0,2},{1,3},{2,0},{3,1},{4,6},{5,7},{6,4},{7,5},{8,10},{9,11},{10,... | collective-permute-start | bytes 208904 | tf_op jit(solution)/shard_map/ppermute | solution.py:427
  36.5 4.0 %collective-permute-start.14 = (bf16[64,384]{1,0:T(8,128)(2,1)S(1)}, bf16[64,384]{1,0:T(8,128)(2,1)S(1)}, u32[]{:S(2)}, u32[]{:S(2)}) collective-permute-start(bf16[64,384]{1,0:T(8,128)(2,1)S(1)} %join_taps.5.near_ref), channel_id=1, source_target_pairs={{0,1},{1,0},{2,3},{3,2},{4,5},{5,4},{6,7},{7,6},{8,9},{9,8},{10,11... | collective-permute-start | bytes 147464 | tf_op jit(solution)/shard_map/ppermute | solution.py:427
  36.9 8.5 %collective-permute-start.10 = (s16[16,2176]{1,0:T(8,128)(2,1)S(1)}, s16[16,2176]{1,0:T(8,128)(2,1)S(1)}, u32[]{:S(2)}, u32[]{:S(2)}) collective-permute-start(s16[16,2176]{1,0:T(8,128)(2,1)S(1)} %get-tuple-element.65), channel_id=1, source_target_pairs={{0,8},{1,9},{2,10},{3,11},{4,12},{5,13},{6,14},{7,15},{8,0},{9,1},... | collective-permute-start | bytes 208904 | tf_op jit(solution)/shard_map/ppermute | solution.py:427
  37.7 10.5 %collective-permute-start.4 = (s16[16,2304]{1,0:T(8,128)(2,1)S(1)}, s16[16,2304]{1,0:T(8,128)(2,1)S(1)}, u32[]{:S(2)}, u32[]{:S(2)}) collective-permute-start(s16[16,2304]{1,0:T(8,128)(2,1)S(1)} %get-tuple-element.54), channel_id=1, source_target_pairs={{0,8},{1,9},{2,10},{3,11},{4,12},{5,13},{6,14},{7,15},{8,0},{9,1},... | collective-permute-start | bytes 221192 | tf_op jit(solution)/shard_map/ppermute | solution.py:427
  50.2 10.4 %all-to-all-start = ((bf16[16,16,128]{2,1,0:T(8,128)(2,1)}), bf16[16,16,128]{2,1,0:T(8,128)(2,1)S(1)}, u32[]{:S(2)}, u32[]{:S(2)}) async-start(bf16[16,16,128]{2,1,0:T(8,128)(2,1)} %values_part.1), calls=%async_computation | async-start | bytes 131072 | tf_op jit(solution)/shard_map/all_to_all | solution.py:520

commit v11 on v9

--- a/solution.py
+++ b/solution.py
@@ -124,10 +124,7 @@
     return total / (1.0 + jnp.exp(-total))
 
 
-def keys_kernel(
-    twist_ref, query_ref, query_got_ref, key_ref, key_got_ref, history_ref, near_ref, far_ref,
-    state_hbm, key_seen_ref, query_seen_ref, pulls_ref, weights_ref, taps_ref, state_ref, sems,
-):
+def start_states(state_hbm, state_ref, sems):
     per_copy = H // STATE_COPIES
     copies = []
     for at in range(STATE_COPIES):
@@ -136,6 +133,32 @@
             pltpu.make_async_copy(state_hbm.at[:, some], state_ref.at[:, some], sems.at[at])
         )
         copies[-1].start()
+    return copies
+
+
+def seen_by(vectors, state_ref, head, row, copies):
+    per_copy = H // STATE_COPIES
+    if head % per_copy == 0:
+        copies[head // per_copy].wait()
+    rows_high = vectors.astype(jnp.bfloat16)
+    rows_low = (vectors - rows_high.astype(jnp.float32)).astype(jnp.bfloat16)
+    stacked = jnp.concatenate([rows_high, rows_low], axis=0)
+    seen = []
+    for r in range(LOCAL):
+        state = state_ref[r, head]
+        high = state.astype(jnp.bfloat16)
+        low = (state - high.astype(jnp.float32)).astype(jnp.bfloat16)
+        main = jnp.dot(stacked, high, preferred_element_type=jnp.float32)
+        rest = jnp.dot(rows_high, low, preferred_element_type=jnp.float32)
+        seen.append(main[:ROWS] + main[ROWS:] + rest)
+    return jnp.where(row < STEPS, seen[0], seen[1])
+
+
+def keys_kernel(
+    twist_ref, kept_ref, got_ref, history_ref, near_ref, far_ref, state_hbm,
+    keys_ref, key_seen_ref, pulls_ref, taps_ref, state_ref, sems,
+):
+    copies = start_states(state_hbm, state_ref, sems)
     twist = twist_ref[0]
     half = TAP_BLOCKS // 2
     for at in range(TAP_BLOCKS):
@@ -145,39 +168,34 @@
         taps_ref[at] = some[at % 4 * TAPS : (at % 4 + 1) * TAPS]
     row = lax.broadcasted_iota(jnp.int32, (ROWS, DK), 0)
     row_step = row % STEPS
-    query_steps, key_steps = steps_of(query_got_ref), steps_of(key_got_ref)
+    steps = steps_of(got_ref)
     for head in range(H):
         key = unit_length(
-            activate(
-                key_ref, key_got_ref, key_steps, 1, head, history_ref, taps_ref, twist, row_step
-            )
+            activate(kept_ref, got_ref, steps, 1, head, history_ref, taps_ref, twist, row_step)
         )
+        keys_ref[head] = key
+        key_seen_ref[head] = seen_by(key, state_ref, head, row, copies)
+        for lag in range(1, STEPS):
+            moved_key = shift_rows(key, lag, row_step)
+            pulls_ref[lag - 1, head] = jnp.broadcast_to(lane_sum(key * moved_key), (ROWS, DK))
+
+
+def queries_kernel(
+    twist_ref, kept_ref, got_ref, history_ref, keys_ref, taps_ref, state_hbm,
+    query_seen_ref, weights_ref, state_ref, sems,
+):
+    copies = start_states(state_hbm, state_ref, sems)
+    twist = twist_ref[0]
+    row = lax.broadcasted_iota(jnp.int32, (ROWS, DK), 0)
+    row_step = row % STEPS
+    steps = steps_of(got_ref)
+    for head in range(H):
         query = unit_length(
-            activate(
-                query_ref, query_got_ref, query_steps, 0, head, history_ref, taps_ref, twist,
-                row_step,
-            )
+            activate(kept_ref, got_ref, steps, 0, head, history_ref, taps_ref, twist, row_step)
         )
-        both = jnp.concatenate([key, query], axis=0)
-        if head % per_copy == 0:
-            copies[head // per_copy].wait()
-        both_high = both.astype(jnp.bfloat16)
-        both_low = (both - both_high.astype(jnp.float32)).astype(jnp.bfloat16)
-        stacked = jnp.concatenate([both_high, both_low], axis=0)
-        seen = []
-        for r in range(LOCAL):
-            state = state_ref[r, head]
-            high = state.astype(jnp.bfloat16)
-            low = (state - high.astype(jnp.float32)).astype(jnp.bfloat16)
-            main = jnp.dot(stacked, high, preferred_element_type=jnp.float32)
-            rest = jnp.dot(both_high, low, preferred_element_type=jnp.float32)
-            seen.append(main[: 2 * ROWS] + main[2 * ROWS :] + rest)
-        key_seen_ref[head] = jnp.where(row < STEPS, seen[0][:ROWS], seen[1][:ROWS])
-        query_seen_ref[head] = jnp.where(row < STEPS, seen[0][ROWS:], seen[1][ROWS:])
+        query_seen_ref[head] = seen_by(query, state_ref, head, row, copies)
         for lag in range(STEPS):
-            moved_key = shift_rows(key, lag, row_step)
-            if lag:
-                pulls_ref[lag - 1, head] = jnp.broadcast_to(lane_sum(key * moved_key), (ROWS, DK))
+            moved_key = shift_rows(keys_ref[head], lag, row_step)
             weights_ref[lag, head] = jnp.broadcast_to(lane_sum(query * moved_key), (ROWS, DK))
 
 
@@ -240,19 +258,31 @@
         jax.ShapeDtypeStruct((count, H, ROWS, DK), jnp.float32) for count in (STEPS - 1, STEPS)
     ]
     tap_blocks = jax.ShapeDtypeStruct((TAP_BLOCKS, TAPS, TAP_WIDTH), jnp.float32)
-    prepared = pl.pallas_call(
-        keys_kernel,
-        out_shape=[per_head] * 2 + lags + [tap_blocks],
-        in_specs=[smem] + [vmem] * 7 + [pl.BlockSpec(memory_space=pl.ANY)],
-        out_specs=[vmem] * 5,
+    states = dict(
         scratch_shapes=[
             pltpu.VMEM(state.shape, jnp.float32),
             pltpu.SemaphoreType.DMA((STATE_COPIES,)),
         ],
         compiler_params=params,
-        cost_estimate=pl.CostEstimate(flops=40_000_000, bytes_accessed=9_000_000, transcendentals=0),
+        cost_estimate=pl.CostEstimate(flops=20_000_000, bytes_accessed=5_000_000, transcendentals=0),
+    )
+    key_rows, key_seen, pulls, tap_rows = pl.pallas_call(
+        keys_kernel,
+        out_shape=[per_head, per_head, lags[0], tap_blocks],
+        in_specs=[smem] + [vmem] * 5 + [pl.BlockSpec(memory_space=pl.ANY)],
+        out_specs=[vmem] * 4,
         name="keys_part",
-    )(twist, *queries, *keys, history, *taps, state)
+        **states,
+    )(twist, *keys, history, *taps, state)
+    query_seen, weights = pl.pallas_call(
+        queries_kernel,
+        out_shape=[per_head, lags[1]],
+        in_specs=[smem] + [vmem] * 5 + [pl.BlockSpec(memory_space=pl.ANY)],
+        out_specs=[vmem] * 2,
+        name="queries_part",
+        **states,
+    )(twist, *queries, history, key_rows, tap_rows, state)
+    prepared = (key_seen, query_seen, pulls, weights, tap_rows)
     return pl.pallas_call(
         values_kernel,
         out_shape=jax.ShapeDtypeStruct((UNITS // 4, 2 * ROWS, DK), jnp.bfloat16),

time: 57.1 us -> 57.9 us (1.014)
  waiting for transfers between devices: 21.8 us -> 19.3 us
  Pallas kernels: 12.2 us -> 14.6 us
  starting transfers between devices: 16 us -> 17 us
    ppermute x15, waiting for transfers between devices: 15.2 us -> 12.5 us  [swap(): return lax.ppermute(value, 'heads', [(i, i ^ bit) for i in range(devices)])]
    pallas_call x1 -> x2, Pallas kernels: 2.81 us -> 5.23 us  [the longest x1 2.62 us: run_delta(): pl.pallas_call(keys_kernel, out_shape=[per_head, per_head, lags[0], tap_b...]
    all_to_all x1, starting transfers between devices: 3.5 us -> 4.49 us  [on_device(): lax.all_to_all(sending, 'heads', split_axis=0, concat_axis=0, tiled=True)]
  transfers between devices with their start and end apart: 16 -> 16, of which waited for: 7 -> 7; matrix products, arithmetic and copies ran while one was open for 3% -> 3% of each run, Pallas kernels for 18% -> 22%
where the time goes in v11:
time: 57.9 us; the launch traced here: 57.6 us
  waiting for transfers between devices  19.3 us (33%)
  starting transfers between devices  17 us (29%)
  Pallas kernels  14.6 us (25%)
  local copies, waits for them, and re-layouts  5.54 us (10%)
  other arithmetic  0.66 us (1%)
    ppermute x15, waiting for transfers between devices, swap(): return lax.ppermute(value, 'heads', [(i, i ^ bit) for i in range(devices)])  12.5 us
    ppermute x15, starting transfers between devices, swap(): return lax.ppermute(value, 'heads', [(i, i ^ bit) for i in range(devices)])  12.5 us
    all_to_all x1, waiting for transfers between devices, on_device(): lax.all_to_all(sending, 'heads', split_axis=0, concat_axis=0, tiled=True)  6.72 us
    all_to_all x1, starting transfers between devices, on_device(): lax.all_to_all(sending, 'heads', split_axis=0, concat_axis=0, tiled=True)  4.49 us
    unnamed x20, local copies, waits for them, and re-layouts  3.76 us
    pallas_call x3, Pallas kernels, run_product(): pl.pallas_call(functools.partial(product_kernel, len(earlier), crossed),...  3.39 us
    pallas_call x6, Pallas kernels, run_combine(): pl.pallas_call(combine_kernel, out_shape=[jax.ShapeDtypeStruct((half, wid...  2.8 us
    pallas_call x1, Pallas kernels, run_delta(): pl.pallas_call(keys_kernel, out_shape=[per_head, per_head, lags[0], tap_b...  2.62 us
  transfers between devices with their start and end apart: 16, of which 7 were waited for; matrix products, arithmetic and copies ran while one was open for 3% of the time, Pallas kernels for 22%

profile of v11, /device:TPU:0, one launch (start us, length us, event | category | flops | bytes accessed | tf_op | source)
XLA Modules:
  0.0 57.6 jit_solution(17771423708421012841)
XLA Ops:
  0.0 0.5 collective-permute-start
  0.5 0.7 %fusion.6 = (bf16[4,384]{1,0:T(4,128)(2,1)S(1)}, bf16[4,384]{1,0:T(4,128)(2,1)S(1)}) fusion(bf16[4,768]{1,0:T(4,128)(2,1)} %param.13), kind=kLoop, calls=%fused_computation.27 | loop fusion | bytes 12288 | tf_op jit(solution)/shard_map/slice | solution.py:482
  1.2 2.6 %collective-permute-start.8 = (bf16[8,384]{1,0:T(8,128)(2,1)S(1)}, bf16[8,384]{1,0:T(8,128)(2,1)S(1)}, u32[]{:S(2)}, u32[]{:S(2)}) collective-permute-start(bf16[8,384]{1,0:T(8,128)(2,1)S(1)} %pad_maximum_fusion.1.first_ref), channel_id=1, source_target_pairs={{0,4},{1,5},{2,6},{3,7},{4,0},{5,1},{6,2},{7,3},{8,12},{9,13},{10,... | collective-permute-start | bytes 18440 | tf_op jit(solution)/shard_map/ppermute | solution.py:457
  4.0 2.0 %copy-done.1 = bf16[144,12288]{1,0:T(8,128)(2,1)S(1)} copy-done((bf16[144,12288]{1,0:T(8,128)(2,1)S(1)}, bf16[144,12288]{1,0:T(8,128)(2,1)}, u32[]{:S(2)}) %copy-start.1) | copy-done | bytes 3538968
  6.0 1.1 %copy-done.2 = bf16[32,4,2304]{2,1,0:T(4,128)(2,1)S(1)} copy-done((bf16[32,4,2304]{2,1,0:T(4,128)(2,1)S(1)}, bf16[32,4,2304]{2,1,0:T(4,128)(2,1)}, u32[]{:S(2)}) %copy-start.2) | copy-done | bytes 589848
  7.1 0.7 %copy-done.4 = s32[32]{0:T(128)S(1)} copy-done((s32[32]{0:T(128)S(1)}, s32[32]{0:T(128)}, u32[]{:S(2)}) %copy-start.4) | copy-done | bytes 152
  7.8 1.2 %token_rows.1 = (bf16[64,144]{1,0:T(8,128)(2,1)S(1)}, bf16[64,144]{1,0:T(8,128)(2,1)S(1)}, bf16[144,12288]{1,0:T(8,128)(2,1)S(1)}) custom-call(s32[1]{0:T(128)} %bitcast.me_ref.twist_ref, s32[1,32]{1,0:T(1,128)S(1)} %bitcast.14, bf16[32,4,2304]{2,1,0:T(4,128)(2,1)S(1)} %copy-done.2, bf16[144,12288]{1,0:T(8,128)(2,1)S(1)} %copy-done.1), custom_call_target="tpu_custom_call" | custom-call | tf_op jit(solution)/shard_map/token_rows/pallas_call | solution.py:340
  9.0 2.7 %collective-permute-start.9 = (bf16[16,384]{1,0:T(8,128)(2,1)S(1)}, bf16[16,384]{1,0:T(8,128)(2,1)S(1)}, u32[]{:S(2)}, u32[]{:S(2)}) collective-permute-start(bf16[16,384]{1,0:T(8,128)(2,1)S(1)} %join_taps.3.first_ref), channel_id=1, source_target_pairs={{0,8},{1,9},{2,10},{3,11},{4,12},{5,13},{6,14},{7,15},{8,0},{9,1},... | collective-permute-start | bytes 36872 | tf_op jit(solution)/shard_map/ppermute | solution.py:457
  11.7 0.8 %partial_product.3 = (f32[32,4096]{1,0:T(8,128)S(1)}, s16[32,4224]{1,0:T(8,128)(2,1)S(1)}) custom-call(bf16[64,144]{1,0:T(8,128)(2,1)S(1)} %get-tuple-element.39.refs_0_.refs_1_.earlier_ref, bf16[64,144]{1,0:T(8,128)(2,1)S(1)} %get-tuple-element.40.refs_1_.refs_2_, bf16[144,12288]{1,0:T(8,128)(2,1)S(1)} %get-tuple-element.41.refs_2_.refs_3_, ...), custom_call_target="tpu_custom_call" | custom-call | tf_op jit(solution)/shard_map/partial_product/pallas_call | solution.py:388
  12.5 1.6 %collective-permute-start.5 = (s16[32,4224]{1,0:T(8,128)(2,1)S(1)}, s16[32,4224]{1,0:T(8,128)(2,1)S(1)}, u32[]{:S(2)}, u32[]{:S(2)}) collective-permute-start(s16[32,4224]{1,0:T(8,128)(2,1)S(1)} %get-tuple-element.56), channel_id=1, source_target_pairs={{0,2},{1,3},{2,0},{3,1},{4,6},{5,7},{6,4},{7,5},{8,10},{9,11},{10,... | collective-permute-start | bytes 811016 | tf_op jit(solution)/shard_map/ppermute | solution.py:457
  14.1 1.7 %partial_product.4 = (f32[32,4352]{1,0:T(8,128)S(1)}, s16[32,4480]{1,0:T(8,128)(2,1)S(1)}) custom-call(f32[32,4096]{1,0:T(8,128)S(1)} %get-tuple-element.42.refs_0_.kept_ref, bf16[64,144]{1,0:T(8,128)(2,1)S(1)} %get-tuple-element.39.refs_0_.refs_1_.earlier_ref, bf16[64,144]{1,0:T(8,128)(2,1)S(1)} %get-tuple-element.40.refs_1_.refs_2_, ...), custom_call_target="tpu_custom_call" | custom-call | tf_op jit(solution)/shard_map/partial_product/pallas_call | solution.py:388
  15.9 0.8 %partial_product.5 = (f32[32,4096]{1,0:T(8,128)S(1)}, s16[32,4224]{1,0:T(8,128)(2,1)S(1)}) custom-call(f32[32,4352]{1,0:T(8,128)S(1)} %get-tuple-element.49.kept_ref.refs_0_, bf16[64,144]{1,0:T(8,128)(2,1)S(1)} %get-tuple-element.39.refs_0_.refs_1_.earlier_ref, bf16[64,144]{1,0:T(8,128)(2,1)S(1)} %get-tuple-element.40.refs_1_.refs_2_, ...), custom_call_target="tpu_custom_call" | custom-call | tf_op jit(solution)/shard_map/partial_product/pallas_call | solution.py:388
  16.8 0.5 collective-permute-start.11
  17.3 0.5 collective-permute-start.2
  18.3 3.6 %collective-permute-done.5.got_ref = s16[32,4224]{1,0:T(8,128)(2,1)S(1)} collective-permute-done((s16[32,4224]{1,0:T(8,128)(2,1)S(1)}, s16[32,4224]{1,0:T(8,128)(2,1)S(1)}, u32[]{:S(2)}, u32[]{:S(2)}) %collective-permute-start.5) | collective-permute-done | bytes 270368 | tf_op jit(solution)/shard_map/ppermute | solution.py:457
  21.9 0.5 combine.8
  22.5 3.7 %collective-permute-done.11.got_ref = s16[32,4224]{1,0:T(8,128)(2,1)S(1)} collective-permute-done((s16[32,4224]{1,0:T(8,128)(2,1)S(1)}, s16[32,4224]{1,0:T(8,128)(2,1)S(1)}, u32[]{:S(2)}, u32[]{:S(2)}) %collective-permute-start.11) | collective-permute-done | bytes 270368 | tf_op jit(solution)/shard_map/ppermute | solution.py:457
  26.2 0.5 combine.10
  26.7 0.4 collective-permute-start.12
  27.1 0.5 combine.6
  27.7 0.5 collective-permute-start.3
  28.4 1.5 %collective-permute-start.10 = (bf16[32,384]{1,0:T(8,128)(2,1)S(1)}, bf16[32,384]{1,0:T(8,128)(2,1)S(1)}, u32[]{:S(2)}, u32[]{:S(2)}) collective-permute-start(bf16[32,384]{1,0:T(8,128)(2,1)S(1)} %join_taps.4.first_ref), channel_id=1, source_target_pairs={{0,2},{1,3},{2,0},{3,1},{4,6},{5,7},{6,4},{7,5},{8,10},{9,11},{10,... | collective-permute-start | bytes 73736 | tf_op jit(solution)/shard_map/ppermute | solution.py:457
  30.5 1.2 %collective-permute-start.7 = (s16[16,2176]{1,0:T(8,128)(2,1)S(1)}, s16[16,2176]{1,0:T(8,128)(2,1)S(1)}, u32[]{:S(2)}, u32[]{:S(2)}) collective-permute-start(s16[16,2176]{1,0:T(8,128)(2,1)S(1)} %get-tuple-element.60), channel_id=1, source_target_pairs={{0,8},{1,9},{2,10},{3,11},{4,12},{5,13},{6,14},{7,15},{8,0},{9,1},... | collective-permute-start | bytes 208904 | tf_op jit(solution)/shard_map/ppermute | solution.py:457
  31.7 3.9 %collective-permute-done.12.got_ref = s16[16,4224]{1,0:T(8,128)(2,1)S(1)} collective-permute-done((s16[16,4224]{1,0:T(8,128)(2,1)S(1)}, s16[16,4224]{1,0:T(8,128)(2,1)S(1)}, u32[]{:S(2)}, u32[]{:S(2)}) %collective-permute-start.12) | collective-permute-done | bytes 135200 | tf_op jit(solution)/shard_map/ppermute | solution.py:457
  36.5 0.4 combine.7
  37.4 2.6 %keys_part.1 = (f32[32,8,128]{2,1,0:T(8,128)S(1)}, f32[32,8,128]{2,1,0:T(8,128)S(1)}, f32[3,32,8,128]{3,2,1,0:T(8,128)S(1)}, f32[32,4,384]{2,1,0:T(4,128)S(1)}) custom-call(s32[1]{0:T(128)} %bitcast.me_ref.twist_ref, f32[8,4096]{1,0:T(8,128)S(1)} %get-tuple-element.59.kept_ref, s16[16,2176]{1,0:T(8,128)(2,1)S(1)} %collective-permute-done.7.got_ref, ...), custom_call_target="tpu_custom_call" | custom-call | flops 20000000 | bytes 5000000 | tf_op jit(solution)/shard_map/keys_part/pallas_call | solution.py:269
  40.0 0.7 %collective-permute-done.14.got_ref = s16[16,2176]{1,0:T(8,128)(2,1)S(1)} collective-permute-done((s16[16,2176]{1,0:T(8,128)(2,1)S(1)}, s16[16,2176]{1,0:T(8,128)(2,1)S(1)}, u32[]{:S(2)}, u32[]{:S(2)}) %collective-permute-start.14) | collective-permute-done | bytes 69664 | tf_op jit(solution)/shard_map/ppermute | solution.py:457
  40.7 2.6 %queries_part.1 = (f32[32,8,128]{2,1,0:T(8,128)S(1)}, f32[4,32,8,128]{3,2,1,0:T(8,128)S(1)}) custom-call(s32[1]{0:T(128)} %bitcast.me_ref.twist_ref, f32[8,4096]{1,0:T(8,128)S(1)} %get-tuple-element.65.earlier_ref.kept_ref, s16[16,2176]{1,0:T(8,128)(2,1)S(1)} %collective-permute-done.14.got_ref, f32[8,12288]{1,0:T(8,128)S(1)} %pad_maximum_fusion.history_ref, ...), custom_call_target="tpu_custom_call" | custom-call | flops 20000000 | bytes 5000000 | tf_op jit(solution)/shard_map/queries_part/pallas_call | solution.py:277
  43.4 1.9 %values_part.1 = bf16[16,16,128]{2,1,0:T(8,128)(2,1)} custom-call(s32[64]{0:T(128)S(1)} %select_reduce_fusion.slots_ref, s32[64]{0:T(128)S(1)} %get-tuple-element.79.halves_ref, s32[2]{0:T(128)S(1)} %fusion.4.lengths_ref, s32[1]{0:T(128)} %bitcast.me_ref.twist_ref, f32[8,4352]{1,0:T(8,128)S(1)} %get-tuple-element.53.value_ref, ...), custom_call_target="tpu_custom_call" | custom-call | flops 4000000 | bytes 2000000 | tf_op jit(solution)/shard_map/values_part/pallas_call | solution.py:286
  45.3 4.5 %all-to-all-start = ((bf16[16,16,128]{2,1,0:T(8,128)(2,1)}), bf16[16,16,128]{2,1,0:T(8,128)(2,1)S(1)}, u32[]{:S(2)}, u32[]{:S(2)}) async-start(bf16[16,16,128]{2,1,0:T(8,128)(2,1)} %values_part.1), calls=%async_computation | async-start | bytes 131072 | tf_op jit(solution)/shard_map/all_to_all | solution.py:550
  50.0 6.7 %all-to-all-done = bf16[16,16,128]{2,1,0:T(8,128)(2,1)S(1)} async-done(((bf16[16,16,128]{2,1,0:T(8,128)(2,1)}), bf16[16,16,128]{2,1,0:T(8,128)(2,1)S(1)}, u32[]{:S(2)}, u32[]{:S(2)}) %all-to-all-start) | async-done | bytes 65568 | tf_op jit(solution)/shard_map/all_to_all | solution.py:550
  56.9 0.7 %reshape.46 = bf16[32,4,256]{2,1,0:T(4,128)(2,1)} reshape(bf16[128,256]{1,0:T(8,128)(2,1)S(1)} %convolution_convert_fusion) | data formatting | bytes 131072 | tf_op jit(solution)/shard_map/reshape | solution.py:561
  (53 shorter events, 3.2 us)
Async XLA Ops:
  0.0 11.7 %collective-permute-start = (bf16[144,12288]{1,0:T(8,128)(2,1)}, bf16[144,12288]{1,0:T(8,128)(2,1)S(1)}, u32[]{:S(2)}, u32[]{:S(2)}) collective-permute-start(bf16[144,12288]{1,0:T(8,128)(2,1)} %weight_hbm.1), channel_id=1, source_target_pairs={{0,1},{1,0},{2,3},{3,2},{4,5},{5,4},{6,7},{7,6},{8,9},{9,8},{10,11... | collective-permute-start | bytes 10616840 | tf_op jit(solution)/shard_map/ppermute | solution.py:457
  1.2 7.8 %collective-permute-start.8 = (bf16[8,384]{1,0:T(8,128)(2,1)S(1)}, bf16[8,384]{1,0:T(8,128)(2,1)S(1)}, u32[]{:S(2)}, u32[]{:S(2)}) collective-permute-start(bf16[8,384]{1,0:T(8,128)(2,1)S(1)} %pad_maximum_fusion.1.first_ref), channel_id=1, source_target_pairs={{0,4},{1,5},{2,6},{3,7},{4,0},{5,1},{6,2},{7,3},{8,12},{9,13},{10,... | collective-permute-start | bytes 18440 | tf_op jit(solution)/shard_map/ppermute | solution.py:457
  3.8 10.3 %collective-permute-start.1 = (bf16[64,144]{1,0:T(8,128)(2,1)}, bf16[64,144]{1,0:T(8,128)(2,1)}, u32[]{:S(2)}, u32[]{:S(2)}) collective-permute-start(bf16[64,144]{1,0:T(8,128)(2,1)} %bitcast.12), channel_id=1, source_target_pairs={{0,1},{1,0},{2,3},{3,2},{4,5},{5,4},{6,7},{7,6},{8,9},{9,8},{10,11... | collective-permute-start | bytes 55304 | tf_op jit(solution)/shard_map/ppermute | solution.py:457
  4.0 2.0 %copy-start.1 = (bf16[144,12288]{1,0:T(8,128)(2,1)S(1)}, bf16[144,12288]{1,0:T(8,128)(2,1)}, u32[]{:S(2)}) copy-start(bf16[144,12288]{1,0:T(8,128)(2,1)} %weight_hbm.1) | copy-start | bytes 10616836
  6.0 1.1 %copy-start.2 = (bf16[32,4,2304]{2,1,0:T(4,128)(2,1)S(1)}, bf16[32,4,2304]{2,1,0:T(4,128)(2,1)}, u32[]{:S(2)}) copy-start(bf16[32,4,2304]{2,1,0:T(4,128)(2,1)} %tokens_hbm.1) | copy-start | bytes 1769476
  7.1 0.7 %copy-start.4 = (s32[32]{0:T(128)S(1)}, s32[32]{0:T(128)}, u32[]{:S(2)}) copy-start(s32[32]{0:T(128)} %param.18) | copy-start | bytes 388
  9.0 19.4 %collective-permute-start.9 = (bf16[16,384]{1,0:T(8,128)(2,1)S(1)}, bf16[16,384]{1,0:T(8,128)(2,1)S(1)}, u32[]{:S(2)}, u32[]{:S(2)}) collective-permute-start(bf16[16,384]{1,0:T(8,128)(2,1)S(1)} %join_taps.3.first_ref), channel_id=1, source_target_pairs={{0,8},{1,9},{2,10},{3,11},{4,12},{5,13},{6,14},{7,15},{8,0},{9,1},... | collective-permute-start | bytes 36872 | tf_op jit(solution)/shard_map/ppermute | solution.py:457
  11.7 2.4 %copy-start.3 = (bf16[144,64]{0,1:T(8,128)(2,1)S(1)}, bf16[144,64]{0,1:T(8,128)(2,1)}, u32[]{:S(2)}) copy-start(bf16[144,64]{0,1:T(8,128)(2,1)} %param.12) | copy-start | bytes 55300
  12.5 9.4 %collective-permute-start.5 = (s16[32,4224]{1,0:T(8,128)(2,1)S(1)}, s16[32,4224]{1,0:T(8,128)(2,1)S(1)}, u32[]{:S(2)}, u32[]{:S(2)}) collective-permute-start(s16[32,4224]{1,0:T(8,128)(2,1)S(1)} %get-tuple-element.56), channel_id=1, source_target_pairs={{0,2},{1,3},{2,0},{3,1},{4,6},{5,7},{6,4},{7,5},{8,10},{9,11},{10,... | collective-permute-start | bytes 811016 | tf_op jit(solution)/shard_map/ppermute | solution.py:457
  15.9 1.9 %copy-start.6 = (f32[2,3,12288]{2,0,1:T(2,128)S(1)}, f32[2,3,12288]{2,0,1:T(2,128)}, u32[]{:S(2)}) copy-start(f32[2,3,12288]{2,0,1:T(2,128)} %param.15) | copy-start | bytes 884740
  15.9 2.4 %copy-start.5 = (s32[32]{0:T(128)S(1)}, s32[32]{0:T(128)}, u32[]{:S(2)}) copy-start(s32[32]{0:T(128)} %param.18) | copy-start | bytes 388
  15.9 2.4 %copy-start.8 = (s32[64]{0:T(128)S(1)}, s32[64]{0:T(128)}, u32[]{:S(2)}) copy-start(s32[64]{0:T(128)} %param.17) | copy-start | bytes 772
  16.7 11.5 %copy-start.7 = (s32[32]{0:T(128)S(1)}, s32[32]{0:T(128)}, u32[]{:S(2)}) copy-start(s32[32]{0:T(128)} %param.19) | copy-start | bytes 388
  16.7 13.2 %copy-start.9 = (s32[32]{0:T(128)S(1)}, s32[32]{0:T(128)}, u32[]{:S(2)}) copy-start(s32[32]{0:T(128)} %param.16) | copy-start | bytes 388
  16.7 20.6 %copy-start = (f32[2,32,128,128]{3,2,1,0:T(8,128)S(1)}, f32[2,32,128,128]{3,2,1,0:T(8,128)}, u32[]{:S(2)}) copy-start(f32[2,32,128,128]{3,2,1,0:T(8,128)} %state_hbm.3) | copy-start | bytes 12582916
  16.8 9.5 %collective-permute-start.11 = (s16[32,4224]{1,0:T(8,128)(2,1)S(1)}, s16[32,4224]{1,0:T(8,128)(2,1)S(1)}, u32[]{:S(2)}, u32[]{:S(2)}) collective-permute-start(s16[32,4224]{1,0:T(8,128)(2,1)S(1)} %get-tuple-element.62), channel_id=1, source_target_pairs={{0,4},{1,5},{2,6},{3,7},{4,0},{5,1},{6,2},{7,3},{8,12},{9,13},{10,... | collective-permute-start | bytes 811016 | tf_op jit(solution)/shard_map/ppermute | solution.py:457
  17.3 9.9 %collective-permute-start.2 = (s16[32,4480]{1,0:T(8,128)(2,1)S(1)}, s16[32,4480]{1,0:T(8,128)(2,1)S(1)}, u32[]{:S(2)}, u32[]{:S(2)}) collective-permute-start(s16[32,4480]{1,0:T(8,128)(2,1)S(1)} %get-tuple-element.50), channel_id=1, source_target_pairs={{0,2},{1,3},{2,0},{3,1},{4,6},{5,7},{6,4},{7,5},{8,10},{9,11},{10,... | collective-permute-start | bytes 860168 | tf_op jit(solution)/shard_map/ppermute | solution.py:457
  22.5 7.6 %collective-permute-start.6 = (s16[16,4224]{1,0:T(8,128)(2,1)S(1)}, s16[16,4224]{1,0:T(8,128)(2,1)S(1)}, u32[]{:S(2)}, u32[]{:S(2)}) collective-permute-start(s16[16,4224]{1,0:T(8,128)(2,1)S(1)} %get-tuple-element.58), channel_id=1, source_target_pairs={{0,4},{1,5},{2,6},{3,7},{4,0},{5,1},{6,2},{7,3},{8,12},{9,13},{10,... | collective-permute-start | bytes 405512 | tf_op jit(solution)/shard_map/ppermute | solution.py:457
  26.7 8.9 %collective-permute-start.12 = (s16[16,4224]{1,0:T(8,128)(2,1)S(1)}, s16[16,4224]{1,0:T(8,128)(2,1)S(1)}, u32[]{:S(2)}, u32[]{:S(2)}) collective-permute-start(s16[16,4224]{1,0:T(8,128)(2,1)S(1)} %get-tuple-element.64), channel_id=1, source_target_pairs={{0,8},{1,9},{2,10},{3,11},{4,12},{5,13},{6,14},{7,15},{8,0},{9,1},... | collective-permute-start | bytes 405512 | tf_op jit(solution)/shard_map/ppermute | solution.py:457
  27.7 8.7 %collective-permute-start.3 = (s16[16,4480]{1,0:T(8,128)(2,1)S(1)}, s16[16,4480]{1,0:T(8,128)(2,1)S(1)}, u32[]{:S(2)}, u32[]{:S(2)}) collective-permute-start(s16[16,4480]{1,0:T(8,128)(2,1)S(1)} %get-tuple-element.52), channel_id=1, source_target_pairs={{0,4},{1,5},{2,6},{3,7},{4,0},{5,1},{6,2},{7,3},{8,12},{9,13},{10,... | collective-permute-start | bytes 430088 | tf_op jit(solution)/shard_map/ppermute | solution.py:457
  28.4 7.6 %collective-permute-start.10 = (bf16[32,384]{1,0:T(8,128)(2,1)S(1)}, bf16[32,384]{1,0:T(8,128)(2,1)S(1)}, u32[]{:S(2)}, u32[]{:S(2)}) collective-permute-start(bf16[32,384]{1,0:T(8,128)(2,1)S(1)} %join_taps.4.first_ref), channel_id=1, source_target_pairs={{0,2},{1,3},{2,0},{3,1},{4,6},{5,7},{6,4},{7,5},{8,10},{9,11},{10,... | collective-permute-start | bytes 73736 | tf_op jit(solution)/shard_map/ppermute | solution.py:457
  30.5 6.9 %collective-permute-start.7 = (s16[16,2176]{1,0:T(8,128)(2,1)S(1)}, s16[16,2176]{1,0:T(8,128)(2,1)S(1)}, u32[]{:S(2)}, u32[]{:S(2)}) collective-permute-start(s16[16,2176]{1,0:T(8,128)(2,1)S(1)} %get-tuple-element.60), channel_id=1, source_target_pairs={{0,8},{1,9},{2,10},{3,11},{4,12},{5,13},{6,14},{7,15},{8,0},{9,1},... | collective-permute-start | bytes 208904 | tf_op jit(solution)/shard_map/ppermute | solution.py:457
  36.1 1.3 %collective-permute-start.13 = (bf16[64,384]{1,0:T(8,128)(2,1)S(1)}, bf16[64,384]{1,0:T(8,128)(2,1)S(1)}, u32[]{:S(2)}, u32[]{:S(2)}) collective-permute-start(bf16[64,384]{1,0:T(8,128)(2,1)S(1)} %join_taps.5.near_ref), channel_id=1, source_target_pairs={{0,1},{1,0},{2,3},{3,2},{4,5},{5,4},{6,7},{7,6},{8,9},{9,8},{10,11... | collective-permute-start | bytes 147464 | tf_op jit(solution)/shard_map/ppermute | solution.py:457
  36.1 4.6 %collective-permute-start.14 = (s16[16,2176]{1,0:T(8,128)(2,1)S(1)}, s16[16,2176]{1,0:T(8,128)(2,1)S(1)}, u32[]{:S(2)}, u32[]{:S(2)}) collective-permute-start(s16[16,2176]{1,0:T(8,128)(2,1)S(1)} %get-tuple-element.67), channel_id=1, source_target_pairs={{0,2},{1,3},{2,0},{3,1},{4,6},{5,7},{6,4},{7,5},{8,10},{9,11},{10,... | collective-permute-start | bytes 208904 | tf_op jit(solution)/shard_map/ppermute | solution.py:457
  36.9 6.5 %collective-permute-start.4 = (s16[16,2304]{1,0:T(8,128)(2,1)S(1)}, s16[16,2304]{1,0:T(8,128)(2,1)S(1)}, u32[]{:S(2)}, u32[]{:S(2)}) collective-permute-start(s16[16,2304]{1,0:T(8,128)(2,1)S(1)} %get-tuple-element.54), channel_id=1, source_target_pairs={{0,8},{1,9},{2,10},{3,11},{4,12},{5,13},{6,14},{7,15},{8,0},{9,1},... | collective-permute-start | bytes 221192 | tf_op jit(solution)/shard_map/ppermute | solution.py:457
  45.3 11.4 %all-to-all-start = ((bf16[16,16,128]{2,1,0:T(8,128)(2,1)}), bf16[16,16,128]{2,1,0:T(8,128)(2,1)S(1)}, u32[]{:S(2)}, u32[]{:S(2)}) async-start(bf16[16,16,128]{2,1,0:T(8,128)(2,1)} %values_part.1), calls=%async_computation | async-start | bytes 131072 | tf_op jit(solution)/shard_map/all_to_all | solution.py:550

commit v12 on v9

--- a/solution.py
+++ b/solution.py
@@ -497,7 +497,7 @@
         for at in range(3):
             kept[at], packed = run_combine(kept[at], got[at])
             got[at] = swap(packed, routes[at][level], devices)
-            if ride and at == 2 - level:
+            if ride and at == level:
                 taps = join(taps, far, kept[at])
                 far = swap(taps, 3 - level, devices)
     if ride:

time: 57.1 us -> 56.8 us (level)
  transfers between devices with their start and end apart: 16 -> 16, of which waited for: 7 -> 6; matrix products, arithmetic and copies ran while one was open for 3% -> 3% of each run, Pallas kernels for 18% -> 18%
where the time goes in v12:
time: 56.8 us; the launch traced here: 56.4 us
  waiting for transfers between devices  21.5 us (38%)
  starting transfers between devices  16 us (28%)
  Pallas kernels  12.2 us (21%)
  local copies, waits for them, and re-layouts  5.54 us (10%)
  other arithmetic  0.66 us (1%)
    ppermute x15, waiting for transfers between devices, swap(): return lax.ppermute(value, 'heads', [(i, i ^ bit) for i in range(devices)])  14.8 us
    ppermute x15, starting transfers between devices, swap(): return lax.ppermute(value, 'heads', [(i, i ^ bit) for i in range(devices)])  12.5 us
    all_to_all x1, waiting for transfers between devices, on_device(): lax.all_to_all(sending, 'heads', split_axis=0, concat_axis=0, tiled=True)  6.68 us
    unnamed x20, local copies, waits for them, and re-layouts  3.76 us
    all_to_all x1, starting transfers between devices, on_device(): lax.all_to_all(sending, 'heads', split_axis=0, concat_axis=0, tiled=True)  3.5 us
    pallas_call x3, Pallas kernels, run_product(): pl.pallas_call(functools.partial(product_kernel, len(earlier), crossed),...  3.39 us
    pallas_call x1, Pallas kernels, run_delta(): pl.pallas_call(keys_kernel, out_shape=[per_head] * 2 + lags + [tap_blocks...  2.81 us
    pallas_call x6, Pallas kernels, run_combine(): pl.pallas_call(combine_kernel, out_shape=[jax.ShapeDtypeStruct((half, wid...  2.8 us
  transfers between devices with their start and end apart: 16, of which 6 were waited for; matrix products, arithmetic and copies ran while one was open for 3% of the time, Pallas kernels for 18%

profile of v12, /device:TPU:0, one launch (start us, length us, event | category | flops | bytes accessed | tf_op | source)
XLA Modules:
  0.0 56.4 jit_solution(15773292122272557145)
XLA Ops:
  0.0 0.5 collective-permute-start
  0.5 0.7 %fusion.6 = (bf16[4,384]{1,0:T(4,128)(2,1)S(1)}, bf16[4,384]{1,0:T(4,128)(2,1)S(1)}) fusion(bf16[4,768]{1,0:T(4,128)(2,1)} %param.13), kind=kLoop, calls=%fused_computation.27 | loop fusion | bytes 12288 | tf_op jit(solution)/shard_map/slice | solution.py:452
  1.2 2.6 %collective-permute-start.11 = (bf16[8,384]{1,0:T(8,128)(2,1)S(1)}, bf16[8,384]{1,0:T(8,128)(2,1)S(1)}, u32[]{:S(2)}, u32[]{:S(2)}) collective-permute-start(bf16[8,384]{1,0:T(8,128)(2,1)S(1)} %pad_maximum_fusion.1.first_ref), channel_id=1, source_target_pairs={{0,4},{1,5},{2,6},{3,7},{4,0},{5,1},{6,2},{7,3},{8,12},{9,13},{10,... | collective-permute-start | bytes 18440 | tf_op jit(solution)/shard_map/ppermute | solution.py:427
  4.0 2.0 %copy-done.1 = bf16[144,12288]{1,0:T(8,128)(2,1)S(1)} copy-done((bf16[144,12288]{1,0:T(8,128)(2,1)S(1)}, bf16[144,12288]{1,0:T(8,128)(2,1)}, u32[]{:S(2)}) %copy-start.1) | copy-done | bytes 3538968
  6.0 1.1 %copy-done.2 = bf16[32,4,2304]{2,1,0:T(4,128)(2,1)S(1)} copy-done((bf16[32,4,2304]{2,1,0:T(4,128)(2,1)S(1)}, bf16[32,4,2304]{2,1,0:T(4,128)(2,1)}, u32[]{:S(2)}) %copy-start.2) | copy-done | bytes 589848
  7.1 0.7 %copy-done.4 = s32[32]{0:T(128)S(1)} copy-done((s32[32]{0:T(128)S(1)}, s32[32]{0:T(128)}, u32[]{:S(2)}) %copy-start.4) | copy-done | bytes 152
  7.8 1.2 %token_rows.1 = (bf16[64,144]{1,0:T(8,128)(2,1)S(1)}, bf16[64,144]{1,0:T(8,128)(2,1)S(1)}, bf16[144,12288]{1,0:T(8,128)(2,1)S(1)}) custom-call(s32[1]{0:T(128)} %bitcast.me_ref.twist_ref, s32[1,32]{1,0:T(1,128)S(1)} %bitcast.14, bf16[32,4,2304]{2,1,0:T(4,128)(2,1)S(1)} %copy-done.2, bf16[144,12288]{1,0:T(8,128)(2,1)S(1)} %copy-done.1), custom_call_target="tpu_custom_call" | custom-call | tf_op jit(solution)/shard_map/token_rows/pallas_call | solution.py:310
  9.0 2.7 %collective-permute-start.12 = (bf16[16,384]{1,0:T(8,128)(2,1)S(1)}, bf16[16,384]{1,0:T(8,128)(2,1)S(1)}, u32[]{:S(2)}, u32[]{:S(2)}) collective-permute-start(bf16[16,384]{1,0:T(8,128)(2,1)S(1)} %join_taps.3.first_ref), channel_id=1, source_target_pairs={{0,8},{1,9},{2,10},{3,11},{4,12},{5,13},{6,14},{7,15},{8,0},{9,1},... | collective-permute-start | bytes 36872 | tf_op jit(solution)/shard_map/ppermute | solution.py:427
  11.7 0.8 %partial_product.3 = (f32[32,4096]{1,0:T(8,128)S(1)}, s16[32,4224]{1,0:T(8,128)(2,1)S(1)}) custom-call(bf16[64,144]{1,0:T(8,128)(2,1)S(1)} %get-tuple-element.38.refs_0_.refs_1_.earlier_ref, bf16[64,144]{1,0:T(8,128)(2,1)S(1)} %get-tuple-element.39.refs_1_.refs_2_, bf16[144,12288]{1,0:T(8,128)(2,1)S(1)} %get-tuple-element.40.refs_2_.refs_3_, ...), custom_call_target="tpu_custom_call" | custom-call | tf_op jit(solution)/shard_map/partial_product/pallas_call | solution.py:358
  12.5 1.6 %collective-permute-start.8 = (s16[32,4224]{1,0:T(8,128)(2,1)S(1)}, s16[32,4224]{1,0:T(8,128)(2,1)S(1)}, u32[]{:S(2)}, u32[]{:S(2)}) collective-permute-start(s16[32,4224]{1,0:T(8,128)(2,1)S(1)} %get-tuple-element.61), channel_id=1, source_target_pairs={{0,2},{1,3},{2,0},{3,1},{4,6},{5,7},{6,4},{7,5},{8,10},{9,11},{10,... | collective-permute-start | bytes 811016 | tf_op jit(solution)/shard_map/ppermute | solution.py:427
  14.1 1.7 %partial_product.4 = (f32[32,4352]{1,0:T(8,128)S(1)}, s16[32,4480]{1,0:T(8,128)(2,1)S(1)}) custom-call(f32[32,4096]{1,0:T(8,128)S(1)} %get-tuple-element.41.refs_0_.kept_ref, bf16[64,144]{1,0:T(8,128)(2,1)S(1)} %get-tuple-element.38.refs_0_.refs_1_.earlier_ref, bf16[64,144]{1,0:T(8,128)(2,1)S(1)} %get-tuple-element.39.refs_1_.refs_2_, ...), custom_call_target="tpu_custom_call" | custom-call | tf_op jit(solution)/shard_map/partial_product/pallas_call | solution.py:358
  15.9 0.8 %partial_product.5 = (f32[32,4096]{1,0:T(8,128)S(1)}, s16[32,4224]{1,0:T(8,128)(2,1)S(1)}) custom-call(f32[32,4352]{1,0:T(8,128)S(1)} %get-tuple-element.48.kept_ref.refs_0_, bf16[64,144]{1,0:T(8,128)(2,1)S(1)} %get-tuple-element.38.refs_0_.refs_1_.earlier_ref, bf16[64,144]{1,0:T(8,128)(2,1)S(1)} %get-tuple-element.39.refs_1_.refs_2_, ...), custom_call_target="tpu_custom_call" | custom-call | tf_op jit(solution)/shard_map/partial_product/pallas_call | solution.py:358
  16.8 0.5 collective-permute-start.5
  17.3 0.5 collective-permute-start.2
  18.3 3.6 %collective-permute-done.8.got_ref = s16[32,4224]{1,0:T(8,128)(2,1)S(1)} collective-permute-done((s16[32,4224]{1,0:T(8,128)(2,1)S(1)}, s16[32,4224]{1,0:T(8,128)(2,1)S(1)}, u32[]{:S(2)}, u32[]{:S(2)}) %collective-permute-start.8) | collective-permute-done | bytes 270368 | tf_op jit(solution)/shard_map/ppermute | solution.py:427
  21.9 0.5 combine.10
  22.5 3.7 %collective-permute-done.5.got_ref = s16[32,4224]{1,0:T(8,128)(2,1)S(1)} collective-permute-done((s16[32,4224]{1,0:T(8,128)(2,1)S(1)}, s16[32,4224]{1,0:T(8,128)(2,1)S(1)}, u32[]{:S(2)}, u32[]{:S(2)}) %collective-permute-start.5) | collective-permute-done | bytes 270368 | tf_op jit(solution)/shard_map/ppermute | solution.py:427
  26.2 0.5 combine.8
  26.7 0.4 collective-permute-start.6
  27.1 0.5 combine.6
  27.7 0.5 collective-permute-start.3
  28.4 1.5 %collective-permute-start.13 = (bf16[32,384]{1,0:T(8,128)(2,1)S(1)}, bf16[32,384]{1,0:T(8,128)(2,1)S(1)}, u32[]{:S(2)}, u32[]{:S(2)}) collective-permute-start(bf16[32,384]{1,0:T(8,128)(2,1)S(1)} %join_taps.4.first_ref), channel_id=1, source_target_pairs={{0,2},{1,3},{2,0},{3,1},{4,6},{5,7},{6,4},{7,5},{8,10},{9,11},{10,... | collective-permute-start | bytes 73736 | tf_op jit(solution)/shard_map/ppermute | solution.py:427
  30.1 0.4 combine.11
  30.5 1.2 %collective-permute-start.10 = (s16[16,2176]{1,0:T(8,128)(2,1)S(1)}, s16[16,2176]{1,0:T(8,128)(2,1)S(1)}, u32[]{:S(2)}, u32[]{:S(2)}) collective-permute-start(s16[16,2176]{1,0:T(8,128)(2,1)S(1)} %get-tuple-element.65), channel_id=1, source_target_pairs={{0,8},{1,9},{2,10},{3,11},{4,12},{5,13},{6,14},{7,15},{8,0},{9,1},... | collective-permute-start | bytes 208904 | tf_op jit(solution)/shard_map/ppermute | solution.py:427
  31.7 3.9 %collective-permute-done.6.got_ref = s16[16,4224]{1,0:T(8,128)(2,1)S(1)} collective-permute-done((s16[16,4224]{1,0:T(8,128)(2,1)S(1)}, s16[16,4224]{1,0:T(8,128)(2,1)S(1)}, u32[]{:S(2)}, u32[]{:S(2)}) %collective-permute-start.6) | collective-permute-done | bytes 135200 | tf_op jit(solution)/shard_map/ppermute | solution.py:427
  36.5 0.4 combine.7
  37.1 3.3 %collective-permute-done.7.query_got_ref = s16[16,2176]{1,0:T(8,128)(2,1)S(1)} collective-permute-done((s16[16,2176]{1,0:T(8,128)(2,1)S(1)}, s16[16,2176]{1,0:T(8,128)(2,1)S(1)}, u32[]{:S(2)}, u32[]{:S(2)}) %collective-permute-start.7) | collective-permute-done | bytes 69664 | tf_op jit(solution)/shard_map/ppermute | solution.py:427
  40.4 2.8 %keys_part.1 = (f32[32,8,128]{2,1,0:T(8,128)S(1)}, f32[32,8,128]{2,1,0:T(8,128)S(1)}, f32[3,32,8,128]{3,2,1,0:T(8,128)S(1)}, f32[4,32,8,128]{3,2,1,0:T(8,128)S(1)}, f32[32,4,384]{2,1,0:T(4,128)S(1)}) custom-call(s32[1]{0:T(128)} %bitcast.me_ref.twist_ref, f32[8,4096]{1,0:T(8,128)S(1)} %get-tuple-element.59.query_ref, ...), custom_call_target="tpu_custom_call" | custom-call | flops 40000000 | bytes 9000000 | tf_op jit(solution)/shard_map/keys_part/pallas_call | solution.py:243
  43.2 1.9 %values_part.1 = bf16[16,16,128]{2,1,0:T(8,128)(2,1)} custom-call(s32[64]{0:T(128)S(1)} %select_reduce_fusion.slots_ref, s32[64]{0:T(128)S(1)} %get-tuple-element.77.halves_ref, s32[2]{0:T(128)S(1)} %fusion.4.lengths_ref, s32[1]{0:T(128)} %bitcast.me_ref.twist_ref, f32[8,4352]{1,0:T(8,128)S(1)} %get-tuple-element.52.earlier_ref.value_ref, ...), custom_call_target="tpu_custom_call" | custom-call | flops 4000000 | bytes 2000000 | tf_op jit(solution)/shard_map/values_part/pallas_call | solution.py:256
  45.2 3.5 %all-to-all-start = ((bf16[16,16,128]{2,1,0:T(8,128)(2,1)}), bf16[16,16,128]{2,1,0:T(8,128)(2,1)S(1)}, u32[]{:S(2)}, u32[]{:S(2)}) async-start(bf16[16,16,128]{2,1,0:T(8,128)(2,1)} %values_part.1), calls=%async_computation | async-start | bytes 131072 | tf_op jit(solution)/shard_map/all_to_all | solution.py:520
  48.9 6.7 %all-to-all-done = bf16[16,16,128]{2,1,0:T(8,128)(2,1)S(1)} async-done(((bf16[16,16,128]{2,1,0:T(8,128)(2,1)}), bf16[16,16,128]{2,1,0:T(8,128)(2,1)S(1)}, u32[]{:S(2)}, u32[]{:S(2)}) %all-to-all-start) | async-done | bytes 65568 | tf_op jit(solution)/shard_map/all_to_all | solution.py:520
  55.8 0.7 %reshape.46 = bf16[32,4,256]{2,1,0:T(4,128)(2,1)} reshape(bf16[128,256]{1,0:T(8,128)(2,1)S(1)} %convolution_convert_fusion) | data formatting | bytes 131072 | tf_op jit(solution)/shard_map/reshape | solution.py:531
  (52 shorter events, 2.6 us)
Async XLA Ops:
  0.0 11.7 %collective-permute-start = (bf16[144,12288]{1,0:T(8,128)(2,1)}, bf16[144,12288]{1,0:T(8,128)(2,1)S(1)}, u32[]{:S(2)}, u32[]{:S(2)}) collective-permute-start(bf16[144,12288]{1,0:T(8,128)(2,1)} %weight_hbm.1), channel_id=1, source_target_pairs={{0,1},{1,0},{2,3},{3,2},{4,5},{5,4},{6,7},{7,6},{8,9},{9,8},{10,11... | collective-permute-start | bytes 10616840 | tf_op jit(solution)/shard_map/ppermute | solution.py:427
  1.2 7.8 %collective-permute-start.11 = (bf16[8,384]{1,0:T(8,128)(2,1)S(1)}, bf16[8,384]{1,0:T(8,128)(2,1)S(1)}, u32[]{:S(2)}, u32[]{:S(2)}) collective-permute-start(bf16[8,384]{1,0:T(8,128)(2,1)S(1)} %pad_maximum_fusion.1.first_ref), channel_id=1, source_target_pairs={{0,4},{1,5},{2,6},{3,7},{4,0},{5,1},{6,2},{7,3},{8,12},{9,13},{10,... | collective-permute-start | bytes 18440 | tf_op jit(solution)/shard_map/ppermute | solution.py:427
  3.8 10.3 %collective-permute-start.1 = (bf16[64,144]{1,0:T(8,128)(2,1)}, bf16[64,144]{1,0:T(8,128)(2,1)}, u32[]{:S(2)}, u32[]{:S(2)}) collective-permute-start(bf16[64,144]{1,0:T(8,128)(2,1)} %bitcast.12), channel_id=1, source_target_pairs={{0,1},{1,0},{2,3},{3,2},{4,5},{5,4},{6,7},{7,6},{8,9},{9,8},{10,11... | collective-permute-start | bytes 55304 | tf_op jit(solution)/shard_map/ppermute | solution.py:427
  4.0 2.0 %copy-start.1 = (bf16[144,12288]{1,0:T(8,128)(2,1)S(1)}, bf16[144,12288]{1,0:T(8,128)(2,1)}, u32[]{:S(2)}) copy-start(bf16[144,12288]{1,0:T(8,128)(2,1)} %weight_hbm.1) | copy-start | bytes 10616836
  6.0 1.1 %copy-start.2 = (bf16[32,4,2304]{2,1,0:T(4,128)(2,1)S(1)}, bf16[32,4,2304]{2,1,0:T(4,128)(2,1)}, u32[]{:S(2)}) copy-start(bf16[32,4,2304]{2,1,0:T(4,128)(2,1)} %tokens_hbm.1) | copy-start | bytes 1769476
  7.1 0.7 %copy-start.4 = (s32[32]{0:T(128)S(1)}, s32[32]{0:T(128)}, u32[]{:S(2)}) copy-start(s32[32]{0:T(128)} %param.18) | copy-start | bytes 388
  9.0 19.4 %collective-permute-start.12 = (bf16[16,384]{1,0:T(8,128)(2,1)S(1)}, bf16[16,384]{1,0:T(8,128)(2,1)S(1)}, u32[]{:S(2)}, u32[]{:S(2)}) collective-permute-start(bf16[16,384]{1,0:T(8,128)(2,1)S(1)} %join_taps.3.first_ref), channel_id=1, source_target_pairs={{0,8},{1,9},{2,10},{3,11},{4,12},{5,13},{6,14},{7,15},{8,0},{9,1},... | collective-permute-start | bytes 36872 | tf_op jit(solution)/shard_map/ppermute | solution.py:427
  11.7 2.4 %copy-start.3 = (bf16[144,64]{0,1:T(8,128)(2,1)S(1)}, bf16[144,64]{0,1:T(8,128)(2,1)}, u32[]{:S(2)}) copy-start(bf16[144,64]{0,1:T(8,128)(2,1)} %param.12) | copy-start | bytes 55300
  12.5 9.4 %collective-permute-start.8 = (s16[32,4224]{1,0:T(8,128)(2,1)S(1)}, s16[32,4224]{1,0:T(8,128)(2,1)S(1)}, u32[]{:S(2)}, u32[]{:S(2)}) collective-permute-start(s16[32,4224]{1,0:T(8,128)(2,1)S(1)} %get-tuple-element.61), channel_id=1, source_target_pairs={{0,2},{1,3},{2,0},{3,1},{4,6},{5,7},{6,4},{7,5},{8,10},{9,11},{10,... | collective-permute-start | bytes 811016 | tf_op jit(solution)/shard_map/ppermute | solution.py:427
  15.9 1.9 %copy-start.6 = (f32[2,3,12288]{2,0,1:T(2,128)S(1)}, f32[2,3,12288]{2,0,1:T(2,128)}, u32[]{:S(2)}) copy-start(f32[2,3,12288]{2,0,1:T(2,128)} %param.15) | copy-start | bytes 884740
  15.9 2.4 %copy-start.5 = (s32[32]{0:T(128)S(1)}, s32[32]{0:T(128)}, u32[]{:S(2)}) copy-start(s32[32]{0:T(128)} %param.18) | copy-start | bytes 388
  15.9 2.4 %copy-start.8 = (s32[64]{0:T(128)S(1)}, s32[64]{0:T(128)}, u32[]{:S(2)}) copy-start(s32[64]{0:T(128)} %param.17) | copy-start | bytes 772
  16.7 11.5 %copy-start.7 = (s32[32]{0:T(128)S(1)}, s32[32]{0:T(128)}, u32[]{:S(2)}) copy-start(s32[32]{0:T(128)} %param.19) | copy-start | bytes 388
  16.7 13.2 %copy-start.9 = (s32[32]{0:T(128)S(1)}, s32[32]{0:T(128)}, u32[]{:S(2)}) copy-start(s32[32]{0:T(128)} %param.16) | copy-start | bytes 388
  16.7 23.7 %copy-start = (f32[2,32,128,128]{3,2,1,0:T(8,128)S(1)}, f32[2,32,128,128]{3,2,1,0:T(8,128)}, u32[]{:S(2)}) copy-start(f32[2,32,128,128]{3,2,1,0:T(8,128)} %state_hbm.1) | copy-start | bytes 12582916
  16.8 9.5 %collective-permute-start.5 = (s16[32,4224]{1,0:T(8,128)(2,1)S(1)}, s16[32,4224]{1,0:T(8,128)(2,1)S(1)}, u32[]{:S(2)}, u32[]{:S(2)}) collective-permute-start(s16[32,4224]{1,0:T(8,128)(2,1)S(1)} %get-tuple-element.56), channel_id=1, source_target_pairs={{0,4},{1,5},{2,6},{3,7},{4,0},{5,1},{6,2},{7,3},{8,12},{9,13},{10,... | collective-permute-start | bytes 811016 | tf_op jit(solution)/shard_map/ppermute | solution.py:427
  17.3 9.9 %collective-permute-start.2 = (s16[32,4480]{1,0:T(8,128)(2,1)S(1)}, s16[32,4480]{1,0:T(8,128)(2,1)S(1)}, u32[]{:S(2)}, u32[]{:S(2)}) collective-permute-start(s16[32,4480]{1,0:T(8,128)(2,1)S(1)} %get-tuple-element.49), channel_id=1, source_target_pairs={{0,2},{1,3},{2,0},{3,1},{4,6},{5,7},{6,4},{7,5},{8,10},{9,11},{10,... | collective-permute-start | bytes 860168 | tf_op jit(solution)/shard_map/ppermute | solution.py:427
  22.5 7.6 %collective-permute-start.9 = (s16[16,4224]{1,0:T(8,128)(2,1)S(1)}, s16[16,4224]{1,0:T(8,128)(2,1)S(1)}, u32[]{:S(2)}, u32[]{:S(2)}) collective-permute-start(s16[16,4224]{1,0:T(8,128)(2,1)S(1)} %get-tuple-element.63), channel_id=1, source_target_pairs={{0,4},{1,5},{2,6},{3,7},{4,0},{5,1},{6,2},{7,3},{8,12},{9,13},{10,... | collective-permute-start | bytes 405512 | tf_op jit(solution)/shard_map/ppermute | solution.py:427
  26.7 8.9 %collective-permute-start.6 = (s16[16,4224]{1,0:T(8,128)(2,1)S(1)}, s16[16,4224]{1,0:T(8,128)(2,1)S(1)}, u32[]{:S(2)}, u32[]{:S(2)}) collective-permute-start(s16[16,4224]{1,0:T(8,128)(2,1)S(1)} %get-tuple-element.58), channel_id=1, source_target_pairs={{0,8},{1,9},{2,10},{3,11},{4,12},{5,13},{6,14},{7,15},{8,0},{9,1},... | collective-permute-start | bytes 405512 | tf_op jit(solution)/shard_map/ppermute | solution.py:427
  27.7 8.7 %collective-permute-start.3 = (s16[16,4480]{1,0:T(8,128)(2,1)S(1)}, s16[16,4480]{1,0:T(8,128)(2,1)S(1)}, u32[]{:S(2)}, u32[]{:S(2)}) collective-permute-start(s16[16,4480]{1,0:T(8,128)(2,1)S(1)} %get-tuple-element.51), channel_id=1, source_target_pairs={{0,4},{1,5},{2,6},{3,7},{4,0},{5,1},{6,2},{7,3},{8,12},{9,13},{10,... | collective-permute-start | bytes 430088 | tf_op jit(solution)/shard_map/ppermute | solution.py:427
  28.4 8.5 %collective-permute-start.13 = (bf16[32,384]{1,0:T(8,128)(2,1)S(1)}, bf16[32,384]{1,0:T(8,128)(2,1)S(1)}, u32[]{:S(2)}, u32[]{:S(2)}) collective-permute-start(bf16[32,384]{1,0:T(8,128)(2,1)S(1)} %join_taps.4.first_ref), channel_id=1, source_target_pairs={{0,2},{1,3},{2,0},{3,1},{4,6},{5,7},{6,4},{7,5},{8,10},{9,11},{10,... | collective-permute-start | bytes 73736 | tf_op jit(solution)/shard_map/ppermute | solution.py:427
  30.5 6.7 %collective-permute-start.10 = (s16[16,2176]{1,0:T(8,128)(2,1)S(1)}, s16[16,2176]{1,0:T(8,128)(2,1)S(1)}, u32[]{:S(2)}, u32[]{:S(2)}) collective-permute-start(s16[16,2176]{1,0:T(8,128)(2,1)S(1)} %get-tuple-element.65), channel_id=1, source_target_pairs={{0,8},{1,9},{2,10},{3,11},{4,12},{5,13},{6,14},{7,15},{8,0},{9,1},... | collective-permute-start | bytes 208904 | tf_op jit(solution)/shard_map/ppermute | solution.py:427
  36.0 4.4 %collective-permute-start.7 = (s16[16,2176]{1,0:T(8,128)(2,1)S(1)}, s16[16,2176]{1,0:T(8,128)(2,1)S(1)}, u32[]{:S(2)}, u32[]{:S(2)}) collective-permute-start(s16[16,2176]{1,0:T(8,128)(2,1)S(1)} %get-tuple-element.60), channel_id=1, source_target_pairs={{0,2},{1,3},{2,0},{3,1},{4,6},{5,7},{6,4},{7,5},{8,10},{9,11},{10,... | collective-permute-start | bytes 208904 | tf_op jit(solution)/shard_map/ppermute | solution.py:427
  36.9 3.5 %collective-permute-start.14 = (bf16[64,384]{1,0:T(8,128)(2,1)S(1)}, bf16[64,384]{1,0:T(8,128)(2,1)S(1)}, u32[]{:S(2)}, u32[]{:S(2)}) collective-permute-start(bf16[64,384]{1,0:T(8,128)(2,1)S(1)} %join_taps.5.near_ref), channel_id=1, source_target_pairs={{0,1},{1,0},{2,3},{3,2},{4,5},{5,4},{6,7},{7,6},{8,9},{9,8},{10,11... | collective-permute-start | bytes 147464 | tf_op jit(solution)/shard_map/ppermute | solution.py:427
  37.0 6.3 %collective-permute-start.4 = (s16[16,2304]{1,0:T(8,128)(2,1)S(1)}, s16[16,2304]{1,0:T(8,128)(2,1)S(1)}, u32[]{:S(2)}, u32[]{:S(2)}) collective-permute-start(s16[16,2304]{1,0:T(8,128)(2,1)S(1)} %get-tuple-element.53), channel_id=1, source_target_pairs={{0,8},{1,9},{2,10},{3,11},{4,12},{5,13},{6,14},{7,15},{8,0},{9,1},... | collective-permute-start | bytes 221192 | tf_op jit(solution)/shard_map/ppermute | solution.py:427
  45.2 10.4 %all-to-all-start = ((bf16[16,16,128]{2,1,0:T(8,128)(2,1)}), bf16[16,16,128]{2,1,0:T(8,128)(2,1)S(1)}, u32[]{:S(2)}, u32[]{:S(2)}) async-start(bf16[16,16,128]{2,1,0:T(8,128)(2,1)} %values_part.1), calls=%async_computation | async-start | bytes 131072 | tf_op jit(solution)/shard_map/all_to_all | solution.py:520
